TPU v7x, 32 devices: a whole 2x2x4 slice. The times are simulated.
32 devices in a mesh: gx: 8 (over y, x, core), gy: 4 (over z).
Axes of the slice: x: 2, y: 2, z: 4, core: 2. Of those that a mesh axis runs over, the one named last changes fastest.
Arguments:
- concentration: float32 [32, 256, 128], P('gx', 'gy'), may hold values from -4 to 4
- potential: float32 [32, 256, 128], P('gx', 'gy'), may hold values from -4 to 4
- mass_source: float32 [32, 256, 128], P('gx', 'gy'), may hold values from -7 to 7
- potential_source: float32 [32, 256, 128], P('gx', 'gy'), may hold values from -7 to 7
- pore_mask: int32 [32, 256, 128], P('gx', 'gy'), may hold values 0 or 1
- mobility_class: int32 [32, 256, 128], P('gx', 'gy'), may hold values from 0 to 7
- mobility_table: float32 [8], replicated, may hold values from 0.05 to 1
- owner_map: int32 [8, 256], P(None, 'gy'), may hold values from 0 to 7, as said below
Outputs:
- conc_out: float32 [32, 256, 128], P('gx', 'gy')
- pot_out: float32 [32, 256, 128], P('gx', 'gy')
Inputs may be any that keep to these rules, and one draw needn't show every extreme that they name: `owner_map`: no owner is named by more than 16 entries of one device; in every draw, for each gy index, one owner is named by exactly 16 entries of every device of that gy index.
All inputs are finite; a program needn't handle non-finite values. No bound on the sum of `pore_mask` on one device may be relied on, other than what follows from the above.
Results may differ from a plain program's by a relative error of at most 0.000058.
Values sent between devices are 32-bit elements; how exact they have to be, the bound alone decides.
No kernel may reach another device: no remote copies, remote signals or barrier semaphores. Data moves between devices by JAX's collectives and lax.ppermute only.
A program may use at most 64 MiB of HBM per device.

v0:
```python
import functools

import jax
import jax.numpy as jnp
from jax import lax
from jax.experimental import pallas as pl
from jax.experimental.pallas import tpu as pltpu
from jax.sharding import PartitionSpec as P

CSWEEP = 3

time_step = 0.25
split_slope = 1.0
interface = 0.5
relax_fine = 0.6
relax_coarse = 0.6
coarse_flux = 0.0625
coarse_bend = 0.125
coarse_det = 1.0 + 2.0 * coarse_flux * (split_slope + 2.0 * coarse_bend)

F32 = jnp.float32
BF16 = jnp.bfloat16
VMEM_LIMIT = 48 * 1024 * 1024
LARGE_LIMIT = 60 * 1024 * 1024


def iota(shape, dim):
    return lax.broadcasted_iota(jnp.int32, shape, dim)


def x_pair(field, low, high):
    return (
        jnp.concatenate([low, field[:-1]], axis=0),
        jnp.concatenate([field[1:], high], axis=0),
    )


def y_pair(field, low, high):
    size = field.shape[1]
    where = iota(field.shape, 1)
    return (
        jnp.where(where == 0, low, pltpu.roll(field, 1, 1)),
        jnp.where(where == size - 1, high, pltpu.roll(field, size - 1, 1)),
    )


def plane_pair(field):
    size = field.shape[2]
    where = iota(field.shape, 2)
    return (
        jnp.where(where == 0, 0.0, pltpu.roll(field, 1, 2)),
        jnp.where(where == size - 1, 0.0, pltpu.roll(field, size - 1, 2)),
    )


def neighbours(field, halo):
    xm, xp, ym, yp = halo
    return (*x_pair(field, xm, xp), *y_pair(field, ym, yp), *plane_pair(field))


def excess_of(conc, pot, conc_halo, pot_halo, faces, mass_source, pot_source):
    flux = jnp.zeros_like(pot)
    for face, other in zip(faces, neighbours(pot, pot_halo)):
        flux = flux + face * (other - pot)
    laplace = -6.0 * conc
    for other in neighbours(conc, conc_halo):
        laplace = laplace + other
    excess_mass = mass_source - (conc - time_step * flux)
    excess_pot = pot_source - (pot - split_slope * conc + interface * laplace)
    return excess_mass, excess_pot


def relax_pair(conc, pot, excess_mass, excess_pot, diagonal):
    other_diagonal = -(split_slope + 6.0 * interface)
    scale = relax_fine / (1.0 - diagonal * other_diagonal)
    new_conc = conc + (excess_mass - diagonal * excess_pot) * scale
    new_pot = pot + (excess_pot - other_diagonal * excess_mass) * scale
    return new_conc, new_pot


def faces_of(mobility, halo):
    faces = tuple(0.5 * (mobility + other) for other in neighbours(mobility, halo))
    diagonal = faces[0]
    for face in faces[1:]:
        diagonal = diagonal + face
    return faces, time_step * diagonal


def split_dot(ones, values, contract):
    dims = (contract, ((), ()))
    total = None
    rest = values
    for _ in range(3):
        term = rest.astype(BF16)
        rest = rest - term.astype(F32)
        part = lax.dot_general(ones, term, dims, preferred_element_type=F32)
        total = part if total is None else total + part
    return total


def round_up(value, unit):
    return -(-value // unit) * unit


class Plan:
    def __init__(self, shape, owners, groups):
        self.x, self.y, self.p = shape
        self.owners, self.groups = owners, groups
        self.half_x, self.half_y = self.x // 2, self.y // 2
        self.id_row = 3 * self.x
        self.count_row = round_up(self.id_row + self.half_x, 8)
        self.y_rows = self.count_row + owners
        self.cells = self.x * self.y
        self.rows = self.cells + 2 * self.y


def side_rows(plan, rows, which):
    return rows[which * plan.y : (which + 1) * plan.y][None]


def side_columns(plan, rows, which):
    return rows[which * plan.x : (which + 1) * plan.x][:, None]


def column_of(plan):
    shape = (plan.rows, plan.half_x * plan.half_y)
    row = iota(shape, 0)
    x = row // plan.y
    y = row % plan.y
    own = (x // 2) * plan.half_y + y // 2
    low = (plan.half_x - 1) * plan.half_y + y // 2
    high = y // 2
    column = jnp.where(x < plan.x, own, jnp.where(x == plan.x, low, high))
    return row, column == iota(shape, 1)


def owner_hits(plan, owner_ref):
    g = lax.axis_index("gx")
    last = plan.owners - 1
    owner = iota((plan.owners, plan.half_x * plan.half_y), 0)
    own = owner_ref[pl.ds(g, 1), :] == owner
    low = (owner_ref[pl.ds(jnp.maximum(g - 1, 0), 1), :] == owner) & (g > 0)
    high = (owner_ref[pl.ds(jnp.minimum(g + 1, last), 1), :] == owner) & (g < last)
    return own, low, high


def membership(plan, owner_ref):
    row, column = column_of(plan)
    spans = ((0, plan.cells), (plan.cells, plan.cells + plan.y), (plan.cells + plan.y, plan.rows))
    gather, spread = None, None
    for (begin, end), hits in zip(spans, owner_hits(plan, owner_ref)):
        place = (column & (row >= begin) & (row < end)).astype(F32).astype(BF16)
        hits = hits.astype(F32).astype(BF16)
        nt = (((1,), (1,)), ((), ()))
        part = lax.dot_general(hits, place, nt, preferred_element_type=F32)
        gather = part if gather is None else gather + part
        part = lax.dot_general(place, hits, nt, preferred_element_type=F32)
        spread = part if spread is None else spread + part
    return gather.astype(BF16), spread


def prepare_kernel(
    plan, conc_hbm, pot_hbm, mask_hbm, class_hbm, owner_hbm, table_hbm,
    mob_ref, x_low_ref, x_high_ref, y_low_ref, y_high_ref,
    conc_ref, pot_ref, owner_ref, mask_ref, class_ref, table_ref, sems,
):
    pairs = (
        (table_hbm, table_ref), (class_hbm, class_ref), (mask_hbm, mask_ref),
        (conc_hbm, conc_ref), (pot_hbm, pot_ref), (owner_hbm, owner_ref),
    )
    copies = [
        pltpu.make_async_copy(source, target, sems.at[i])
        for i, (source, target) in enumerate(pairs)
    ]
    for copy in copies:
        copy.start()
    for copy in copies:
        copy.wait()
    kind = class_ref[...]
    values = jnp.zeros(kind.shape, F32)
    for marker in range(table_ref.shape[0]):
        values = jnp.where(kind == marker, table_ref[marker], values)
    mobility = mask_ref[...].astype(F32) * values
    mob_ref[...] = mobility
    fields = (conc_ref[...], pot_ref[...], mobility)
    for which, field in enumerate(fields):
        x_low_ref[pl.ds(which * plan.y, plan.y), :] = field[0]
        x_high_ref[pl.ds(which * plan.y, plan.y), :] = field[plan.x - 1]
        for x in range(plan.x):
            y_low_ref[pl.ds(which * plan.x + x, 1), :] = field[x, 0:1]
            y_high_ref[pl.ds(which * plan.x + x, 1), :] = field[x, plan.y - 1 : plan.y]
    columns = plan.half_x * plan.half_y
    owner = iota((plan.owners, columns), 0)
    hits = jnp.zeros((plan.owners, columns), F32)
    for g in range(plan.owners):
        hits = hits + (owner_ref[g : g + 1, :] == owner).astype(F32)
    count = jnp.broadcast_to(jnp.sum(hits, axis=1, keepdims=True), (plan.owners, plan.p))
    own = owner_ref[pl.ds(lax.axis_index("gx"), 1), :].astype(F32)
    for ref, at in ((y_low_ref, 0), (y_high_ref, plan.half_y - 1)):
        ref[pl.ds(plan.count_row, plan.owners), :] = count
        ref[pl.ds(plan.id_row, plan.count_row - plan.id_row), :] = jnp.zeros(
            (plan.count_row - plan.id_row, plan.p), F32
        )
        for i in range(plan.half_x):
            b = i * plan.half_y + at
            ref[pl.ds(plan.id_row + i, 1), :] = jnp.broadcast_to(own[:, b : b + 1], (1, plan.p))


def first_kernel(
    plan, conc_ref, pot_ref, mob_ref, mass_ref, pots_ref, x_low_ref, x_high_ref,
    y_low_ref, y_high_ref, owner_ref,
    conc_out, pot_out, total_out, spread_out, x_low_out, x_high_out, y_low_out, y_high_out,
):
    sides = (x_low_ref[...], x_high_ref[...])
    ends = (y_low_ref[...], y_high_ref[...])

    def halo(which):
        return tuple(side_rows(plan, rows, which) for rows in sides) + tuple(
            side_columns(plan, rows, which) for rows in ends
        )

    mobility, mob_halo = mob_ref[...], halo(2)
    faces, diagonal = faces_of(mobility, mob_halo)
    mass_source, pot_source = mass_ref[...], pots_ref[...]
    conc, pot = conc_ref[...], pot_ref[...]
    excess = excess_of(conc, pot, halo(0), halo(1), faces, mass_source, pot_source)
    conc, pot = relax_pair(conc, pot, *excess, diagonal)
    conc_out[...] = conc
    pot_out[...] = pot
    x_low_out[...] = jnp.concatenate([conc[0], pot[0]], axis=0)
    x_high_out[...] = jnp.concatenate([conc[plan.x - 1], pot[plan.x - 1]], axis=0)
    for which, field in enumerate((conc, pot)):
        for x in range(plan.x):
            y_low_out[pl.ds(which * plan.x + x, 1), :] = field[x, 0:1]
            y_high_out[pl.ds(which * plan.x + x, 1), :] = field[x, plan.y - 1 : plan.y]

    nothing = tuple(jnp.zeros_like(part) for part in mob_halo)
    own_mass, own_pot = excess_of(conc, pot, nothing, nothing, faces, mass_source, pot_source)
    give_mass = [own_mass.reshape(plan.cells, plan.p)]
    give_pot = [own_pot.reshape(plan.cells, plan.p)]
    for x, side in ((0, 0), (plan.x - 1, 1)):
        face = 0.5 * (mobility[x] + mob_halo[side][0])
        give_mass.append(time_step * face * pot[x])
        give_pot.append(-interface * conc[x])
    gather, spread = membership(plan, owner_ref)
    spread_out[...] = spread
    give = jnp.concatenate(
        [jnp.concatenate(give_mass, axis=0), jnp.concatenate(give_pot, axis=0)], axis=1
    )
    total = split_dot(gather, give, ((1,), (0,)))

    def packed(both):
        mass, other = both[:, : plan.p], both[:, plan.p :]
        even = iota(mass.shape, 1) % 2 == 0
        return jnp.where(
            even, mass + pltpu.roll(mass, plan.p - 1, 1), other + pltpu.roll(other, 1, 1)
        )

    owner = iota((plan.owners, 1), 0)
    h = lax.axis_index("gy")

    def scale_of(count):
        return 0.125 / jnp.maximum(count, 1.0)

    def put(place, values):
        total_out[pl.ds(place * plan.owners, plan.owners), :] = values

    own_hits = jnp.zeros((plan.owners, plan.half_x * plan.half_y), F32)
    owner_grid = iota(own_hits.shape, 0)
    for g in range(plan.owners):
        own_hits = own_hits + (owner_ref[g : g + 1, :] == owner_grid).astype(F32)
    own_count = jnp.sum(own_hits, axis=1, keepdims=True)
    put(1, packed(total) * scale_of(own_count))
    for place, y, side in ((0, 0, 2), (2, plan.y - 1, 3)):
        rows = ends[side - 2]
        inside = (h > 0) if place == 0 else (h < plan.groups - 1)
        edge_mob = jnp.concatenate([mobility[x, y : y + 1] for x in range(plan.x)], axis=0)
        edge_pot = jnp.concatenate([pot[x, y : y + 1] for x in range(plan.x)], axis=0)
        edge_conc = jnp.concatenate([conc[x, y : y + 1] for x in range(plan.x)], axis=0)
        face = 0.5 * (edge_mob + mob_halo[side][:, 0])
        both = jnp.concatenate([time_step * face * edge_pot, -interface * edge_conc], axis=1)
        part = jnp.zeros((plan.owners, 2 * plan.p), F32)
        for i in range(plan.half_x):
            ident = rows[plan.id_row + i : plan.id_row + i + 1, 0:1].astype(jnp.int32)
            pair = both[2 * i : 2 * i + 1] + both[2 * i + 1 : 2 * i + 2]
            part = part + jnp.where((owner == ident) & inside, pair, 0.0)
        put(place, packed(part) * scale_of(rows[plan.count_row : plan.count_row + plan.owners]))


def coarse_solve(packed, planes):
    lane = iota(packed.shape, 1)
    even = lane % 2 == 0
    mass_mean = jnp.where(even, packed, pltpu.roll(packed, 1, 1))
    pot_mean = jnp.where(even, pltpu.roll(packed, planes - 1, 1), packed)

    def neighbour_sum(values):
        return jnp.where(lane >= 2, pltpu.roll(values, 2, 1), 0.0) + jnp.where(
            lane < planes - 2, pltpu.roll(values, planes - 2, 1), 0.0
        )

    coarse_conc = jnp.zeros_like(mass_mean)
    coarse_pot = jnp.zeros_like(pot_mean)
    for _ in range(CSWEEP):
        mass_gap = mass_mean - (
            coarse_conc + coarse_flux * (2.0 * coarse_pot - neighbour_sum(coarse_pot))
        )
        pot_gap = pot_mean - (
            coarse_pot
            - split_slope * coarse_conc
            + coarse_bend * (neighbour_sum(coarse_conc) - 2.0 * coarse_conc)
        )
        coarse_conc = coarse_conc + (relax_coarse / coarse_det) * (
            mass_gap - 2.0 * coarse_flux * pot_gap
        )
        coarse_pot = coarse_pot + (relax_coarse / coarse_det) * (
            pot_gap + (split_slope + 2.0 * coarse_bend) * mass_gap
        )
    return coarse_conc, coarse_pot


def last_kernel(
    plan, conc_ref, pot_ref, mob_ref, mass_ref, pots_ref, x_low_mob, x_high_mob,
    y_low_msg, y_high_msg, x_low_ref, x_high_ref, y_low_ref, y_high_ref, total_ref, spread_ref,
    conc_out, pot_out, frame,
):
    h = lax.axis_index("gy")
    frame[...] = jnp.zeros_like(frame)
    for group in range(plan.groups):
        part = total_ref[0, group]
        for i in range(1, total_ref.shape[0]):
            part = part + total_ref[i, group]
        frame[pl.ds(group * plan.owners, 3 * plan.owners), :] += part
    base = pl.multiple_of(h * plan.owners, 8)
    means = frame[pl.ds(base, 3 * plan.owners), :]
    solved = jnp.concatenate(coarse_solve(means, plan.p), axis=1)
    own = split_dot(
        spread_ref[...].astype(BF16), solved[plan.owners : 2 * plan.owners], ((1,), (0,))
    )
    owner = iota((plan.owners, 1), 0)

    def edge_correction(place, rows, inside):
        part = solved[place * plan.owners : (place + 1) * plan.owners]
        out = []
        for i in range(plan.half_x):
            ident = rows[plan.id_row + i : plan.id_row + i + 1, 0:1].astype(jnp.int32)
            row = jnp.sum(jnp.where((owner == ident) & inside, part, 0.0), axis=0, keepdims=True)
            out += [row, row]
        return jnp.concatenate(out, axis=0)

    y_corr = (
        edge_correction(0, y_low_msg[...], h > 0),
        edge_correction(2, y_high_msg[...], h < plan.groups - 1),
    )

    def updated(which, ref):
        lanes = slice(which * plan.p, (which + 1) * plan.p)
        corr = own[:, lanes]
        field = ref[...] + corr[: plan.cells].reshape(plan.x, plan.y, plan.p)
        halo = []
        for side, rows in enumerate((x_low_ref[...], x_high_ref[...])):
            begin = plan.cells + side * plan.y
            halo.append(side_rows(plan, rows, which) + corr[begin : begin + plan.y][None])
        for rows, edge in zip((y_low_ref[...], y_high_ref[...]), y_corr):
            halo.append((rows[which * plan.x : (which + 1) * plan.x] + edge[:, lanes])[:, None])
        return field, halo

    conc, conc_halo = updated(0, conc_ref)
    pot, pot_halo = updated(1, pot_ref)
    mob_halo = (
        x_low_mob[pl.ds(2 * plan.y, plan.y), :][None],
        x_high_mob[pl.ds(2 * plan.y, plan.y), :][None],
        side_columns(plan, y_low_msg[...], 2),
        side_columns(plan, y_high_msg[...], 2),
    )
    faces, diagonal = faces_of(mob_ref[...], mob_halo)
    excess = excess_of(conc, pot, conc_halo, pot_halo, faces, mass_ref[...], pots_ref[...])
    conc_out[...], pot_out[...] = relax_pair(conc, pot, *excess, diagonal)


def call(kernel, plan, outs, args, far=(), scratch=(), limit=VMEM_LIMIT):
    return pl.pallas_call(
        functools.partial(kernel, plan),
        out_shape=[jax.ShapeDtypeStruct(shape, F32) for shape in outs],
        in_specs=[
            pl.BlockSpec(memory_space=pl.ANY if i in far else pltpu.VMEM)
            for i in range(len(args))
        ],
        out_specs=[pl.BlockSpec(memory_space=pltpu.VMEM)] * len(outs),
        scratch_shapes=list(scratch),
        compiler_params=pltpu.CompilerParams(vmem_limit_bytes=limit),
    )(*args)


def swap_sides(low, high, axis):
    count = lax.axis_size(axis)
    from_below = lax.ppermute(high, axis, [(i, i + 1) for i in range(count - 1)])
    from_above = lax.ppermute(low, axis, [(i + 1, i) for i in range(count - 1)])
    return from_below, from_above


def gather_totals(plan, total):
    if plan.owners * plan.groups <= 64:
        parts = lax.all_gather(total, ("gx", "gy"))
        return parts.reshape(plan.owners, plan.groups, *total.shape)
    parts = lax.all_gather(lax.psum(total, "gx"), "gy")
    return parts[None]


def on_device(conc, pot, mass_source, pot_source, mask, kind, table, owner_map):
    plan = Plan(conc.shape, lax.axis_size("gx"), lax.axis_size("gy"))
    block = conc.shape
    mob, x_low, x_high, y_low, y_high = call(
        prepare_kernel,
        plan,
        [block, *[(3 * plan.y, plan.p)] * 2, *[(plan.y_rows, plan.p)] * 2],
        [conc, pot, mask, kind, owner_map, table],
        far=range(6),
        limit=LARGE_LIMIT,
        scratch=(
            pltpu.VMEM(block, F32),
            pltpu.VMEM(block, F32),
            pltpu.VMEM(owner_map.shape, owner_map.dtype),
            pltpu.VMEM(block, mask.dtype),
            pltpu.VMEM(block, kind.dtype),
            pltpu.SMEM(table.shape, table.dtype),
            pltpu.SemaphoreType.DMA((6,)),
        ),
    )
    x_low, x_high = swap_sides(x_low, x_high, "gx")
    y_low, y_high = swap_sides(y_low, y_high, "gy")
    conc, pot, total, spread, x_low1, x_high1, y_low1, y_high1 = call(
        first_kernel,
        plan,
        [
            block,
            block,
            (3 * plan.owners, plan.p),
            (plan.rows, plan.owners),
            *[(2 * plan.y, plan.p)] * 2,
            *[(2 * plan.x, plan.p)] * 2,
        ],
        [conc, pot, mob, mass_source, pot_source, x_low, x_high, y_low, y_high, owner_map],
    )
    total = gather_totals(plan, total)
    x_low1, x_high1 = swap_sides(x_low1, x_high1, "gx")
    y_low1, y_high1 = swap_sides(y_low1, y_high1, "gy")
    return tuple(
        call(
            last_kernel,
            plan,
            [block, block],
            [
                conc, pot, mob, mass_source, pot_source, x_low, x_high, y_low, y_high,
                x_low1, x_high1, y_low1, y_high1, total, spread,
            ],
            scratch=[pltpu.VMEM(((plan.groups + 2) * plan.owners, plan.p), F32)],
        )
    )


def solution(mesh):
    grid = P("gx", "gy", None)
    return jax.shard_map(
        on_device,
        mesh=mesh,
        in_specs=(grid,) * 6 + (P(), P(None, "gy")),
        out_specs=(grid, grid),
        check_vma=False,
    )
```

profile of v0, /device:TPU:0, one launch (start us, length us, event | category | flops | bytes accessed | tf_op | source)
XLA Modules:
  0.0 102.8 jit_solution(2354958646000295244)
XLA Ops:
  0.6 0.0 copy-start.1
  0.6 0.0 copy-start
  0.7 0.0 copy-start.3
  0.7 0.0 copy-start.2
  0.7 2.0 %shard_map.95 = (f32[4,64,128]{2,1,0:T(8,128)}, f32[192,128]{1,0:T(8,128)}, f32[192,128]{1,0:T(8,128)}, f32[24,128]{1,0:T(8,128)}, f32[24,128]{1,0:T(8,128)}) custom-call(f32[4,64,128]{2,1,0:T(8,128)} %conc_ref.1, f32[4,64,128]{2,1,0:T(8,128)} %pot_ref.1, s32[4,64,128]{2,1,0:T(8,128)} %mask_hbm.1, s32[4,64,128]{2,1,0:T(8,128)} %class_hbm.1, ...), custom_call_target="tpu_custom_call" | custom-call | tf_op jit(solution)/shard_map/pallas_call | solution.py:381
  2.7 0.0 copy-start.5
  2.7 2.4 %collective-permute-start = (f32[192,128]{1,0:T(8,128)}, f32[192,128]{1,0:T(8,128)S(1)}, u32[]{:S(2)}, u32[]{:S(2)}) collective-permute-start(f32[192,128]{1,0:T(8,128)} %get-tuple-element.16), channel_id=1, source_target_pairs={{0,4},{4,8},{8,12},{12,16},{16,20},{20,24},{24,28},{1,5},{5,9},{9,... | collective-permute-start | bytes 294920 | tf_op jit(solution)/shard_map/ppermute | solution.py:396
  5.1 1.3 %collective-permute-start.1 = (f32[192,128]{1,0:T(8,128)}, f32[192,128]{1,0:T(8,128)S(1)}, u32[]{:S(2)}, u32[]{:S(2)}) collective-permute-start(f32[192,128]{1,0:T(8,128)} %get-tuple-element.17), channel_id=1, source_target_pairs={{4,0},{8,4},{12,8},{16,12},{20,16},{24,20},{28,24},{5,1},{9,5},{13... | collective-permute-start | bytes 294920 | tf_op jit(solution)/shard_map/ppermute | solution.py:397
  6.4 4.3 %collective-permute-start.2 = (f32[24,128]{1,0:T(8,128)}, f32[24,128]{1,0:T(8,128)S(1)}, u32[]{:S(2)}, u32[]{:S(2)}) collective-permute-start(f32[24,128]{1,0:T(8,128)} %get-tuple-element.18), channel_id=1, source_target_pairs={{0,1},{1,2},{2,3},{4,5},{5,6},{6,7},{8,9},{9,10},{10,11},{12,13},{... | collective-permute-start | bytes 36872 | tf_op jit(solution)/shard_map/ppermute | solution.py:396
  10.7 1.3 %collective-permute-start.3 = (f32[24,128]{1,0:T(8,128)}, f32[24,128]{1,0:T(8,128)S(1)}, u32[]{:S(2)}, u32[]{:S(2)}) collective-permute-start(f32[24,128]{1,0:T(8,128)} %get-tuple-element.19), channel_id=1, source_target_pairs={{1,0},{2,1},{3,2},{5,4},{6,5},{7,6},{9,8},{10,9},{11,10},{13,12},{... | collective-permute-start | bytes 36872 | tf_op jit(solution)/shard_map/ppermute | solution.py:397
  12.0 0.3 collective-permute-done.2.y_low_ref.y_low_msg
  12.3 4.2 %collective-permute-done.3.y_high_ref.y_high_msg = f32[24,128]{1,0:T(8,128)S(1)} collective-permute-done((f32[24,128]{1,0:T(8,128)}, f32[24,128]{1,0:T(8,128)S(1)}, u32[]{:S(2)}, u32[]{:S(2)}) %collective-permute-start.3) | collective-permute-done | bytes 12320 | tf_op jit(solution)/shard_map/ppermute | solution.py:397
  16.5 0.0 collective-permute-done.x_low_ref.x_low_mob
  16.5 0.0 collective-permute-done.1.x_high_ref.x_high_mob
  16.5 0.0 copy-done.1
  16.5 0.0 copy-done
  16.5 0.0 copy-done.3
  16.5 0.0 copy-done.2
  16.5 0.0 copy-done.5
  16.5 0.0 copy-start.4
  16.5 0.9 copy-done.4
  17.4 1.0 shard_map.96
  18.4 3.5 %collective-permute-start.6 = (f32[8,128]{1,0:T(8,128)S(1)}, f32[8,128]{1,0:T(8,128)S(1)}, u32[]{:S(2)}, u32[]{:S(2)}) collective-permute-start(f32[8,128]{1,0:T(8,128)S(1)} %get-tuple-element.24), channel_id=1, source_target_pairs={{0,1},{1,2},{2,3},{4,5},{5,6},{6,7},{8,9},{9,10},{10,11},{12,13},{... | collective-permute-start | bytes 12296 | tf_op jit(solution)/shard_map/ppermute | solution.py:396
  22.0 1.3 %collective-permute-start.7 = (f32[8,128]{1,0:T(8,128)S(1)}, f32[8,128]{1,0:T(8,128)S(1)}, u32[]{:S(2)}, u32[]{:S(2)}) collective-permute-start(f32[8,128]{1,0:T(8,128)S(1)} %get-tuple-element.25), channel_id=1, source_target_pairs={{1,0},{2,1},{3,2},{5,4},{6,5},{7,6},{9,8},{10,9},{11,10},{13,12},{... | collective-permute-start | bytes 12296 | tf_op jit(solution)/shard_map/ppermute | solution.py:397
  23.3 2.6 %collective-permute-start.4 = (f32[128,128]{1,0:T(8,128)S(1)}, f32[128,128]{1,0:T(8,128)S(1)}, u32[]{:S(2)}, u32[]{:S(2)}) collective-permute-start(f32[128,128]{1,0:T(8,128)S(1)} %get-tuple-element.22), channel_id=1, source_target_pairs={{0,4},{4,8},{8,12},{12,16},{16,20},{20,24},{24,28},{1,5},{5,9},{9,... | collective-permute-start | bytes 196616 | tf_op jit(solution)/shard_map/ppermute | solution.py:396
  25.9 1.3 %collective-permute-start.5 = (f32[128,128]{1,0:T(8,128)S(1)}, f32[128,128]{1,0:T(8,128)S(1)}, u32[]{:S(2)}, u32[]{:S(2)}) collective-permute-start(f32[128,128]{1,0:T(8,128)S(1)} %get-tuple-element.23), channel_id=1, source_target_pairs={{4,0},{8,4},{12,8},{16,12},{20,16},{24,20},{28,24},{5,1},{9,5},{13... | collective-permute-start | bytes 196616 | tf_op jit(solution)/shard_map/ppermute | solution.py:397
  27.2 74.2 %all-gather = f32[768,128]{1,0:T(8,128)S(1)} all-gather(f32[24,128]{1,0:T(8,128)S(1)} %get-tuple-element.26), channel_id=2, replica_groups=mesh['gx'=8,'gy'=4] {'gx','gy'}, dimensions={0}, use_global_device_ids=true | all-gather | bytes 405504 | tf_op jit(solution)/shard_map/all_gather | solution.py:403
  101.3 0.0 collective-permute-done.6.y_low_ref
  101.3 0.0 collective-permute-done.7.y_high_ref
  101.3 0.0 collective-permute-done.4.x_low_ref
  101.3 0.0 collective-permute-done.5.x_high_ref
  101.4 1.5 %shard_map.97 = (f32[4,64,128]{2,1,0:T(8,128)}, f32[4,64,128]{2,1,0:T(8,128)}) custom-call(f32[4,64,128]{2,1,0:T(8,128)S(1)} %get-tuple-element.20.conc_ref, f32[4,64,128]{2,1,0:T(8,128)S(1)} %get-tuple-element.21.pot_ref, f32[4,64,128]{2,1,0:T(8,128)S(1)} %copy-done.4, f32[4,64,128]{2,1,0:T(8,128)S(1)} %copy-done.2, f32[4,64,128]{2,1,0:T(8,128)S(1)} %copy-done.3, ...), custom_call_target="tpu_custom_call" | custom-call | tf_op jit(solution)/shard_map/pallas_call | solution.py:381
Async XLA Ops:
  0.6 15.9 %copy-start.1 = (f32[4,64,128]{2,1,0:T(8,128)S(1)}, f32[4,64,128]{2,1,0:T(8,128)}, u32[]{:S(2)}) copy-start(f32[4,64,128]{2,1,0:T(8,128)} %pot_ref.1) | copy-start | bytes 393220
  0.6 15.9 %copy-start = (f32[4,64,128]{2,1,0:T(8,128)S(1)}, f32[4,64,128]{2,1,0:T(8,128)}, u32[]{:S(2)}) copy-start(f32[4,64,128]{2,1,0:T(8,128)} %conc_ref.1) | copy-start | bytes 393220
  0.7 15.9 %copy-start.3 = (f32[4,64,128]{2,1,0:T(8,128)S(1)}, f32[4,64,128]{2,1,0:T(8,128)}, u32[]{:S(2)}) copy-start(f32[4,64,128]{2,1,0:T(8,128)} %pots_ref.3) | copy-start | bytes 393220
  0.7 15.9 %copy-start.2 = (f32[4,64,128]{2,1,0:T(8,128)S(1)}, f32[4,64,128]{2,1,0:T(8,128)}, u32[]{:S(2)}) copy-start(f32[4,64,128]{2,1,0:T(8,128)} %mass_ref.3) | copy-start | bytes 393220
  2.7 13.8 %copy-start.5 = (s32[8,64]{1,0:T(8,128)S(1)}, s32[8,64]{1,0:T(8,128)}, u32[]{:S(2)}) copy-start(s32[8,64]{1,0:T(8,128)} %owner_ref.1) | copy-start | bytes 6148
  2.7 13.8 %collective-permute-start = (f32[192,128]{1,0:T(8,128)}, f32[192,128]{1,0:T(8,128)S(1)}, u32[]{:S(2)}, u32[]{:S(2)}) collective-permute-start(f32[192,128]{1,0:T(8,128)} %get-tuple-element.16), channel_id=1, source_target_pairs={{0,4},{4,8},{8,12},{12,16},{16,20},{20,24},{24,28},{1,5},{5,9},{9,... | collective-permute-start | bytes 294920 | tf_op jit(solution)/shard_map/ppermute | solution.py:396
  5.1 11.4 %collective-permute-start.1 = (f32[192,128]{1,0:T(8,128)}, f32[192,128]{1,0:T(8,128)S(1)}, u32[]{:S(2)}, u32[]{:S(2)}) collective-permute-start(f32[192,128]{1,0:T(8,128)} %get-tuple-element.17), channel_id=1, source_target_pairs={{4,0},{8,4},{12,8},{16,12},{20,16},{24,20},{28,24},{5,1},{9,5},{13... | collective-permute-start | bytes 294920 | tf_op jit(solution)/shard_map/ppermute | solution.py:397
  6.4 5.9 %collective-permute-start.2 = (f32[24,128]{1,0:T(8,128)}, f32[24,128]{1,0:T(8,128)S(1)}, u32[]{:S(2)}, u32[]{:S(2)}) collective-permute-start(f32[24,128]{1,0:T(8,128)} %get-tuple-element.18), channel_id=1, source_target_pairs={{0,1},{1,2},{2,3},{4,5},{5,6},{6,7},{8,9},{9,10},{10,11},{12,13},{... | collective-permute-start | bytes 36872 | tf_op jit(solution)/shard_map/ppermute | solution.py:396
  10.7 5.8 %collective-permute-start.3 = (f32[24,128]{1,0:T(8,128)}, f32[24,128]{1,0:T(8,128)S(1)}, u32[]{:S(2)}, u32[]{:S(2)}) collective-permute-start(f32[24,128]{1,0:T(8,128)} %get-tuple-element.19), channel_id=1, source_target_pairs={{1,0},{2,1},{3,2},{5,4},{6,5},{7,6},{9,8},{10,9},{11,10},{13,12},{... | collective-permute-start | bytes 36872 | tf_op jit(solution)/shard_map/ppermute | solution.py:397
  16.5 0.9 copy-start.4
  18.4 82.9 %collective-permute-start.6 = (f32[8,128]{1,0:T(8,128)S(1)}, f32[8,128]{1,0:T(8,128)S(1)}, u32[]{:S(2)}, u32[]{:S(2)}) collective-permute-start(f32[8,128]{1,0:T(8,128)S(1)} %get-tuple-element.24), channel_id=1, source_target_pairs={{0,1},{1,2},{2,3},{4,5},{5,6},{6,7},{8,9},{9,10},{10,11},{12,13},{... | collective-permute-start | bytes 12296 | tf_op jit(solution)/shard_map/ppermute | solution.py:396
  22.0 79.4 %collective-permute-start.7 = (f32[8,128]{1,0:T(8,128)S(1)}, f32[8,128]{1,0:T(8,128)S(1)}, u32[]{:S(2)}, u32[]{:S(2)}) collective-permute-start(f32[8,128]{1,0:T(8,128)S(1)} %get-tuple-element.25), channel_id=1, source_target_pairs={{1,0},{2,1},{3,2},{5,4},{6,5},{7,6},{9,8},{10,9},{11,10},{13,12},{... | collective-permute-start | bytes 12296 | tf_op jit(solution)/shard_map/ppermute | solution.py:397
  23.3 78.1 %collective-permute-start.4 = (f32[128,128]{1,0:T(8,128)S(1)}, f32[128,128]{1,0:T(8,128)S(1)}, u32[]{:S(2)}, u32[]{:S(2)}) collective-permute-start(f32[128,128]{1,0:T(8,128)S(1)} %get-tuple-element.22), channel_id=1, source_target_pairs={{0,4},{4,8},{8,12},{12,16},{16,20},{20,24},{24,28},{1,5},{5,9},{9,... | collective-permute-start | bytes 196616 | tf_op jit(solution)/shard_map/ppermute | solution.py:396
  25.9 75.5 %collective-permute-start.5 = (f32[128,128]{1,0:T(8,128)S(1)}, f32[128,128]{1,0:T(8,128)S(1)}, u32[]{:S(2)}, u32[]{:S(2)}) collective-permute-start(f32[128,128]{1,0:T(8,128)S(1)} %get-tuple-element.23), channel_id=1, source_target_pairs={{4,0},{8,4},{12,8},{16,12},{20,16},{24,20},{28,24},{5,1},{9,5},{13... | collective-permute-start | bytes 196616 | tf_op jit(solution)/shard_map/ppermute | solution.py:397
where the time goes:
time: 103 us
  blocking collectives  74.2 us (72%)
  starting transfers between devices  18 us (17%)
  waiting for transfers between devices  4.51 us (4%)
  Pallas kernels  4.47 us (4%)
    all_gather x1, blocking collectives, gather_totals(): parts = lax.all_gather(total, ('gx', 'gy'))  74.2 us
    ppermute x4, starting transfers between devices, swap_sides(): lax.ppermute(high, axis, [(i, i + 1) for i in range(count - 1)])  12.8 us
    ppermute x4, starting transfers between devices, swap_sides(): from_above = lax.ppermute(low, axis, [(i + 1, i) for i in range(count - 1)])  5.17 us
    pallas_call x3, Pallas kernels, call(): pl.pallas_call(functools.partial(kernel, plan), out_shape=[jax.ShapeDtype...  4.47 us
    ppermute x4, waiting for transfers between devices, swap_sides(): from_above = lax.ppermute(low, axis, [(i + 1, i) for i in range(count - 1)])  4.21 us
  transfers between devices with their start and end apart: 8, of which 2 were waited for; matrix products, arithmetic and copies ran while one was open for 0% of the time, Pallas kernels for 0%

commit v1 on v0

--- a/solution.py
+++ b/solution.py
@@ -159,9 +159,52 @@
     return gather.astype(BF16), spread
 
 
+def mobility_of(mask_ref, class_ref, table_ref):
+    kind = class_ref[...]
+    values = jnp.zeros(kind.shape, F32)
+    for marker in range(table_ref.shape[0]):
+        values = jnp.where(kind == marker, table_ref[marker], values)
+    return mask_ref[...].astype(F32) * values
+
+
+def x_even():
+    return lax.rem(lax.axis_index("gx"), 2) == 0
+
+
+def put_x(plan, fields, near_ref, far_ref):
+    even = x_even()
+    for which, field in enumerate(fields):
+        low, high = field[0], field[plan.x - 1]
+        near_ref[pl.ds(which * plan.y, plan.y), :] = jnp.where(even, high, low)
+        far_ref[pl.ds(which * plan.y, plan.y), :] = jnp.where(even, low, high)
+
+
+def get_x(near_ref, far_ref):
+    even = x_even()
+    near, far = near_ref[...], far_ref[...]
+    return jnp.where(even, far, near), jnp.where(even, near, far)
+
+
+def put_y(plan, fields, slots_ref):
+    h = lax.axis_index("gy")
+    for which, field in enumerate(fields):
+        for x in range(plan.x):
+            low, high = field[x, 0:1], field[x, plan.y - 1 : plan.y]
+            for slot in range(plan.groups):
+                slots_ref[slot, pl.ds(which * plan.x + x, 1), :] = jnp.where(h < slot, high, low)
+
+
+def get_y(plan, slots_ref):
+    h = lax.axis_index("gy")
+    last = plan.groups - 1
+    low = slots_ref[pl.ds(jnp.maximum(h - 1, 0), 1)][0]
+    high = slots_ref[pl.ds(jnp.minimum(h + 1, last), 1)][0]
+    return jnp.where(h > 0, low, 0.0), jnp.where(h < last, high, 0.0)
+
+
 def prepare_kernel(
     plan, conc_hbm, pot_hbm, mask_hbm, class_hbm, owner_hbm, table_hbm,
-    mob_ref, x_low_ref, x_high_ref, y_low_ref, y_high_ref,
+    x_near_ref, x_far_ref, y_ref,
     conc_ref, pot_ref, owner_ref, mask_ref, class_ref, table_ref, sems,
 ):
     pairs = (
@@ -176,19 +219,10 @@
         copy.start()
     for copy in copies:
         copy.wait()
-    kind = class_ref[...]
-    values = jnp.zeros(kind.shape, F32)
-    for marker in range(table_ref.shape[0]):
-        values = jnp.where(kind == marker, table_ref[marker], values)
-    mobility = mask_ref[...].astype(F32) * values
-    mob_ref[...] = mobility
+    mobility = mobility_of(mask_ref, class_ref, table_ref)
     fields = (conc_ref[...], pot_ref[...], mobility)
-    for which, field in enumerate(fields):
-        x_low_ref[pl.ds(which * plan.y, plan.y), :] = field[0]
-        x_high_ref[pl.ds(which * plan.y, plan.y), :] = field[plan.x - 1]
-        for x in range(plan.x):
-            y_low_ref[pl.ds(which * plan.x + x, 1), :] = field[x, 0:1]
-            y_high_ref[pl.ds(which * plan.x + x, 1), :] = field[x, plan.y - 1 : plan.y]
+    put_x(plan, fields, x_near_ref, x_far_ref)
+    put_y(plan, fields, y_ref)
     columns = plan.half_x * plan.half_y
     owner = iota((plan.owners, columns), 0)
     hits = jnp.zeros((plan.owners, columns), F32)
@@ -196,30 +230,33 @@
         hits = hits + (owner_ref[g : g + 1, :] == owner).astype(F32)
     count = jnp.broadcast_to(jnp.sum(hits, axis=1, keepdims=True), (plan.owners, plan.p))
     own = owner_ref[pl.ds(lax.axis_index("gx"), 1), :].astype(F32)
-    for ref, at in ((y_low_ref, 0), (y_high_ref, plan.half_y - 1)):
-        ref[pl.ds(plan.count_row, plan.owners), :] = count
-        ref[pl.ds(plan.id_row, plan.count_row - plan.id_row), :] = jnp.zeros(
-            (plan.count_row - plan.id_row, plan.p), F32
-        )
+    blank = plan.count_row - plan.id_row - plan.half_x
+    for slot in range(plan.groups):
+        y_ref[slot, pl.ds(plan.count_row, plan.owners), :] = count
+        if blank:
+            y_ref[slot, pl.ds(plan.id_row + plan.half_x, blank), :] = jnp.zeros((blank, plan.p), F32)
         for i in range(plan.half_x):
-            b = i * plan.half_y + at
-            ref[pl.ds(plan.id_row + i, 1), :] = jnp.broadcast_to(own[:, b : b + 1], (1, plan.p))
+            b = i * plan.half_y
+            low, high = own[:, b : b + 1], own[:, b + plan.half_y - 1 : b + plan.half_y]
+            ident = jnp.where(lax.axis_index("gy") < slot, high, low)
+            y_ref[slot, pl.ds(plan.id_row + i, 1), :] = jnp.broadcast_to(ident, (1, plan.p))
 
 
 def first_kernel(
-    plan, conc_ref, pot_ref, mob_ref, mass_ref, pots_ref, x_low_ref, x_high_ref,
-    y_low_ref, y_high_ref, owner_ref,
-    conc_out, pot_out, total_out, spread_out, x_low_out, x_high_out, y_low_out, y_high_out,
+    plan, conc_ref, pot_ref, mask_ref, class_ref, table_ref, mass_ref, pots_ref,
+    x_near_ref, x_far_ref, y_ref, owner_ref,
+    conc_out, pot_out, mob_out, total_out, spread_out, x_near_out, x_far_out, y_out,
 ):
-    sides = (x_low_ref[...], x_high_ref[...])
-    ends = (y_low_ref[...], y_high_ref[...])
+    sides = get_x(x_near_ref, x_far_ref)
+    ends = get_y(plan, y_ref)
 
     def halo(which):
         return tuple(side_rows(plan, rows, which) for rows in sides) + tuple(
             side_columns(plan, rows, which) for rows in ends
         )
 
-    mobility, mob_halo = mob_ref[...], halo(2)
+    mobility, mob_halo = mobility_of(mask_ref, class_ref, table_ref), halo(2)
+    mob_out[...] = mobility
     faces, diagonal = faces_of(mobility, mob_halo)
     mass_source, pot_source = mass_ref[...], pots_ref[...]
     conc, pot = conc_ref[...], pot_ref[...]
@@ -227,12 +264,8 @@
     conc, pot = relax_pair(conc, pot, *excess, diagonal)
     conc_out[...] = conc
     pot_out[...] = pot
-    x_low_out[...] = jnp.concatenate([conc[0], pot[0]], axis=0)
-    x_high_out[...] = jnp.concatenate([conc[plan.x - 1], pot[plan.x - 1]], axis=0)
-    for which, field in enumerate((conc, pot)):
-        for x in range(plan.x):
-            y_low_out[pl.ds(which * plan.x + x, 1), :] = field[x, 0:1]
-            y_high_out[pl.ds(which * plan.x + x, 1), :] = field[x, plan.y - 1 : plan.y]
+    put_x(plan, (conc, pot), x_near_out, x_far_out)
+    put_y(plan, (conc, pot), y_out)
 
     nothing = tuple(jnp.zeros_like(part) for part in mob_halo)
     own_mass, own_pot = excess_of(conc, pot, nothing, nothing, faces, mass_source, pot_source)
@@ -263,7 +296,8 @@
         return 0.125 / jnp.maximum(count, 1.0)
 
     def put(place, values):
-        total_out[pl.ds(place * plan.owners, plan.owners), :] = values
+        for slot in range(total_out.shape[0]):
+            total_out[slot, pl.ds(place * plan.owners, plan.owners), :] = values
 
     own_hits = jnp.zeros((plan.owners, plan.half_x * plan.half_y), F32)
     owner_grid = iota(own_hits.shape, 0)
@@ -319,8 +353,8 @@
 
 
 def last_kernel(
-    plan, conc_ref, pot_ref, mob_ref, mass_ref, pots_ref, x_low_mob, x_high_mob,
-    y_low_msg, y_high_msg, x_low_ref, x_high_ref, y_low_ref, y_high_ref, total_ref, spread_ref,
+    plan, conc_ref, pot_ref, mob_ref, mass_ref, pots_ref, x_near_msg, x_far_msg, y_msg,
+    x_near_ref, x_far_ref, y_ref, total_ref, spread_ref,
     conc_out, pot_out, frame,
 ):
     h = lax.axis_index("gy")
@@ -347,72 +381,83 @@
             out += [row, row]
         return jnp.concatenate(out, axis=0)
 
+    ends = get_y(plan, y_msg)
+    sides = get_x(x_near_msg, x_far_msg)
     y_corr = (
-        edge_correction(0, y_low_msg[...], h > 0),
-        edge_correction(2, y_high_msg[...], h < plan.groups - 1),
-    )
+        edge_correction(0, ends[0], h > 0),
+        edge_correction(2, ends[1], h < plan.groups - 1),
+    )
+    new_ends = get_y(plan, y_ref)
+    new_sides = get_x(x_near_ref, x_far_ref)
 
     def updated(which, ref):
         lanes = slice(which * plan.p, (which + 1) * plan.p)
         corr = own[:, lanes]
         field = ref[...] + corr[: plan.cells].reshape(plan.x, plan.y, plan.p)
         halo = []
-        for side, rows in enumerate((x_low_ref[...], x_high_ref[...])):
+        for side, rows in enumerate(new_sides):
             begin = plan.cells + side * plan.y
             halo.append(side_rows(plan, rows, which) + corr[begin : begin + plan.y][None])
-        for rows, edge in zip((y_low_ref[...], y_high_ref[...]), y_corr):
+        for rows, edge in zip(new_ends, y_corr):
             halo.append((rows[which * plan.x : (which + 1) * plan.x] + edge[:, lanes])[:, None])
         return field, halo
 
     conc, conc_halo = updated(0, conc_ref)
     pot, pot_halo = updated(1, pot_ref)
     mob_halo = (
-        x_low_mob[pl.ds(2 * plan.y, plan.y), :][None],
-        x_high_mob[pl.ds(2 * plan.y, plan.y), :][None],
-        side_columns(plan, y_low_msg[...], 2),
-        side_columns(plan, y_high_msg[...], 2),
+        side_rows(plan, sides[0], 2),
+        side_rows(plan, sides[1], 2),
+        side_columns(plan, ends[0], 2),
+        side_columns(plan, ends[1], 2),
     )
     faces, diagonal = faces_of(mob_ref[...], mob_halo)
     excess = excess_of(conc, pot, conc_halo, pot_halo, faces, mass_ref[...], pots_ref[...])
     conc_out[...], pot_out[...] = relax_pair(conc, pot, *excess, diagonal)
 
 
-def call(kernel, plan, outs, args, far=(), scratch=(), limit=VMEM_LIMIT):
+def call(kernel, plan, outs, args, far=(), smem=(), scratch=(), limit=VMEM_LIMIT):
+    def space(i):
+        return pl.ANY if i in far else pltpu.SMEM if i in smem else pltpu.VMEM
+
     return pl.pallas_call(
         functools.partial(kernel, plan),
         out_shape=[jax.ShapeDtypeStruct(shape, F32) for shape in outs],
-        in_specs=[
-            pl.BlockSpec(memory_space=pl.ANY if i in far else pltpu.VMEM)
-            for i in range(len(args))
-        ],
+        in_specs=[pl.BlockSpec(memory_space=space(i)) for i in range(len(args))],
         out_specs=[pl.BlockSpec(memory_space=pltpu.VMEM)] * len(outs),
         scratch_shapes=list(scratch),
         compiler_params=pltpu.CompilerParams(vmem_limit_bytes=limit),
     )(*args)
 
 
-def swap_sides(low, high, axis):
-    count = lax.axis_size(axis)
-    from_below = lax.ppermute(high, axis, [(i, i + 1) for i in range(count - 1)])
-    from_above = lax.ppermute(low, axis, [(i + 1, i) for i in range(count - 1)])
-    return from_below, from_above
+def swap_x(near, far):
+    count = lax.axis_size("gx")
+    out = []
+    for rows, begin in ((near, 0), (far, 1)):
+        pairs = [(i, i + 1) for i in range(begin, count - 1, 2)]
+        out.append(lax.ppermute(rows, "gx", pairs + [(j, i) for i, j in pairs]))
+    return out
+
+
+def swap_y(slots):
+    return lax.all_to_all(slots, "gy", split_axis=0, concat_axis=0, tiled=True)
 
 
 def gather_totals(plan, total):
-    if plan.owners * plan.groups <= 64:
-        parts = lax.all_gather(total, ("gx", "gy"))
-        return parts.reshape(plan.owners, plan.groups, *total.shape)
-    parts = lax.all_gather(lax.psum(total, "gx"), "gy")
-    return parts[None]
+    if total.shape[0] > 1:
+        parts = lax.all_to_all(total, ("gx", "gy"), split_axis=0, concat_axis=0, tiled=True)
+        return parts.reshape(plan.owners, plan.groups, *total.shape[1:])
+    return lax.all_gather(lax.psum(total, "gx"), "gy", axis=1)
 
 
 def on_device(conc, pot, mass_source, pot_source, mask, kind, table, owner_map):
     plan = Plan(conc.shape, lax.axis_size("gx"), lax.axis_size("gy"))
     block = conc.shape
-    mob, x_low, x_high, y_low, y_high = call(
+    slots = plan.owners * plan.groups
+    slots = slots if slots <= 64 else 1
+    messages = call(
         prepare_kernel,
         plan,
-        [block, *[(3 * plan.y, plan.p)] * 2, *[(plan.y_rows, plan.p)] * 2],
+        [*[(3 * plan.y, plan.p)] * 2, (plan.groups, plan.y_rows, plan.p)],
         [conc, pot, mask, kind, owner_map, table],
         far=range(6),
         limit=LARGE_LIMIT,
@@ -426,33 +471,32 @@
             pltpu.SemaphoreType.DMA((6,)),
         ),
     )
-    x_low, x_high = swap_sides(x_low, x_high, "gx")
-    y_low, y_high = swap_sides(y_low, y_high, "gy")
-    conc, pot, total, spread, x_low1, x_high1, y_low1, y_high1 = call(
+    y_msg = swap_y(messages[2])
+    x_msg = swap_x(*messages[:2])
+    conc, pot, mob, total, spread, *messages = call(
         first_kernel,
         plan,
         [
             block,
             block,
-            (3 * plan.owners, plan.p),
+            block,
+            (slots, 3 * plan.owners, plan.p),
             (plan.rows, plan.owners),
             *[(2 * plan.y, plan.p)] * 2,
-            *[(2 * plan.x, plan.p)] * 2,
+            (plan.groups, 2 * plan.x, plan.p),
         ],
-        [conc, pot, mob, mass_source, pot_source, x_low, x_high, y_low, y_high, owner_map],
+        [conc, pot, mask, kind, table, mass_source, pot_source, *x_msg, y_msg, owner_map],
+        smem=(4,),
     )
     total = gather_totals(plan, total)
-    x_low1, x_high1 = swap_sides(x_low1, x_high1, "gx")
-    y_low1, y_high1 = swap_sides(y_low1, y_high1, "gy")
+    y_new = swap_y(messages[2])
+    x_new = swap_x(*messages[:2])
     return tuple(
         call(
             last_kernel,
             plan,
             [block, block],
-            [
-                conc, pot, mob, mass_source, pot_source, x_low, x_high, y_low, y_high,
-                x_low1, x_high1, y_low1, y_high1, total, spread,
-            ],
+            [conc, pot, mob, mass_source, pot_source, *x_msg, y_msg, *x_new, y_new, total, spread],
             scratch=[pltpu.VMEM(((plan.groups + 2) * plan.owners, plan.p), F32)],
         )
     )

time: 103 us -> 47 us (0.46)
  the two profiles are of different devices: /device:TPU:0 before, /device:TPU:1 now
where the time goes in v1:
time: 47 us; the launch traced here: 46.6 us
  blocking collectives  16 us (34%)
  starting transfers between devices  13.1 us (28%)
  waiting for transfers between devices  8.99 us (19%)
  Pallas kernels  5.92 us (13%)
  local copies, waits for them, and re-layouts  1.84 us (4%)
  between operations  0.78 us (2%)
    all_to_all x2, blocking collectives, swap_y(): return lax.all_to_all(slots, 'gy', split_axis=0, concat_axis=0, tiled=True)  16 us
    ppermute x4, starting transfers between devices, swap_x(): out.append(lax.ppermute(rows, 'gx', pairs + [(j, i) for i, j in pairs]))  8.33 us
    pallas_call x3, Pallas kernels, call(): pl.pallas_call(functools.partial(kernel, plan), out_shape=[jax.ShapeDtype...  5.92 us
    all_to_all x1, waiting for transfers between devices, gather_totals(): lax.all_to_all(total, ('gx', 'gy'), split_axis=0, concat_axis=0, tiled=True)  5.73 us
    all_to_all x1, starting transfers between devices, gather_totals(): lax.all_to_all(total, ('gx', 'gy'), split_axis=0, concat_axis=0, tiled=True)  4.75 us
    ppermute x4, waiting for transfers between devices, swap_x(): out.append(lax.ppermute(rows, 'gx', pairs + [(j, i) for i, j in pairs]))  3.26 us
    unnamed x20, local copies, waits for them, and re-layouts  1.84 us
  transfers between devices with their start and end apart: 5, of which 2 were waited for; matrix products, arithmetic and copies ran while one was open for 0% of the time, Pallas kernels for 0%

profile of v1, /device:TPU:1, one launch (start us, length us, event | category | flops | bytes accessed | tf_op | source)
XLA Modules:
  0.0 46.6 jit_solution(13493965172613234012)
XLA Ops:
  0.6 0.0 copy-start
  0.6 0.0 copy-start.1
  0.7 0.0 copy-start.2
  0.7 0.0 copy-start.3
  0.7 2.0 %shard_map.95 = (f32[192,128]{1,0:T(8,128)}, f32[192,128]{1,0:T(8,128)}, f32[4,24,128]{2,1,0:T(8,128)}) custom-call(f32[4,64,128]{2,1,0:T(8,128)} %conc_ref.1, f32[4,64,128]{2,1,0:T(8,128)} %pot_ref.1, s32[4,64,128]{2,1,0:T(8,128)} %mask_ref.1, s32[4,64,128]{2,1,0:T(8,128)} %class_ref.1, s32[8,64]{1,0:T(8,128)} %owner_ref.1, f32[8]{0:T(128)} %table_ref.1), custom_call_target="tpu_custom_call" | custom-call | tf_op jit(solution)/shard_map/pallas_call | solution.py:422
  2.7 0.1 collective-permute-start
  2.8 4.5 %collective-permute-start.1 = (f32[192,128]{1,0:T(8,128)}, f32[192,128]{1,0:T(8,128)S(1)}, u32[]{:S(2)}, u32[]{:S(2)}) collective-permute-start(f32[192,128]{1,0:T(8,128)} %get-tuple-element.14), channel_id=1, source_target_pairs={{4,8},{12,16},{20,24},{8,4},{16,12},{24,20},{5,9},{13,17},{21,25},... | collective-permute-start | bytes 294920 | tf_op jit(solution)/shard_map/ppermute | solution.py:437
  7.3 0.0 copy-start.8
  7.3 0.0 copy-start.9
  7.3 9.2 %all_to_all.15.y_ref.y_msg = f32[4,24,128]{2,1,0:T(8,128)S(1)} all-to-all(f32[4,24,128]{2,1,0:T(8,128)} %get-tuple-element.15), channel_id=1, replica_groups=mesh['gx'=8,'gy'=4] {'gy'}, dimensions={0} | all-to-all | bytes 98304 | tf_op jit(solution)/shard_map/all_to_all | solution.py:442
  16.5 0.0 collective-permute-done.x_near_ref.x_near_msg
  16.5 0.0 collective-permute-done.1.x_far_ref.x_far_msg
  16.5 0.0 copy-done
  16.5 0.0 copy-done.1
  16.5 0.0 copy-done.2
  16.5 0.0 copy-done.3
  16.5 0.0 copy-done.8
  16.5 0.0 copy-done.9
  16.5 0.0 copy-start.4
  16.5 0.9 %copy-done.4 = f32[4,64,128]{2,1,0:T(8,128)S(1)} copy-done((f32[4,64,128]{2,1,0:T(8,128)S(1)}, f32[4,64,128]{2,1,0:T(8,128)}, u32[]{:S(2)}) %copy-start.4) | copy-done | bytes 131096
  17.4 0.0 copy-start.6
  17.4 0.9 %copy-done.6 = f32[4,64,128]{2,1,0:T(8,128)S(1)} copy-done((f32[4,64,128]{2,1,0:T(8,128)S(1)}, f32[4,64,128]{2,1,0:T(8,128)}, u32[]{:S(2)}) %copy-start.6) | copy-done | bytes 131096
  18.3 2.4 %shard_map.96 = (f32[4,64,128]{2,1,0:T(8,128)S(1)}, f32[4,64,128]{2,1,0:T(8,128)S(1)}, f32[4,64,128]{2,1,0:T(8,128)S(1)}, f32[32,24,128]{2,1,0:T(8,128)}, f32[38...) custom-call(f32[4,64,128]{2,1,0:T(8,128)S(1)} %copy-done, ...), custom_call_target="tpu_custom_call" | custom-call | tf_op jit(solution)/shard_map/pallas_call | solution.py:422
  20.8 6.8 %all_to_all.16.y_ref = f32[4,8,128]{2,1,0:T(8,128)S(1)} all-to-all(f32[4,8,128]{2,1,0:T(8,128)S(1)} %get-tuple-element.21), channel_id=1, replica_groups=mesh['gx'=8,'gy'=4] {'gy'}, dimensions={0} | all-to-all | bytes 32768 | tf_op jit(solution)/shard_map/all_to_all | solution.py:442
  27.6 0.0 copy-start.5
  27.6 0.0 copy-start.7
  27.6 4.7 %all-to-all-start.2 = ((f32[32,24,128]{2,1,0:T(8,128)}), f32[32,24,128]{2,1,0:T(8,128)S(1)}, u32[]{:S(2)}, u32[]{:S(2)}) async-start(f32[32,24,128]{2,1,0:T(8,128)} %get-tuple-element.22), calls=%async_computation.2 | async-start | bytes 786432 | tf_op jit(solution)/shard_map/all_to_all | solution.py:447
  32.3 0.3 collective-permute-start.2
  32.7 3.4 %collective-permute-start.3 = (f32[128,128]{1,0:T(8,128)S(1)}, f32[128,128]{1,0:T(8,128)S(1)}, u32[]{:S(2)}, u32[]{:S(2)}) collective-permute-start(f32[128,128]{1,0:T(8,128)S(1)} %get-tuple-element.20), channel_id=1, source_target_pairs={{4,8},{12,16},{20,24},{8,4},{16,12},{24,20},{5,9},{13,17},{21,25},... | collective-permute-start | bytes 196616 | tf_op jit(solution)/shard_map/ppermute | solution.py:437
  36.1 0.0 collective-permute-done.2.x_near_ref
  36.1 3.3 %collective-permute-done.3.x_far_ref = f32[128,128]{1,0:T(8,128)S(1)} collective-permute-done((f32[128,128]{1,0:T(8,128)S(1)}, f32[128,128]{1,0:T(8,128)S(1)}, u32[]{:S(2)}, u32[]{:S(2)}) %collective-permute-start.3) | collective-permute-done | bytes 65568 | tf_op jit(solution)/shard_map/ppermute | solution.py:437
  39.3 5.7 %all-to-all-done.2 = f32[32,24,128]{2,1,0:T(8,128)S(1)} async-done(((f32[32,24,128]{2,1,0:T(8,128)}), f32[32,24,128]{2,1,0:T(8,128)S(1)}, u32[]{:S(2)}, u32[]{:S(2)}) %all-to-all-start.2) | async-done | bytes 393248 | tf_op jit(solution)/shard_map/all_to_all | solution.py:447
  45.1 0.0 copy-done.5
  45.1 0.0 copy-done.7
  45.1 1.5 %shard_map.97 = (f32[4,64,128]{2,1,0:T(8,128)}, f32[4,64,128]{2,1,0:T(8,128)}) custom-call(f32[4,64,128]{2,1,0:T(8,128)S(1)} %get-tuple-element.16.conc_ref, f32[4,64,128]{2,1,0:T(8,128)S(1)} %get-tuple-element.17.pot_ref, f32[4,64,128]{2,1,0:T(8,128)S(1)} %get-tuple-element.18.mob_ref, f32[4,64,128]{2,1,0:T(8,128)S(1)} %copy-done.5, ...), custom_call_target="tpu_custom_call" | custom-call | tf_op jit(solution)/shard_map/pallas_call | solution.py:422
Async XLA Ops:
  0.6 15.8 %copy-start = (f32[4,64,128]{2,1,0:T(8,128)S(1)}, f32[4,64,128]{2,1,0:T(8,128)}, u32[]{:S(2)}) copy-start(f32[4,64,128]{2,1,0:T(8,128)} %conc_ref.1) | copy-start | bytes 393220
  0.6 15.8 %copy-start.1 = (f32[4,64,128]{2,1,0:T(8,128)S(1)}, f32[4,64,128]{2,1,0:T(8,128)}, u32[]{:S(2)}) copy-start(f32[4,64,128]{2,1,0:T(8,128)} %pot_ref.1) | copy-start | bytes 393220
  0.7 15.8 %copy-start.2 = (s32[4,64,128]{2,1,0:T(8,128)S(1)}, s32[4,64,128]{2,1,0:T(8,128)}, u32[]{:S(2)}) copy-start(s32[4,64,128]{2,1,0:T(8,128)} %mask_ref.1) | copy-start | bytes 393220
  0.7 15.8 %copy-start.3 = (s32[4,64,128]{2,1,0:T(8,128)S(1)}, s32[4,64,128]{2,1,0:T(8,128)}, u32[]{:S(2)}) copy-start(s32[4,64,128]{2,1,0:T(8,128)} %class_ref.1) | copy-start | bytes 393220
  2.7 13.8 %collective-permute-start = (f32[192,128]{1,0:T(8,128)}, f32[192,128]{1,0:T(8,128)S(1)}, u32[]{:S(2)}, u32[]{:S(2)}) collective-permute-start(f32[192,128]{1,0:T(8,128)} %get-tuple-element.13), channel_id=1, source_target_pairs={{0,4},{8,12},{16,20},{24,28},{4,0},{12,8},{20,16},{28,24},{1,5},{9... | collective-permute-start | bytes 294920 | tf_op jit(solution)/shard_map/ppermute | solution.py:437
  2.8 13.7 %collective-permute-start.1 = (f32[192,128]{1,0:T(8,128)}, f32[192,128]{1,0:T(8,128)S(1)}, u32[]{:S(2)}, u32[]{:S(2)}) collective-permute-start(f32[192,128]{1,0:T(8,128)} %get-tuple-element.14), channel_id=1, source_target_pairs={{4,8},{12,16},{20,24},{8,4},{16,12},{24,20},{5,9},{13,17},{21,25},... | collective-permute-start | bytes 294920 | tf_op jit(solution)/shard_map/ppermute | solution.py:437
  7.3 9.2 %copy-start.8 = (s32[8,64]{1,0:T(8,128)S(1)}, s32[8,64]{1,0:T(8,128)}, u32[]{:S(2)}) copy-start(s32[8,64]{1,0:T(8,128)} %owner_ref.1) | copy-start | bytes 6148
  7.3 9.2 %copy-start.9 = (f32[8]{0:T(128)S(1)}, f32[8]{0:T(128)}, u32[]{:S(2)}) copy-start(f32[8]{0:T(128)} %table_ref.1) | copy-start | bytes 100
  16.5 0.9 %copy-start.4 = (f32[4,64,128]{2,1,0:T(8,128)S(1)}, f32[4,64,128]{2,1,0:T(8,128)}, u32[]{:S(2)}) copy-start(f32[4,64,128]{2,1,0:T(8,128)} %mass_ref.3) | copy-start | bytes 393220
  17.4 0.9 %copy-start.6 = (f32[4,64,128]{2,1,0:T(8,128)S(1)}, f32[4,64,128]{2,1,0:T(8,128)}, u32[]{:S(2)}) copy-start(f32[4,64,128]{2,1,0:T(8,128)} %pots_ref.3) | copy-start | bytes 393220
  27.6 17.5 %copy-start.5 = (f32[4,64,128]{2,1,0:T(8,128)S(1)}, f32[4,64,128]{2,1,0:T(8,128)}, u32[]{:S(2)}) copy-start(f32[4,64,128]{2,1,0:T(8,128)} %mass_ref.3) | copy-start | bytes 393220
  27.6 17.5 %copy-start.7 = (f32[4,64,128]{2,1,0:T(8,128)S(1)}, f32[4,64,128]{2,1,0:T(8,128)}, u32[]{:S(2)}) copy-start(f32[4,64,128]{2,1,0:T(8,128)} %pots_ref.3) | copy-start | bytes 393220
  27.6 17.5 %all-to-all-start.2 = ((f32[32,24,128]{2,1,0:T(8,128)}), f32[32,24,128]{2,1,0:T(8,128)S(1)}, u32[]{:S(2)}, u32[]{:S(2)}) async-start(f32[32,24,128]{2,1,0:T(8,128)} %get-tuple-element.22), calls=%async_computation.2 | async-start | bytes 786432 | tf_op jit(solution)/shard_map/all_to_all | solution.py:447
  32.3 3.8 %collective-permute-start.2 = (f32[128,128]{1,0:T(8,128)S(1)}, f32[128,128]{1,0:T(8,128)S(1)}, u32[]{:S(2)}, u32[]{:S(2)}) collective-permute-start(f32[128,128]{1,0:T(8,128)S(1)} %get-tuple-element.19), channel_id=1, source_target_pairs={{0,4},{8,12},{16,20},{24,28},{4,0},{12,8},{20,16},{28,24},{1,5},{9... | collective-permute-start | bytes 196616 | tf_op jit(solution)/shard_map/ppermute | solution.py:437
  32.7 6.7 %collective-permute-start.3 = (f32[128,128]{1,0:T(8,128)S(1)}, f32[128,128]{1,0:T(8,128)S(1)}, u32[]{:S(2)}, u32[]{:S(2)}) collective-permute-start(f32[128,128]{1,0:T(8,128)S(1)} %get-tuple-element.20), channel_id=1, source_target_pairs={{4,8},{12,16},{20,24},{8,4},{16,12},{24,20},{5,9},{13,17},{21,25},... | collective-permute-start | bytes 196616 | tf_op jit(solution)/shard_map/ppermute | solution.py:437

commit v2 on v1

--- a/solution.py
+++ b/solution.py
@@ -167,44 +167,36 @@
     return mask_ref[...].astype(F32) * values
 
 
-def x_even():
-    return lax.rem(lax.axis_index("gx"), 2) == 0
+def even(axis):
+    return lax.rem(lax.axis_index(axis), 2) == 0
 
 
 def put_x(plan, fields, near_ref, far_ref):
-    even = x_even()
+    up = even("gx")
     for which, field in enumerate(fields):
         low, high = field[0], field[plan.x - 1]
-        near_ref[pl.ds(which * plan.y, plan.y), :] = jnp.where(even, high, low)
-        far_ref[pl.ds(which * plan.y, plan.y), :] = jnp.where(even, low, high)
-
-
-def get_x(near_ref, far_ref):
-    even = x_even()
-    near, far = near_ref[...], far_ref[...]
-    return jnp.where(even, far, near), jnp.where(even, near, far)
-
-
-def put_y(plan, fields, slots_ref):
-    h = lax.axis_index("gy")
+        near_ref[pl.ds(which * plan.y, plan.y), :] = jnp.where(up, high, low)
+        far_ref[pl.ds(which * plan.y, plan.y), :] = jnp.where(up, low, high)
+
+
+def put_y(plan, fields, near_ref, far_ref):
+    up = even("gy")
     for which, field in enumerate(fields):
         for x in range(plan.x):
             low, high = field[x, 0:1], field[x, plan.y - 1 : plan.y]
-            for slot in range(plan.groups):
-                slots_ref[slot, pl.ds(which * plan.x + x, 1), :] = jnp.where(h < slot, high, low)
-
-
-def get_y(plan, slots_ref):
-    h = lax.axis_index("gy")
-    last = plan.groups - 1
-    low = slots_ref[pl.ds(jnp.maximum(h - 1, 0), 1)][0]
-    high = slots_ref[pl.ds(jnp.minimum(h + 1, last), 1)][0]
-    return jnp.where(h > 0, low, 0.0), jnp.where(h < last, high, 0.0)
+            near_ref[pl.ds(which * plan.x + x, 1), :] = jnp.where(up, high, low)
+            far_ref[pl.ds(which * plan.x + x, 1), :] = jnp.where(up, low, high)
+
+
+def received(axis, near_ref, far_ref):
+    up = even(axis)
+    near, far = near_ref[...], far_ref[...]
+    return jnp.where(up, far, near), jnp.where(up, near, far)
 
 
 def prepare_kernel(
     plan, conc_hbm, pot_hbm, mask_hbm, class_hbm, owner_hbm, table_hbm,
-    x_near_ref, x_far_ref, y_ref,
+    x_near_ref, x_far_ref, y_near_ref, y_far_ref,
     conc_ref, pot_ref, owner_ref, mask_ref, class_ref, table_ref, sems,
 ):
     pairs = (
@@ -222,7 +214,7 @@
     mobility = mobility_of(mask_ref, class_ref, table_ref)
     fields = (conc_ref[...], pot_ref[...], mobility)
     put_x(plan, fields, x_near_ref, x_far_ref)
-    put_y(plan, fields, y_ref)
+    put_y(plan, fields, y_near_ref, y_far_ref)
     columns = plan.half_x * plan.half_y
     owner = iota((plan.owners, columns), 0)
     hits = jnp.zeros((plan.owners, columns), F32)
@@ -231,24 +223,26 @@
     count = jnp.broadcast_to(jnp.sum(hits, axis=1, keepdims=True), (plan.owners, plan.p))
     own = owner_ref[pl.ds(lax.axis_index("gx"), 1), :].astype(F32)
     blank = plan.count_row - plan.id_row - plan.half_x
-    for slot in range(plan.groups):
-        y_ref[slot, pl.ds(plan.count_row, plan.owners), :] = count
+    up = even("gy")
+    for ref, top in ((y_near_ref, up), (y_far_ref, jnp.logical_not(up))):
+        ref[pl.ds(plan.count_row, plan.owners), :] = count
         if blank:
-            y_ref[slot, pl.ds(plan.id_row + plan.half_x, blank), :] = jnp.zeros((blank, plan.p), F32)
+            ref[pl.ds(plan.id_row + plan.half_x, blank), :] = jnp.zeros((blank, plan.p), F32)
         for i in range(plan.half_x):
             b = i * plan.half_y
             low, high = own[:, b : b + 1], own[:, b + plan.half_y - 1 : b + plan.half_y]
-            ident = jnp.where(lax.axis_index("gy") < slot, high, low)
-            y_ref[slot, pl.ds(plan.id_row + i, 1), :] = jnp.broadcast_to(ident, (1, plan.p))
+            ident = jnp.where(top, high, low)
+            ref[pl.ds(plan.id_row + i, 1), :] = jnp.broadcast_to(ident, (1, plan.p))
 
 
 def first_kernel(
     plan, conc_ref, pot_ref, mask_ref, class_ref, table_ref, mass_ref, pots_ref,
-    x_near_ref, x_far_ref, y_ref, owner_ref,
-    conc_out, pot_out, mob_out, total_out, spread_out, x_near_out, x_far_out, y_out,
+    x_near_ref, x_far_ref, y_near_ref, y_far_ref, owner_ref,
+    conc_out, pot_out, mob_out, total_out, spread_out,
+    x_near_out, x_far_out, y_near_out, y_far_out,
 ):
-    sides = get_x(x_near_ref, x_far_ref)
-    ends = get_y(plan, y_ref)
+    sides = received("gx", x_near_ref, x_far_ref)
+    ends = received("gy", y_near_ref, y_far_ref)
 
     def halo(which):
         return tuple(side_rows(plan, rows, which) for rows in sides) + tuple(
@@ -265,7 +259,7 @@
     conc_out[...] = conc
     pot_out[...] = pot
     put_x(plan, (conc, pot), x_near_out, x_far_out)
-    put_y(plan, (conc, pot), y_out)
+    put_y(plan, (conc, pot), y_near_out, y_far_out)
 
     nothing = tuple(jnp.zeros_like(part) for part in mob_halo)
     own_mass, own_pot = excess_of(conc, pot, nothing, nothing, faces, mass_source, pot_source)
@@ -353,8 +347,8 @@
 
 
 def last_kernel(
-    plan, conc_ref, pot_ref, mob_ref, mass_ref, pots_ref, x_near_msg, x_far_msg, y_msg,
-    x_near_ref, x_far_ref, y_ref, total_ref, spread_ref,
+    plan, conc_ref, pot_ref, mob_ref, mass_ref, pots_ref, x_near_msg, x_far_msg,
+    y_near_msg, y_far_msg, x_near_ref, x_far_ref, y_near_ref, y_far_ref, total_ref, spread_ref,
     conc_out, pot_out, frame,
 ):
     h = lax.axis_index("gy")
@@ -381,14 +375,14 @@
             out += [row, row]
         return jnp.concatenate(out, axis=0)
 
-    ends = get_y(plan, y_msg)
-    sides = get_x(x_near_msg, x_far_msg)
+    ends = received("gy", y_near_msg, y_far_msg)
+    sides = received("gx", x_near_msg, x_far_msg)
     y_corr = (
         edge_correction(0, ends[0], h > 0),
         edge_correction(2, ends[1], h < plan.groups - 1),
     )
-    new_ends = get_y(plan, y_ref)
-    new_sides = get_x(x_near_ref, x_far_ref)
+    new_ends = received("gy", y_near_ref, y_far_ref)
+    new_sides = received("gx", x_near_ref, x_far_ref)
 
     def updated(which, ref):
         lanes = slice(which * plan.p, (which + 1) * plan.p)
@@ -429,17 +423,17 @@
     )(*args)
 
 
-def swap_x(near, far):
-    count = lax.axis_size("gx")
+def swap(axis, near, far):
+    count = lax.axis_size(axis)
     out = []
     for rows, begin in ((near, 0), (far, 1)):
         pairs = [(i, i + 1) for i in range(begin, count - 1, 2)]
-        out.append(lax.ppermute(rows, "gx", pairs + [(j, i) for i, j in pairs]))
+        out.append(lax.ppermute(rows, axis, pairs + [(j, i) for i, j in pairs]))
     return out
 
 
-def swap_y(slots):
-    return lax.all_to_all(slots, "gy", split_axis=0, concat_axis=0, tiled=True)
+def swap_all(x_near, x_far, y_near, y_far):
+    return *swap("gx", x_near, x_far), *swap("gy", y_near, y_far)
 
 
 def gather_totals(plan, total):
@@ -457,7 +451,7 @@
     messages = call(
         prepare_kernel,
         plan,
-        [*[(3 * plan.y, plan.p)] * 2, (plan.groups, plan.y_rows, plan.p)],
+        [*[(3 * plan.y, plan.p)] * 2, *[(plan.y_rows, plan.p)] * 2],
         [conc, pot, mask, kind, owner_map, table],
         far=range(6),
         limit=LARGE_LIMIT,
@@ -471,8 +465,7 @@
             pltpu.SemaphoreType.DMA((6,)),
         ),
     )
-    y_msg = swap_y(messages[2])
-    x_msg = swap_x(*messages[:2])
+    old = swap_all(*messages)
     conc, pot, mob, total, spread, *messages = call(
         first_kernel,
         plan,
@@ -483,20 +476,19 @@
             (slots, 3 * plan.owners, plan.p),
             (plan.rows, plan.owners),
             *[(2 * plan.y, plan.p)] * 2,
-            (plan.groups, 2 * plan.x, plan.p),
+            *[(2 * plan.x, plan.p)] * 2,
         ],
-        [conc, pot, mask, kind, table, mass_source, pot_source, *x_msg, y_msg, owner_map],
+        [conc, pot, mask, kind, table, mass_source, pot_source, *old, owner_map],
         smem=(4,),
     )
     total = gather_totals(plan, total)
-    y_new = swap_y(messages[2])
-    x_new = swap_x(*messages[:2])
+    new = swap_all(*messages)
     return tuple(
         call(
             last_kernel,
             plan,
             [block, block],
-            [conc, pot, mob, mass_source, pot_source, *x_msg, y_msg, *x_new, y_new, total, spread],
+            [conc, pot, mob, mass_source, pot_source, *old, *new, total, spread],
             scratch=[pltpu.VMEM(((plan.groups + 2) * plan.owners, plan.p), F32)],
         )
     )

time: 47 us -> 37.7 us (0.80)
  blocking collectives: 16 us -> 0 us
  starting transfers between devices: 13.1 us -> 20.9 us
  waiting for transfers between devices: 8.99 us -> 7.89 us
    all_to_all x2 -> x0, blocking collectives: 16 us -> none  [swap_y(): return lax.all_to_all(slots, 'gy', split_axis=0, concat_axis=0, tiled=True)]
    all_to_all x1, starting transfers between devices: 4.75 us -> 8.7 us  [gather_totals(): lax.all_to_all(total, ('gx', 'gy'), split_axis=0, concat_axis=0, tiled=True)]
    ppermute x4 -> x8, starting transfers between devices: 8.33 us -> 12.2 us  [swap(): out.append(lax.ppermute(rows, axis, pairs + [(j, i) for i, j in pairs]))]
    ppermute x4 -> x8, waiting for transfers between devices: 3.26 us -> 2.21 us  [swap(): out.append(lax.ppermute(rows, axis, pairs + [(j, i) for i, j in pairs]))]
  transfers between devices with their start and end apart: 5 -> 9, of which waited for: 2 -> 4; matrix products, arithmetic and copies ran while one was open for 0% -> 0% of each run, Pallas kernels for 0% -> 0%
where the time goes in v2:
time: 37.7 us; the launch traced here: 37.4 us
  starting transfers between devices  20.9 us (55%)
  waiting for transfers between devices  7.89 us (21%)
  Pallas kernels  5.94 us (16%)
  local copies, waits for them, and re-layouts  1.84 us (5%)
  between operations  0.79 us (2%)
    ppermute x8, starting transfers between devices, swap(): out.append(lax.ppermute(rows, axis, pairs + [(j, i) for i, j in pairs]))  12.2 us
    all_to_all x1, starting transfers between devices, gather_totals(): lax.all_to_all(total, ('gx', 'gy'), split_axis=0, concat_axis=0, tiled=True)  8.7 us
    pallas_call x3, Pallas kernels, call(): pl.pallas_call(functools.partial(kernel, plan), out_shape=[jax.ShapeDtype...  5.94 us
    all_to_all x1, waiting for transfers between devices, gather_totals(): lax.all_to_all(total, ('gx', 'gy'), split_axis=0, concat_axis=0, tiled=True)  5.68 us
    ppermute x8, waiting for transfers between devices, swap(): out.append(lax.ppermute(rows, axis, pairs + [(j, i) for i, j in pairs]))  2.21 us
    unnamed x20, local copies, waits for them, and re-layouts  1.84 us
  transfers between devices with their start and end apart: 9, of which 4 were waited for; matrix products, arithmetic and copies ran while one was open for 0% of the time, Pallas kernels for 0%

profile of v2, /device:TPU:1, one launch (start us, length us, event | category | flops | bytes accessed | tf_op | source)
XLA Modules:
  0.0 37.4 jit_solution(12413584753371784463)
XLA Ops:
  0.6 0.0 copy-start.3
  0.6 0.0 copy-start.2
  0.7 0.0 copy-start.1
  0.7 0.0 copy-start
  0.7 2.0 %shard_map.95 = (f32[192,128]{1,0:T(8,128)}, f32[192,128]{1,0:T(8,128)}, f32[24,128]{1,0:T(8,128)}, f32[24,128]{1,0:T(8,128)}) custom-call(f32[4,64,128]{2,1,0:T(8,128)} %conc_ref.1, f32[4,64,128]{2,1,0:T(8,128)} %pot_ref.1, s32[4,64,128]{2,1,0:T(8,128)} %mask_ref.1, s32[4,64,128]{2,1,0:T(8,128)} %class_ref.1, s32[8,64]{1,0:T(8,128)} %owner_ref.1, f32[8]{0:T(128)} %table_ref.1), custom_call_target="tpu_custom_call" | custom-call | tf_op jit(solution)/shard_map/pallas_call | solution.py:416
  2.7 0.0 copy-start.8
  2.7 0.1 collective-permute-start
  2.8 4.5 %collective-permute-start.1 = (f32[192,128]{1,0:T(8,128)}, f32[192,128]{1,0:T(8,128)S(1)}, u32[]{:S(2)}, u32[]{:S(2)}) collective-permute-start(f32[192,128]{1,0:T(8,128)} %get-tuple-element.16), channel_id=1, source_target_pairs={{4,8},{12,16},{20,24},{8,4},{16,12},{24,20},{5,9},{13,17},{21,25},... | collective-permute-start | bytes 294920 | tf_op jit(solution)/shard_map/ppermute | solution.py:431
  7.3 0.0 copy-start.9
  7.3 1.4 %collective-permute-start.2 = (f32[24,128]{1,0:T(8,128)}, f32[24,128]{1,0:T(8,128)S(1)}, u32[]{:S(2)}, u32[]{:S(2)}) collective-permute-start(f32[24,128]{1,0:T(8,128)} %get-tuple-element.17), channel_id=1, source_target_pairs={{0,1},{2,3},{1,0},{3,2},{4,5},{6,7},{5,4},{7,6},{8,9},{10,11},{9,8... | collective-permute-start | bytes 36872 | tf_op jit(solution)/shard_map/ppermute | solution.py:431
  8.7 0.7 %collective-permute-start.3 = (f32[24,128]{1,0:T(8,128)}, f32[24,128]{1,0:T(8,128)S(1)}, u32[]{:S(2)}, u32[]{:S(2)}) collective-permute-start(f32[24,128]{1,0:T(8,128)} %get-tuple-element.18), channel_id=1, source_target_pairs={{1,2},{2,1},{5,6},{6,5},{9,10},{10,9},{13,14},{14,13},{17,18},{18,... | collective-permute-start | bytes 36872 | tf_op jit(solution)/shard_map/ppermute | solution.py:431
  9.3 0.8 %collective-permute-done.2.y_near_ref.y_near_msg = f32[24,128]{1,0:T(8,128)S(1)} collective-permute-done((f32[24,128]{1,0:T(8,128)}, f32[24,128]{1,0:T(8,128)S(1)}, u32[]{:S(2)}, u32[]{:S(2)}) %collective-permute-start.2) | collective-permute-done | bytes 12320 | tf_op jit(solution)/shard_map/ppermute | solution.py:431
  10.1 0.0 collective-permute-done.3.y_far_ref.y_far_msg
  10.1 0.0 collective-permute-done.x_near_ref.x_near_msg
  10.1 0.0 collective-permute-done.1.x_far_ref.x_far_msg
  10.1 0.0 copy-done.3
  10.2 0.0 copy-done.2
  10.2 0.0 copy-done.1
  10.2 0.0 copy-done
  10.2 0.0 copy-done.8
  10.2 0.0 copy-done.9
  10.2 0.0 copy-start.4
  10.2 0.9 %copy-done.4 = f32[4,64,128]{2,1,0:T(8,128)S(1)} copy-done((f32[4,64,128]{2,1,0:T(8,128)S(1)}, f32[4,64,128]{2,1,0:T(8,128)}, u32[]{:S(2)}) %copy-start.4) | copy-done | bytes 131096
  11.1 0.0 copy-start.6
  11.1 0.9 %copy-done.6 = f32[4,64,128]{2,1,0:T(8,128)S(1)} copy-done((f32[4,64,128]{2,1,0:T(8,128)S(1)}, f32[4,64,128]{2,1,0:T(8,128)}, u32[]{:S(2)}) %copy-start.6) | copy-done | bytes 131096
  12.0 2.4 %shard_map.96 = (f32[4,64,128]{2,1,0:T(8,128)S(1)}, f32[4,64,128]{2,1,0:T(8,128)S(1)}, f32[4,64,128]{2,1,0:T(8,128)S(1)}, f32[32,24,128]{2,1,0:T(8,128)}, f32[38...) custom-call(f32[4,64,128]{2,1,0:T(8,128)S(1)} %copy-done, ...), custom_call_target="tpu_custom_call" | custom-call | tf_op jit(solution)/shard_map/pallas_call | solution.py:416
  14.5 0.0 copy-start.5
  14.5 0.0 copy-start.7
  14.5 8.7 %all-to-all-start = ((f32[32,24,128]{2,1,0:T(8,128)}), f32[32,24,128]{2,1,0:T(8,128)S(1)}, u32[]{:S(2)}, u32[]{:S(2)}) async-start(f32[32,24,128]{2,1,0:T(8,128)} %get-tuple-element.26), calls=%async_computation | async-start | bytes 786432 | tf_op jit(solution)/shard_map/all_to_all | solution.py:441
  23.2 0.3 collective-permute-start.4
  23.5 3.4 %collective-permute-start.5 = (f32[128,128]{1,0:T(8,128)S(1)}, f32[128,128]{1,0:T(8,128)S(1)}, u32[]{:S(2)}, u32[]{:S(2)}) collective-permute-start(f32[128,128]{1,0:T(8,128)S(1)} %get-tuple-element.23), channel_id=1, source_target_pairs={{4,8},{12,16},{20,24},{8,4},{16,12},{24,20},{5,9},{13,17},{21,25},... | collective-permute-start | bytes 196616 | tf_op jit(solution)/shard_map/ppermute | solution.py:431
  26.9 1.3 %collective-permute-start.6 = (f32[8,128]{1,0:T(8,128)S(1)}, f32[8,128]{1,0:T(8,128)S(1)}, u32[]{:S(2)}, u32[]{:S(2)}) collective-permute-start(f32[8,128]{1,0:T(8,128)S(1)} %get-tuple-element.24), channel_id=1, source_target_pairs={{0,1},{2,3},{1,0},{3,2},{4,5},{6,7},{5,4},{7,6},{8,9},{10,11},{9,8... | collective-permute-start | bytes 12296 | tf_op jit(solution)/shard_map/ppermute | solution.py:431
  28.2 0.6 %collective-permute-start.7 = (f32[8,128]{1,0:T(8,128)S(1)}, f32[8,128]{1,0:T(8,128)S(1)}, u32[]{:S(2)}, u32[]{:S(2)}) collective-permute-start(f32[8,128]{1,0:T(8,128)S(1)} %get-tuple-element.25), channel_id=1, source_target_pairs={{1,2},{2,1},{5,6},{6,5},{9,10},{10,9},{13,14},{14,13},{17,18},{18,... | collective-permute-start | bytes 12296 | tf_op jit(solution)/shard_map/ppermute | solution.py:431
  28.8 1.0 %collective-permute-done.6.y_near_ref = f32[8,128]{1,0:T(8,128)S(1)} collective-permute-done((f32[8,128]{1,0:T(8,128)S(1)}, f32[8,128]{1,0:T(8,128)S(1)}, u32[]{:S(2)}, u32[]{:S(2)}) %collective-permute-start.6) | collective-permute-done | bytes 4128 | tf_op jit(solution)/shard_map/ppermute | solution.py:431
  29.9 0.0 collective-permute-done.7.y_far_ref
  29.9 0.0 collective-permute-done.4.x_near_ref
  29.9 0.4 collective-permute-done.5.x_far_ref
  30.2 5.7 %all-to-all-done = f32[32,24,128]{2,1,0:T(8,128)S(1)} async-done(((f32[32,24,128]{2,1,0:T(8,128)}), f32[32,24,128]{2,1,0:T(8,128)S(1)}, u32[]{:S(2)}, u32[]{:S(2)}) %all-to-all-start) | async-done | bytes 393248 | tf_op jit(solution)/shard_map/all_to_all | solution.py:441
  35.9 0.0 copy-done.5
  35.9 0.0 copy-done.7
  35.9 1.5 %shard_map.97 = (f32[4,64,128]{2,1,0:T(8,128)}, f32[4,64,128]{2,1,0:T(8,128)}) custom-call(f32[4,64,128]{2,1,0:T(8,128)S(1)} %get-tuple-element.19.conc_ref, f32[4,64,128]{2,1,0:T(8,128)S(1)} %get-tuple-element.20.pot_ref, f32[4,64,128]{2,1,0:T(8,128)S(1)} %get-tuple-element.21.mob_ref, f32[4,64,128]{2,1,0:T(8,128)S(1)} %copy-done.5, ...), custom_call_target="tpu_custom_call" | custom-call | tf_op jit(solution)/shard_map/pallas_call | solution.py:416
Async XLA Ops:
  0.6 9.5 %copy-start.3 = (s32[4,64,128]{2,1,0:T(8,128)S(1)}, s32[4,64,128]{2,1,0:T(8,128)}, u32[]{:S(2)}) copy-start(s32[4,64,128]{2,1,0:T(8,128)} %class_ref.1) | copy-start | bytes 393220
  0.6 9.5 %copy-start.2 = (s32[4,64,128]{2,1,0:T(8,128)S(1)}, s32[4,64,128]{2,1,0:T(8,128)}, u32[]{:S(2)}) copy-start(s32[4,64,128]{2,1,0:T(8,128)} %mask_ref.1) | copy-start | bytes 393220
  0.7 9.5 %copy-start.1 = (f32[4,64,128]{2,1,0:T(8,128)S(1)}, f32[4,64,128]{2,1,0:T(8,128)}, u32[]{:S(2)}) copy-start(f32[4,64,128]{2,1,0:T(8,128)} %pot_ref.1) | copy-start | bytes 393220
  0.7 9.5 %copy-start = (f32[4,64,128]{2,1,0:T(8,128)S(1)}, f32[4,64,128]{2,1,0:T(8,128)}, u32[]{:S(2)}) copy-start(f32[4,64,128]{2,1,0:T(8,128)} %conc_ref.1) | copy-start | bytes 393220
  2.7 7.5 %copy-start.8 = (s32[8,64]{1,0:T(8,128)S(1)}, s32[8,64]{1,0:T(8,128)}, u32[]{:S(2)}) copy-start(s32[8,64]{1,0:T(8,128)} %owner_ref.1) | copy-start | bytes 6148
  2.7 7.4 %collective-permute-start = (f32[192,128]{1,0:T(8,128)}, f32[192,128]{1,0:T(8,128)S(1)}, u32[]{:S(2)}, u32[]{:S(2)}) collective-permute-start(f32[192,128]{1,0:T(8,128)} %get-tuple-element.15), channel_id=1, source_target_pairs={{0,4},{8,12},{16,20},{24,28},{4,0},{12,8},{20,16},{28,24},{1,5},{9... | collective-permute-start | bytes 294920 | tf_op jit(solution)/shard_map/ppermute | solution.py:431
  2.8 7.3 %collective-permute-start.1 = (f32[192,128]{1,0:T(8,128)}, f32[192,128]{1,0:T(8,128)S(1)}, u32[]{:S(2)}, u32[]{:S(2)}) collective-permute-start(f32[192,128]{1,0:T(8,128)} %get-tuple-element.16), channel_id=1, source_target_pairs={{4,8},{12,16},{20,24},{8,4},{16,12},{24,20},{5,9},{13,17},{21,25},... | collective-permute-start | bytes 294920 | tf_op jit(solution)/shard_map/ppermute | solution.py:431
  7.3 2.9 %copy-start.9 = (f32[8]{0:T(128)S(1)}, f32[8]{0:T(128)}, u32[]{:S(2)}) copy-start(f32[8]{0:T(128)} %table_ref.1) | copy-start | bytes 100
  7.3 2.8 %collective-permute-start.2 = (f32[24,128]{1,0:T(8,128)}, f32[24,128]{1,0:T(8,128)S(1)}, u32[]{:S(2)}, u32[]{:S(2)}) collective-permute-start(f32[24,128]{1,0:T(8,128)} %get-tuple-element.17), channel_id=1, source_target_pairs={{0,1},{2,3},{1,0},{3,2},{4,5},{6,7},{5,4},{7,6},{8,9},{10,11},{9,8... | collective-permute-start | bytes 36872 | tf_op jit(solution)/shard_map/ppermute | solution.py:431
  8.7 1.5 %collective-permute-start.3 = (f32[24,128]{1,0:T(8,128)}, f32[24,128]{1,0:T(8,128)S(1)}, u32[]{:S(2)}, u32[]{:S(2)}) collective-permute-start(f32[24,128]{1,0:T(8,128)} %get-tuple-element.18), channel_id=1, source_target_pairs={{1,2},{2,1},{5,6},{6,5},{9,10},{10,9},{13,14},{14,13},{17,18},{18,... | collective-permute-start | bytes 36872 | tf_op jit(solution)/shard_map/ppermute | solution.py:431
  10.2 0.9 %copy-start.4 = (f32[4,64,128]{2,1,0:T(8,128)S(1)}, f32[4,64,128]{2,1,0:T(8,128)}, u32[]{:S(2)}) copy-start(f32[4,64,128]{2,1,0:T(8,128)} %mass_ref.3) | copy-start | bytes 393220
  11.1 0.9 %copy-start.6 = (f32[4,64,128]{2,1,0:T(8,128)S(1)}, f32[4,64,128]{2,1,0:T(8,128)}, u32[]{:S(2)}) copy-start(f32[4,64,128]{2,1,0:T(8,128)} %pots_ref.3) | copy-start | bytes 393220
  14.5 21.5 %copy-start.5 = (f32[4,64,128]{2,1,0:T(8,128)S(1)}, f32[4,64,128]{2,1,0:T(8,128)}, u32[]{:S(2)}) copy-start(f32[4,64,128]{2,1,0:T(8,128)} %mass_ref.3) | copy-start | bytes 393220
  14.5 21.5 %copy-start.7 = (f32[4,64,128]{2,1,0:T(8,128)S(1)}, f32[4,64,128]{2,1,0:T(8,128)}, u32[]{:S(2)}) copy-start(f32[4,64,128]{2,1,0:T(8,128)} %pots_ref.3) | copy-start | bytes 393220
  14.5 21.5 %all-to-all-start = ((f32[32,24,128]{2,1,0:T(8,128)}), f32[32,24,128]{2,1,0:T(8,128)S(1)}, u32[]{:S(2)}, u32[]{:S(2)}) async-start(f32[32,24,128]{2,1,0:T(8,128)} %get-tuple-element.26), calls=%async_computation | async-start | bytes 786432 | tf_op jit(solution)/shard_map/all_to_all | solution.py:441
  23.2 6.7 %collective-permute-start.4 = (f32[128,128]{1,0:T(8,128)S(1)}, f32[128,128]{1,0:T(8,128)S(1)}, u32[]{:S(2)}, u32[]{:S(2)}) collective-permute-start(f32[128,128]{1,0:T(8,128)S(1)} %get-tuple-element.22), channel_id=1, source_target_pairs={{0,4},{8,12},{16,20},{24,28},{4,0},{12,8},{20,16},{28,24},{1,5},{9... | collective-permute-start | bytes 196616 | tf_op jit(solution)/shard_map/ppermute | solution.py:431
  23.5 6.7 %collective-permute-start.5 = (f32[128,128]{1,0:T(8,128)S(1)}, f32[128,128]{1,0:T(8,128)S(1)}, u32[]{:S(2)}, u32[]{:S(2)}) collective-permute-start(f32[128,128]{1,0:T(8,128)S(1)} %get-tuple-element.23), channel_id=1, source_target_pairs={{4,8},{12,16},{20,24},{8,4},{16,12},{24,20},{5,9},{13,17},{21,25},... | collective-permute-start | bytes 196616 | tf_op jit(solution)/shard_map/ppermute | solution.py:431
  26.9 2.9 %collective-permute-start.6 = (f32[8,128]{1,0:T(8,128)S(1)}, f32[8,128]{1,0:T(8,128)S(1)}, u32[]{:S(2)}, u32[]{:S(2)}) collective-permute-start(f32[8,128]{1,0:T(8,128)S(1)} %get-tuple-element.24), channel_id=1, source_target_pairs={{0,1},{2,3},{1,0},{3,2},{4,5},{6,7},{5,4},{7,6},{8,9},{10,11},{9,8... | collective-permute-start | bytes 12296 | tf_op jit(solution)/shard_map/ppermute | solution.py:431
  28.2 1.7 %collective-permute-start.7 = (f32[8,128]{1,0:T(8,128)S(1)}, f32[8,128]{1,0:T(8,128)S(1)}, u32[]{:S(2)}, u32[]{:S(2)}) collective-permute-start(f32[8,128]{1,0:T(8,128)S(1)} %get-tuple-element.25), channel_id=1, source_target_pairs={{1,2},{2,1},{5,6},{6,5},{9,10},{10,9},{13,14},{14,13},{17,18},{18,... | collective-permute-start | bytes 12296 | tf_op jit(solution)/shard_map/ppermute | solution.py:431

commit v3 on v2

v3 whole, which is shorter than its diff:
```python
import functools

import jax
import jax.numpy as jnp
from jax import lax
from jax.experimental import pallas as pl
from jax.experimental.pallas import tpu as pltpu
from jax.sharding import PartitionSpec as P

CSWEEP = 3

time_step = 0.25
split_slope = 1.0
interface = 0.5
relax_fine = 0.6
relax_coarse = 0.6
coarse_flux = 0.0625
coarse_bend = 0.125
coarse_det = 1.0 + 2.0 * coarse_flux * (split_slope + 2.0 * coarse_bend)

F32 = jnp.float32
BF16 = jnp.bfloat16
VMEM_LIMIT = 48 * 1024 * 1024
LARGE_LIMIT = 60 * 1024 * 1024


def iota(shape, dim):
    return lax.broadcasted_iota(jnp.int32, shape, dim)


def x_pair(field, low, high):
    return (
        jnp.concatenate([low, field[:-1]], axis=0),
        jnp.concatenate([field[1:], high], axis=0),
    )


def y_pair(field, low, high):
    size = field.shape[1]
    where = iota(field.shape, 1)
    return (
        jnp.where(where == 0, low, pltpu.roll(field, 1, 1)),
        jnp.where(where == size - 1, high, pltpu.roll(field, size - 1, 1)),
    )


def plane_pair(field):
    size = field.shape[2]
    where = iota(field.shape, 2)
    return (
        jnp.where(where == 0, 0.0, pltpu.roll(field, 1, 2)),
        jnp.where(where == size - 1, 0.0, pltpu.roll(field, size - 1, 2)),
    )


def neighbours(field, halo):
    xm, xp, ym, yp = halo
    return (*x_pair(field, xm, xp), *y_pair(field, ym, yp), *plane_pair(field))


def excess_of(conc, pot, conc_halo, pot_halo, faces, mass_source, pot_source):
    flux = jnp.zeros_like(pot)
    for face, other in zip(faces, neighbours(pot, pot_halo)):
        flux = flux + face * (other - pot)
    laplace = -6.0 * conc
    for other in neighbours(conc, conc_halo):
        laplace = laplace + other
    excess_mass = mass_source - (conc - time_step * flux)
    excess_pot = pot_source - (pot - split_slope * conc + interface * laplace)
    return excess_mass, excess_pot


def relax_pair(conc, pot, excess_mass, excess_pot, diagonal):
    other_diagonal = -(split_slope + 6.0 * interface)
    scale = relax_fine / (1.0 - diagonal * other_diagonal)
    new_conc = conc + (excess_mass - diagonal * excess_pot) * scale
    new_pot = pot + (excess_pot - other_diagonal * excess_mass) * scale
    return new_conc, new_pot


def faces_of(mobility, halo):
    faces = tuple(0.5 * (mobility + other) for other in neighbours(mobility, halo))
    diagonal = faces[0]
    for face in faces[1:]:
        diagonal = diagonal + face
    return faces, time_step * diagonal


def split_dot(ones, values, contract):
    dims = (contract, ((), ()))
    total = None
    rest = values
    for _ in range(3):
        term = rest.astype(BF16)
        rest = rest - term.astype(F32)
        part = lax.dot_general(ones, term, dims, preferred_element_type=F32)
        total = part if total is None else total + part
    return total


def round_up(value, unit):
    return -(-value // unit) * unit


class Plan:
    def __init__(self, shape, owners, groups):
        self.x, self.y, self.p = shape
        self.owners, self.groups = owners, groups
        self.half_x, self.half_y = self.x // 2, self.y // 2
        self.columns = self.half_x * self.half_y
        self.map_row = round_up(3 * self.x, 8)
        self.y_rows = self.map_row + owners
        self.cells = self.x * self.y
        self.rows = self.cells + 2 * self.y
        self.low_row = owners
        self.high_row = owners + self.half_x
        self.slot_rows = round_up(owners + 2 * self.half_x, 8)
        slots = owners * groups
        self.slots = slots if slots <= 64 else 0


def side_rows(plan, rows, which):
    return rows[which * plan.y : (which + 1) * plan.y][None]


def side_columns(plan, rows, which):
    return rows[which * plan.x : (which + 1) * plan.x][:, None]


def membership(plan, owner_ref):
    g = lax.axis_index("gx")
    last = plan.owners - 1
    owner = iota((plan.owners, plan.columns), 0)
    shape = (plan.x + 2, plan.y, plan.columns)
    x, y, column = iota(shape, 0), iota(shape, 1), iota(shape, 2)
    half = jnp.where(x < plan.x, x >> 1, jnp.where(x == plan.x, plan.half_x - 1, 0))
    place = column == half * plan.half_y + (y >> 1)
    sides = (
        (x < plan.x, g, True),
        (x == plan.x, jnp.maximum(g - 1, 0), g > 0),
        (x == plan.x + 1, jnp.minimum(g + 1, last), g < last),
    )
    gather, spread = None, None
    for part, row, inside in sides:
        hits = ((owner_ref[pl.ds(row, 1), :] == owner) & inside).astype(F32).astype(BF16)
        where = (place & part).astype(F32).reshape(plan.rows, plan.columns).astype(BF16)
        nt = (((1,), (1,)), ((), ()))
        some = lax.dot_general(hits, where, nt, preferred_element_type=F32)
        gather = some if gather is None else gather + some
        some = lax.dot_general(where, hits, nt, preferred_element_type=F32)
        spread = some if spread is None else spread + some
    return gather, spread


def scale_of(plan, owners):
    owner = iota((plan.owners, plan.columns), 0).astype(owners.dtype)
    hits = jnp.zeros((plan.owners, plan.columns), F32)
    for g in range(plan.owners):
        hits = hits + (owners[g : g + 1] == owner).astype(F32)
    count = jnp.sum(hits, axis=1, keepdims=True)
    return jnp.broadcast_to(0.125 / jnp.maximum(count, 1.0), (plan.owners, plan.p))


def mobility_of(mask, kind, table):
    values = jnp.zeros(kind.shape, F32)
    for marker, value in enumerate(table):
        values = jnp.where(kind == marker, value, values)
    return mask.astype(F32) * values


def even(axis):
    return lax.rem(lax.axis_index(axis), 2) == 0


def put_edges(plan, fields, x_near, x_far, y_near, y_far):
    up_x, up_y = even("gx"), even("gy")
    whole = slice(0, plan.y)
    for which, field in enumerate(fields):
        low, high = field(0, whole), field(plan.x - 1, whole)
        x_near[pl.ds(which * plan.y, plan.y), :] = jnp.where(up_x, high, low)
        x_far[pl.ds(which * plan.y, plan.y), :] = jnp.where(up_x, low, high)
        for x in range(plan.x):
            low, high = field(x, slice(0, 1)), field(x, slice(plan.y - 1, plan.y))
            y_near[pl.ds(which * plan.x + x, 1), :] = jnp.where(up_y, high, low)
            y_far[pl.ds(which * plan.x + x, 1), :] = jnp.where(up_y, low, high)


def received(axis, near_ref, far_ref):
    up = even(axis)
    near, far = near_ref[...], far_ref[...]
    return jnp.where(up, far, near), jnp.where(up, near, far)


def prepare_kernel(
    plan, conc_hbm, pot_hbm, mask_hbm, class_hbm, owner_hbm, table_hbm,
    x_near_ref, x_far_ref, y_near_ref, y_far_ref,
    conc_ref, pot_ref, owner_ref, mask_ref, class_ref, table_ref, sems,
):
    pairs = (
        (table_hbm, table_ref), (class_hbm, class_ref), (mask_hbm, mask_ref),
        (conc_hbm, conc_ref), (pot_hbm, pot_ref), (owner_hbm, owner_ref),
    )
    copies = [
        pltpu.make_async_copy(source, target, sems.at[i])
        for i, (source, target) in enumerate(pairs)
    ]
    for copy in copies:
        copy.start()
    for copy in copies:
        copy.wait()
    table = [table_ref[marker] for marker in range(table_ref.shape[0])]
    send = (x_near_ref, x_far_ref, y_near_ref, y_far_ref)
    edges = [lambda x, y: conc_ref[x, y], lambda x, y: pot_ref[x, y]]
    edges.append(lambda x, y: mobility_of(mask_ref[x, y], class_ref[x, y], table))
    put_edges(plan, edges, *send)
    used = 3 * plan.x
    for ref in (y_near_ref, y_far_ref):
        ref[pl.ds(used, plan.y_rows - used), :] = jnp.zeros((plan.y_rows - used, plan.p), F32)
        ref[pl.ds(plan.map_row, plan.owners), pl.ds(0, plan.columns)] = owner_ref[...].astype(F32)


def local_kernel(
    plan, mask_ref, class_ref, table_ref, owner_ref, mob_ref, gather_ref, spread_ref, scale_ref
):
    table = [table_ref[marker] for marker in range(table_ref.shape[0])]
    mob_ref[...] = mobility_of(mask_ref[...], class_ref[...], table)
    gather_ref[...], spread_ref[...] = membership(plan, owner_ref)
    scale_ref[...] = scale_of(plan, owner_ref[...])


def first_kernel(
    plan, conc_ref, pot_ref, mob_ref, mass_ref, pots_ref, gather_ref, scale_ref, owner_ref,
    x_near_ref, x_far_ref, y_near_ref, y_far_ref,
    conc_out, pot_out, total_out, *send,
):
    sides = received("gx", x_near_ref, x_far_ref)
    ends = received("gy", y_near_ref, y_far_ref)

    def halo(which):
        return tuple(side_rows(plan, rows, which) for rows in sides) + tuple(
            side_columns(plan, rows, which) for rows in ends
        )

    mobility, mob_halo = mob_ref[...], halo(2)
    faces, diagonal = faces_of(mobility, mob_halo)
    mass_source, pot_source = mass_ref[...], pots_ref[...]
    conc, pot = conc_ref[...], pot_ref[...]
    excess = excess_of(conc, pot, halo(0), halo(1), faces, mass_source, pot_source)
    conc, pot = relax_pair(conc, pot, *excess, diagonal)
    conc_out[...] = conc
    pot_out[...] = pot
    put_edges(plan, (lambda x, y: conc[x, y], lambda x, y: pot[x, y]), *send)

    nothing = tuple(jnp.zeros_like(part) for part in mob_halo)
    own_mass, own_pot = excess_of(conc, pot, nothing, nothing, faces, mass_source, pot_source)
    give_mass = [own_mass.reshape(plan.cells, plan.p)]
    give_pot = [own_pot.reshape(plan.cells, plan.p)]
    for x, side in ((0, 0), (plan.x - 1, 1)):
        face = 0.5 * (mobility[x] + mob_halo[side][0])
        give_mass.append(time_step * face * pot[x])
        give_pot.append(-interface * conc[x])
    give = jnp.concatenate(
        [jnp.concatenate(give_mass, axis=0), jnp.concatenate(give_pot, axis=0)], axis=1
    )

    def packed(both):
        mass, other = both[:, : plan.p], both[:, plan.p :]
        first = iota(mass.shape, 1) & 1 == 0
        return jnp.where(
            first, mass + pltpu.roll(mass, plan.p - 1, 1), other + pltpu.roll(other, 1, 1)
        )

    h = lax.axis_index("gy")
    inside = (h > 0, None, h < plan.groups - 1)
    maps = [rows[plan.map_row : plan.map_row + plan.owners, : plan.columns] for rows in ends]
    maps.insert(1, owner_ref[...].astype(F32))
    owner = iota((plan.owners, 1), 0)
    is_mine = owner == lax.axis_index("gx")

    def column(place, i, at):
        b = i * plan.half_y + at
        return maps[place][:, b : b + 1]

    sums = [None, packed(split_dot(gather_ref[...].astype(BF16), give, ((1,), (0,)))), None]
    sums[1] = sums[1] * scale_ref[...]
    for place, y, at, side in ((0, 0, plan.half_y - 1, 2), (2, plan.y - 1, 0, 3)):
        edge_mob, edge_pot, edge_conc = (
            jnp.concatenate([field[x, y : y + 1] for x in range(plan.x)], axis=0)
            for field in (mobility, pot, conc)
        )
        face = 0.5 * (edge_mob + mob_halo[side][:, 0])
        both = jnp.concatenate([time_step * face * edge_pot, -interface * edge_conc], axis=1)
        part = jnp.zeros((plan.owners, 2 * plan.p), F32)
        for i in range(plan.half_x):
            ident = jnp.sum(jnp.where(is_mine, column(place, i, at), 0.0), axis=0, keepdims=True)
            pair = both[2 * i : 2 * i + 1] + both[2 * i + 1 : 2 * i + 2]
            part = part + jnp.where((owner.astype(F32) == ident) & inside[place], pair, 0.0)
        sums[place] = packed(part) * scale_of(plan, maps[place])

    if not plan.slots:
        total_out[...] = jnp.concatenate(sums, axis=0)
        return

    def picked(place, i, at):
        ident = jnp.broadcast_to(column(place, i, at), (plan.owners, plan.p))
        out = jnp.zeros((plan.owners, plan.p), F32)
        for o in range(plan.owners):
            out = jnp.where(ident == float(o), sums[place][o : o + 1], out)
        return out

    below = [[picked(k, i, plan.half_y - 1) for i in range(plan.half_x)] for k in range(3)]
    above = [[picked(k, i, 0) for i in range(plan.half_x)] for k in range(3)]

    def of_plane(plane, choices):
        out = jnp.zeros_like(choices[0])
        for k in range(3):
            out = jnp.where(plane == h + (k - 1), choices[k], out)
        return out

    blank = plan.slot_rows - plan.high_row - plan.half_x
    for plane in range(plan.groups):
        main = of_plane(plane, sums)
        beside = []
        for i in range(plan.half_x):
            beside.append((plan.low_row + i, of_plane(plane - 1, [k[i] for k in below])))
            beside.append((plan.high_row + i, of_plane(plane + 1, [k[i] for k in above])))
        for g in range(plan.owners):
            slot = g * plan.groups + plane
            total_out[slot, pl.ds(0, plan.owners), :] = main
            for row, values in beside:
                total_out[slot, pl.ds(row, 1), :] = values[g : g + 1]
            if blank:
                total_out[slot, pl.ds(plan.slot_rows - blank, blank), :] = jnp.zeros(
                    (blank, plan.p), F32
                )


def coarse_solve(packed, planes):
    lane = iota(packed.shape, 1)
    even = lane & 1 == 0
    mass_mean = jnp.where(even, packed, pltpu.roll(packed, 1, 1))
    pot_mean = jnp.where(even, pltpu.roll(packed, planes - 1, 1), packed)

    def neighbour_sum(values):
        return jnp.where(lane >= 2, pltpu.roll(values, 2, 1), 0.0) + jnp.where(
            lane < planes - 2, pltpu.roll(values, planes - 2, 1), 0.0
        )

    coarse_conc = jnp.zeros_like(mass_mean)
    coarse_pot = jnp.zeros_like(pot_mean)
    for _ in range(CSWEEP):
        mass_gap = mass_mean - (
            coarse_conc + coarse_flux * (2.0 * coarse_pot - neighbour_sum(coarse_pot))
        )
        pot_gap = pot_mean - (
            coarse_pot
            - split_slope * coarse_conc
            + coarse_bend * (neighbour_sum(coarse_conc) - 2.0 * coarse_conc)
        )
        coarse_conc = coarse_conc + (relax_coarse / coarse_det) * (
            mass_gap - 2.0 * coarse_flux * pot_gap
        )
        coarse_pot = coarse_pot + (relax_coarse / coarse_det) * (
            pot_gap + (split_slope + 2.0 * coarse_bend) * mass_gap
        )
    return coarse_conc, coarse_pot


def last_kernel(
    plan, conc_ref, pot_ref, mob_ref, mass_ref, pots_ref, x_near_msg, x_far_msg,
    y_near_msg, y_far_msg, x_near_ref, x_far_ref, y_near_ref, y_far_ref, total_ref, spread_ref,
    conc_out, pot_out,
):
    means = total_ref[0]
    for slot in range(1, total_ref.shape[0]):
        means = means + total_ref[slot]
    solved = jnp.concatenate(coarse_solve(means, plan.p), axis=1)
    own = split_dot(spread_ref[...].astype(BF16), solved[: plan.owners], ((1,), (0,)))
    ends = received("gy", y_near_msg, y_far_msg)
    sides = received("gx", x_near_msg, x_far_msg)
    y_corr = []
    for begin in (plan.low_row, plan.high_row):
        rows = [solved[begin + (x >> 1) : begin + (x >> 1) + 1] for x in range(plan.x)]
        y_corr.append(jnp.concatenate(rows, axis=0))
    new_ends = received("gy", y_near_ref, y_far_ref)
    new_sides = received("gx", x_near_ref, x_far_ref)

    def updated(which, ref):
        lanes = slice(which * plan.p, (which + 1) * plan.p)
        corr = own[:, lanes]
        field = ref[...] + corr[: plan.cells].reshape(plan.x, plan.y, plan.p)
        halo = []
        for side, rows in enumerate(new_sides):
            begin = plan.cells + side * plan.y
            halo.append(side_rows(plan, rows, which) + corr[begin : begin + plan.y][None])
        for rows, edge in zip(new_ends, y_corr):
            halo.append((rows[which * plan.x : (which + 1) * plan.x] + edge[:, lanes])[:, None])
        return field, halo

    conc, conc_halo = updated(0, conc_ref)
    pot, pot_halo = updated(1, pot_ref)
    mob_halo = (
        side_rows(plan, sides[0], 2),
        side_rows(plan, sides[1], 2),
        side_columns(plan, ends[0], 2),
        side_columns(plan, ends[1], 2),
    )
    faces, diagonal = faces_of(mob_ref[...], mob_halo)
    excess = excess_of(conc, pot, conc_halo, pot_halo, faces, mass_ref[...], pots_ref[...])
    conc_out[...], pot_out[...] = relax_pair(conc, pot, *excess, diagonal)


def call(kernel, plan, outs, args, far=(), smem=(), scratch=(), limit=VMEM_LIMIT):
    def space(i):
        return pl.ANY if i in far else pltpu.SMEM if i in smem else pltpu.VMEM

    return pl.pallas_call(
        functools.partial(kernel, plan),
        out_shape=[jax.ShapeDtypeStruct(shape, F32) for shape in outs],
        in_specs=[pl.BlockSpec(memory_space=space(i)) for i in range(len(args))],
        out_specs=[pl.BlockSpec(memory_space=pltpu.VMEM)] * len(outs),
        scratch_shapes=list(scratch),
        compiler_params=pltpu.CompilerParams(vmem_limit_bytes=limit),
    )(*args)


def swap(axis, near, far):
    count = lax.axis_size(axis)
    out = []
    for rows, begin in ((near, 0), (far, 1)):
        pairs = [(i, i + 1) for i in range(begin, count - 1, 2)]
        out.append(lax.ppermute(rows, axis, pairs + [(j, i) for i, j in pairs]))
    return out


def swap_all(x_near, x_far, y_near, y_far):
    return *swap("gx", x_near, x_far), *swap("gy", y_near, y_far)


def gather_totals(plan, total, y_near, y_far):
    if plan.slots:
        return lax.all_to_all(total, ("gx", "gy"), split_axis=0, concat_axis=0, tiled=True)
    shape = (plan.groups, 3, plan.owners, plan.p)
    parts = lax.all_gather(lax.psum(total, "gx"), "gy").reshape(shape)
    blank = jnp.zeros((1, plan.owners, plan.p), F32)
    to_below, own, to_above = (parts[:, k] for k in range(3))
    own = own + jnp.concatenate([blank, to_above[:-1]]) + jnp.concatenate([to_below[1:], blank])
    own = jnp.concatenate([blank, own, blank])
    g, h = lax.axis_index("gx"), lax.axis_index("gy")
    rows = [lax.dynamic_index_in_dim(own, h + 1, 0, False)]
    up = lax.rem(h, 2) == 0
    for place, at, msg in (
        (h, plan.half_y - 1, jnp.where(up, y_far, y_near)),
        (h + 2, 0, jnp.where(up, y_near, y_far)),
    ):
        ident = lax.dynamic_index_in_dim(msg, plan.map_row + g, 0, False).astype(jnp.int32)
        ident = jnp.stack([ident[i * plan.half_y + at] for i in range(plan.half_x)])
        rows.append(lax.dynamic_index_in_dim(own, place, 0, False)[ident])
    rows = jnp.concatenate(rows)
    return jnp.pad(rows, ((0, plan.slot_rows - rows.shape[0]), (0, 0)))[None]


def on_device(conc, pot, mass_source, pot_source, mask, kind, table, owner_map):
    plan = Plan(conc.shape, lax.axis_size("gx"), lax.axis_size("gy"))
    block = conc.shape
    messages = call(
        prepare_kernel,
        plan,
        [*[(3 * plan.y, plan.p)] * 2, *[(plan.y_rows, plan.p)] * 2],
        [conc, pot, mask, kind, owner_map, table],
        far=range(6),
        limit=LARGE_LIMIT,
        scratch=(
            pltpu.VMEM(block, F32),
            pltpu.VMEM(block, F32),
            pltpu.VMEM(owner_map.shape, owner_map.dtype),
            pltpu.VMEM(block, mask.dtype),
            pltpu.VMEM(block, kind.dtype),
            pltpu.SMEM(table.shape, table.dtype),
            pltpu.SemaphoreType.DMA((6,)),
        ),
    )
    old = swap_all(*messages)
    near, mask, kind = lax.optimization_barrier((old[0], mask, kind))
    old = (near, *old[1:])
    mob, gather, spread, scale = call(
        local_kernel,
        plan,
        [block, (plan.owners, plan.rows), (plan.rows, plan.owners), (plan.owners, plan.p)],
        [mask, kind, table, owner_map],
        smem=(2,),
    )
    conc, pot, total, *messages = call(
        first_kernel,
        plan,
        [
            block,
            block,
            (plan.slots, plan.slot_rows, plan.p) if plan.slots else (3 * plan.owners, plan.p),
            *[(2 * plan.y, plan.p)] * 2,
            *[(2 * plan.x, plan.p)] * 2,
        ],
        [conc, pot, mob, mass_source, pot_source, gather, scale, owner_map, *old],
    )
    total = gather_totals(plan, total, *old[2:])
    new = swap_all(*messages)
    return tuple(
        call(
            last_kernel,
            plan,
            [block, block],
            [conc, pot, mob, mass_source, pot_source, *old, *new, total, spread],
        )
    )


def solution(mesh):
    grid = P("gx", "gy", None)
    return jax.shard_map(
        on_device,
        mesh=mesh,
        in_specs=(grid,) * 6 + (P(), P(None, "gy")),
        out_specs=(grid, grid),
        check_vma=False,
    )
```

time: 37.7 us -> 32.9 us (0.87)
  the two profiles are of different devices: /device:TPU:1 before, /device:TPU:0 now
where the time goes in v3:
time: 32.9 us; the launch traced here: 32.6 us
  starting transfers between devices  18.7 us (57%)
  waiting for transfers between devices  7.01 us (21%)
  Pallas kernels  6.04 us (18%)
  between operations  0.81 us (2%)
    all_to_all x1, starting transfers between devices, gather_totals(): lax.all_to_all(total, ('gx', 'gy'), split_axis=0, concat_axis=0, tiled=True)  10.7 us
    ppermute x8, starting transfers between devices, swap(): out.append(lax.ppermute(rows, axis, pairs + [(j, i) for i, j in pairs]))  7.97 us
    pallas_call x4, Pallas kernels, call(): pl.pallas_call(functools.partial(kernel, plan), out_shape=[jax.ShapeDtype...  6.04 us
    all_to_all x1, waiting for transfers between devices, gather_totals(): lax.all_to_all(total, ('gx', 'gy'), split_axis=0, concat_axis=0, tiled=True)  5.19 us
    ppermute x8, waiting for transfers between devices, swap(): out.append(lax.ppermute(rows, axis, pairs + [(j, i) for i, j in pairs]))  1.82 us
  transfers between devices with their start and end apart: 9, of which 3 were waited for; matrix products, arithmetic and copies ran while one was open for 0% of the time, Pallas kernels for 3%

profile of v3, /device:TPU:0, one launch (start us, length us, event | category | flops | bytes accessed | tf_op | source)
XLA Modules:
  0.0 32.6 jit_solution(9939693119498048477)
XLA Ops:
  0.6 0.0 copy-start.5
  0.6 0.0 copy-start.4
  0.7 0.0 copy-start.2
  0.7 0.0 copy-start.3
  0.7 1.9 %shard_map.95 = (f32[192,128]{1,0:T(8,128)}, f32[192,128]{1,0:T(8,128)}, f32[24,128]{1,0:T(8,128)}, f32[24,128]{1,0:T(8,128)}) custom-call(f32[4,64,128]{2,1,0:T(8,128)} %conc_ref.1, f32[4,64,128]{2,1,0:T(8,128)} %pot_ref.1, s32[4,64,128]{2,1,0:T(8,128)} %mask_ref, s32[4,64,128]{2,1,0:T(8,128)} %class_ref, s32[8,64]{1,0:T(8,128)} %owner_ref.3, f32[8]{0:T(128)} %table_ref.1), custom_call_target="tpu_custom_call" | custom-call | tf_op jit(solution)/shard_map/pallas_call | solution.py:417
  2.6 0.0 copy-start.6
  2.6 0.5 %collective-permute-start = (f32[192,128]{1,0:T(8,128)}, f32[192,128]{1,0:T(8,128)S(1)}, u32[]{:S(2)}, u32[]{:S(2)}) collective-permute-start(f32[192,128]{1,0:T(8,128)} %get-tuple-element.20), channel_id=1, source_target_pairs={{0,4},{8,12},{16,20},{24,28},{4,0},{12,8},{20,16},{28,24},{1,5},{9... | collective-permute-start | bytes 294920 | tf_op jit(solution)/shard_map/ppermute | solution.py:432
  3.1 0.7 %collective-permute-start.1 = (f32[192,128]{1,0:T(8,128)}, f32[192,128]{1,0:T(8,128)S(1)}, u32[]{:S(2)}, u32[]{:S(2)}) collective-permute-start(f32[192,128]{1,0:T(8,128)} %get-tuple-element.27), channel_id=1, source_target_pairs={{4,8},{12,16},{20,24},{8,4},{16,12},{24,20},{5,9},{13,17},{21,25},... | collective-permute-start | bytes 294920 | tf_op jit(solution)/shard_map/ppermute | solution.py:432
  3.8 0.0 copy-start.7
  3.8 2.7 %collective-permute-start.2 = (f32[24,128]{1,0:T(8,128)}, f32[24,128]{1,0:T(8,128)S(1)}, u32[]{:S(2)}, u32[]{:S(2)}) collective-permute-start(f32[24,128]{1,0:T(8,128)} %get-tuple-element.28), channel_id=1, source_target_pairs={{0,1},{2,3},{1,0},{3,2},{4,5},{6,7},{5,4},{7,6},{8,9},{10,11},{9,8... | collective-permute-start | bytes 36872 | tf_op jit(solution)/shard_map/ppermute | solution.py:432
  6.5 0.0 copy-start
  6.5 0.0 copy-start.1
  6.5 0.8 %collective-permute-start.3 = (f32[24,128]{1,0:T(8,128)}, f32[24,128]{1,0:T(8,128)S(1)}, u32[]{:S(2)}, u32[]{:S(2)}) collective-permute-start(f32[24,128]{1,0:T(8,128)} %get-tuple-element.29), channel_id=1, source_target_pairs={{1,2},{2,1},{5,6},{6,5},{9,10},{10,9},{13,14},{14,13},{17,18},{18,... | collective-permute-start | bytes 36872 | tf_op jit(solution)/shard_map/ppermute | solution.py:432
  7.3 0.0 collective-permute-done.x_near_ref.x_near_msg
  7.3 0.0 copy-done.5
  7.3 0.0 copy-done.4
  7.3 0.0 copy-done.6
  7.3 0.0 copy-done.7
  7.3 0.9 %shard_map.96 = (f32[4,64,128]{2,1,0:T(8,128)S(1)}, f32[8,384]{1,0:T(8,128)S(1)}, f32[384,8]{1,0:T(8,128)S(1)}, f32[8,128]{1,0:T(8,128)S(1)}) custom-call(s32[4,64,128]{2,1,0:T(8,128)S(1)} %copy-done.4, s32[4,64,128]{2,1,0:T(8,128)S(1)} %copy-done.5, f32[8]{0:T(128)S(1)} %copy-done.7, s32[8,64]{1,0:T(8,128)S(1)} %copy-done.6), custom_call_target="tpu_custom_call" | custom-call | tf_op jit(solution)/shard_map/pallas_call | solution.py:417
  8.2 0.2 collective-permute-done.2.y_near_ref.y_near_msg
  8.4 0.0 collective-permute-done.3.y_far_ref.y_far_msg
  8.4 0.0 collective-permute-done.1.x_far_ref.x_far_msg
  8.4 0.0 copy-done.2
  8.4 0.0 copy-done.3
  8.4 0.0 copy-done
  8.4 0.0 copy-done.1
  8.4 1.8 %shard_map.97 = (f32[4,64,128]{2,1,0:T(8,128)S(1)}, f32[4,64,128]{2,1,0:T(8,128)S(1)}, f32[32,16,128]{2,1,0:T(8,128)}, f32[128,128]{1,0:T(8,128)S(1)}, f32[128,1...) custom-call(f32[4,64,128]{2,1,0:T(8,128)S(1)} %copy-done, f32[4,64,128]{2,1,0:T(8,128)S(1)} %copy-done.1, ...), custom_call_target="tpu_custom_call" | custom-call | tf_op jit(solution)/shard_map/pallas_call | solution.py:417
  10.2 10.7 %all-to-all-start = ((f32[32,16,128]{2,1,0:T(8,128)}), f32[32,16,128]{2,1,0:T(8,128)S(1)}, u32[]{:S(2)}, u32[]{:S(2)}) async-start(f32[32,16,128]{2,1,0:T(8,128)} %get-tuple-element.36), calls=%async_computation | async-start | bytes 524288 | tf_op jit(solution)/shard_map/all_to_all | solution.py:442
  20.9 0.3 collective-permute-start.4
  21.2 0.7 %collective-permute-start.5 = (f32[128,128]{1,0:T(8,128)S(1)}, f32[128,128]{1,0:T(8,128)S(1)}, u32[]{:S(2)}, u32[]{:S(2)}) collective-permute-start(f32[128,128]{1,0:T(8,128)S(1)} %get-tuple-element.33), channel_id=1, source_target_pairs={{4,8},{12,16},{20,24},{8,4},{16,12},{24,20},{5,9},{13,17},{21,25},... | collective-permute-start | bytes 196616 | tf_op jit(solution)/shard_map/ppermute | solution.py:432
  21.9 1.7 %collective-permute-start.6 = (f32[8,128]{1,0:T(8,128)S(1)}, f32[8,128]{1,0:T(8,128)S(1)}, u32[]{:S(2)}, u32[]{:S(2)}) collective-permute-start(f32[8,128]{1,0:T(8,128)S(1)} %get-tuple-element.34), channel_id=1, source_target_pairs={{0,1},{2,3},{1,0},{3,2},{4,5},{6,7},{5,4},{7,6},{8,9},{10,11},{9,8... | collective-permute-start | bytes 12296 | tf_op jit(solution)/shard_map/ppermute | solution.py:432
  23.6 0.6 %collective-permute-start.7 = (f32[8,128]{1,0:T(8,128)S(1)}, f32[8,128]{1,0:T(8,128)S(1)}, u32[]{:S(2)}, u32[]{:S(2)}) collective-permute-start(f32[8,128]{1,0:T(8,128)S(1)} %get-tuple-element.35), channel_id=1, source_target_pairs={{1,2},{2,1},{5,6},{6,5},{9,10},{10,9},{13,14},{14,13},{17,18},{18,... | collective-permute-start | bytes 12296 | tf_op jit(solution)/shard_map/ppermute | solution.py:432
  24.3 1.6 %collective-permute-done.6.y_near_ref = f32[8,128]{1,0:T(8,128)S(1)} collective-permute-done((f32[8,128]{1,0:T(8,128)S(1)}, f32[8,128]{1,0:T(8,128)S(1)}, u32[]{:S(2)}, u32[]{:S(2)}) %collective-permute-start.6) | collective-permute-done | bytes 4128 | tf_op jit(solution)/shard_map/ppermute | solution.py:432
  25.9 0.0 collective-permute-done.7.y_far_ref
  25.9 0.0 collective-permute-done.4.x_near_ref
  25.9 0.0 collective-permute-done.5.x_far_ref
  25.9 5.2 %all-to-all-done.total_ref = f32[32,16,128]{2,1,0:T(8,128)S(1)} async-done(((f32[32,16,128]{2,1,0:T(8,128)}), f32[32,16,128]{2,1,0:T(8,128)S(1)}, u32[]{:S(2)}, u32[]{:S(2)}) %all-to-all-start) | async-done | bytes 262176 | tf_op jit(solution)/shard_map/all_to_all | solution.py:442
  31.1 1.5 %shard_map.98 = (f32[4,64,128]{2,1,0:T(8,128)}, f32[4,64,128]{2,1,0:T(8,128)}) custom-call(f32[4,64,128]{2,1,0:T(8,128)S(1)} %get-tuple-element.30.conc_ref, f32[4,64,128]{2,1,0:T(8,128)S(1)} %get-tuple-element.31.pot_ref, f32[4,64,128]{2,1,0:T(8,128)S(1)} %get-tuple-element.23.mob_ref, f32[4,64,128]{2,1,0:T(8,128)S(1)} %copy-done.2, ...), custom_call_target="tpu_custom_call" | custom-call | tf_op jit(solution)/shard_map/pallas_call | solution.py:417
Async XLA Ops:
  0.6 6.7 %copy-start.5 = (s32[4,64,128]{2,1,0:T(8,128)S(1)}, s32[4,64,128]{2,1,0:T(8,128)}, u32[]{:S(2)}) copy-start(s32[4,64,128]{2,1,0:T(8,128)} %class_ref) | copy-start | bytes 393220
  0.6 6.7 %copy-start.4 = (s32[4,64,128]{2,1,0:T(8,128)S(1)}, s32[4,64,128]{2,1,0:T(8,128)}, u32[]{:S(2)}) copy-start(s32[4,64,128]{2,1,0:T(8,128)} %mask_ref) | copy-start | bytes 393220
  0.7 7.7 %copy-start.2 = (f32[4,64,128]{2,1,0:T(8,128)S(1)}, f32[4,64,128]{2,1,0:T(8,128)}, u32[]{:S(2)}) copy-start(f32[4,64,128]{2,1,0:T(8,128)} %mass_ref.3) | copy-start | bytes 393220
  0.7 7.7 %copy-start.3 = (f32[4,64,128]{2,1,0:T(8,128)S(1)}, f32[4,64,128]{2,1,0:T(8,128)}, u32[]{:S(2)}) copy-start(f32[4,64,128]{2,1,0:T(8,128)} %pots_ref.3) | copy-start | bytes 393220
  2.6 4.7 %copy-start.6 = (s32[8,64]{1,0:T(8,128)S(1)}, s32[8,64]{1,0:T(8,128)}, u32[]{:S(2)}) copy-start(s32[8,64]{1,0:T(8,128)} %owner_ref.3) | copy-start | bytes 6148
  2.6 4.7 %collective-permute-start = (f32[192,128]{1,0:T(8,128)}, f32[192,128]{1,0:T(8,128)S(1)}, u32[]{:S(2)}, u32[]{:S(2)}) collective-permute-start(f32[192,128]{1,0:T(8,128)} %get-tuple-element.20), channel_id=1, source_target_pairs={{0,4},{8,12},{16,20},{24,28},{4,0},{12,8},{20,16},{28,24},{1,5},{9... | collective-permute-start | bytes 294920 | tf_op jit(solution)/shard_map/ppermute | solution.py:432
  3.1 5.2 %collective-permute-start.1 = (f32[192,128]{1,0:T(8,128)}, f32[192,128]{1,0:T(8,128)S(1)}, u32[]{:S(2)}, u32[]{:S(2)}) collective-permute-start(f32[192,128]{1,0:T(8,128)} %get-tuple-element.27), channel_id=1, source_target_pairs={{4,8},{12,16},{20,24},{8,4},{16,12},{24,20},{5,9},{13,17},{21,25},... | collective-permute-start | bytes 294920 | tf_op jit(solution)/shard_map/ppermute | solution.py:432
  3.8 3.5 %copy-start.7 = (f32[8]{0:T(128)S(1)}, f32[8]{0:T(128)}, u32[]{:S(2)}) copy-start(f32[8]{0:T(128)} %table_ref.1) | copy-start | bytes 100
  3.8 4.5 %collective-permute-start.2 = (f32[24,128]{1,0:T(8,128)}, f32[24,128]{1,0:T(8,128)S(1)}, u32[]{:S(2)}, u32[]{:S(2)}) collective-permute-start(f32[24,128]{1,0:T(8,128)} %get-tuple-element.28), channel_id=1, source_target_pairs={{0,1},{2,3},{1,0},{3,2},{4,5},{6,7},{5,4},{7,6},{8,9},{10,11},{9,8... | collective-permute-start | bytes 36872 | tf_op jit(solution)/shard_map/ppermute | solution.py:432
  6.5 1.9 %copy-start = (f32[4,64,128]{2,1,0:T(8,128)S(1)}, f32[4,64,128]{2,1,0:T(8,128)}, u32[]{:S(2)}) copy-start(f32[4,64,128]{2,1,0:T(8,128)} %conc_ref.1) | copy-start | bytes 393220
  6.5 1.9 %copy-start.1 = (f32[4,64,128]{2,1,0:T(8,128)S(1)}, f32[4,64,128]{2,1,0:T(8,128)}, u32[]{:S(2)}) copy-start(f32[4,64,128]{2,1,0:T(8,128)} %pot_ref.1) | copy-start | bytes 393220
  6.5 1.9 %collective-permute-start.3 = (f32[24,128]{1,0:T(8,128)}, f32[24,128]{1,0:T(8,128)S(1)}, u32[]{:S(2)}, u32[]{:S(2)}) collective-permute-start(f32[24,128]{1,0:T(8,128)} %get-tuple-element.29), channel_id=1, source_target_pairs={{1,2},{2,1},{5,6},{6,5},{9,10},{10,9},{13,14},{14,13},{17,18},{18,... | collective-permute-start | bytes 36872 | tf_op jit(solution)/shard_map/ppermute | solution.py:432
  10.2 20.9 %all-to-all-start = ((f32[32,16,128]{2,1,0:T(8,128)}), f32[32,16,128]{2,1,0:T(8,128)S(1)}, u32[]{:S(2)}, u32[]{:S(2)}) async-start(f32[32,16,128]{2,1,0:T(8,128)} %get-tuple-element.36), calls=%async_computation | async-start | bytes 524288 | tf_op jit(solution)/shard_map/all_to_all | solution.py:442
  20.9 5.0 %collective-permute-start.4 = (f32[128,128]{1,0:T(8,128)S(1)}, f32[128,128]{1,0:T(8,128)S(1)}, u32[]{:S(2)}, u32[]{:S(2)}) collective-permute-start(f32[128,128]{1,0:T(8,128)S(1)} %get-tuple-element.32), channel_id=1, source_target_pairs={{0,4},{8,12},{16,20},{24,28},{4,0},{12,8},{20,16},{28,24},{1,5},{9... | collective-permute-start | bytes 196616 | tf_op jit(solution)/shard_map/ppermute | solution.py:432
  21.2 4.7 %collective-permute-start.5 = (f32[128,128]{1,0:T(8,128)S(1)}, f32[128,128]{1,0:T(8,128)S(1)}, u32[]{:S(2)}, u32[]{:S(2)}) collective-permute-start(f32[128,128]{1,0:T(8,128)S(1)} %get-tuple-element.33), channel_id=1, source_target_pairs={{4,8},{12,16},{20,24},{8,4},{16,12},{24,20},{5,9},{13,17},{21,25},... | collective-permute-start | bytes 196616 | tf_op jit(solution)/shard_map/ppermute | solution.py:432
  21.9 4.0 %collective-permute-start.6 = (f32[8,128]{1,0:T(8,128)S(1)}, f32[8,128]{1,0:T(8,128)S(1)}, u32[]{:S(2)}, u32[]{:S(2)}) collective-permute-start(f32[8,128]{1,0:T(8,128)S(1)} %get-tuple-element.34), channel_id=1, source_target_pairs={{0,1},{2,3},{1,0},{3,2},{4,5},{6,7},{5,4},{7,6},{8,9},{10,11},{9,8... | collective-permute-start | bytes 12296 | tf_op jit(solution)/shard_map/ppermute | solution.py:432
  23.6 2.3 %collective-permute-start.7 = (f32[8,128]{1,0:T(8,128)S(1)}, f32[8,128]{1,0:T(8,128)S(1)}, u32[]{:S(2)}, u32[]{:S(2)}) collective-permute-start(f32[8,128]{1,0:T(8,128)S(1)} %get-tuple-element.35), channel_id=1, source_target_pairs={{1,2},{2,1},{5,6},{6,5},{9,10},{10,9},{13,14},{14,13},{17,18},{18,... | collective-permute-start | bytes 12296 | tf_op jit(solution)/shard_map/ppermute | solution.py:432

commit v4 on v3

--- a/solution.py
+++ b/solution.py
@@ -58,32 +58,33 @@
     return (*x_pair(field, xm, xp), *y_pair(field, ym, yp), *plane_pair(field))
 
 
-def excess_of(conc, pot, conc_halo, pot_halo, faces, mass_source, pot_source):
-    flux = jnp.zeros_like(pot)
-    for face, other in zip(faces, neighbours(pot, pot_halo)):
-        flux = flux + face * (other - pot)
-    laplace = -6.0 * conc
-    for other in neighbours(conc, conc_halo):
-        laplace = laplace + other
-    excess_mass = mass_source - (conc - time_step * flux)
-    excess_pot = pot_source - (pot - split_slope * conc + interface * laplace)
+def excess_of(conc, pot, conc_beside, pot_beside, faces, diagonal, mass_source, pot_source):
+    excess_mass = (mass_source - conc) - diagonal * pot
+    for face, other in zip(faces, pot_beside):
+        excess_mass = excess_mass + face * other
+    beside = conc_beside[0]
+    for other in conc_beside[1:]:
+        beside = beside + other
+    excess_pot = (pot_source - pot) + (split_slope + 6.0 * interface) * conc - interface * beside
     return excess_mass, excess_pot
 
 
-def relax_pair(conc, pot, excess_mass, excess_pot, diagonal):
-    other_diagonal = -(split_slope + 6.0 * interface)
-    scale = relax_fine / (1.0 - diagonal * other_diagonal)
+def scale_from(diagonal):
+    return relax_fine / (1.0 + (split_slope + 6.0 * interface) * diagonal)
+
+
+def relax_pair(conc, pot, excess_mass, excess_pot, diagonal, scale):
     new_conc = conc + (excess_mass - diagonal * excess_pot) * scale
-    new_pot = pot + (excess_pot - other_diagonal * excess_mass) * scale
+    new_pot = pot + (excess_pot + (split_slope + 6.0 * interface) * excess_mass) * scale
     return new_conc, new_pot
 
 
-def faces_of(mobility, halo):
-    faces = tuple(0.5 * (mobility + other) for other in neighbours(mobility, halo))
+def faces_of(mobility, beside):
+    faces = tuple((0.5 * time_step) * (mobility + other) for other in beside)
     diagonal = faces[0]
     for face in faces[1:]:
         diagonal = diagonal + face
-    return faces, time_step * diagonal
+    return faces, diagonal
 
 
 def split_dot(ones, values, contract):
@@ -98,6 +99,14 @@
     return total
 
 
+def three_terms(values):
+    out = []
+    for _ in range(3):
+        out.append(values.astype(BF16).astype(F32))
+        values = values - out[-1]
+    return jnp.concatenate(out, axis=0)
+
+
 def round_up(value, unit):
     return -(-value // unit) * unit
 
@@ -108,13 +117,13 @@
         self.owners, self.groups = owners, groups
         self.half_x, self.half_y = self.x // 2, self.y // 2
         self.columns = self.half_x * self.half_y
-        self.map_row = round_up(3 * self.x, 8)
+        self.map_row = round_up(8 * self.x, 8)
         self.y_rows = self.map_row + owners
         self.cells = self.x * self.y
         self.rows = self.cells + 2 * self.y
         self.low_row = owners
         self.high_row = owners + self.half_x
-        self.slot_rows = round_up(owners + 2 * self.half_x, 8)
+        self.slot_parts = -(-(owners + 2 * self.half_x) // 4)
         slots = owners * groups
         self.slots = slots if slots <= 64 else 0
 
@@ -149,7 +158,7 @@
         gather = some if gather is None else gather + some
         some = lax.dot_general(where, hits, nt, preferred_element_type=F32)
         spread = some if spread is None else spread + some
-    return gather, spread
+    return gather, jnp.concatenate([spread] * 3, axis=1)
 
 
 def scale_of(plan, owners):
@@ -172,17 +181,11 @@
     return lax.rem(lax.axis_index(axis), 2) == 0
 
 
-def put_edges(plan, fields, x_near, x_far, y_near, y_far):
-    up_x, up_y = even("gx"), even("gy")
-    whole = slice(0, plan.y)
-    for which, field in enumerate(fields):
-        low, high = field(0, whole), field(plan.x - 1, whole)
-        x_near[pl.ds(which * plan.y, plan.y), :] = jnp.where(up_x, high, low)
-        x_far[pl.ds(which * plan.y, plan.y), :] = jnp.where(up_x, low, high)
-        for x in range(plan.x):
-            low, high = field(x, slice(0, 1)), field(x, slice(plan.y - 1, plan.y))
-            y_near[pl.ds(which * plan.x + x, 1), :] = jnp.where(up_y, high, low)
-            y_far[pl.ds(which * plan.x + x, 1), :] = jnp.where(up_y, low, high)
+def put_x(plan, lows, highs, near, far):
+    up = even("gx")
+    for which, (low, high) in enumerate(zip(lows, highs)):
+        near[pl.ds(which * plan.y, plan.y), :] = jnp.where(up, high, low)
+        far[pl.ds(which * plan.y, plan.y), :] = jnp.where(up, low, high)
 
 
 def received(axis, near_ref, far_ref):
@@ -191,29 +194,40 @@
     return jnp.where(up, far, near), jnp.where(up, near, far)
 
 
-def prepare_kernel(
-    plan, conc_hbm, pot_hbm, mask_hbm, class_hbm, owner_hbm, table_hbm,
-    x_near_ref, x_far_ref, y_near_ref, y_far_ref,
-    conc_ref, pot_ref, owner_ref, mask_ref, class_ref, table_ref, sems,
-):
-    pairs = (
-        (table_hbm, table_ref), (class_hbm, class_ref), (mask_hbm, mask_ref),
-        (conc_hbm, conc_ref), (pot_hbm, pot_ref), (owner_hbm, owner_ref),
-    )
-    copies = [
-        pltpu.make_async_copy(source, target, sems.at[i])
-        for i, (source, target) in enumerate(pairs)
-    ]
-    for copy in copies:
-        copy.start()
+def prepare_kernel(plan, *refs):
+    hbm, refs = refs[:8], refs[8:]
+    x_near_ref, x_far_ref, y_near_ref, y_far_ref = refs[:4]
+    x_refs, y_refs, (owner_ref, table_ref, sems) = refs[4:8], refs[8:14], refs[14:]
+    copies = []
+
+    def start(source, target):
+        copies.append(pltpu.make_async_copy(source, target, sems.at[len(copies)]))
+        copies[-1].start()
+
+    start(hbm[7], table_ref)
+    start(hbm[6], owner_ref)
+    for source, target in zip(hbm[:4], x_refs):
+        start(source.at[0], target.at[0])
+        start(source.at[plan.x - 1], target.at[1])
+    for source, target in zip(hbm[:6], y_refs):
+        start(source.at[:, pl.ds(0, 8)], target.at[0])
+        start(source.at[:, pl.ds(plan.y - 8, 8)], target.at[1])
     for copy in copies:
         copy.wait()
     table = [table_ref[marker] for marker in range(table_ref.shape[0])]
-    send = (x_near_ref, x_far_ref, y_near_ref, y_far_ref)
-    edges = [lambda x, y: conc_ref[x, y], lambda x, y: pot_ref[x, y]]
-    edges.append(lambda x, y: mobility_of(mask_ref[x, y], class_ref[x, y], table))
-    put_edges(plan, edges, *send)
-    used = 3 * plan.x
+    conc, pot, mask, kind = (ref[...] for ref in x_refs)
+    fields = (conc, pot, mobility_of(mask, kind, table))
+    put_x(plan, [f[0] for f in fields], [f[1] for f in fields], x_near_ref, x_far_ref)
+    conc, pot, mask, kind, mass, pots = (ref[...] for ref in y_refs)
+    fields = (conc, pot, mobility_of(mask, kind, table))
+    up = even("gy")
+    rows = [(field, at) for at in range(2) for field in fields] + [(mass, 0), (pots, 0)]
+    for which, (field, at) in enumerate(rows):
+        for x in range(plan.x):
+            low, high = field[0, x, at : at + 1], field[1, x, 7 - at : 8 - at]
+            y_near_ref[pl.ds(which * plan.x + x, 1), :] = jnp.where(up, high, low)
+            y_far_ref[pl.ds(which * plan.x + x, 1), :] = jnp.where(up, low, high)
+    used = 8 * plan.x
     for ref in (y_near_ref, y_far_ref):
         ref[pl.ds(used, plan.y_rows - used), :] = jnp.zeros((plan.y_rows - used, plan.p), F32)
         ref[pl.ds(plan.map_row, plan.owners), pl.ds(0, plan.columns)] = owner_ref[...].astype(F32)
@@ -231,7 +245,7 @@
 def first_kernel(
     plan, conc_ref, pot_ref, mob_ref, mass_ref, pots_ref, gather_ref, scale_ref, owner_ref,
     x_near_ref, x_far_ref, y_near_ref, y_far_ref,
-    conc_out, pot_out, total_out, *send,
+    conc_out, pot_out, total_out, raw_out, x_near_out, x_far_out,
 ):
     sides = received("gx", x_near_ref, x_far_ref)
     ends = received("gy", y_near_ref, y_far_ref)
@@ -242,17 +256,37 @@
         )
 
     mobility, mob_halo = mob_ref[...], halo(2)
-    faces, diagonal = faces_of(mobility, mob_halo)
+    faces, diagonal = faces_of(mobility, neighbours(mobility, mob_halo))
     mass_source, pot_source = mass_ref[...], pots_ref[...]
     conc, pot = conc_ref[...], pot_ref[...]
-    excess = excess_of(conc, pot, halo(0), halo(1), faces, mass_source, pot_source)
-    conc, pot = relax_pair(conc, pot, *excess, diagonal)
+    for at, field in enumerate((conc, pot)):
+        for x in range(plan.x):
+            raw_out[pl.ds(2 * at * plan.x + x, 1), :] = field[x, 0:1]
+            raw_out[pl.ds((2 * at + 1) * plan.x + x, 1), :] = field[x, plan.y - 1 : plan.y]
+    excess = excess_of(
+        conc, pot, neighbours(conc, halo(0)), neighbours(pot, halo(1)), faces, diagonal,
+        mass_source, pot_source,
+    )
+    conc, pot = relax_pair(conc, pot, *excess, diagonal, scale_from(diagonal))
     conc_out[...] = conc
     pot_out[...] = pot
-    put_edges(plan, (lambda x, y: conc[x, y], lambda x, y: pot[x, y]), *send)
+    put_x(plan, (conc[0], pot[0]), (conc[plan.x - 1], pot[plan.x - 1]), x_near_out, x_far_out)
+    up = even("gx")
+    base = 2 * plan.y
+    for which in range(3):
+        for end, rows in enumerate(ends):
+            low = rows[which * plan.x : which * plan.x + 1]
+            high = rows[(which + 1) * plan.x - 1 : (which + 1) * plan.x]
+            x_near_out[pl.ds(base + 2 * which + end, 1), :] = jnp.where(up, high, low)
+            x_far_out[pl.ds(base + 2 * which + end, 1), :] = jnp.where(up, low, high)
+    for ref in (x_near_out, x_far_out):
+        ref[pl.ds(base + 6, 2), :] = jnp.zeros((2, plan.p), F32)
 
     nothing = tuple(jnp.zeros_like(part) for part in mob_halo)
-    own_mass, own_pot = excess_of(conc, pot, nothing, nothing, faces, mass_source, pot_source)
+    own_mass, own_pot = excess_of(
+        conc, pot, neighbours(conc, nothing), neighbours(pot, nothing), faces, diagonal,
+        mass_source, pot_source,
+    )
     give_mass = [own_mass.reshape(plan.cells, plan.p)]
     give_pot = [own_pot.reshape(plan.cells, plan.p)]
     for x, side in ((0, 0), (plan.x - 1, 1)):
@@ -317,22 +351,19 @@
             out = jnp.where(plane == h + (k - 1), choices[k], out)
         return out
 
-    blank = plan.slot_rows - plan.high_row - plan.half_x
     for plane in range(plan.groups):
         main = of_plane(plane, sums)
         beside = []
         for i in range(plan.half_x):
             beside.append((plan.low_row + i, of_plane(plane - 1, [k[i] for k in below])))
             beside.append((plan.high_row + i, of_plane(plane + 1, [k[i] for k in above])))
+        beside += [(row, jnp.zeros_like(main)) for row in range(plan.high_row + plan.half_x, 4 * plan.slot_parts)]
         for g in range(plan.owners):
             slot = g * plan.groups + plane
-            total_out[slot, pl.ds(0, plan.owners), :] = main
+            for part in range(plan.owners // 4):
+                total_out[slot, part] = main[4 * part : 4 * part + 4]
             for row, values in beside:
-                total_out[slot, pl.ds(row, 1), :] = values[g : g + 1]
-            if blank:
-                total_out[slot, pl.ds(plan.slot_rows - blank, blank), :] = jnp.zeros(
-                    (blank, plan.p), F32
-                )
+                total_out[slot, row // 4, pl.ds(row % 4, 1), :] = values[g : g + 1]
 
 
 def coarse_solve(packed, planes):
@@ -366,51 +397,128 @@
     return coarse_conc, coarse_pot
 
 
+def beside_kernel(
+    plan, mob_ref, raw_ref, x_near_msg, x_far_msg, y_near_msg, y_far_msg, x_near_ref, x_far_ref,
+    faces_out, diagonal_out, scale_out, ends_out,
+):
+    mobility = mob_ref[...]
+    sides = received("gx", x_near_msg, x_far_msg)
+    ends = received("gy", y_near_msg, y_far_msg)
+    halo = tuple(side_rows(plan, rows, 2) for rows in sides) + tuple(
+        side_columns(plan, rows, 2) for rows in ends
+    )
+    faces, diagonal = faces_of(mobility, neighbours(mobility, halo))
+    for i, face in enumerate(faces):
+        faces_out[i] = face
+    diagonal_out[...] = diagonal
+    scale_out[...] = scale_from(diagonal)
+
+    corners = received("gx", x_near_ref, x_far_ref)
+    h = lax.axis_index("gy")
+    inside = (h > 0, h < plan.groups - 1)
+    own_mob = [
+        jnp.concatenate([mobility[x, y : y + 1] for x in range(plan.x)], axis=0)
+        for y in (0, plan.y - 1)
+    ]
+    for end, rows in enumerate(ends):
+
+        def row(which):
+            return rows[which * plan.x : (which + 1) * plan.x]
+
+        def beside(which, own):
+            here = row(which)
+            at = 2 * plan.y + 2 * which + end
+            wide = jnp.concatenate([corners[0][at : at + 1], here, corners[1][at : at + 1]], axis=0)
+            return (
+                wide[: plan.x], wide[2:], own, row(which + 3),
+                *(part[0] for part in plane_pair(here[None])),
+            )
+
+        raw = [
+            raw_ref[pl.ds((2 * which + end) * plan.x, plan.x), :] for which in range(2)
+        ]
+        faces, diagonal = faces_of(row(2), beside(2, own_mob[end]))
+        excess = excess_of(
+            row(0), row(1), beside(0, raw[0]), beside(1, raw[1]), faces, diagonal, row(6), row(7)
+        )
+        new = relax_pair(row(0), row(1), *excess, diagonal, scale_from(diagonal))
+        for which, values in enumerate(new):
+            ends_out[pl.ds((2 * which + end) * plan.x, plan.x), :] = jnp.where(
+                inside[end], values, 0.0
+            )
+
+
 def last_kernel(
-    plan, conc_ref, pot_ref, mob_ref, mass_ref, pots_ref, x_near_msg, x_far_msg,
-    y_near_msg, y_far_msg, x_near_ref, x_far_ref, y_near_ref, y_far_ref, total_ref, spread_ref,
-    conc_out, pot_out,
+    plan, conc_ref, pot_ref, mass_ref, pots_ref, faces_ref, diagonal_ref, scale_ref,
+    x_near_ref, x_far_ref, ends_ref, spread_ref, total_ref,
+    conc_hbm, pot_hbm, conc_out, pot_out, sems,
 ):
-    means = total_ref[0]
-    for slot in range(1, total_ref.shape[0]):
-        means = means + total_ref[slot]
-    solved = jnp.concatenate(coarse_solve(means, plan.p), axis=1)
-    own = split_dot(spread_ref[...].astype(BF16), solved[: plan.owners], ((1,), (0,)))
-    ends = received("gy", y_near_msg, y_far_msg)
-    sides = received("gx", x_near_msg, x_far_msg)
-    y_corr = []
-    for begin in (plan.low_row, plan.high_row):
-        rows = [solved[begin + (x >> 1) : begin + (x >> 1) + 1] for x in range(plan.x)]
-        y_corr.append(jnp.concatenate(rows, axis=0))
-    new_ends = received("gy", y_near_ref, y_far_ref)
-    new_sides = received("gx", x_near_ref, x_far_ref)
+    parts = []
+    for part in range(plan.slot_parts):
+        mean = total_ref[0, part]
+        for slot in range(1, total_ref.shape[0]):
+            mean = mean + total_ref[slot, part]
+        parts.append(mean)
+    solved = jnp.concatenate(
+        coarse_solve(jnp.concatenate(parts, axis=0), plan.p), axis=1
+    )
+    own = lax.dot_general(
+        spread_ref[...].astype(BF16),
+        three_terms(solved[: plan.owners]).astype(BF16),
+        (((1,), (0,)), ((), ())),
+        preferred_element_type=F32,
+    )
+    sides = received("gx", x_near_ref, x_far_ref)
 
     def updated(which, ref):
         lanes = slice(which * plan.p, (which + 1) * plan.p)
         corr = own[:, lanes]
-        field = ref[...] + corr[: plan.cells].reshape(plan.x, plan.y, plan.p)
-        halo = []
-        for side, rows in enumerate(new_sides):
-            begin = plan.cells + side * plan.y
-            halo.append(side_rows(plan, rows, which) + corr[begin : begin + plan.y][None])
-        for rows, edge in zip(new_ends, y_corr):
-            halo.append((rows[which * plan.x : (which + 1) * plan.x] + edge[:, lanes])[:, None])
-        return field, halo
-
-    conc, conc_halo = updated(0, conc_ref)
-    pot, pot_halo = updated(1, pot_ref)
-    mob_halo = (
-        side_rows(plan, sides[0], 2),
-        side_rows(plan, sides[1], 2),
-        side_columns(plan, ends[0], 2),
-        side_columns(plan, ends[1], 2),
-    )
-    faces, diagonal = faces_of(mob_ref[...], mob_halo)
-    excess = excess_of(conc, pot, conc_halo, pot_halo, faces, mass_ref[...], pots_ref[...])
-    conc_out[...], pot_out[...] = relax_pair(conc, pot, *excess, diagonal)
-
-
-def call(kernel, plan, outs, args, far=(), smem=(), scratch=(), limit=VMEM_LIMIT):
+        slabs = [side_rows(plan, sides[0], which)]
+        slabs += [ref[pl.ds(x, 1)] for x in range(plan.x)]
+        slabs.append(side_rows(plan, sides[1], which))
+        order = [plan.x, *range(plan.x), plan.x + 1]
+        slabs = [
+            slab + corr[x * plan.y : (x + 1) * plan.y][None] for slab, x in zip(slabs, order)
+        ]
+        ends = []
+        for end, begin in enumerate((plan.low_row, plan.high_row)):
+            rows = ends_ref[pl.ds((2 * which + end) * plan.x, plan.x), :]
+            ends.append([
+                (rows[x : x + 1] + solved[begin + (x >> 1) : begin + (x >> 1) + 1, lanes])[None]
+                for x in range(plan.x)
+            ])
+        return slabs, ends
+
+    conc, conc_ends = updated(0, conc_ref)
+    pot, pot_ends = updated(1, pot_ref)
+
+    def beside(slabs, ends, x):
+        here = slabs[x + 1]
+        return (
+            slabs[x], slabs[x + 2], *y_pair(here, ends[0][x], ends[1][x]), *plane_pair(here)
+        )
+
+    copies = []
+    for x in range(plan.x):
+        one = pl.ds(x, 1)
+        diagonal = diagonal_ref[one]
+        excess = excess_of(
+            conc[x + 1], pot[x + 1], beside(conc, conc_ends, x), beside(pot, pot_ends, x),
+            [faces_ref[i, one] for i in range(6)], diagonal, mass_ref[one], pots_ref[one],
+        )
+        conc_out[one], pot_out[one] = relax_pair(
+            conc[x + 1], pot[x + 1], *excess, diagonal, scale_ref[one]
+        )
+        for source, target in ((conc_out, conc_hbm), (pot_out, pot_hbm)):
+            copies.append(
+                pltpu.make_async_copy(source.at[one], target.at[one], sems.at[len(copies)])
+            )
+            copies[-1].start()
+    for copy in copies:
+        copy.wait()
+
+
+def call(kernel, plan, outs, args, far=(), smem=(), scratch=(), limit=VMEM_LIMIT, out_far=False):
     def space(i):
         return pl.ANY if i in far else pltpu.SMEM if i in smem else pltpu.VMEM
 
@@ -418,7 +526,7 @@
         functools.partial(kernel, plan),
         out_shape=[jax.ShapeDtypeStruct(shape, F32) for shape in outs],
         in_specs=[pl.BlockSpec(memory_space=space(i)) for i in range(len(args))],
-        out_specs=[pl.BlockSpec(memory_space=pltpu.VMEM)] * len(outs),
+        out_specs=[pl.BlockSpec(memory_space=pl.ANY if out_far else pltpu.VMEM)] * len(outs),
         scratch_shapes=list(scratch),
         compiler_params=pltpu.CompilerParams(vmem_limit_bytes=limit),
     )(*args)
@@ -431,10 +539,6 @@
         pairs = [(i, i + 1) for i in range(begin, count - 1, 2)]
         out.append(lax.ppermute(rows, axis, pairs + [(j, i) for i, j in pairs]))
     return out
-
-
-def swap_all(x_near, x_far, y_near, y_far):
-    return *swap("gx", x_near, x_far), *swap("gy", y_near, y_far)
 
 
 def gather_totals(plan, total, y_near, y_far):
@@ -457,59 +561,71 @@
         ident = jnp.stack([ident[i * plan.half_y + at] for i in range(plan.half_x)])
         rows.append(lax.dynamic_index_in_dim(own, place, 0, False)[ident])
     rows = jnp.concatenate(rows)
-    return jnp.pad(rows, ((0, plan.slot_rows - rows.shape[0]), (0, 0)))[None]
+    rows = jnp.pad(rows, ((0, 4 * plan.slot_parts - rows.shape[0]), (0, 0)))
+    return rows.reshape(1, plan.slot_parts, 4, plan.p)
 
 
 def on_device(conc, pot, mass_source, pot_source, mask, kind, table, owner_map):
     plan = Plan(conc.shape, lax.axis_size("gx"), lax.axis_size("gy"))
     block = conc.shape
+    fields = [conc, pot, mask, kind, mass_source, pot_source]
     messages = call(
         prepare_kernel,
         plan,
         [*[(3 * plan.y, plan.p)] * 2, *[(plan.y_rows, plan.p)] * 2],
-        [conc, pot, mask, kind, owner_map, table],
-        far=range(6),
+        [*fields, owner_map, table],
+        far=range(8),
         limit=LARGE_LIMIT,
         scratch=(
-            pltpu.VMEM(block, F32),
-            pltpu.VMEM(block, F32),
+            *[pltpu.VMEM((2, plan.y, plan.p), field.dtype) for field in fields[:4]],
+            *[pltpu.VMEM((2, plan.x, 8, plan.p), field.dtype) for field in fields],
             pltpu.VMEM(owner_map.shape, owner_map.dtype),
-            pltpu.VMEM(block, mask.dtype),
-            pltpu.VMEM(block, kind.dtype),
             pltpu.SMEM(table.shape, table.dtype),
-            pltpu.SemaphoreType.DMA((6,)),
+            pltpu.SemaphoreType.DMA((22,)),
         ),
     )
-    old = swap_all(*messages)
-    near, mask, kind = lax.optimization_barrier((old[0], mask, kind))
-    old = (near, *old[1:])
+    old = [*swap("gx", *messages[:2]), *swap("gy", *messages[2:])]
+    old[0], mask, kind = lax.optimization_barrier((old[0], mask, kind))
     mob, gather, spread, scale = call(
         local_kernel,
         plan,
-        [block, (plan.owners, plan.rows), (plan.rows, plan.owners), (plan.owners, plan.p)],
+        [block, (plan.owners, plan.rows), (plan.rows, 3 * plan.owners), (plan.owners, plan.p)],
         [mask, kind, table, owner_map],
         smem=(2,),
     )
-    conc, pot, total, *messages = call(
+    slots = (plan.slots, plan.slot_parts, 4, plan.p)
+    conc, pot, total, raw, *messages = call(
         first_kernel,
         plan,
         [
             block,
             block,
-            (plan.slots, plan.slot_rows, plan.p) if plan.slots else (3 * plan.owners, plan.p),
-            *[(2 * plan.y, plan.p)] * 2,
-            *[(2 * plan.x, plan.p)] * 2,
+            slots if plan.slots else (3 * plan.owners, plan.p),
+            (4 * plan.x, plan.p),
+            *[(2 * plan.y + 8, plan.p)] * 2,
         ],
         [conc, pot, mob, mass_source, pot_source, gather, scale, owner_map, *old],
     )
     total = gather_totals(plan, total, *old[2:])
-    new = swap_all(*messages)
+    new = swap("gx", *messages)
+    faces, diagonal, scale, ends = call(
+        beside_kernel,
+        plan,
+        [(6, *block), block, block, (4 * plan.x, plan.p)],
+        [mob, raw, *old, *new],
+    )
     return tuple(
         call(
             last_kernel,
             plan,
             [block, block],
-            [conc, pot, mob, mass_source, pot_source, *old, *new, total, spread],
+            [conc, pot, mass_source, pot_source, faces, diagonal, scale, *new, ends, spread, total],
+            out_far=True,
+            scratch=(
+                pltpu.VMEM(block, F32),
+                pltpu.VMEM(block, F32),
+                pltpu.SemaphoreType.DMA((2 * plan.x,)),
+            ),
         )
     )
 

time: 32.9 us -> 31.8 us (0.967)
  starting transfers between devices: 18.7 us -> 16.3 us
  waiting for transfers between devices: 7.01 us -> 8.32 us
    all_to_all x1, waiting for transfers between devices: 5.19 us -> 7.83 us  [gather_totals(): lax.all_to_all(total, ('gx', 'gy'), split_axis=0, concat_axis=0, tiled=True)]
    ppermute x8 -> x6, starting transfers between devices: 7.97 us -> 5.59 us  [swap(): out.append(lax.ppermute(rows, axis, pairs + [(j, i) for i, j in pairs]))]
    ppermute x8 -> x6, waiting for transfers between devices: 1.82 us -> 0.5 us  [swap(): out.append(lax.ppermute(rows, axis, pairs + [(j, i) for i, j in pairs]))]
    pallas_call x4 -> x5, Pallas kernels: 6.04 us -> 6.08 us  [call(): pl.pallas_call(functools.partial(kernel, plan), out_shape=[jax.ShapeDtype...]
  transfers between devices with their start and end apart: 9 -> 7, of which waited for: 3 -> 3; matrix products, arithmetic and copies ran while one was open for 0% -> 0% of each run, Pallas kernels for 3% -> 4%
where the time goes in v4:
time: 31.8 us; the launch traced here: 31.6 us
  starting transfers between devices  16.3 us (51%)
  waiting for transfers between devices  8.32 us (26%)
  Pallas kernels  6.08 us (19%)
  between operations  0.8 us (3%)
    all_to_all x1, starting transfers between devices, gather_totals(): lax.all_to_all(total, ('gx', 'gy'), split_axis=0, concat_axis=0, tiled=True)  10.7 us
    all_to_all x1, waiting for transfers between devices, gather_totals(): lax.all_to_all(total, ('gx', 'gy'), split_axis=0, concat_axis=0, tiled=True)  7.83 us
    pallas_call x5, Pallas kernels, call(): pl.pallas_call(functools.partial(kernel, plan), out_shape=[jax.ShapeDtype...  6.08 us
    ppermute x6, starting transfers between devices, swap(): out.append(lax.ppermute(rows, axis, pairs + [(j, i) for i, j in pairs]))  5.59 us
  transfers between devices with their start and end apart: 7, of which 3 were waited for; matrix products, arithmetic and copies ran while one was open for 0% of the time, Pallas kernels for 4%

profile of v4, /device:TPU:0, one launch (start us, length us, event | category | flops | bytes accessed | tf_op | source)
XLA Modules:
  0.0 31.6 jit_solution(13329175457650496669)
XLA Ops:
  0.6 0.0 copy-start.5
  0.6 0.0 copy-start.4
  0.7 0.0 copy-start.2
  0.7 0.0 copy-start.3
  0.7 1.9 %shard_map.95 = (f32[192,128]{1,0:T(8,128)}, f32[192,128]{1,0:T(8,128)}, f32[40,128]{1,0:T(8,128)}, f32[40,128]{1,0:T(8,128)}) custom-call(f32[4,64,128]{2,1,0:T(8,128)} %conc_ref.1, f32[4,64,128]{2,1,0:T(8,128)} %pot_ref.1, s32[4,64,128]{2,1,0:T(8,128)} %mask_ref, s32[4,64,128]{2,1,0:T(8,128)} %class_ref, f32[4,64,128]{2,1,0:T(8,128)} %mass_ref.3, ...), custom_call_target="tpu_custom_call" | custom-call | tf_op jit(solution)/shard_map/pallas_call | solution.py:525
  2.6 0.0 copy-start.6
  2.6 0.5 %collective-permute-start = (f32[192,128]{1,0:T(8,128)}, f32[192,128]{1,0:T(8,128)S(1)}, u32[]{:S(2)}, u32[]{:S(2)}) collective-permute-start(f32[192,128]{1,0:T(8,128)} %get-tuple-element.23), channel_id=1, source_target_pairs={{0,4},{8,12},{16,20},{24,28},{4,0},{12,8},{20,16},{28,24},{1,5},{9... | collective-permute-start | bytes 294920 | tf_op jit(solution)/shard_map/ppermute | solution.py:540
  3.1 0.7 %collective-permute-start.1 = (f32[192,128]{1,0:T(8,128)}, f32[192,128]{1,0:T(8,128)S(1)}, u32[]{:S(2)}, u32[]{:S(2)}) collective-permute-start(f32[192,128]{1,0:T(8,128)} %get-tuple-element.30), channel_id=1, source_target_pairs={{4,8},{12,16},{20,24},{8,4},{16,12},{24,20},{5,9},{13,17},{21,25},... | collective-permute-start | bytes 294920 | tf_op jit(solution)/shard_map/ppermute | solution.py:540
  3.8 0.0 copy-start.7
  3.8 2.7 %collective-permute-start.2 = (f32[40,128]{1,0:T(8,128)}, f32[40,128]{1,0:T(8,128)S(1)}, u32[]{:S(2)}, u32[]{:S(2)}) collective-permute-start(f32[40,128]{1,0:T(8,128)} %get-tuple-element.31), channel_id=1, source_target_pairs={{0,1},{2,3},{1,0},{3,2},{4,5},{6,7},{5,4},{7,6},{8,9},{10,11},{9,8... | collective-permute-start | bytes 61448 | tf_op jit(solution)/shard_map/ppermute | solution.py:540
  6.5 0.0 copy-start
  6.5 0.0 copy-start.1
  6.5 0.8 %collective-permute-start.3 = (f32[40,128]{1,0:T(8,128)}, f32[40,128]{1,0:T(8,128)S(1)}, u32[]{:S(2)}, u32[]{:S(2)}) collective-permute-start(f32[40,128]{1,0:T(8,128)} %get-tuple-element.32), channel_id=1, source_target_pairs={{1,2},{2,1},{5,6},{6,5},{9,10},{10,9},{13,14},{14,13},{17,18},{18,... | collective-permute-start | bytes 61448 | tf_op jit(solution)/shard_map/ppermute | solution.py:540
  7.2 0.0 collective-permute-done.x_near_ref.x_near_msg
  7.3 0.0 copy-done.5
  7.3 0.0 copy-done.4
  7.3 0.0 copy-done.6
  7.3 0.0 copy-done.7
  7.3 1.0 %shard_map.96 = (f32[4,64,128]{2,1,0:T(8,128)S(1)}, f32[8,384]{1,0:T(8,128)S(1)}, f32[384,24]{1,0:T(8,128)S(1)}, f32[8,128]{1,0:T(8,128)S(1)}) custom-call(s32[4,64,128]{2,1,0:T(8,128)S(1)} %copy-done.4, s32[4,64,128]{2,1,0:T(8,128)S(1)} %copy-done.5, f32[8]{0:T(128)S(1)} %copy-done.7, s32[8,64]{1,0:T(8,128)S(1)} %copy-done.6), custom_call_target="tpu_custom_call" | custom-call | tf_op jit(solution)/shard_map/pallas_call | solution.py:525
  8.3 0.1 collective-permute-done.2.y_near_ref.y_near_msg
  8.4 0.0 collective-permute-done.3.y_far_ref.y_far_msg
  8.4 0.0 collective-permute-done.1.x_far_ref.x_far_msg
  8.4 0.0 copy-done.2
  8.4 0.0 copy-done.3
  8.4 0.0 copy-done
  8.5 0.0 copy-done.1
  8.5 1.6 %shard_map.97 = (f32[4,64,128]{2,1,0:T(8,128)S(1)}, f32[4,64,128]{2,1,0:T(8,128)S(1)}, f32[32,3,4,128]{3,2,1,0:T(4,128)}, f32[16,128]{1,0:T(8,128)S(1)}, f32[136,128]{1,0:T(8,128)S(1)}, /*index=5*/f32[136,128]{1,0:T(8,128)S(1)}) custom-call(f32[4,64,128]{2,1,0:T(8,128)S(1)} %copy-done.2, f32[4,64,128]{2,1,0:T(8,128)S(1)} %copy-done.3, ...), custom_call_target="tpu_custom_call" | custom-call | tf_op jit(solution)/shard_map/pallas_call | solution.py:525
  10.1 10.7 %all-to-all-start = ((f32[32,3,4,128]{3,2,1,0:T(4,128)}), f32[32,3,4,128]{3,2,1,0:T(4,128)S(1)}, u32[]{:S(2)}, u32[]{:S(2)}) async-start(f32[32,3,4,128]{3,2,1,0:T(4,128)} %get-tuple-element.43), calls=%async_computation | async-start | bytes 393216 | tf_op jit(solution)/shard_map/all_to_all | solution.py:546
  20.9 0.3 %collective-permute-start.4 = (f32[136,128]{1,0:T(8,128)S(1)}, f32[136,128]{1,0:T(8,128)S(1)}, u32[]{:S(2)}, u32[]{:S(2)}) collective-permute-start(f32[136,128]{1,0:T(8,128)S(1)} %get-tuple-element.36), channel_id=1, source_target_pairs={{0,4},{8,12},{16,20},{24,28},{4,0},{12,8},{20,16},{28,24},{1,5},{9... | collective-permute-start | bytes 208904 | tf_op jit(solution)/shard_map/ppermute | solution.py:540
  21.2 0.7 %collective-permute-start.5 = (f32[136,128]{1,0:T(8,128)S(1)}, f32[136,128]{1,0:T(8,128)S(1)}, u32[]{:S(2)}, u32[]{:S(2)}) collective-permute-start(f32[136,128]{1,0:T(8,128)S(1)} %get-tuple-element.37), channel_id=1, source_target_pairs={{4,8},{12,16},{20,24},{8,4},{16,12},{24,20},{5,9},{13,17},{21,25},... | collective-permute-start | bytes 208904 | tf_op jit(solution)/shard_map/ppermute | solution.py:540
  21.8 0.3 %collective-permute-done.4.x_near_ref = f32[136,128]{1,0:T(8,128)S(1)} collective-permute-done((f32[136,128]{1,0:T(8,128)S(1)}, f32[136,128]{1,0:T(8,128)S(1)}, u32[]{:S(2)}, u32[]{:S(2)}) %collective-permute-start.4) | collective-permute-done | bytes 69664 | tf_op jit(solution)/shard_map/ppermute | solution.py:540
  22.2 0.0 collective-permute-done.5.x_far_ref
  22.2 0.2 shard_map.98
  22.4 7.8 %all-to-all-done.total_ref = f32[32,3,4,128]{3,2,1,0:T(4,128)S(1)} async-done(((f32[32,3,4,128]{3,2,1,0:T(4,128)}), f32[32,3,4,128]{3,2,1,0:T(4,128)S(1)}, u32[]{:S(2)}, u32[]{:S(2)}) %all-to-all-start) | async-done | bytes 196640 | tf_op jit(solution)/shard_map/all_to_all | solution.py:546
  30.2 1.4 %shard_map.99 = (f32[4,64,128]{2,1,0:T(8,128)}, f32[4,64,128]{2,1,0:T(8,128)}) custom-call(f32[4,64,128]{2,1,0:T(8,128)S(1)} %get-tuple-element.33.conc_ref, f32[4,64,128]{2,1,0:T(8,128)S(1)} %get-tuple-element.34.pot_ref, f32[4,64,128]{2,1,0:T(8,128)S(1)} %copy-done, f32[4,64,128]{2,1,0:T(8,128)S(1)} %copy-done.1, ...), custom_call_target="tpu_custom_call" | custom-call | tf_op jit(solution)/shard_map/pallas_call | solution.py:525
Async XLA Ops:
  0.6 6.6 %copy-start.5 = (s32[4,64,128]{2,1,0:T(8,128)S(1)}, s32[4,64,128]{2,1,0:T(8,128)}, u32[]{:S(2)}) copy-start(s32[4,64,128]{2,1,0:T(8,128)} %class_ref) | copy-start | bytes 393220
  0.6 6.6 %copy-start.4 = (s32[4,64,128]{2,1,0:T(8,128)S(1)}, s32[4,64,128]{2,1,0:T(8,128)}, u32[]{:S(2)}) copy-start(s32[4,64,128]{2,1,0:T(8,128)} %mask_ref) | copy-start | bytes 393220
  0.7 7.8 %copy-start.2 = (f32[4,64,128]{2,1,0:T(8,128)S(1)}, f32[4,64,128]{2,1,0:T(8,128)}, u32[]{:S(2)}) copy-start(f32[4,64,128]{2,1,0:T(8,128)} %conc_ref.1) | copy-start | bytes 393220
  0.7 7.8 %copy-start.3 = (f32[4,64,128]{2,1,0:T(8,128)S(1)}, f32[4,64,128]{2,1,0:T(8,128)}, u32[]{:S(2)}) copy-start(f32[4,64,128]{2,1,0:T(8,128)} %pot_ref.1) | copy-start | bytes 393220
  2.6 4.7 %copy-start.6 = (s32[8,64]{1,0:T(8,128)S(1)}, s32[8,64]{1,0:T(8,128)}, u32[]{:S(2)}) copy-start(s32[8,64]{1,0:T(8,128)} %owner_ref.3) | copy-start | bytes 6148
  2.6 4.7 %collective-permute-start = (f32[192,128]{1,0:T(8,128)}, f32[192,128]{1,0:T(8,128)S(1)}, u32[]{:S(2)}, u32[]{:S(2)}) collective-permute-start(f32[192,128]{1,0:T(8,128)} %get-tuple-element.23), channel_id=1, source_target_pairs={{0,4},{8,12},{16,20},{24,28},{4,0},{12,8},{20,16},{28,24},{1,5},{9... | collective-permute-start | bytes 294920 | tf_op jit(solution)/shard_map/ppermute | solution.py:540
  3.1 5.3 %collective-permute-start.1 = (f32[192,128]{1,0:T(8,128)}, f32[192,128]{1,0:T(8,128)S(1)}, u32[]{:S(2)}, u32[]{:S(2)}) collective-permute-start(f32[192,128]{1,0:T(8,128)} %get-tuple-element.30), channel_id=1, source_target_pairs={{4,8},{12,16},{20,24},{8,4},{16,12},{24,20},{5,9},{13,17},{21,25},... | collective-permute-start | bytes 294920 | tf_op jit(solution)/shard_map/ppermute | solution.py:540
  3.8 3.5 %copy-start.7 = (f32[8]{0:T(128)S(1)}, f32[8]{0:T(128)}, u32[]{:S(2)}) copy-start(f32[8]{0:T(128)} %table_ref.1) | copy-start | bytes 100
  3.8 4.6 %collective-permute-start.2 = (f32[40,128]{1,0:T(8,128)}, f32[40,128]{1,0:T(8,128)S(1)}, u32[]{:S(2)}, u32[]{:S(2)}) collective-permute-start(f32[40,128]{1,0:T(8,128)} %get-tuple-element.31), channel_id=1, source_target_pairs={{0,1},{2,3},{1,0},{3,2},{4,5},{6,7},{5,4},{7,6},{8,9},{10,11},{9,8... | collective-permute-start | bytes 61448 | tf_op jit(solution)/shard_map/ppermute | solution.py:540
  6.5 2.0 %copy-start = (f32[4,64,128]{2,1,0:T(8,128)S(1)}, f32[4,64,128]{2,1,0:T(8,128)}, u32[]{:S(2)}) copy-start(f32[4,64,128]{2,1,0:T(8,128)} %mass_ref.3) | copy-start | bytes 393220
  6.5 2.0 %copy-start.1 = (f32[4,64,128]{2,1,0:T(8,128)S(1)}, f32[4,64,128]{2,1,0:T(8,128)}, u32[]{:S(2)}) copy-start(f32[4,64,128]{2,1,0:T(8,128)} %pots_ref.3) | copy-start | bytes 393220
  6.5 2.0 %collective-permute-start.3 = (f32[40,128]{1,0:T(8,128)}, f32[40,128]{1,0:T(8,128)S(1)}, u32[]{:S(2)}, u32[]{:S(2)}) collective-permute-start(f32[40,128]{1,0:T(8,128)} %get-tuple-element.32), channel_id=1, source_target_pairs={{1,2},{2,1},{5,6},{6,5},{9,10},{10,9},{13,14},{14,13},{17,18},{18,... | collective-permute-start | bytes 61448 | tf_op jit(solution)/shard_map/ppermute | solution.py:540
  10.1 20.1 %all-to-all-start = ((f32[32,3,4,128]{3,2,1,0:T(4,128)}), f32[32,3,4,128]{3,2,1,0:T(4,128)S(1)}, u32[]{:S(2)}, u32[]{:S(2)}) async-start(f32[32,3,4,128]{3,2,1,0:T(4,128)} %get-tuple-element.43), calls=%async_computation | async-start | bytes 393216 | tf_op jit(solution)/shard_map/all_to_all | solution.py:546
  20.9 1.3 %collective-permute-start.4 = (f32[136,128]{1,0:T(8,128)S(1)}, f32[136,128]{1,0:T(8,128)S(1)}, u32[]{:S(2)}, u32[]{:S(2)}) collective-permute-start(f32[136,128]{1,0:T(8,128)S(1)} %get-tuple-element.36), channel_id=1, source_target_pairs={{0,4},{8,12},{16,20},{24,28},{4,0},{12,8},{20,16},{28,24},{1,5},{9... | collective-permute-start | bytes 208904 | tf_op jit(solution)/shard_map/ppermute | solution.py:540
  21.2 1.0 %collective-permute-start.5 = (f32[136,128]{1,0:T(8,128)S(1)}, f32[136,128]{1,0:T(8,128)S(1)}, u32[]{:S(2)}, u32[]{:S(2)}) collective-permute-start(f32[136,128]{1,0:T(8,128)S(1)} %get-tuple-element.37), channel_id=1, source_target_pairs={{4,8},{12,16},{20,24},{8,4},{16,12},{24,20},{5,9},{13,17},{21,25},... | collective-permute-start | bytes 208904 | tf_op jit(solution)/shard_map/ppermute | solution.py:540

commit v5 on v4

--- a/solution.py
+++ b/solution.py
@@ -120,12 +120,13 @@
         self.map_row = round_up(8 * self.x, 8)
         self.y_rows = self.map_row + owners
         self.cells = self.x * self.y
-        self.rows = self.cells + 2 * self.y
+        self.rows = (self.half_x + 2) * self.y
+        self.sums_row = 2 * self.y + 8
         self.low_row = owners
         self.high_row = owners + self.half_x
         self.slot_parts = -(-(owners + 2 * self.half_x) // 4)
-        slots = owners * groups
-        self.slots = slots if slots <= 64 else 0
+        slots = owners * groups // 2
+        self.slots = slots if slots <= 32 and 9 * owners <= self.p and owners % 2 == 0 else 0
 
 
 def side_rows(plan, rows, which):
@@ -140,14 +141,15 @@
     g = lax.axis_index("gx")
     last = plan.owners - 1
     owner = iota((plan.owners, plan.columns), 0)
-    shape = (plan.x + 2, plan.y, plan.columns)
+    low, high = plan.half_x, plan.half_x + 1
+    shape = (plan.half_x + 2, plan.y, plan.columns)
     x, y, column = iota(shape, 0), iota(shape, 1), iota(shape, 2)
-    half = jnp.where(x < plan.x, x >> 1, jnp.where(x == plan.x, plan.half_x - 1, 0))
+    half = jnp.where(x < low, x, jnp.where(x == low, plan.half_x - 1, 0))
     place = column == half * plan.half_y + (y >> 1)
     sides = (
-        (x < plan.x, g, True),
-        (x == plan.x, jnp.maximum(g - 1, 0), g > 0),
-        (x == plan.x + 1, jnp.minimum(g + 1, last), g < last),
+        (x < low, g, True),
+        (x == low, jnp.maximum(g - 1, 0), g > 0),
+        (x == high, jnp.minimum(g + 1, last), g < last),
     )
     gather, spread = None, None
     for part, row, inside in sides:
@@ -190,7 +192,8 @@
 
 def received(axis, near_ref, far_ref):
     up = even(axis)
-    near, far = near_ref[...], far_ref[...]
+    rows = pl.ds(0, min(near_ref.shape[0], far_ref.shape[0]))
+    near, far = near_ref[rows, :], far_ref[rows, :]
     return jnp.where(up, far, near), jnp.where(up, near, far)
 
 
@@ -245,7 +248,7 @@
 def first_kernel(
     plan, conc_ref, pot_ref, mob_ref, mass_ref, pots_ref, gather_ref, scale_ref, owner_ref,
     x_near_ref, x_far_ref, y_near_ref, y_far_ref,
-    conc_out, pot_out, total_out, raw_out, x_near_out, x_far_out,
+    conc_out, pot_out, raw_out, x_near_out, x_far_out,
 ):
     sides = received("gx", x_near_ref, x_far_ref)
     ends = received("gy", y_near_ref, y_far_ref)
@@ -287,23 +290,21 @@
         conc, pot, neighbours(conc, nothing), neighbours(pot, nothing), faces, diagonal,
         mass_source, pot_source,
     )
-    give_mass = [own_mass.reshape(plan.cells, plan.p)]
-    give_pot = [own_pot.reshape(plan.cells, plan.p)]
+    give_mass, give_pot = (
+        [field[x] + field[x + 1] for x in range(0, plan.x, 2)] for field in (own_mass, own_pot)
+    )
     for x, side in ((0, 0), (plan.x - 1, 1)):
         face = 0.5 * (mobility[x] + mob_halo[side][0])
         give_mass.append(time_step * face * pot[x])
         give_pot.append(-interface * conc[x])
-    give = jnp.concatenate(
-        [jnp.concatenate(give_mass, axis=0), jnp.concatenate(give_pot, axis=0)], axis=1
-    )
-
-    def packed(both):
-        mass, other = both[:, : plan.p], both[:, plan.p :]
+
+    def packed(mass, other):
         first = iota(mass.shape, 1) & 1 == 0
         return jnp.where(
             first, mass + pltpu.roll(mass, plan.p - 1, 1), other + pltpu.roll(other, 1, 1)
         )
 
+    give = packed(jnp.concatenate(give_mass, axis=0), jnp.concatenate(give_pot, axis=0))
     h = lax.axis_index("gy")
     inside = (h > 0, None, h < plan.groups - 1)
     maps = [rows[plan.map_row : plan.map_row + plan.owners, : plan.columns] for rows in ends]
@@ -311,11 +312,7 @@
     owner = iota((plan.owners, 1), 0)
     is_mine = owner == lax.axis_index("gx")
 
-    def column(place, i, at):
-        b = i * plan.half_y + at
-        return maps[place][:, b : b + 1]
-
-    sums = [None, packed(split_dot(gather_ref[...].astype(BF16), give, ((1,), (0,)))), None]
+    sums = [None, split_dot(gather_ref[...].astype(BF16), give, ((1,), (0,))), None]
     sums[1] = sums[1] * scale_ref[...]
     for place, y, at, side in ((0, 0, plan.half_y - 1, 2), (2, plan.y - 1, 0, 3)):
         edge_mob, edge_pot, edge_conc = (
@@ -323,21 +320,41 @@
             for field in (mobility, pot, conc)
         )
         face = 0.5 * (edge_mob + mob_halo[side][:, 0])
-        both = jnp.concatenate([time_step * face * edge_pot, -interface * edge_conc], axis=1)
-        part = jnp.zeros((plan.owners, 2 * plan.p), F32)
+        both = packed(time_step * face * edge_pot, -interface * edge_conc)
+        part = jnp.zeros((plan.owners, plan.p), F32)
         for i in range(plan.half_x):
-            ident = jnp.sum(jnp.where(is_mine, column(place, i, at), 0.0), axis=0, keepdims=True)
+            column = owner_column(plan, maps[place], i, at)
+            ident = jnp.sum(jnp.where(is_mine, column, 0.0), axis=0, keepdims=True)
             pair = both[2 * i : 2 * i + 1] + both[2 * i + 1 : 2 * i + 2]
             part = part + jnp.where((owner.astype(F32) == ident) & inside[place], pair, 0.0)
-        sums[place] = packed(part) * scale_of(plan, maps[place])
-
-    if not plan.slots:
-        total_out[...] = jnp.concatenate(sums, axis=0)
-        return
+        sums[place] = part * scale_of(plan, maps[place])
+    x_near_out[pl.ds(plan.sums_row, 3 * plan.owners), :] = jnp.concatenate(sums, axis=0)
+
+
+def owner_column(plan, owners, i, at):
+    b = i * plan.half_y + at
+    return owners[:, b : b + 1]
+
+
+def pick_kernel(plan, owner_ref, y_near_ref, y_far_ref, pick_out):
+    h = lax.axis_index("gy")
+    maps = [
+        rows[plan.map_row : plan.map_row + plan.owners, : plan.columns]
+        for rows in received("gy", y_near_ref, y_far_ref)
+    ]
+    maps.insert(1, owner_ref[...].astype(F32))
+    inside = (h > 0, True, h < plan.groups - 1)
+    shape = (plan.owners, plan.p)
+    lane, row = iota(shape, 1), iota(shape, 0)
+    sums = []
+    for k in range(3):
+        first = k * plan.owners + row
+        hits = (lane == first) | (lane == first + 3 * plan.owners) | (lane == first + 6 * plan.owners)
+        sums.append(jnp.where(hits & inside[k], 1.0, 0.0))
 
     def picked(place, i, at):
-        ident = jnp.broadcast_to(column(place, i, at), (plan.owners, plan.p))
-        out = jnp.zeros((plan.owners, plan.p), F32)
+        ident = jnp.broadcast_to(owner_column(plan, maps[place], i, at), shape)
+        out = jnp.zeros(shape, F32)
         for o in range(plan.owners):
             out = jnp.where(ident == float(o), sums[place][o : o + 1], out)
         return out
@@ -346,24 +363,43 @@
     above = [[picked(k, i, 0) for i in range(plan.half_x)] for k in range(3)]
 
     def of_plane(plane, choices):
-        out = jnp.zeros_like(choices[0])
+        out = jnp.zeros(shape, F32)
         for k in range(3):
             out = jnp.where(plane == h + (k - 1), choices[k], out)
         return out
 
+    up = even("gx")
+    size = 4 * plan.slot_parts
     for plane in range(plan.groups):
         main = of_plane(plane, sums)
         beside = []
         for i in range(plan.half_x):
             beside.append((plan.low_row + i, of_plane(plane - 1, [k[i] for k in below])))
             beside.append((plan.high_row + i, of_plane(plane + 1, [k[i] for k in above])))
-        beside += [(row, jnp.zeros_like(main)) for row in range(plan.high_row + plan.half_x, 4 * plan.slot_parts)]
-        for g in range(plan.owners):
-            slot = g * plan.groups + plane
-            for part in range(plan.owners // 4):
-                total_out[slot, part] = main[4 * part : 4 * part + 4]
-            for row, values in beside:
-                total_out[slot, row // 4, pl.ds(row % 4, 1), :] = values[g : g + 1]
+        beside += [(at, jnp.zeros(shape, F32)) for at in range(plan.high_row + plan.half_x, size)]
+        for pair in range(plan.owners // 2):
+            base = (pair * plan.groups + plane) * size
+            pick_out[pl.ds(base, plan.owners), :] = main
+            for at, values in beside:
+                mine = jnp.where(up, values[2 * pair : 2 * pair + 1], values[2 * pair + 1 : 2 * pair + 2])
+                pick_out[pl.ds(base + at, 1), :] = mine
+
+
+def slots_kernel(plan, pick_ref, own_ref, other_ref, total_out):
+    rows = pl.ds(plan.sums_row, 3 * plan.owners)
+    terms = three_terms(own_ref[rows, :] + other_ref[rows, :])
+    blank = jnp.zeros((plan.p - 9 * plan.owners, plan.p), F32)
+    terms = jnp.concatenate([terms, blank], axis=0)
+    out = lax.dot_general(
+        pick_ref[...].astype(BF16),
+        terms.astype(BF16),
+        (((1,), (0,)), ((), ())),
+        preferred_element_type=F32,
+    )
+    for slot in range(plan.slots):
+        for part in range(plan.slot_parts):
+            begin = 4 * (slot * plan.slot_parts + part)
+            total_out[slot, part] = out[begin : begin + 4]
 
 
 def coarse_solve(packed, planes):
@@ -476,7 +512,7 @@
         slabs = [side_rows(plan, sides[0], which)]
         slabs += [ref[pl.ds(x, 1)] for x in range(plan.x)]
         slabs.append(side_rows(plan, sides[1], which))
-        order = [plan.x, *range(plan.x), plan.x + 1]
+        order = [plan.half_x, *[x >> 1 for x in range(plan.x)], plan.half_x + 1]
         slabs = [
             slab + corr[x * plan.y : (x + 1) * plan.y][None] for slab, x in zip(slabs, order)
         ]
@@ -532,18 +568,24 @@
     )(*args)
 
 
-def swap(axis, near, far):
-    count = lax.axis_size(axis)
-    out = []
-    for rows, begin in ((near, 0), (far, 1)):
-        pairs = [(i, i + 1) for i in range(begin, count - 1, 2)]
-        out.append(lax.ppermute(rows, axis, pairs + [(j, i) for i, j in pairs]))
-    return out
+def swap_near(axis, rows, begin=0):
+    pairs = [(i, i + 1) for i in range(begin, lax.axis_size(axis) - 1, 2)]
+    return lax.ppermute(rows, axis, pairs + [(j, i) for i, j in pairs])
+
+
+def swap_far(axis, rows):
+    return swap_near(axis, rows, 1)
 
 
 def gather_totals(plan, total, y_near, y_far):
     if plan.slots:
-        return lax.all_to_all(total, ("gx", "gy"), split_axis=0, concat_axis=0, tiled=True)
+        groups = [
+            [g * plan.groups + h for g in range(core, plan.owners, 2) for h in range(plan.groups)]
+            for core in range(2)
+        ]
+        return lax.all_to_all(
+            total, ("gx", "gy"), split_axis=0, concat_axis=0, axis_index_groups=groups, tiled=True
+        )
     shape = (plan.groups, 3, plan.owners, plan.p)
     parts = lax.all_gather(lax.psum(total, "gx"), "gy").reshape(shape)
     blank = jnp.zeros((1, plan.owners, plan.p), F32)
@@ -584,7 +626,10 @@
             pltpu.SemaphoreType.DMA((22,)),
         ),
     )
-    old = [*swap("gx", *messages[:2]), *swap("gy", *messages[2:])]
+    old = [
+        swap_near("gx", messages[0]), swap_far("gx", messages[1]),
+        swap_near("gy", messages[2]), swap_far("gy", messages[3]),
+    ]
     old[0], mask, kind = lax.optimization_barrier((old[0], mask, kind))
     mob, gather, spread, scale = call(
         local_kernel,
@@ -593,21 +638,33 @@
         [mask, kind, table, owner_map],
         smem=(2,),
     )
-    slots = (plan.slots, plan.slot_parts, 4, plan.p)
-    conc, pot, total, raw, *messages = call(
+    conc, pot, raw, near, far = call(
         first_kernel,
         plan,
         [
             block,
             block,
-            slots if plan.slots else (3 * plan.owners, plan.p),
             (4 * plan.x, plan.p),
-            *[(2 * plan.y + 8, plan.p)] * 2,
+            (plan.sums_row + 3 * plan.owners, plan.p),
+            (plan.sums_row, plan.p),
         ],
         [conc, pot, mob, mass_source, pot_source, gather, scale, owner_map, *old],
     )
+    new_near = swap_near("gx", near)
+    if plan.slots:
+        raw, owner_map = lax.optimization_barrier((raw, owner_map))
+        size = 4 * plan.slot_parts
+        (pick,) = call(
+            pick_kernel, plan, [(plan.slots * size, plan.p)], [owner_map, *old[2:]]
+        )
+        (total,) = call(
+            slots_kernel, plan, [(plan.slots, plan.slot_parts, 4, plan.p)], [pick, near, new_near]
+        )
+        total, far = lax.optimization_barrier((total, far))
+    else:
+        total = near[plan.sums_row :]
     total = gather_totals(plan, total, *old[2:])
-    new = swap("gx", *messages)
+    new = [new_near, swap_far("gx", far)]
     faces, diagonal, scale, ends = call(
         beside_kernel,
         plan,

time: 31.8 us -> 32.3 us (1.016)
  starting transfers between devices: 16.3 us -> 17.4 us
  waiting for transfers between devices: 8.32 us -> 7.64 us
    ppermute x6, starting transfers between devices: 5.59 us -> 7.74 us  [swap_near(): return lax.ppermute(rows, axis, pairs + [(j, i) for i, j in pairs])]
    all_to_all x1, waiting for transfers between devices: 7.83 us -> 6.67 us  [gather_totals(): lax.all_to_all(total, ('gx', 'gy'), split_axis=0, concat_axis=0, axis_ind...]
    all_to_all x1, starting transfers between devices: 10.7 us -> 9.66 us  [gather_totals(): lax.all_to_all(total, ('gx', 'gy'), split_axis=0, concat_axis=0, axis_ind...]
    ppermute x6, waiting for transfers between devices: 0.5 us -> 0.97 us  [swap_near(): return lax.ppermute(rows, axis, pairs + [(j, i) for i, j in pairs])]
    pallas_call x5 -> x7, Pallas kernels: 6.08 us -> 6.11 us  [call(): pl.pallas_call(functools.partial(kernel, plan), out_shape=[jax.ShapeDtype...]
where the time goes in v5:
time: 32.3 us; the launch traced here: 32 us
  starting transfers between devices  17.4 us (54%)
  waiting for transfers between devices  7.64 us (24%)
  Pallas kernels  6.11 us (19%)
  between operations  0.82 us (3%)
    all_to_all x1, starting transfers between devices, gather_totals(): lax.all_to_all(total, ('gx', 'gy'), split_axis=0, concat_axis=0, axis_ind...  9.66 us
    ppermute x6, starting transfers between devices, swap_near(): return lax.ppermute(rows, axis, pairs + [(j, i) for i, j in pairs])  7.74 us
    all_to_all x1, waiting for transfers between devices, gather_totals(): lax.all_to_all(total, ('gx', 'gy'), split_axis=0, concat_axis=0, axis_ind...  6.67 us
    pallas_call x7, Pallas kernels, call(): pl.pallas_call(functools.partial(kernel, plan), out_shape=[jax.ShapeDtype...  6.11 us
    ppermute x6, waiting for transfers between devices, swap_near(): return lax.ppermute(rows, axis, pairs + [(j, i) for i, j in pairs])  0.97 us
  transfers between devices with their start and end apart: 7, of which 3 were waited for; matrix products, arithmetic and copies ran while one was open for 0% of the time, Pallas kernels for 4%

profile of v5, /device:TPU:0, one launch (start us, length us, event | category | flops | bytes accessed | tf_op | source)
XLA Modules:
  0.0 32.0 jit_solution(9583203183775460640)
XLA Ops:
  0.6 0.0 copy-start.5
  0.6 0.0 copy-start.4
  0.7 0.0 copy-start.2
  0.7 0.0 copy-start.3
  0.7 1.9 %shard_map.95 = (f32[192,128]{1,0:T(8,128)}, f32[192,128]{1,0:T(8,128)}, f32[40,128]{1,0:T(8,128)}, f32[40,128]{1,0:T(8,128)}) custom-call(f32[4,64,128]{2,1,0:T(8,128)} %conc_ref.1, f32[4,64,128]{2,1,0:T(8,128)} %pot_ref.1, s32[4,64,128]{2,1,0:T(8,128)} %mask_ref, s32[4,64,128]{2,1,0:T(8,128)} %class_ref, f32[4,64,128]{2,1,0:T(8,128)} %mass_ref.3, ...), custom_call_target="tpu_custom_call" | custom-call | tf_op jit(solution)/shard_map/pallas_call | solution.py:561
  2.6 0.0 copy-start.6
  2.6 0.5 %collective-permute-start = (f32[192,128]{1,0:T(8,128)}, f32[192,128]{1,0:T(8,128)S(1)}, u32[]{:S(2)}, u32[]{:S(2)}) collective-permute-start(f32[192,128]{1,0:T(8,128)} %get-tuple-element.26), channel_id=1, source_target_pairs={{0,4},{8,12},{16,20},{24,28},{4,0},{12,8},{20,16},{28,24},{1,5},{9... | collective-permute-start | bytes 294920 | tf_op jit(solution)/shard_map/ppermute | solution.py:573
  3.1 0.7 %collective-permute-start.1 = (f32[192,128]{1,0:T(8,128)}, f32[192,128]{1,0:T(8,128)S(1)}, u32[]{:S(2)}, u32[]{:S(2)}) collective-permute-start(f32[192,128]{1,0:T(8,128)} %get-tuple-element.33), channel_id=1, source_target_pairs={{4,8},{12,16},{20,24},{8,4},{16,12},{24,20},{5,9},{13,17},{21,25},... | collective-permute-start | bytes 294920 | tf_op jit(solution)/shard_map/ppermute | solution.py:573
  3.8 0.0 copy-start.7
  3.8 2.7 %collective-permute-start.2 = (f32[40,128]{1,0:T(8,128)}, f32[40,128]{1,0:T(8,128)S(1)}, u32[]{:S(2)}, u32[]{:S(2)}) collective-permute-start(f32[40,128]{1,0:T(8,128)} %get-tuple-element.34), channel_id=1, source_target_pairs={{0,1},{2,3},{1,0},{3,2},{4,5},{6,7},{5,4},{7,6},{8,9},{10,11},{9,8... | collective-permute-start | bytes 61448 | tf_op jit(solution)/shard_map/ppermute | solution.py:573
  6.5 0.0 copy-start
  6.5 0.0 copy-start.1
  6.5 0.8 %collective-permute-start.3 = (f32[40,128]{1,0:T(8,128)}, f32[40,128]{1,0:T(8,128)S(1)}, u32[]{:S(2)}, u32[]{:S(2)}) collective-permute-start(f32[40,128]{1,0:T(8,128)} %get-tuple-element.35), channel_id=1, source_target_pairs={{1,2},{2,1},{5,6},{6,5},{9,10},{10,9},{13,14},{14,13},{17,18},{18,... | collective-permute-start | bytes 61448 | tf_op jit(solution)/shard_map/ppermute | solution.py:573
  7.2 0.0 collective-permute-done.x_near_ref.x_near_msg
  7.3 0.0 copy-done.5
  7.3 0.0 copy-done.4
  7.3 0.0 copy-done.6
  7.3 0.0 copy-done.7
  7.3 1.0 %shard_map.96 = (f32[4,64,128]{2,1,0:T(8,128)S(1)}, f32[8,256]{1,0:T(8,128)S(1)}, f32[256,24]{1,0:T(8,128)S(1)}, f32[8,128]{1,0:T(8,128)S(1)}) custom-call(s32[4,64,128]{2,1,0:T(8,128)S(1)} %copy-done.4, s32[4,64,128]{2,1,0:T(8,128)S(1)} %copy-done.5, f32[8]{0:T(128)S(1)} %copy-done.7, s32[8,64]{1,0:T(8,128)S(1)} %copy-done.6), custom_call_target="tpu_custom_call" | custom-call | tf_op jit(solution)/shard_map/pallas_call | solution.py:561
  8.3 0.2 collective-permute-done.2.y_near_ref.y_near_msg
  8.4 0.0 collective-permute-done.3.y_far_ref.y_far_msg
  8.4 0.0 collective-permute-done.1.x_far_ref.x_far_msg
  8.4 0.0 copy-done.2
  8.4 0.0 copy-done.3
  8.4 0.0 copy-done
  8.5 0.0 copy-done.1
  8.5 0.8 %shard_map.97 = (f32[4,64,128]{2,1,0:T(8,128)S(1)}, f32[4,64,128]{2,1,0:T(8,128)S(1)}, f32[16,128]{1,0:T(8,128)S(1)}, f32[160,128]{1,0:T(8,128)S(1)}, f32[136,128]{1,0:T(8,128)S(1)}) custom-call(f32[4,64,128]{2,1,0:T(8,128)S(1)} %copy-done.2, f32[4,64,128]{2,1,0:T(8,128)S(1)} %copy-done.3, f32[4,64,128]{2,1,0:T(8,128)S(1)} %get-tuple-element.29.mob_ref, ...), custom_call_target="tpu_custom_call" | custom-call | tf_op jit(solution)/shard_map/pallas_call | solution.py:561
  9.3 2.5 %collective-permute-start.4 = (f32[160,128]{1,0:T(8,128)S(1)}, f32[160,128]{1,0:T(8,128)S(1)}, u32[]{:S(2)}, u32[]{:S(2)}) collective-permute-start(f32[160,128]{1,0:T(8,128)S(1)} %get-tuple-element.40.own_ref), channel_id=1, source_target_pairs={{0,4},{8,12},{16,20},{24,28},{4,0},{12,8},{20,16},{28,24},{1,5},{9... | collective-permute-start | bytes 245768 | tf_op jit(solution)/shard_map/ppermute | solution.py:573
  11.7 0.1 shard_map.98.pick_ref
  11.9 0.8 %collective-permute-done.4.other_ref.x_near_ref = f32[160,128]{1,0:T(8,128)S(1)} collective-permute-done((f32[160,128]{1,0:T(8,128)S(1)}, f32[160,128]{1,0:T(8,128)S(1)}, u32[]{:S(2)}, u32[]{:S(2)}) %collective-permute-start.4) | collective-permute-done | bytes 81952 | tf_op jit(solution)/shard_map/ppermute | solution.py:573
  12.7 0.8 %shard_map.99 = f32[16,3,4,128]{3,2,1,0:T(4,128)} custom-call(f32[192,128]{1,0:T(8,128)S(1)} %shard_map.98.pick_ref, f32[160,128]{1,0:T(8,128)S(1)} %get-tuple-element.40.own_ref, f32[160,128]{1,0:T(8,128)S(1)} %collective-permute-done.4.other_ref.x_near_ref), custom_call_target="tpu_custom_call" | custom-call | tf_op jit(solution)/shard_map/pallas_call | solution.py:561
  13.4 9.7 %all-to-all-start = ((f32[16,3,4,128]{3,2,1,0:T(4,128)}), f32[16,3,4,128]{3,2,1,0:T(4,128)S(1)}, u32[]{:S(2)}, u32[]{:S(2)}) async-start(f32[16,3,4,128]{3,2,1,0:T(4,128)} %shard_map.99), calls=%async_computation | async-start | bytes 196608 | tf_op jit(solution)/shard_map/all_to_all | solution.py:586
  23.1 0.7 %collective-permute-start.5 = (f32[136,128]{1,0:T(8,128)S(1)}, f32[136,128]{1,0:T(8,128)S(1)}, u32[]{:S(2)}, u32[]{:S(2)}) collective-permute-start(f32[136,128]{1,0:T(8,128)S(1)} %get-tuple-element.43), channel_id=1, source_target_pairs={{4,8},{12,16},{20,24},{8,4},{16,12},{24,20},{5,9},{13,17},{21,25},... | collective-permute-start | bytes 208904 | tf_op jit(solution)/shard_map/ppermute | solution.py:573
  23.8 0.0 collective-permute-done.5.x_far_ref
  23.8 0.2 shard_map.100
  24.0 6.7 %all-to-all-done.total_ref = f32[16,3,4,128]{3,2,1,0:T(4,128)S(1)} async-done(((f32[16,3,4,128]{3,2,1,0:T(4,128)}), f32[16,3,4,128]{3,2,1,0:T(4,128)S(1)}, u32[]{:S(2)}, u32[]{:S(2)}) %all-to-all-start) | async-done | bytes 98336 | tf_op jit(solution)/shard_map/all_to_all | solution.py:586
  30.6 1.4 %shard_map.101 = (f32[4,64,128]{2,1,0:T(8,128)}, f32[4,64,128]{2,1,0:T(8,128)}) custom-call(f32[4,64,128]{2,1,0:T(8,128)S(1)} %get-tuple-element.36.conc_ref, f32[4,64,128]{2,1,0:T(8,128)S(1)} %get-tuple-element.37.pot_ref, f32[4,64,128]{2,1,0:T(8,128)S(1)} %copy-done, f32[4,64,128]{2,1,0:T(8,128)S(1)} %copy-done.1, ...), custom_call_target="tpu_custom_call" | custom-call | tf_op jit(solution)/shard_map/pallas_call | solution.py:561
Async XLA Ops:
  0.6 6.6 %copy-start.5 = (s32[4,64,128]{2,1,0:T(8,128)S(1)}, s32[4,64,128]{2,1,0:T(8,128)}, u32[]{:S(2)}) copy-start(s32[4,64,128]{2,1,0:T(8,128)} %class_ref) | copy-start | bytes 393220
  0.6 6.6 %copy-start.4 = (s32[4,64,128]{2,1,0:T(8,128)S(1)}, s32[4,64,128]{2,1,0:T(8,128)}, u32[]{:S(2)}) copy-start(s32[4,64,128]{2,1,0:T(8,128)} %mask_ref) | copy-start | bytes 393220
  0.7 7.8 %copy-start.2 = (f32[4,64,128]{2,1,0:T(8,128)S(1)}, f32[4,64,128]{2,1,0:T(8,128)}, u32[]{:S(2)}) copy-start(f32[4,64,128]{2,1,0:T(8,128)} %conc_ref.1) | copy-start | bytes 393220
  0.7 7.8 %copy-start.3 = (f32[4,64,128]{2,1,0:T(8,128)S(1)}, f32[4,64,128]{2,1,0:T(8,128)}, u32[]{:S(2)}) copy-start(f32[4,64,128]{2,1,0:T(8,128)} %pot_ref.1) | copy-start | bytes 393220
  2.6 4.7 %copy-start.6 = (s32[8,64]{1,0:T(8,128)S(1)}, s32[8,64]{1,0:T(8,128)}, u32[]{:S(2)}) copy-start(s32[8,64]{1,0:T(8,128)} %owner_ref.4) | copy-start | bytes 6148
  2.6 4.7 %collective-permute-start = (f32[192,128]{1,0:T(8,128)}, f32[192,128]{1,0:T(8,128)S(1)}, u32[]{:S(2)}, u32[]{:S(2)}) collective-permute-start(f32[192,128]{1,0:T(8,128)} %get-tuple-element.26), channel_id=1, source_target_pairs={{0,4},{8,12},{16,20},{24,28},{4,0},{12,8},{20,16},{28,24},{1,5},{9... | collective-permute-start | bytes 294920 | tf_op jit(solution)/shard_map/ppermute | solution.py:573
  3.1 5.3 %collective-permute-start.1 = (f32[192,128]{1,0:T(8,128)}, f32[192,128]{1,0:T(8,128)S(1)}, u32[]{:S(2)}, u32[]{:S(2)}) collective-permute-start(f32[192,128]{1,0:T(8,128)} %get-tuple-element.33), channel_id=1, source_target_pairs={{4,8},{12,16},{20,24},{8,4},{16,12},{24,20},{5,9},{13,17},{21,25},... | collective-permute-start | bytes 294920 | tf_op jit(solution)/shard_map/ppermute | solution.py:573
  3.8 3.5 %copy-start.7 = (f32[8]{0:T(128)S(1)}, f32[8]{0:T(128)}, u32[]{:S(2)}) copy-start(f32[8]{0:T(128)} %table_ref.1) | copy-start | bytes 100
  3.8 4.6 %collective-permute-start.2 = (f32[40,128]{1,0:T(8,128)}, f32[40,128]{1,0:T(8,128)S(1)}, u32[]{:S(2)}, u32[]{:S(2)}) collective-permute-start(f32[40,128]{1,0:T(8,128)} %get-tuple-element.34), channel_id=1, source_target_pairs={{0,1},{2,3},{1,0},{3,2},{4,5},{6,7},{5,4},{7,6},{8,9},{10,11},{9,8... | collective-permute-start | bytes 61448 | tf_op jit(solution)/shard_map/ppermute | solution.py:573
  6.5 2.0 %copy-start = (f32[4,64,128]{2,1,0:T(8,128)S(1)}, f32[4,64,128]{2,1,0:T(8,128)}, u32[]{:S(2)}) copy-start(f32[4,64,128]{2,1,0:T(8,128)} %mass_ref.3) | copy-start | bytes 393220
  6.5 2.0 %copy-start.1 = (f32[4,64,128]{2,1,0:T(8,128)S(1)}, f32[4,64,128]{2,1,0:T(8,128)}, u32[]{:S(2)}) copy-start(f32[4,64,128]{2,1,0:T(8,128)} %pots_ref.3) | copy-start | bytes 393220
  6.5 2.0 %collective-permute-start.3 = (f32[40,128]{1,0:T(8,128)}, f32[40,128]{1,0:T(8,128)S(1)}, u32[]{:S(2)}, u32[]{:S(2)}) collective-permute-start(f32[40,128]{1,0:T(8,128)} %get-tuple-element.35), channel_id=1, source_target_pairs={{1,2},{2,1},{5,6},{6,5},{9,10},{10,9},{13,14},{14,13},{17,18},{18,... | collective-permute-start | bytes 61448 | tf_op jit(solution)/shard_map/ppermute | solution.py:573
  9.3 3.4 %collective-permute-start.4 = (f32[160,128]{1,0:T(8,128)S(1)}, f32[160,128]{1,0:T(8,128)S(1)}, u32[]{:S(2)}, u32[]{:S(2)}) collective-permute-start(f32[160,128]{1,0:T(8,128)S(1)} %get-tuple-element.40.own_ref), channel_id=1, source_target_pairs={{0,4},{8,12},{16,20},{24,28},{4,0},{12,8},{20,16},{28,24},{1,5},{9... | collective-permute-start | bytes 245768 | tf_op jit(solution)/shard_map/ppermute | solution.py:573
  13.4 17.2 %all-to-all-start = ((f32[16,3,4,128]{3,2,1,0:T(4,128)}), f32[16,3,4,128]{3,2,1,0:T(4,128)S(1)}, u32[]{:S(2)}, u32[]{:S(2)}) async-start(f32[16,3,4,128]{3,2,1,0:T(4,128)} %shard_map.99), calls=%async_computation | async-start | bytes 196608 | tf_op jit(solution)/shard_map/all_to_all | solution.py:586
  23.1 0.7 %collective-permute-start.5 = (f32[136,128]{1,0:T(8,128)S(1)}, f32[136,128]{1,0:T(8,128)S(1)}, u32[]{:S(2)}, u32[]{:S(2)}) collective-permute-start(f32[136,128]{1,0:T(8,128)S(1)} %get-tuple-element.43), channel_id=1, source_target_pairs={{4,8},{12,16},{20,24},{8,4},{16,12},{24,20},{5,9},{13,17},{21,25},... | collective-permute-start | bytes 208904 | tf_op jit(solution)/shard_map/ppermute | solution.py:573

commit v6 on v4

--- a/solution.py
+++ b/solution.py
@@ -21,7 +21,6 @@
 F32 = jnp.float32
 BF16 = jnp.bfloat16
 VMEM_LIMIT = 48 * 1024 * 1024
-LARGE_LIMIT = 60 * 1024 * 1024
 
 
 def iota(shape, dim):
@@ -120,7 +119,7 @@
         self.map_row = round_up(8 * self.x, 8)
         self.y_rows = self.map_row + owners
         self.cells = self.x * self.y
-        self.rows = self.cells + 2 * self.y
+        self.rows = (self.half_x + 2) * self.y
         self.low_row = owners
         self.high_row = owners + self.half_x
         self.slot_parts = -(-(owners + 2 * self.half_x) // 4)
@@ -140,14 +139,15 @@
     g = lax.axis_index("gx")
     last = plan.owners - 1
     owner = iota((plan.owners, plan.columns), 0)
-    shape = (plan.x + 2, plan.y, plan.columns)
+    low, high = plan.half_x, plan.half_x + 1
+    shape = (plan.half_x + 2, plan.y, plan.columns)
     x, y, column = iota(shape, 0), iota(shape, 1), iota(shape, 2)
-    half = jnp.where(x < plan.x, x >> 1, jnp.where(x == plan.x, plan.half_x - 1, 0))
+    half = jnp.where(x < low, x, jnp.where(x == low, plan.half_x - 1, 0))
     place = column == half * plan.half_y + (y >> 1)
     sides = (
-        (x < plan.x, g, True),
-        (x == plan.x, jnp.maximum(g - 1, 0), g > 0),
-        (x == plan.x + 1, jnp.minimum(g + 1, last), g < last),
+        (x < low, g, True),
+        (x == low, jnp.maximum(g - 1, 0), g > 0),
+        (x == high, jnp.minimum(g + 1, last), g < last),
     )
     gather, spread = None, None
     for part, row, inside in sides:
@@ -190,7 +190,8 @@
 
 def received(axis, near_ref, far_ref):
     up = even(axis)
-    near, far = near_ref[...], far_ref[...]
+    rows = pl.ds(0, min(near_ref.shape[0], far_ref.shape[0]))
+    near, far = near_ref[rows, :], far_ref[rows, :]
     return jnp.where(up, far, near), jnp.where(up, near, far)
 
 
@@ -243,8 +244,8 @@
 
 
 def first_kernel(
-    plan, conc_ref, pot_ref, mob_ref, mass_ref, pots_ref, gather_ref, scale_ref, owner_ref,
-    x_near_ref, x_far_ref, y_near_ref, y_far_ref,
+    plan, x_far_ref, y_far_ref, y_near_ref, x_near_ref,
+    conc_ref, pot_ref, mob_ref, mass_ref, pots_ref, gather_ref, scale_ref, owner_ref,
     conc_out, pot_out, total_out, raw_out, x_near_out, x_far_out,
 ):
     sides = received("gx", x_near_ref, x_far_ref)
@@ -287,23 +288,21 @@
         conc, pot, neighbours(conc, nothing), neighbours(pot, nothing), faces, diagonal,
         mass_source, pot_source,
     )
-    give_mass = [own_mass.reshape(plan.cells, plan.p)]
-    give_pot = [own_pot.reshape(plan.cells, plan.p)]
+    give_mass, give_pot = (
+        [field[x] + field[x + 1] for x in range(0, plan.x, 2)] for field in (own_mass, own_pot)
+    )
     for x, side in ((0, 0), (plan.x - 1, 1)):
         face = 0.5 * (mobility[x] + mob_halo[side][0])
         give_mass.append(time_step * face * pot[x])
         give_pot.append(-interface * conc[x])
-    give = jnp.concatenate(
-        [jnp.concatenate(give_mass, axis=0), jnp.concatenate(give_pot, axis=0)], axis=1
-    )
-
-    def packed(both):
-        mass, other = both[:, : plan.p], both[:, plan.p :]
+
+    def packed(mass, other):
         first = iota(mass.shape, 1) & 1 == 0
         return jnp.where(
             first, mass + pltpu.roll(mass, plan.p - 1, 1), other + pltpu.roll(other, 1, 1)
         )
 
+    give = packed(jnp.concatenate(give_mass, axis=0), jnp.concatenate(give_pot, axis=0))
     h = lax.axis_index("gy")
     inside = (h > 0, None, h < plan.groups - 1)
     maps = [rows[plan.map_row : plan.map_row + plan.owners, : plan.columns] for rows in ends]
@@ -311,11 +310,7 @@
     owner = iota((plan.owners, 1), 0)
     is_mine = owner == lax.axis_index("gx")
 
-    def column(place, i, at):
-        b = i * plan.half_y + at
-        return maps[place][:, b : b + 1]
-
-    sums = [None, packed(split_dot(gather_ref[...].astype(BF16), give, ((1,), (0,)))), None]
+    sums = [None, split_dot(gather_ref[...].astype(BF16), give, ((1,), (0,))), None]
     sums[1] = sums[1] * scale_ref[...]
     for place, y, at, side in ((0, 0, plan.half_y - 1, 2), (2, plan.y - 1, 0, 3)):
         edge_mob, edge_pot, edge_conc = (
@@ -323,20 +318,21 @@
             for field in (mobility, pot, conc)
         )
         face = 0.5 * (edge_mob + mob_halo[side][:, 0])
-        both = jnp.concatenate([time_step * face * edge_pot, -interface * edge_conc], axis=1)
-        part = jnp.zeros((plan.owners, 2 * plan.p), F32)
+        both = packed(time_step * face * edge_pot, -interface * edge_conc)
+        part = jnp.zeros((plan.owners, plan.p), F32)
         for i in range(plan.half_x):
-            ident = jnp.sum(jnp.where(is_mine, column(place, i, at), 0.0), axis=0, keepdims=True)
+            column = owner_column(plan, maps[place], i, at)
+            ident = jnp.sum(jnp.where(is_mine, column, 0.0), axis=0, keepdims=True)
             pair = both[2 * i : 2 * i + 1] + both[2 * i + 1 : 2 * i + 2]
             part = part + jnp.where((owner.astype(F32) == ident) & inside[place], pair, 0.0)
-        sums[place] = packed(part) * scale_of(plan, maps[place])
-
+        sums[place] = part * scale_of(plan, maps[place])
     if not plan.slots:
         total_out[...] = jnp.concatenate(sums, axis=0)
         return
 
     def picked(place, i, at):
-        ident = jnp.broadcast_to(column(place, i, at), (plan.owners, plan.p))
+        column = owner_column(plan, maps[place], i, at)
+        ident = jnp.broadcast_to(column, (plan.owners, plan.p))
         out = jnp.zeros((plan.owners, plan.p), F32)
         for o in range(plan.owners):
             out = jnp.where(ident == float(o), sums[place][o : o + 1], out)
@@ -346,18 +342,19 @@
     above = [[picked(k, i, 0) for i in range(plan.half_x)] for k in range(3)]
 
     def of_plane(plane, choices):
-        out = jnp.zeros_like(choices[0])
+        out = jnp.zeros((plan.owners, plan.p), F32)
         for k in range(3):
             out = jnp.where(plane == h + (k - 1), choices[k], out)
         return out
 
+    size = 4 * plan.slot_parts
     for plane in range(plan.groups):
         main = of_plane(plane, sums)
         beside = []
         for i in range(plan.half_x):
             beside.append((plan.low_row + i, of_plane(plane - 1, [k[i] for k in below])))
             beside.append((plan.high_row + i, of_plane(plane + 1, [k[i] for k in above])))
-        beside += [(row, jnp.zeros_like(main)) for row in range(plan.high_row + plan.half_x, 4 * plan.slot_parts)]
+        beside += [(at, jnp.zeros_like(main)) for at in range(plan.high_row + plan.half_x, size)]
         for g in range(plan.owners):
             slot = g * plan.groups + plane
             for part in range(plan.owners // 4):
@@ -366,6 +363,11 @@
                 total_out[slot, row // 4, pl.ds(row % 4, 1), :] = values[g : g + 1]
 
 
+def owner_column(plan, owners, i, at):
+    b = i * plan.half_y + at
+    return owners[:, b : b + 1]
+
+
 def coarse_solve(packed, planes):
     lane = iota(packed.shape, 1)
     even = lane & 1 == 0
@@ -398,7 +400,7 @@
 
 
 def beside_kernel(
-    plan, mob_ref, raw_ref, x_near_msg, x_far_msg, y_near_msg, y_far_msg, x_near_ref, x_far_ref,
+    plan, x_far_ref, x_near_ref, mob_ref, raw_ref, x_near_msg, x_far_msg, y_near_msg, y_far_msg,
     faces_out, diagonal_out, scale_out, ends_out,
 ):
     mobility = mob_ref[...]
@@ -476,7 +478,7 @@
         slabs = [side_rows(plan, sides[0], which)]
         slabs += [ref[pl.ds(x, 1)] for x in range(plan.x)]
         slabs.append(side_rows(plan, sides[1], which))
-        order = [plan.x, *range(plan.x), plan.x + 1]
+        order = [plan.half_x, *[x >> 1 for x in range(plan.x)], plan.half_x + 1]
         slabs = [
             slab + corr[x * plan.y : (x + 1) * plan.y][None] for slab, x in zip(slabs, order)
         ]
@@ -518,7 +520,7 @@
         copy.wait()
 
 
-def call(kernel, plan, outs, args, far=(), smem=(), scratch=(), limit=VMEM_LIMIT, out_far=False):
+def call(kernel, plan, outs, args, far=(), smem=(), scratch=(), out_far=False):
     def space(i):
         return pl.ANY if i in far else pltpu.SMEM if i in smem else pltpu.VMEM
 
@@ -528,17 +530,20 @@
         in_specs=[pl.BlockSpec(memory_space=space(i)) for i in range(len(args))],
         out_specs=[pl.BlockSpec(memory_space=pl.ANY if out_far else pltpu.VMEM)] * len(outs),
         scratch_shapes=list(scratch),
-        compiler_params=pltpu.CompilerParams(vmem_limit_bytes=limit),
-    )(*args)
-
-
-def swap(axis, near, far):
-    count = lax.axis_size(axis)
-    out = []
-    for rows, begin in ((near, 0), (far, 1)):
-        pairs = [(i, i + 1) for i in range(begin, count - 1, 2)]
-        out.append(lax.ppermute(rows, axis, pairs + [(j, i) for i, j in pairs]))
-    return out
+        compiler_params=pltpu.CompilerParams(vmem_limit_bytes=VMEM_LIMIT),
+    )(*[
+        pltpu.with_memory_space_constraint(arg, pltpu.HBM) if i in far else arg
+        for i, arg in enumerate(args)
+    ])
+
+
+def swap_near(axis, rows, begin=0):
+    pairs = [(i, i + 1) for i in range(begin, lax.axis_size(axis) - 1, 2)]
+    return lax.ppermute(rows, axis, pairs + [(j, i) for i, j in pairs])
+
+
+def swap_far(axis, rows):
+    return swap_near(axis, rows, 1)
 
 
 def gather_totals(plan, total, y_near, y_far):
@@ -575,7 +580,6 @@
         [*[(3 * plan.y, plan.p)] * 2, *[(plan.y_rows, plan.p)] * 2],
         [*fields, owner_map, table],
         far=range(8),
-        limit=LARGE_LIMIT,
         scratch=(
             *[pltpu.VMEM((2, plan.y, plan.p), field.dtype) for field in fields[:4]],
             *[pltpu.VMEM((2, plan.x, 8, plan.p), field.dtype) for field in fields],
@@ -584,8 +588,11 @@
             pltpu.SemaphoreType.DMA((22,)),
         ),
     )
-    old = [*swap("gx", *messages[:2]), *swap("gy", *messages[2:])]
-    old[0], mask, kind = lax.optimization_barrier((old[0], mask, kind))
+    x_far = swap_far("gx", messages[1])
+    y_far = swap_far("gy", messages[3])
+    y_near = swap_near("gy", messages[2])
+    x_far, x_near, mask, kind = lax.optimization_barrier((x_far, messages[0], mask, kind))
+    x_near = swap_near("gx", x_near)
     mob, gather, spread, scale = call(
         local_kernel,
         plan,
@@ -594,7 +601,7 @@
         smem=(2,),
     )
     slots = (plan.slots, plan.slot_parts, 4, plan.p)
-    conc, pot, total, raw, *messages = call(
+    conc, pot, total, raw, near, far = call(
         first_kernel,
         plan,
         [
@@ -604,22 +611,26 @@
             (4 * plan.x, plan.p),
             *[(2 * plan.y + 8, plan.p)] * 2,
         ],
-        [conc, pot, mob, mass_source, pot_source, gather, scale, owner_map, *old],
-    )
-    total = gather_totals(plan, total, *old[2:])
-    new = swap("gx", *messages)
+        [
+            x_far, y_far, y_near, x_near,
+            conc, pot, mob, mass_source, pot_source, gather, scale, owner_map,
+        ],
+    )
+    total = gather_totals(plan, total, y_near, y_far)
+    far = swap_far("gx", far)
+    near = swap_near("gx", near)
     faces, diagonal, scale, ends = call(
         beside_kernel,
         plan,
         [(6, *block), block, block, (4 * plan.x, plan.p)],
-        [mob, raw, *old, *new],
+        [far, near, mob, raw, x_near, x_far, y_near, y_far],
     )
     return tuple(
         call(
             last_kernel,
             plan,
             [block, block],
-            [conc, pot, mass_source, pot_source, faces, diagonal, scale, *new, ends, spread, total],
+            [conc, pot, mass_source, pot_source, faces, diagonal, scale, near, far, ends, spread, total],
             out_far=True,
             scratch=(
                 pltpu.VMEM(block, F32),

time: 31.8 us -> 34.2 us (1.075)
  starting transfers between devices: 16.3 us -> 21.7 us
  waiting for transfers between devices: 8.32 us -> 6.07 us
  Pallas kernels: 6.08 us -> 5.33 us
    ppermute x6, starting transfers between devices: 5.59 us -> 16.5 us  [swap_near(): return lax.ppermute(rows, axis, pairs + [(j, i) for i, j in pairs])]
    all_to_all x1, starting transfers between devices: 10.7 us -> 5.24 us  [gather_totals(): lax.all_to_all(total, ('gx', 'gy'), split_axis=0, concat_axis=0, tiled=True)]
    all_to_all x1, waiting for transfers between devices: 7.83 us -> 4.39 us  [gather_totals(): lax.all_to_all(total, ('gx', 'gy'), split_axis=0, concat_axis=0, tiled=True)]
    ppermute x6, waiting for transfers between devices: 0.5 us -> 1.68 us  [swap_near(): return lax.ppermute(rows, axis, pairs + [(j, i) for i, j in pairs])]
    pallas_call x5, Pallas kernels: 6.08 us -> 5.33 us  [call(): pl.pallas_call(functools.partial(kernel, plan), out_shape=[jax.ShapeDtype...]
  transfers between devices with their start and end apart: 7 -> 7, of which waited for: 3 -> 3; matrix products, arithmetic and copies ran while one was open for 0% -> 0% of each run, Pallas kernels for 4% -> 3%
where the time goes in v6:
time: 34.2 us; the launch traced here: 34 us
  starting transfers between devices  21.7 us (63%)
  waiting for transfers between devices  6.07 us (18%)
  Pallas kernels  5.33 us (16%)
  between operations  0.78 us (2%)
    ppermute x6, starting transfers between devices, swap_near(): return lax.ppermute(rows, axis, pairs + [(j, i) for i, j in pairs])  16.5 us
    pallas_call x5, Pallas kernels, call(): pl.pallas_call(functools.partial(kernel, plan), out_shape=[jax.ShapeDtype...  5.33 us
    all_to_all x1, starting transfers between devices, gather_totals(): lax.all_to_all(total, ('gx', 'gy'), split_axis=0, concat_axis=0, tiled=True)  5.24 us
    all_to_all x1, waiting for transfers between devices, gather_totals(): lax.all_to_all(total, ('gx', 'gy'), split_axis=0, concat_axis=0, tiled=True)  4.39 us
    ppermute x6, waiting for transfers between devices, swap_near(): return lax.ppermute(rows, axis, pairs + [(j, i) for i, j in pairs])  1.68 us
  transfers between devices with their start and end apart: 7, of which 3 were waited for; matrix products, arithmetic and copies ran while one was open for 0% of the time, Pallas kernels for 3%

profile of v6, /device:TPU:0, one launch (start us, length us, event | category | flops | bytes accessed | tf_op | source)
XLA Modules:
  0.0 34.0 jit_solution(17989066324770250266)
XLA Ops:
  0.6 0.0 copy-start.5
  0.6 0.0 copy-start.4
  0.7 0.0 copy-start.2
  0.7 0.0 copy-start.3
  0.7 1.3 %shard_map.95 = (f32[192,128]{1,0:T(8,128)S(1)}, f32[192,128]{1,0:T(8,128)S(1)}, f32[40,128]{1,0:T(8,128)S(1)}, f32[40,128]{1,0:T(8,128)S(1)}) custom-call(f32[4,64,128]{2,1,0:T(8,128)} %conc_ref.1, f32[4,64,128]{2,1,0:T(8,128)} %pot_ref.1, s32[4,64,128]{2,1,0:T(8,128)} %mask_ref, s32[4,64,128]{2,1,0:T(8,128)} %class_ref, f32[4,64,128]{2,1,0:T(8,128)} %mass_ref.3, ...), custom_call_target="tpu_custom_call" | custom-call | tf_op jit(solution)/shard_map/pallas_call | solution.py:527
  1.9 0.0 copy-start.6
  2.0 0.7 %collective-permute-start = (f32[192,128]{1,0:T(8,128)S(1)}, f32[192,128]{1,0:T(8,128)S(1)}, u32[]{:S(2)}, u32[]{:S(2)}) collective-permute-start(f32[192,128]{1,0:T(8,128)S(1)} %get-tuple-element.24), channel_id=1, source_target_pairs={{4,8},{12,16},{20,24},{8,4},{16,12},{24,20},{5,9},{13,17},{21,25},... | collective-permute-start | bytes 294920 | tf_op jit(solution)/shard_map/ppermute | solution.py:542
  2.6 0.0 collective-permute-done.x_far_ref.x_far_msg
  2.6 6.7 %collective-permute-start.3 = (f32[192,128]{1,0:T(8,128)S(1)}, f32[192,128]{1,0:T(8,128)S(1)}, u32[]{:S(2)}, u32[]{:S(2)}) collective-permute-start(f32[192,128]{1,0:T(8,128)S(1)} %get-tuple-element.29), channel_id=1, source_target_pairs={{0,4},{8,12},{16,20},{24,28},{4,0},{12,8},{20,16},{28,24},{1,5},{9... | collective-permute-start | bytes 294920 | tf_op jit(solution)/shard_map/ppermute | solution.py:542
  9.4 0.0 copy-start.7
  9.4 0.8 %collective-permute-start.1 = (f32[40,128]{1,0:T(8,128)S(1)}, f32[40,128]{1,0:T(8,128)S(1)}, u32[]{:S(2)}, u32[]{:S(2)}) collective-permute-start(f32[40,128]{1,0:T(8,128)S(1)} %get-tuple-element.27), channel_id=1, source_target_pairs={{1,2},{2,1},{5,6},{6,5},{9,10},{10,9},{13,14},{14,13},{17,18},{18,... | collective-permute-start | bytes 61448 | tf_op jit(solution)/shard_map/ppermute | solution.py:542
  10.2 0.0 copy-start
  10.2 0.0 copy-start.1
  10.2 4.5 %collective-permute-start.2 = (f32[40,128]{1,0:T(8,128)S(1)}, f32[40,128]{1,0:T(8,128)S(1)}, u32[]{:S(2)}, u32[]{:S(2)}) collective-permute-start(f32[40,128]{1,0:T(8,128)S(1)} %get-tuple-element.28), channel_id=1, source_target_pairs={{0,1},{2,3},{1,0},{3,2},{4,5},{6,7},{5,4},{7,6},{8,9},{10,11},{9,8... | collective-permute-start | bytes 61448 | tf_op jit(solution)/shard_map/ppermute | solution.py:542
  14.7 0.0 copy-done.5
  14.7 0.0 copy-done.4
  14.7 0.0 copy-done.6
  14.7 0.0 copy-done.7
  14.7 1.0 %shard_map.96 = (f32[4,64,128]{2,1,0:T(8,128)S(1)}, f32[8,256]{1,0:T(8,128)S(1)}, f32[256,24]{1,0:T(8,128)S(1)}, f32[8,128]{1,0:T(8,128)S(1)}) custom-call(s32[4,64,128]{2,1,0:T(8,128)S(1)} %copy-done.4, s32[4,64,128]{2,1,0:T(8,128)S(1)} %copy-done.5, f32[8]{0:T(128)S(1)} %copy-done.7, s32[8,64]{1,0:T(8,128)S(1)} %copy-done.6), custom_call_target="tpu_custom_call" | custom-call | tf_op jit(solution)/shard_map/pallas_call | solution.py:527
  15.6 0.0 collective-permute-done.1.y_far_ref.y_far_msg
  15.7 0.8 %collective-permute-done.2.y_near_ref.y_near_msg = f32[40,128]{1,0:T(8,128)S(1)} collective-permute-done((f32[40,128]{1,0:T(8,128)S(1)}, f32[40,128]{1,0:T(8,128)S(1)}, u32[]{:S(2)}, u32[]{:S(2)}) %collective-permute-start.2) | collective-permute-done | bytes 20512 | tf_op jit(solution)/shard_map/ppermute | solution.py:542
  16.4 0.0 collective-permute-done.3.x_near_ref.x_near_msg
  16.4 0.0 copy-done.2
  16.4 0.0 copy-done.3
  16.4 0.0 copy-done
  16.4 0.0 copy-done.1
  16.5 1.6 %shard_map.97 = (f32[4,64,128]{2,1,0:T(8,128)S(1)}, f32[4,64,128]{2,1,0:T(8,128)S(1)}, f32[32,3,4,128]{3,2,1,0:T(4,128)}, f32[16,128]{1,0:T(8,128)S(1)}, f32[136,128]{1,0:T(8,128)S(1)}, /*index=5*/f32[136,128]{1,0:T(8,128)S(1)}) custom-call(f32[192,128]{1,0:T(8,128)S(1)} %collective-permute-done.x_far_ref.x_far_msg, ...), custom_call_target="tpu_custom_call" | custom-call | tf_op jit(solution)/shard_map/pallas_call | solution.py:527
  18.0 5.2 %all-to-all-start = ((f32[32,3,4,128]{3,2,1,0:T(4,128)}), f32[32,3,4,128]{3,2,1,0:T(4,128)S(1)}, u32[]{:S(2)}, u32[]{:S(2)}) async-start(f32[32,3,4,128]{3,2,1,0:T(4,128)} %get-tuple-element.45), calls=%async_computation | async-start | bytes 393216 | tf_op jit(solution)/shard_map/all_to_all | solution.py:551
  23.3 0.7 %collective-permute-start.4 = (f32[136,128]{1,0:T(8,128)S(1)}, f32[136,128]{1,0:T(8,128)S(1)}, u32[]{:S(2)}, u32[]{:S(2)}) collective-permute-start(f32[136,128]{1,0:T(8,128)S(1)} %get-tuple-element.37), channel_id=1, source_target_pairs={{4,8},{12,16},{20,24},{8,4},{16,12},{24,20},{5,9},{13,17},{21,25},... | collective-permute-start | bytes 208904 | tf_op jit(solution)/shard_map/ppermute | solution.py:542
  23.9 3.2 %collective-permute-start.5 = (f32[136,128]{1,0:T(8,128)S(1)}, f32[136,128]{1,0:T(8,128)S(1)}, u32[]{:S(2)}, u32[]{:S(2)}) collective-permute-start(f32[136,128]{1,0:T(8,128)S(1)} %get-tuple-element.38), channel_id=1, source_target_pairs={{0,4},{8,12},{16,20},{24,28},{4,0},{12,8},{20,16},{28,24},{1,5},{9... | collective-permute-start | bytes 208904 | tf_op jit(solution)/shard_map/ppermute | solution.py:542
  27.1 0.0 collective-permute-done.4.x_far_ref
  27.1 0.9 %collective-permute-done.5.x_near_ref = f32[136,128]{1,0:T(8,128)S(1)} collective-permute-done((f32[136,128]{1,0:T(8,128)S(1)}, f32[136,128]{1,0:T(8,128)S(1)}, u32[]{:S(2)}, u32[]{:S(2)}) %collective-permute-start.5) | collective-permute-done | bytes 69664 | tf_op jit(solution)/shard_map/ppermute | solution.py:542
  28.0 0.2 shard_map.98
  28.2 4.4 %all-to-all-done.total_ref = f32[32,3,4,128]{3,2,1,0:T(4,128)S(1)} async-done(((f32[32,3,4,128]{3,2,1,0:T(4,128)}), f32[32,3,4,128]{3,2,1,0:T(4,128)S(1)}, u32[]{:S(2)}, u32[]{:S(2)}) %all-to-all-start) | async-done | bytes 196640 | tf_op jit(solution)/shard_map/all_to_all | solution.py:551
  32.6 1.4 %shard_map.99 = (f32[4,64,128]{2,1,0:T(8,128)}, f32[4,64,128]{2,1,0:T(8,128)}) custom-call(f32[4,64,128]{2,1,0:T(8,128)S(1)} %get-tuple-element.35.conc_ref, f32[4,64,128]{2,1,0:T(8,128)S(1)} %get-tuple-element.36.pot_ref, f32[4,64,128]{2,1,0:T(8,128)S(1)} %copy-done, f32[4,64,128]{2,1,0:T(8,128)S(1)} %copy-done.1, ...), custom_call_target="tpu_custom_call" | custom-call | tf_op jit(solution)/shard_map/pallas_call | solution.py:527
Async XLA Ops:
  0.6 14.0 %copy-start.5 = (s32[4,64,128]{2,1,0:T(8,128)S(1)}, s32[4,64,128]{2,1,0:T(8,128)}, u32[]{:S(2)}) copy-start(s32[4,64,128]{2,1,0:T(8,128)} %class_ref) | copy-start | bytes 393220
  0.6 14.0 %copy-start.4 = (s32[4,64,128]{2,1,0:T(8,128)S(1)}, s32[4,64,128]{2,1,0:T(8,128)}, u32[]{:S(2)}) copy-start(s32[4,64,128]{2,1,0:T(8,128)} %mask_ref) | copy-start | bytes 393220
  0.7 15.8 %copy-start.2 = (f32[4,64,128]{2,1,0:T(8,128)S(1)}, f32[4,64,128]{2,1,0:T(8,128)}, u32[]{:S(2)}) copy-start(f32[4,64,128]{2,1,0:T(8,128)} %conc_ref.1) | copy-start | bytes 393220
  0.7 15.8 %copy-start.3 = (f32[4,64,128]{2,1,0:T(8,128)S(1)}, f32[4,64,128]{2,1,0:T(8,128)}, u32[]{:S(2)}) copy-start(f32[4,64,128]{2,1,0:T(8,128)} %pot_ref.1) | copy-start | bytes 393220
  1.9 12.7 %copy-start.6 = (s32[8,64]{1,0:T(8,128)S(1)}, s32[8,64]{1,0:T(8,128)}, u32[]{:S(2)}) copy-start(s32[8,64]{1,0:T(8,128)} %owner_ref.3) | copy-start | bytes 6148
  2.0 0.7 %collective-permute-start = (f32[192,128]{1,0:T(8,128)S(1)}, f32[192,128]{1,0:T(8,128)S(1)}, u32[]{:S(2)}, u32[]{:S(2)}) collective-permute-start(f32[192,128]{1,0:T(8,128)S(1)} %get-tuple-element.24), channel_id=1, source_target_pairs={{4,8},{12,16},{20,24},{8,4},{16,12},{24,20},{5,9},{13,17},{21,25},... | collective-permute-start | bytes 294920 | tf_op jit(solution)/shard_map/ppermute | solution.py:542
  2.6 13.8 %collective-permute-start.3 = (f32[192,128]{1,0:T(8,128)S(1)}, f32[192,128]{1,0:T(8,128)S(1)}, u32[]{:S(2)}, u32[]{:S(2)}) collective-permute-start(f32[192,128]{1,0:T(8,128)S(1)} %get-tuple-element.29), channel_id=1, source_target_pairs={{0,4},{8,12},{16,20},{24,28},{4,0},{12,8},{20,16},{28,24},{1,5},{9... | collective-permute-start | bytes 294920 | tf_op jit(solution)/shard_map/ppermute | solution.py:542
  9.4 5.3 %copy-start.7 = (f32[8]{0:T(128)S(1)}, f32[8]{0:T(128)}, u32[]{:S(2)}) copy-start(f32[8]{0:T(128)} %table_ref.1) | copy-start | bytes 100
  9.4 6.3 %collective-permute-start.1 = (f32[40,128]{1,0:T(8,128)S(1)}, f32[40,128]{1,0:T(8,128)S(1)}, u32[]{:S(2)}, u32[]{:S(2)}) collective-permute-start(f32[40,128]{1,0:T(8,128)S(1)} %get-tuple-element.27), channel_id=1, source_target_pairs={{1,2},{2,1},{5,6},{6,5},{9,10},{10,9},{13,14},{14,13},{17,18},{18,... | collective-permute-start | bytes 61448 | tf_op jit(solution)/shard_map/ppermute | solution.py:542
  10.2 6.3 %copy-start = (f32[4,64,128]{2,1,0:T(8,128)S(1)}, f32[4,64,128]{2,1,0:T(8,128)}, u32[]{:S(2)}) copy-start(f32[4,64,128]{2,1,0:T(8,128)} %mass_ref.3) | copy-start | bytes 393220
  10.2 6.3 %copy-start.1 = (f32[4,64,128]{2,1,0:T(8,128)S(1)}, f32[4,64,128]{2,1,0:T(8,128)}, u32[]{:S(2)}) copy-start(f32[4,64,128]{2,1,0:T(8,128)} %pots_ref.3) | copy-start | bytes 393220
  10.2 6.2 %collective-permute-start.2 = (f32[40,128]{1,0:T(8,128)S(1)}, f32[40,128]{1,0:T(8,128)S(1)}, u32[]{:S(2)}, u32[]{:S(2)}) collective-permute-start(f32[40,128]{1,0:T(8,128)S(1)} %get-tuple-element.28), channel_id=1, source_target_pairs={{0,1},{2,3},{1,0},{3,2},{4,5},{6,7},{5,4},{7,6},{8,9},{10,11},{9,8... | collective-permute-start | bytes 61448 | tf_op jit(solution)/shard_map/ppermute | solution.py:542
  18.0 14.6 %all-to-all-start = ((f32[32,3,4,128]{3,2,1,0:T(4,128)}), f32[32,3,4,128]{3,2,1,0:T(4,128)S(1)}, u32[]{:S(2)}, u32[]{:S(2)}) async-start(f32[32,3,4,128]{3,2,1,0:T(4,128)} %get-tuple-element.45), calls=%async_computation | async-start | bytes 393216 | tf_op jit(solution)/shard_map/all_to_all | solution.py:551
  23.3 3.9 %collective-permute-start.4 = (f32[136,128]{1,0:T(8,128)S(1)}, f32[136,128]{1,0:T(8,128)S(1)}, u32[]{:S(2)}, u32[]{:S(2)}) collective-permute-start(f32[136,128]{1,0:T(8,128)S(1)} %get-tuple-element.37), channel_id=1, source_target_pairs={{4,8},{12,16},{20,24},{8,4},{16,12},{24,20},{5,9},{13,17},{21,25},... | collective-permute-start | bytes 208904 | tf_op jit(solution)/shard_map/ppermute | solution.py:542
  23.9 4.1 %collective-permute-start.5 = (f32[136,128]{1,0:T(8,128)S(1)}, f32[136,128]{1,0:T(8,128)S(1)}, u32[]{:S(2)}, u32[]{:S(2)}) collective-permute-start(f32[136,128]{1,0:T(8,128)S(1)} %get-tuple-element.38), channel_id=1, source_target_pairs={{0,4},{8,12},{16,20},{24,28},{4,0},{12,8},{20,16},{28,24},{1,5},{9... | collective-permute-start | bytes 208904 | tf_op jit(solution)/shard_map/ppermute | solution.py:542

commit v7 on v6

--- a/solution.py
+++ b/solution.py
@@ -244,9 +244,9 @@
 
 
 def first_kernel(
-    plan, x_far_ref, y_far_ref, y_near_ref, x_near_ref,
+    plan, x_near_ref, x_far_ref, y_near_ref, y_far_ref,
     conc_ref, pot_ref, mob_ref, mass_ref, pots_ref, gather_ref, scale_ref, owner_ref,
-    conc_out, pot_out, total_out, raw_out, x_near_out, x_far_out,
+    conc_out, pot_out, total_hbm, raw_out, x_near_out, x_far_out, total_out, sems,
 ):
     sides = received("gx", x_near_ref, x_far_ref)
     ends = received("gy", y_near_ref, y_far_ref)
@@ -328,6 +328,9 @@
         sums[place] = part * scale_of(plan, maps[place])
     if not plan.slots:
         total_out[...] = jnp.concatenate(sums, axis=0)
+        copy = pltpu.make_async_copy(total_out, total_hbm, sems.at[0])
+        copy.start()
+        copy.wait()
         return
 
     def picked(place, i, at):
@@ -348,19 +351,31 @@
         return out
 
     size = 4 * plan.slot_parts
+    rows = []
     for plane in range(plan.groups):
-        main = of_plane(plane, sums)
         beside = []
         for i in range(plan.half_x):
             beside.append((plan.low_row + i, of_plane(plane - 1, [k[i] for k in below])))
             beside.append((plan.high_row + i, of_plane(plane + 1, [k[i] for k in above])))
-        beside += [(at, jnp.zeros_like(main)) for at in range(plan.high_row + plan.half_x, size)]
-        for g in range(plan.owners):
+        blank = jnp.zeros((plan.owners, plan.p), F32)
+        beside += [(at, blank) for at in range(plan.high_row + plan.half_x, size)]
+        rows.append((of_plane(plane, sums), beside))
+    copies = []
+    for g in range(plan.owners):
+        for plane, (main, beside) in enumerate(rows):
             slot = g * plan.groups + plane
             for part in range(plan.owners // 4):
                 total_out[slot, part] = main[4 * part : 4 * part + 4]
             for row, values in beside:
                 total_out[slot, row // 4, pl.ds(row % 4, 1), :] = values[g : g + 1]
+        if g % 2:
+            some = pl.ds((g - 1) * plan.groups, 2 * plan.groups)
+            copies.append(
+                pltpu.make_async_copy(total_out.at[some], total_hbm.at[some], sems.at[g // 2])
+            )
+            copies[-1].start()
+    for copy in copies:
+        copy.wait()
 
 
 def owner_column(plan, owners, i, at):
@@ -379,9 +394,15 @@
             lane < planes - 2, pltpu.roll(values, planes - 2, 1), 0.0
         )
 
-    coarse_conc = jnp.zeros_like(mass_mean)
-    coarse_pot = jnp.zeros_like(pot_mean)
-    for _ in range(CSWEEP):
+    def step(mass_gap, pot_gap):
+        scale = relax_coarse / coarse_det
+        return (
+            scale * (mass_gap - 2.0 * coarse_flux * pot_gap),
+            scale * (pot_gap + (split_slope + 2.0 * coarse_bend) * mass_gap),
+        )
+
+    coarse_conc, coarse_pot = step(mass_mean, pot_mean)
+    for _ in range(CSWEEP - 1):
         mass_gap = mass_mean - (
             coarse_conc + coarse_flux * (2.0 * coarse_pot - neighbour_sum(coarse_pot))
         )
@@ -390,17 +411,13 @@
             - split_slope * coarse_conc
             + coarse_bend * (neighbour_sum(coarse_conc) - 2.0 * coarse_conc)
         )
-        coarse_conc = coarse_conc + (relax_coarse / coarse_det) * (
-            mass_gap - 2.0 * coarse_flux * pot_gap
-        )
-        coarse_pot = coarse_pot + (relax_coarse / coarse_det) * (
-            pot_gap + (split_slope + 2.0 * coarse_bend) * mass_gap
-        )
+        more_conc, more_pot = step(mass_gap, pot_gap)
+        coarse_conc, coarse_pot = coarse_conc + more_conc, coarse_pot + more_pot
     return coarse_conc, coarse_pot
 
 
 def beside_kernel(
-    plan, x_far_ref, x_near_ref, mob_ref, raw_ref, x_near_msg, x_far_msg, y_near_msg, y_far_msg,
+    plan, x_near_ref, x_far_ref, mob_ref, raw_ref, x_near_msg, x_far_msg, y_near_msg, y_far_msg,
     faces_out, diagonal_out, scale_out, ends_out,
 ):
     mobility = mob_ref[...]
@@ -457,10 +474,11 @@
 ):
     parts = []
     for part in range(plan.slot_parts):
-        mean = total_ref[0, part]
-        for slot in range(1, total_ref.shape[0]):
-            mean = mean + total_ref[slot, part]
-        parts.append(mean)
+        terms = [total_ref[slot, part] for slot in range(total_ref.shape[0])]
+        while len(terms) > 1:
+            pairs = [a + b for a, b in zip(terms[::2], terms[1::2])]
+            terms = pairs + terms[len(pairs) * 2 :]
+        parts.append(terms[0])
     solved = jnp.concatenate(
         coarse_solve(jnp.concatenate(parts, axis=0), plan.p), axis=1
     )
@@ -520,7 +538,7 @@
         copy.wait()
 
 
-def call(kernel, plan, outs, args, far=(), smem=(), scratch=(), out_far=False):
+def call(kernel, plan, outs, args, far=(), smem=(), scratch=(), out_far=()):
     def space(i):
         return pl.ANY if i in far else pltpu.SMEM if i in smem else pltpu.VMEM
 
@@ -528,7 +546,10 @@
         functools.partial(kernel, plan),
         out_shape=[jax.ShapeDtypeStruct(shape, F32) for shape in outs],
         in_specs=[pl.BlockSpec(memory_space=space(i)) for i in range(len(args))],
-        out_specs=[pl.BlockSpec(memory_space=pl.ANY if out_far else pltpu.VMEM)] * len(outs),
+        out_specs=[
+            pl.BlockSpec(memory_space=pl.ANY if i in out_far else pltpu.VMEM)
+            for i in range(len(outs))
+        ],
         scratch_shapes=list(scratch),
         compiler_params=pltpu.CompilerParams(vmem_limit_bytes=VMEM_LIMIT),
     )(*[
@@ -588,11 +609,9 @@
             pltpu.SemaphoreType.DMA((22,)),
         ),
     )
-    x_far = swap_far("gx", messages[1])
-    y_far = swap_far("gy", messages[3])
-    y_near = swap_near("gy", messages[2])
-    x_far, x_near, mask, kind = lax.optimization_barrier((x_far, messages[0], mask, kind))
-    x_near = swap_near("gx", x_near)
+    x_near, x_far = swap_near("gx", messages[0]), swap_far("gx", messages[1])
+    y_near, y_far = swap_near("gy", messages[2]), swap_far("gy", messages[3])
+    x_near, mask, kind = lax.optimization_barrier((x_near, mask, kind))
     mob, gather, spread, scale = call(
         local_kernel,
         plan,
@@ -600,21 +619,23 @@
         [mask, kind, table, owner_map],
         smem=(2,),
     )
-    slots = (plan.slots, plan.slot_parts, 4, plan.p)
+    slots = (plan.slots, plan.slot_parts, 4, plan.p) if plan.slots else (3 * plan.owners, plan.p)
     conc, pot, total, raw, near, far = call(
         first_kernel,
         plan,
         [
             block,
             block,
-            slots if plan.slots else (3 * plan.owners, plan.p),
+            slots,
             (4 * plan.x, plan.p),
             *[(2 * plan.y + 8, plan.p)] * 2,
         ],
         [
-            x_far, y_far, y_near, x_near,
+            x_near, x_far, y_near, y_far,
             conc, pot, mob, mass_source, pot_source, gather, scale, owner_map,
         ],
+        out_far=(2,),
+        scratch=(pltpu.VMEM(slots, F32), pltpu.SemaphoreType.DMA((plan.owners // 2,))),
     )
     total = gather_totals(plan, total, y_near, y_far)
     far = swap_far("gx", far)
@@ -623,7 +644,7 @@
         beside_kernel,
         plan,
         [(6, *block), block, block, (4 * plan.x, plan.p)],
-        [far, near, mob, raw, x_near, x_far, y_near, y_far],
+        [near, far, mob, raw, x_near, x_far, y_near, y_far],
     )
     return tuple(
         call(
@@ -631,7 +652,7 @@
             plan,
             [block, block],
             [conc, pot, mass_source, pot_source, faces, diagonal, scale, near, far, ends, spread, total],
-            out_far=True,
+            out_far=(0, 1),
             scratch=(
                 pltpu.VMEM(block, F32),
                 pltpu.VMEM(block, F32),

time: 34.2 us -> 30.9 us (0.904)
  starting transfers between devices: 21.7 us -> 16.2 us
  waiting for transfers between devices: 6.07 us -> 8.19 us
    ppermute x6, starting transfers between devices: 16.5 us -> 5.59 us  [swap_near(): return lax.ppermute(rows, axis, pairs + [(j, i) for i, j in pairs])]
    all_to_all x1, starting transfers between devices: 5.24 us -> 10.7 us  [gather_totals(): lax.all_to_all(total, ('gx', 'gy'), split_axis=0, concat_axis=0, tiled=True)]
    all_to_all x1, waiting for transfers between devices: 4.39 us -> 7.83 us  [gather_totals(): lax.all_to_all(total, ('gx', 'gy'), split_axis=0, concat_axis=0, tiled=True)]
    ppermute x6, waiting for transfers between devices: 1.68 us -> 0.36 us  [swap_near(): return lax.ppermute(rows, axis, pairs + [(j, i) for i, j in pairs])]
  transfers between devices with their start and end apart: 7 -> 7, of which waited for: 3 -> 2; matrix products, arithmetic and copies ran while one was open for 0% -> 0% of each run, Pallas kernels for 3% -> 4%
where the time goes in v7:
time: 30.9 us; the launch traced here: 30.6 us
  starting transfers between devices  16.2 us (52%)
  waiting for transfers between devices  8.19 us (27%)
  Pallas kernels  5.32 us (17%)
  between operations  0.84 us (3%)
    all_to_all x1, starting transfers between devices, gather_totals(): lax.all_to_all(total, ('gx', 'gy'), split_axis=0, concat_axis=0, tiled=True)  10.7 us
    all_to_all x1, waiting for transfers between devices, gather_totals(): lax.all_to_all(total, ('gx', 'gy'), split_axis=0, concat_axis=0, tiled=True)  7.83 us
    ppermute x6, starting transfers between devices, swap_near(): return lax.ppermute(rows, axis, pairs + [(j, i) for i, j in pairs])  5.59 us
    pallas_call x5, Pallas kernels, call(): pl.pallas_call(functools.partial(kernel, plan), out_shape=[jax.ShapeDtype...  5.32 us
  transfers between devices with their start and end apart: 7, of which 2 were waited for; matrix products, arithmetic and copies ran while one was open for 0% of the time, Pallas kernels for 4%

profile of v7, /device:TPU:0, one launch (start us, length us, event | category | flops | bytes accessed | tf_op | source)
XLA Modules:
  0.0 30.6 jit_solution(4525247539192216486)
XLA Ops:
  0.6 0.0 copy-start.5
  0.6 0.0 copy-start.4
  0.7 0.0 copy-start.2
  0.7 0.0 copy-start.3
  0.7 1.3 %shard_map.95 = (f32[192,128]{1,0:T(8,128)S(1)}, f32[192,128]{1,0:T(8,128)S(1)}, f32[40,128]{1,0:T(8,128)S(1)}, f32[40,128]{1,0:T(8,128)S(1)}) custom-call(f32[4,64,128]{2,1,0:T(8,128)} %conc_ref.1, f32[4,64,128]{2,1,0:T(8,128)} %pot_ref.1, s32[4,64,128]{2,1,0:T(8,128)} %mask_ref, s32[4,64,128]{2,1,0:T(8,128)} %class_ref, f32[4,64,128]{2,1,0:T(8,128)} %mass_ref.3, ...), custom_call_target="tpu_custom_call" | custom-call | tf_op jit(solution)/shard_map/pallas_call | solution.py:545
  1.9 0.0 copy-start.6
  2.0 0.5 %collective-permute-start = (f32[192,128]{1,0:T(8,128)S(1)}, f32[192,128]{1,0:T(8,128)S(1)}, u32[]{:S(2)}, u32[]{:S(2)}) collective-permute-start(f32[192,128]{1,0:T(8,128)S(1)} %get-tuple-element.23), channel_id=1, source_target_pairs={{0,4},{8,12},{16,20},{24,28},{4,0},{12,8},{20,16},{28,24},{1,5},{9... | collective-permute-start | bytes 294920 | tf_op jit(solution)/shard_map/ppermute | solution.py:563
  2.5 0.7 %collective-permute-start.1 = (f32[192,128]{1,0:T(8,128)S(1)}, f32[192,128]{1,0:T(8,128)S(1)}, u32[]{:S(2)}, u32[]{:S(2)}) collective-permute-start(f32[192,128]{1,0:T(8,128)S(1)} %get-tuple-element.25), channel_id=1, source_target_pairs={{4,8},{12,16},{20,24},{8,4},{16,12},{24,20},{5,9},{13,17},{21,25},... | collective-permute-start | bytes 294920 | tf_op jit(solution)/shard_map/ppermute | solution.py:563
  3.1 0.0 copy-start.7
  3.2 2.7 %collective-permute-start.2 = (f32[40,128]{1,0:T(8,128)S(1)}, f32[40,128]{1,0:T(8,128)S(1)}, u32[]{:S(2)}, u32[]{:S(2)}) collective-permute-start(f32[40,128]{1,0:T(8,128)S(1)} %get-tuple-element.26), channel_id=1, source_target_pairs={{0,1},{2,3},{1,0},{3,2},{4,5},{6,7},{5,4},{7,6},{8,9},{10,11},{9,8... | collective-permute-start | bytes 61448 | tf_op jit(solution)/shard_map/ppermute | solution.py:563
  5.8 0.0 copy-start
  5.8 0.0 copy-start.1
  5.8 0.8 %collective-permute-start.3 = (f32[40,128]{1,0:T(8,128)S(1)}, f32[40,128]{1,0:T(8,128)S(1)}, u32[]{:S(2)}, u32[]{:S(2)}) collective-permute-start(f32[40,128]{1,0:T(8,128)S(1)} %get-tuple-element.27), channel_id=1, source_target_pairs={{1,2},{2,1},{5,6},{6,5},{9,10},{10,9},{13,14},{14,13},{17,18},{18,... | collective-permute-start | bytes 61448 | tf_op jit(solution)/shard_map/ppermute | solution.py:563
  6.6 0.0 collective-permute-done.x_near_ref.x_near_msg
  6.6 0.0 copy-done.5
  6.6 0.0 copy-done.4
  6.6 0.0 copy-done.6
  6.6 0.0 copy-done.7
  6.7 1.0 %shard_map.96 = (f32[4,64,128]{2,1,0:T(8,128)S(1)}, f32[8,256]{1,0:T(8,128)S(1)}, f32[256,24]{1,0:T(8,128)S(1)}, f32[8,128]{1,0:T(8,128)S(1)}) custom-call(s32[4,64,128]{2,1,0:T(8,128)S(1)} %copy-done.4, s32[4,64,128]{2,1,0:T(8,128)S(1)} %copy-done.5, f32[8]{0:T(128)S(1)} %copy-done.7, s32[8,64]{1,0:T(8,128)S(1)} %copy-done.6), custom_call_target="tpu_custom_call" | custom-call | tf_op jit(solution)/shard_map/pallas_call | solution.py:545
  7.6 0.0 collective-permute-done.2.y_near_ref.y_near_msg
  7.6 0.0 collective-permute-done.3.y_far_ref.y_far_msg
  7.7 0.0 collective-permute-done.1.x_far_ref.x_far_msg
  7.7 0.0 copy-done.2
  7.7 0.0 copy-done.3
  7.7 0.0 copy-done
  7.7 0.0 copy-done.1
  7.7 1.6 %shard_map.97 = (f32[4,64,128]{2,1,0:T(8,128)S(1)}, f32[4,64,128]{2,1,0:T(8,128)S(1)}, f32[32,3,4,128]{3,2,1,0:T(4,128)}, f32[16,128]{1,0:T(8,128)S(1)}, f32[136,128]{1,0:T(8,128)S(1)}, /*index=5*/f32[136,128]{1,0:T(8,128)S(1)}) custom-call(f32[192,128]{1,0:T(8,128)S(1)} %collective-permute-done.x_near_ref.x_near_msg, ...), custom_call_target="tpu_custom_call" | custom-call | tf_op jit(solution)/shard_map/pallas_call | solution.py:545
  9.3 10.7 %all-to-all-start = ((f32[32,3,4,128]{3,2,1,0:T(4,128)}), f32[32,3,4,128]{3,2,1,0:T(4,128)S(1)}, u32[]{:S(2)}, u32[]{:S(2)}) async-start(f32[32,3,4,128]{3,2,1,0:T(4,128)} %get-tuple-element.43), calls=%async_computation | async-start | bytes 393216 | tf_op jit(solution)/shard_map/all_to_all | solution.py:572
  19.9 0.3 %collective-permute-start.4 = (f32[136,128]{1,0:T(8,128)S(1)}, f32[136,128]{1,0:T(8,128)S(1)}, u32[]{:S(2)}, u32[]{:S(2)}) collective-permute-start(f32[136,128]{1,0:T(8,128)S(1)} %get-tuple-element.35), channel_id=1, source_target_pairs={{0,4},{8,12},{16,20},{24,28},{4,0},{12,8},{20,16},{28,24},{1,5},{9... | collective-permute-start | bytes 208904 | tf_op jit(solution)/shard_map/ppermute | solution.py:563
  20.3 0.7 %collective-permute-start.5 = (f32[136,128]{1,0:T(8,128)S(1)}, f32[136,128]{1,0:T(8,128)S(1)}, u32[]{:S(2)}, u32[]{:S(2)}) collective-permute-start(f32[136,128]{1,0:T(8,128)S(1)} %get-tuple-element.36), channel_id=1, source_target_pairs={{4,8},{12,16},{20,24},{8,4},{16,12},{24,20},{5,9},{13,17},{21,25},... | collective-permute-start | bytes 208904 | tf_op jit(solution)/shard_map/ppermute | solution.py:563
  20.9 0.3 %collective-permute-done.4.x_near_ref = f32[136,128]{1,0:T(8,128)S(1)} collective-permute-done((f32[136,128]{1,0:T(8,128)S(1)}, f32[136,128]{1,0:T(8,128)S(1)}, u32[]{:S(2)}, u32[]{:S(2)}) %collective-permute-start.4) | collective-permute-done | bytes 69664 | tf_op jit(solution)/shard_map/ppermute | solution.py:563
  21.3 0.0 collective-permute-done.5.x_far_ref
  21.3 0.2 shard_map.98
  21.4 7.8 %all-to-all-done.total_ref = f32[32,3,4,128]{3,2,1,0:T(4,128)S(1)} async-done(((f32[32,3,4,128]{3,2,1,0:T(4,128)}), f32[32,3,4,128]{3,2,1,0:T(4,128)S(1)}, u32[]{:S(2)}, u32[]{:S(2)}) %all-to-all-start) | async-done | bytes 196640 | tf_op jit(solution)/shard_map/all_to_all | solution.py:572
  29.3 1.3 %shard_map.99 = (f32[4,64,128]{2,1,0:T(8,128)}, f32[4,64,128]{2,1,0:T(8,128)}) custom-call(f32[4,64,128]{2,1,0:T(8,128)S(1)} %get-tuple-element.33.conc_ref, f32[4,64,128]{2,1,0:T(8,128)S(1)} %get-tuple-element.34.pot_ref, f32[4,64,128]{2,1,0:T(8,128)S(1)} %copy-done, f32[4,64,128]{2,1,0:T(8,128)S(1)} %copy-done.1, ...), custom_call_target="tpu_custom_call" | custom-call | tf_op jit(solution)/shard_map/pallas_call | solution.py:545
Async XLA Ops:
  0.6 6.0 %copy-start.5 = (s32[4,64,128]{2,1,0:T(8,128)S(1)}, s32[4,64,128]{2,1,0:T(8,128)}, u32[]{:S(2)}) copy-start(s32[4,64,128]{2,1,0:T(8,128)} %class_ref) | copy-start | bytes 393220
  0.6 6.0 %copy-start.4 = (s32[4,64,128]{2,1,0:T(8,128)S(1)}, s32[4,64,128]{2,1,0:T(8,128)}, u32[]{:S(2)}) copy-start(s32[4,64,128]{2,1,0:T(8,128)} %mask_ref) | copy-start | bytes 393220
  0.7 7.0 %copy-start.2 = (f32[4,64,128]{2,1,0:T(8,128)S(1)}, f32[4,64,128]{2,1,0:T(8,128)}, u32[]{:S(2)}) copy-start(f32[4,64,128]{2,1,0:T(8,128)} %conc_ref.1) | copy-start | bytes 393220
  0.7 7.0 %copy-start.3 = (f32[4,64,128]{2,1,0:T(8,128)S(1)}, f32[4,64,128]{2,1,0:T(8,128)}, u32[]{:S(2)}) copy-start(f32[4,64,128]{2,1,0:T(8,128)} %pot_ref.1) | copy-start | bytes 393220
  1.9 4.7 %copy-start.6 = (s32[8,64]{1,0:T(8,128)S(1)}, s32[8,64]{1,0:T(8,128)}, u32[]{:S(2)}) copy-start(s32[8,64]{1,0:T(8,128)} %owner_ref.3) | copy-start | bytes 6148
  2.0 4.7 %collective-permute-start = (f32[192,128]{1,0:T(8,128)S(1)}, f32[192,128]{1,0:T(8,128)S(1)}, u32[]{:S(2)}, u32[]{:S(2)}) collective-permute-start(f32[192,128]{1,0:T(8,128)S(1)} %get-tuple-element.23), channel_id=1, source_target_pairs={{0,4},{8,12},{16,20},{24,28},{4,0},{12,8},{20,16},{28,24},{1,5},{9... | collective-permute-start | bytes 294920 | tf_op jit(solution)/shard_map/ppermute | solution.py:563
  2.5 5.2 %collective-permute-start.1 = (f32[192,128]{1,0:T(8,128)S(1)}, f32[192,128]{1,0:T(8,128)S(1)}, u32[]{:S(2)}, u32[]{:S(2)}) collective-permute-start(f32[192,128]{1,0:T(8,128)S(1)} %get-tuple-element.25), channel_id=1, source_target_pairs={{4,8},{12,16},{20,24},{8,4},{16,12},{24,20},{5,9},{13,17},{21,25},... | collective-permute-start | bytes 294920 | tf_op jit(solution)/shard_map/ppermute | solution.py:563
  3.1 3.5 %copy-start.7 = (f32[8]{0:T(128)S(1)}, f32[8]{0:T(128)}, u32[]{:S(2)}) copy-start(f32[8]{0:T(128)} %table_ref.1) | copy-start | bytes 100
  3.2 4.5 %collective-permute-start.2 = (f32[40,128]{1,0:T(8,128)S(1)}, f32[40,128]{1,0:T(8,128)S(1)}, u32[]{:S(2)}, u32[]{:S(2)}) collective-permute-start(f32[40,128]{1,0:T(8,128)S(1)} %get-tuple-element.26), channel_id=1, source_target_pairs={{0,1},{2,3},{1,0},{3,2},{4,5},{6,7},{5,4},{7,6},{8,9},{10,11},{9,8... | collective-permute-start | bytes 61448 | tf_op jit(solution)/shard_map/ppermute | solution.py:563
  5.8 1.9 %copy-start = (f32[4,64,128]{2,1,0:T(8,128)S(1)}, f32[4,64,128]{2,1,0:T(8,128)}, u32[]{:S(2)}) copy-start(f32[4,64,128]{2,1,0:T(8,128)} %mass_ref.3) | copy-start | bytes 393220
  5.8 1.9 %copy-start.1 = (f32[4,64,128]{2,1,0:T(8,128)S(1)}, f32[4,64,128]{2,1,0:T(8,128)}, u32[]{:S(2)}) copy-start(f32[4,64,128]{2,1,0:T(8,128)} %pots_ref.3) | copy-start | bytes 393220
  5.8 1.8 %collective-permute-start.3 = (f32[40,128]{1,0:T(8,128)S(1)}, f32[40,128]{1,0:T(8,128)S(1)}, u32[]{:S(2)}, u32[]{:S(2)}) collective-permute-start(f32[40,128]{1,0:T(8,128)S(1)} %get-tuple-element.27), channel_id=1, source_target_pairs={{1,2},{2,1},{5,6},{6,5},{9,10},{10,9},{13,14},{14,13},{17,18},{18,... | collective-permute-start | bytes 61448 | tf_op jit(solution)/shard_map/ppermute | solution.py:563
  9.3 20.0 %all-to-all-start = ((f32[32,3,4,128]{3,2,1,0:T(4,128)}), f32[32,3,4,128]{3,2,1,0:T(4,128)S(1)}, u32[]{:S(2)}, u32[]{:S(2)}) async-start(f32[32,3,4,128]{3,2,1,0:T(4,128)} %get-tuple-element.43), calls=%async_computation | async-start | bytes 393216 | tf_op jit(solution)/shard_map/all_to_all | solution.py:572
  19.9 1.3 %collective-permute-start.4 = (f32[136,128]{1,0:T(8,128)S(1)}, f32[136,128]{1,0:T(8,128)S(1)}, u32[]{:S(2)}, u32[]{:S(2)}) collective-permute-start(f32[136,128]{1,0:T(8,128)S(1)} %get-tuple-element.35), channel_id=1, source_target_pairs={{0,4},{8,12},{16,20},{24,28},{4,0},{12,8},{20,16},{28,24},{1,5},{9... | collective-permute-start | bytes 208904 | tf_op jit(solution)/shard_map/ppermute | solution.py:563
  20.3 1.0 %collective-permute-start.5 = (f32[136,128]{1,0:T(8,128)S(1)}, f32[136,128]{1,0:T(8,128)S(1)}, u32[]{:S(2)}, u32[]{:S(2)}) collective-permute-start(f32[136,128]{1,0:T(8,128)S(1)} %get-tuple-element.36), channel_id=1, source_target_pairs={{4,8},{12,16},{20,24},{8,4},{16,12},{24,20},{5,9},{13,17},{21,25},... | collective-permute-start | bytes 208904 | tf_op jit(solution)/shard_map/ppermute | solution.py:563

commit v8 on v7

--- a/solution.py
+++ b/solution.py
@@ -118,6 +118,7 @@
         self.columns = self.half_x * self.half_y
         self.map_row = round_up(8 * self.x, 8)
         self.y_rows = self.map_row + owners
+        self.y_near_rows = max(self.y_rows, 3 * self.y + 8)
         self.cells = self.x * self.y
         self.rows = (self.half_x + 2) * self.y
         self.low_row = owners
@@ -229,8 +230,8 @@
             y_near_ref[pl.ds(which * plan.x + x, 1), :] = jnp.where(up, high, low)
             y_far_ref[pl.ds(which * plan.x + x, 1), :] = jnp.where(up, low, high)
     used = 8 * plan.x
-    for ref in (y_near_ref, y_far_ref):
-        ref[pl.ds(used, plan.y_rows - used), :] = jnp.zeros((plan.y_rows - used, plan.p), F32)
+    for ref, rows in ((y_near_ref, plan.y_near_rows), (y_far_ref, plan.y_rows)):
+        ref[pl.ds(used, rows - used), :] = jnp.zeros((rows - used, plan.p), F32)
         ref[pl.ds(plan.map_row, plan.owners), pl.ds(0, plan.columns)] = owner_ref[...].astype(F32)
 
 
@@ -244,7 +245,7 @@
 
 
 def first_kernel(
-    plan, x_near_ref, x_far_ref, y_near_ref, y_far_ref,
+    plan, x_far_ref, x_near_ref, y_far_ref, y_near_ref,
     conc_ref, pot_ref, mob_ref, mass_ref, pots_ref, gather_ref, scale_ref, owner_ref,
     conc_out, pot_out, total_hbm, raw_out, x_near_out, x_far_out, total_out, sems,
 ):
@@ -579,9 +580,10 @@
     g, h = lax.axis_index("gx"), lax.axis_index("gy")
     rows = [lax.dynamic_index_in_dim(own, h + 1, 0, False)]
     up = lax.rem(h, 2) == 0
+    near = y_near[: y_far.shape[0]]
     for place, at, msg in (
-        (h, plan.half_y - 1, jnp.where(up, y_far, y_near)),
-        (h + 2, 0, jnp.where(up, y_near, y_far)),
+        (h, plan.half_y - 1, jnp.where(up, y_far, near)),
+        (h + 2, 0, jnp.where(up, near, y_far)),
     ):
         ident = lax.dynamic_index_in_dim(msg, plan.map_row + g, 0, False).astype(jnp.int32)
         ident = jnp.stack([ident[i * plan.half_y + at] for i in range(plan.half_x)])
@@ -598,7 +600,7 @@
     messages = call(
         prepare_kernel,
         plan,
-        [*[(3 * plan.y, plan.p)] * 2, *[(plan.y_rows, plan.p)] * 2],
+        [*[(3 * plan.y, plan.p)] * 2, (plan.y_near_rows, plan.p), (plan.y_rows, plan.p)],
         [*fields, owner_map, table],
         far=range(8),
         scratch=(
@@ -611,7 +613,7 @@
     )
     x_near, x_far = swap_near("gx", messages[0]), swap_far("gx", messages[1])
     y_near, y_far = swap_near("gy", messages[2]), swap_far("gy", messages[3])
-    x_near, mask, kind = lax.optimization_barrier((x_near, mask, kind))
+    y_near, mask, kind = lax.optimization_barrier((y_near, mask, kind))
     mob, gather, spread, scale = call(
         local_kernel,
         plan,
@@ -631,7 +633,7 @@
             *[(2 * plan.y + 8, plan.p)] * 2,
         ],
         [
-            x_near, x_far, y_near, y_far,
+            x_far, x_near, y_far, y_near,
             conc, pot, mob, mass_source, pot_source, gather, scale, owner_map,
         ],
         out_far=(2,),

time: 30.9 us -> 30.9 us (level)
    ppermute x6, starting transfers between devices: 5.59 us -> 8.41 us  [swap_near(): return lax.ppermute(rows, axis, pairs + [(j, i) for i, j in pairs])]
    all_to_all x1, starting transfers between devices: 10.7 us -> 7.87 us  [gather_totals(): lax.all_to_all(total, ('gx', 'gy'), split_axis=0, concat_axis=0, tiled=True)]
where the time goes in v8:
time: 30.9 us; the launch traced here: 30.7 us
  starting transfers between devices  16.3 us (53%)
  waiting for transfers between devices  8.19 us (27%)
  Pallas kernels  5.35 us (17%)
  between operations  0.84 us (3%)
    ppermute x6, starting transfers between devices, swap_near(): return lax.ppermute(rows, axis, pairs + [(j, i) for i, j in pairs])  8.41 us
    all_to_all x1, starting transfers between devices, gather_totals(): lax.all_to_all(total, ('gx', 'gy'), split_axis=0, concat_axis=0, tiled=True)  7.87 us
    all_to_all x1, waiting for transfers between devices, gather_totals(): lax.all_to_all(total, ('gx', 'gy'), split_axis=0, concat_axis=0, tiled=True)  7.83 us
    pallas_call x5, Pallas kernels, call(): pl.pallas_call(functools.partial(kernel, plan), out_shape=[jax.ShapeDtype...  5.35 us
  transfers between devices with their start and end apart: 7, of which 2 were waited for; matrix products, arithmetic and copies ran while one was open for 0% of the time, Pallas kernels for 4%

profile of v8, /device:TPU:0, one launch (start us, length us, event | category | flops | bytes accessed | tf_op | source)
XLA Modules:
  0.0 30.7 jit_solution(5854475127396426435)
XLA Ops:
  0.6 0.0 copy-start.5
  0.6 0.0 copy-start.4
  0.7 0.0 copy-start.2
  0.7 0.0 copy-start.3
  0.7 1.3 %shard_map.95 = (f32[192,128]{1,0:T(8,128)S(1)}, f32[192,128]{1,0:T(8,128)S(1)}, f32[200,128]{1,0:T(8,128)S(1)}, f32[40,128]{1,0:T(8,128)S(1)}) custom-call(f32[4,64,128]{2,1,0:T(8,128)} %conc_ref.1, f32[4,64,128]{2,1,0:T(8,128)} %pot_ref.1, s32[4,64,128]{2,1,0:T(8,128)} %mask_ref, s32[4,64,128]{2,1,0:T(8,128)} %class_ref, f32[4,64,128]{2,1,0:T(8,128)} %mass_ref.3, ...), custom_call_target="tpu_custom_call" | custom-call | tf_op jit(solution)/shard_map/pallas_call | solution.py:546
  1.9 0.0 copy-start.6
  2.0 3.1 %collective-permute-start.3 = (f32[200,128]{1,0:T(8,128)S(1)}, f32[200,128]{1,0:T(8,128)S(1)}, u32[]{:S(2)}, u32[]{:S(2)}) collective-permute-start(f32[200,128]{1,0:T(8,128)S(1)} %get-tuple-element.26), channel_id=1, source_target_pairs={{0,1},{2,3},{1,0},{3,2},{4,5},{6,7},{5,4},{7,6},{8,9},{10,11},{9,8... | collective-permute-start | bytes 307208 | tf_op jit(solution)/shard_map/ppermute | solution.py:564
  5.0 0.7 %collective-permute-start = (f32[192,128]{1,0:T(8,128)S(1)}, f32[192,128]{1,0:T(8,128)S(1)}, u32[]{:S(2)}, u32[]{:S(2)}) collective-permute-start(f32[192,128]{1,0:T(8,128)S(1)} %get-tuple-element.23), channel_id=1, source_target_pairs={{4,8},{12,16},{20,24},{8,4},{16,12},{24,20},{5,9},{13,17},{21,25},... | collective-permute-start | bytes 294920 | tf_op jit(solution)/shard_map/ppermute | solution.py:564
  5.7 0.0 copy-start.7
  5.7 2.9 %collective-permute-start.1 = (f32[192,128]{1,0:T(8,128)S(1)}, f32[192,128]{1,0:T(8,128)S(1)}, u32[]{:S(2)}, u32[]{:S(2)}) collective-permute-start(f32[192,128]{1,0:T(8,128)S(1)} %get-tuple-element.24), channel_id=1, source_target_pairs={{0,4},{8,12},{16,20},{24,28},{4,0},{12,8},{20,16},{28,24},{1,5},{9... | collective-permute-start | bytes 294920 | tf_op jit(solution)/shard_map/ppermute | solution.py:564
  8.6 0.0 copy-start
  8.6 0.0 copy-start.1
  8.6 0.8 %collective-permute-start.2 = (f32[40,128]{1,0:T(8,128)S(1)}, f32[40,128]{1,0:T(8,128)S(1)}, u32[]{:S(2)}, u32[]{:S(2)}) collective-permute-start(f32[40,128]{1,0:T(8,128)S(1)} %get-tuple-element.25), channel_id=1, source_target_pairs={{1,2},{2,1},{5,6},{6,5},{9,10},{10,9},{13,14},{14,13},{17,18},{18,... | collective-permute-start | bytes 61448 | tf_op jit(solution)/shard_map/ppermute | solution.py:564
  9.4 0.0 collective-permute-done.3.y_near_ref.y_near_msg
  9.4 0.0 copy-done.5
  9.5 0.0 copy-done.4
  9.5 0.0 copy-done.6
  9.5 0.0 copy-done.7
  9.5 1.0 %shard_map.96 = (f32[4,64,128]{2,1,0:T(8,128)S(1)}, f32[8,256]{1,0:T(8,128)S(1)}, f32[256,24]{1,0:T(8,128)S(1)}, f32[8,128]{1,0:T(8,128)S(1)}) custom-call(s32[4,64,128]{2,1,0:T(8,128)S(1)} %copy-done.4, s32[4,64,128]{2,1,0:T(8,128)S(1)} %copy-done.5, f32[8]{0:T(128)S(1)} %copy-done.7, s32[8,64]{1,0:T(8,128)S(1)} %copy-done.6), custom_call_target="tpu_custom_call" | custom-call | tf_op jit(solution)/shard_map/pallas_call | solution.py:546
  10.5 0.0 collective-permute-done.2.y_far_ref.y_far_msg
  10.5 0.0 collective-permute-done.x_far_ref.x_far_msg
  10.5 0.0 collective-permute-done.1.x_near_ref.x_near_msg
  10.5 0.0 copy-done.2
  10.5 0.0 copy-done.3
  10.5 0.0 copy-done
  10.5 0.0 copy-done.1
  10.5 1.6 %shard_map.97 = (f32[4,64,128]{2,1,0:T(8,128)S(1)}, f32[4,64,128]{2,1,0:T(8,128)S(1)}, f32[32,3,4,128]{3,2,1,0:T(4,128)}, f32[16,128]{1,0:T(8,128)S(1)}, f32[136,128]{1,0:T(8,128)S(1)}, /*index=5*/f32[136,128]{1,0:T(8,128)S(1)}) custom-call(f32[192,128]{1,0:T(8,128)S(1)} %collective-permute-done.x_far_ref.x_far_msg, ...), custom_call_target="tpu_custom_call" | custom-call | tf_op jit(solution)/shard_map/pallas_call | solution.py:546
  12.1 7.9 %all-to-all-start = ((f32[32,3,4,128]{3,2,1,0:T(4,128)}), f32[32,3,4,128]{3,2,1,0:T(4,128)S(1)}, u32[]{:S(2)}, u32[]{:S(2)}) async-start(f32[32,3,4,128]{3,2,1,0:T(4,128)} %get-tuple-element.43), calls=%async_computation | async-start | bytes 393216 | tf_op jit(solution)/shard_map/all_to_all | solution.py:573
  20.0 0.3 %collective-permute-start.4 = (f32[136,128]{1,0:T(8,128)S(1)}, f32[136,128]{1,0:T(8,128)S(1)}, u32[]{:S(2)}, u32[]{:S(2)}) collective-permute-start(f32[136,128]{1,0:T(8,128)S(1)} %get-tuple-element.35), channel_id=1, source_target_pairs={{0,4},{8,12},{16,20},{24,28},{4,0},{12,8},{20,16},{28,24},{1,5},{9... | collective-permute-start | bytes 208904 | tf_op jit(solution)/shard_map/ppermute | solution.py:564
  20.3 0.7 %collective-permute-start.5 = (f32[136,128]{1,0:T(8,128)S(1)}, f32[136,128]{1,0:T(8,128)S(1)}, u32[]{:S(2)}, u32[]{:S(2)}) collective-permute-start(f32[136,128]{1,0:T(8,128)S(1)} %get-tuple-element.36), channel_id=1, source_target_pairs={{4,8},{12,16},{20,24},{8,4},{16,12},{24,20},{5,9},{13,17},{21,25},... | collective-permute-start | bytes 208904 | tf_op jit(solution)/shard_map/ppermute | solution.py:564
  21.0 0.3 %collective-permute-done.4.x_near_ref = f32[136,128]{1,0:T(8,128)S(1)} collective-permute-done((f32[136,128]{1,0:T(8,128)S(1)}, f32[136,128]{1,0:T(8,128)S(1)}, u32[]{:S(2)}, u32[]{:S(2)}) %collective-permute-start.4) | collective-permute-done | bytes 69664 | tf_op jit(solution)/shard_map/ppermute | solution.py:564
  21.3 0.0 collective-permute-done.5.x_far_ref
  21.3 0.2 shard_map.98
  21.5 7.8 %all-to-all-done.total_ref = f32[32,3,4,128]{3,2,1,0:T(4,128)S(1)} async-done(((f32[32,3,4,128]{3,2,1,0:T(4,128)}), f32[32,3,4,128]{3,2,1,0:T(4,128)S(1)}, u32[]{:S(2)}, u32[]{:S(2)}) %all-to-all-start) | async-done | bytes 196640 | tf_op jit(solution)/shard_map/all_to_all | solution.py:573
  29.3 1.4 %shard_map.99 = (f32[4,64,128]{2,1,0:T(8,128)}, f32[4,64,128]{2,1,0:T(8,128)}) custom-call(f32[4,64,128]{2,1,0:T(8,128)S(1)} %get-tuple-element.33.conc_ref, f32[4,64,128]{2,1,0:T(8,128)S(1)} %get-tuple-element.34.pot_ref, f32[4,64,128]{2,1,0:T(8,128)S(1)} %copy-done, f32[4,64,128]{2,1,0:T(8,128)S(1)} %copy-done.1, ...), custom_call_target="tpu_custom_call" | custom-call | tf_op jit(solution)/shard_map/pallas_call | solution.py:546
Async XLA Ops:
  0.6 8.8 %copy-start.5 = (s32[4,64,128]{2,1,0:T(8,128)S(1)}, s32[4,64,128]{2,1,0:T(8,128)}, u32[]{:S(2)}) copy-start(s32[4,64,128]{2,1,0:T(8,128)} %class_ref) | copy-start | bytes 393220
  0.6 8.8 %copy-start.4 = (s32[4,64,128]{2,1,0:T(8,128)S(1)}, s32[4,64,128]{2,1,0:T(8,128)}, u32[]{:S(2)}) copy-start(s32[4,64,128]{2,1,0:T(8,128)} %mask_ref) | copy-start | bytes 393220
  0.7 9.8 %copy-start.2 = (f32[4,64,128]{2,1,0:T(8,128)S(1)}, f32[4,64,128]{2,1,0:T(8,128)}, u32[]{:S(2)}) copy-start(f32[4,64,128]{2,1,0:T(8,128)} %conc_ref.1) | copy-start | bytes 393220
  0.7 9.8 %copy-start.3 = (f32[4,64,128]{2,1,0:T(8,128)S(1)}, f32[4,64,128]{2,1,0:T(8,128)}, u32[]{:S(2)}) copy-start(f32[4,64,128]{2,1,0:T(8,128)} %pot_ref.1) | copy-start | bytes 393220
  1.9 7.5 %copy-start.6 = (s32[8,64]{1,0:T(8,128)S(1)}, s32[8,64]{1,0:T(8,128)}, u32[]{:S(2)}) copy-start(s32[8,64]{1,0:T(8,128)} %owner_ref.3) | copy-start | bytes 6148
  2.0 7.5 %collective-permute-start.3 = (f32[200,128]{1,0:T(8,128)S(1)}, f32[200,128]{1,0:T(8,128)S(1)}, u32[]{:S(2)}, u32[]{:S(2)}) collective-permute-start(f32[200,128]{1,0:T(8,128)S(1)} %get-tuple-element.26), channel_id=1, source_target_pairs={{0,1},{2,3},{1,0},{3,2},{4,5},{6,7},{5,4},{7,6},{8,9},{10,11},{9,8... | collective-permute-start | bytes 307208 | tf_op jit(solution)/shard_map/ppermute | solution.py:564
  5.0 5.4 %collective-permute-start = (f32[192,128]{1,0:T(8,128)S(1)}, f32[192,128]{1,0:T(8,128)S(1)}, u32[]{:S(2)}, u32[]{:S(2)}) collective-permute-start(f32[192,128]{1,0:T(8,128)S(1)} %get-tuple-element.23), channel_id=1, source_target_pairs={{4,8},{12,16},{20,24},{8,4},{16,12},{24,20},{5,9},{13,17},{21,25},... | collective-permute-start | bytes 294920 | tf_op jit(solution)/shard_map/ppermute | solution.py:564
  5.7 3.8 %copy-start.7 = (f32[8]{0:T(128)S(1)}, f32[8]{0:T(128)}, u32[]{:S(2)}) copy-start(f32[8]{0:T(128)} %table_ref.1) | copy-start | bytes 100
  5.7 4.8 %collective-permute-start.1 = (f32[192,128]{1,0:T(8,128)S(1)}, f32[192,128]{1,0:T(8,128)S(1)}, u32[]{:S(2)}, u32[]{:S(2)}) collective-permute-start(f32[192,128]{1,0:T(8,128)S(1)} %get-tuple-element.24), channel_id=1, source_target_pairs={{0,4},{8,12},{16,20},{24,28},{4,0},{12,8},{20,16},{28,24},{1,5},{9... | collective-permute-start | bytes 294920 | tf_op jit(solution)/shard_map/ppermute | solution.py:564
  8.6 1.9 %copy-start = (f32[4,64,128]{2,1,0:T(8,128)S(1)}, f32[4,64,128]{2,1,0:T(8,128)}, u32[]{:S(2)}) copy-start(f32[4,64,128]{2,1,0:T(8,128)} %mass_ref.3) | copy-start | bytes 393220
  8.6 1.9 %copy-start.1 = (f32[4,64,128]{2,1,0:T(8,128)S(1)}, f32[4,64,128]{2,1,0:T(8,128)}, u32[]{:S(2)}) copy-start(f32[4,64,128]{2,1,0:T(8,128)} %pots_ref.3) | copy-start | bytes 393220
  8.6 1.8 %collective-permute-start.2 = (f32[40,128]{1,0:T(8,128)S(1)}, f32[40,128]{1,0:T(8,128)S(1)}, u32[]{:S(2)}, u32[]{:S(2)}) collective-permute-start(f32[40,128]{1,0:T(8,128)S(1)} %get-tuple-element.25), channel_id=1, source_target_pairs={{1,2},{2,1},{5,6},{6,5},{9,10},{10,9},{13,14},{14,13},{17,18},{18,... | collective-permute-start | bytes 61448 | tf_op jit(solution)/shard_map/ppermute | solution.py:564
  12.1 17.2 %all-to-all-start = ((f32[32,3,4,128]{3,2,1,0:T(4,128)}), f32[32,3,4,128]{3,2,1,0:T(4,128)S(1)}, u32[]{:S(2)}, u32[]{:S(2)}) async-start(f32[32,3,4,128]{3,2,1,0:T(4,128)} %get-tuple-element.43), calls=%async_computation | async-start | bytes 393216 | tf_op jit(solution)/shard_map/all_to_all | solution.py:573
  20.0 1.3 %collective-permute-start.4 = (f32[136,128]{1,0:T(8,128)S(1)}, f32[136,128]{1,0:T(8,128)S(1)}, u32[]{:S(2)}, u32[]{:S(2)}) collective-permute-start(f32[136,128]{1,0:T(8,128)S(1)} %get-tuple-element.35), channel_id=1, source_target_pairs={{0,4},{8,12},{16,20},{24,28},{4,0},{12,8},{20,16},{28,24},{1,5},{9... | collective-permute-start | bytes 208904 | tf_op jit(solution)/shard_map/ppermute | solution.py:564
  20.3 1.0 %collective-permute-start.5 = (f32[136,128]{1,0:T(8,128)S(1)}, f32[136,128]{1,0:T(8,128)S(1)}, u32[]{:S(2)}, u32[]{:S(2)}) collective-permute-start(f32[136,128]{1,0:T(8,128)S(1)} %get-tuple-element.36), channel_id=1, source_target_pairs={{4,8},{12,16},{20,24},{8,4},{16,12},{24,20},{5,9},{13,17},{21,25},... | collective-permute-start | bytes 208904 | tf_op jit(solution)/shard_map/ppermute | solution.py:564

commit v9 on v8

--- a/solution.py
+++ b/solution.py
@@ -118,7 +118,7 @@
         self.columns = self.half_x * self.half_y
         self.map_row = round_up(8 * self.x, 8)
         self.y_rows = self.map_row + owners
-        self.y_near_rows = max(self.y_rows, 3 * self.y + 8)
+        self.y_far_rows = max(self.y_rows, 3 * self.y + 8)
         self.cells = self.x * self.y
         self.rows = (self.half_x + 2) * self.y
         self.low_row = owners
@@ -230,7 +230,7 @@
             y_near_ref[pl.ds(which * plan.x + x, 1), :] = jnp.where(up, high, low)
             y_far_ref[pl.ds(which * plan.x + x, 1), :] = jnp.where(up, low, high)
     used = 8 * plan.x
-    for ref, rows in ((y_near_ref, plan.y_near_rows), (y_far_ref, plan.y_rows)):
+    for ref, rows in ((y_near_ref, plan.y_rows), (y_far_ref, plan.y_far_rows)):
         ref[pl.ds(used, rows - used), :] = jnp.zeros((rows - used, plan.p), F32)
         ref[pl.ds(plan.map_row, plan.owners), pl.ds(0, plan.columns)] = owner_ref[...].astype(F32)
 
@@ -580,10 +580,10 @@
     g, h = lax.axis_index("gx"), lax.axis_index("gy")
     rows = [lax.dynamic_index_in_dim(own, h + 1, 0, False)]
     up = lax.rem(h, 2) == 0
-    near = y_near[: y_far.shape[0]]
+    far = y_far[: y_near.shape[0]]
     for place, at, msg in (
-        (h, plan.half_y - 1, jnp.where(up, y_far, near)),
-        (h + 2, 0, jnp.where(up, near, y_far)),
+        (h, plan.half_y - 1, jnp.where(up, far, y_near)),
+        (h + 2, 0, jnp.where(up, y_near, far)),
     ):
         ident = lax.dynamic_index_in_dim(msg, plan.map_row + g, 0, False).astype(jnp.int32)
         ident = jnp.stack([ident[i * plan.half_y + at] for i in range(plan.half_x)])
@@ -600,7 +600,7 @@
     messages = call(
         prepare_kernel,
         plan,
-        [*[(3 * plan.y, plan.p)] * 2, (plan.y_near_rows, plan.p), (plan.y_rows, plan.p)],
+        [*[(3 * plan.y, plan.p)] * 2, (plan.y_rows, plan.p), (plan.y_far_rows, plan.p)],
         [*fields, owner_map, table],
         far=range(8),
         scratch=(
@@ -613,7 +613,7 @@
     )
     x_near, x_far = swap_near("gx", messages[0]), swap_far("gx", messages[1])
     y_near, y_far = swap_near("gy", messages[2]), swap_far("gy", messages[3])
-    y_near, mask, kind = lax.optimization_barrier((y_near, mask, kind))
+    y_far, mask, kind = lax.optimization_barrier((y_far, mask, kind))
     mob, gather, spread, scale = call(
         local_kernel,
         plan,

time: 30.9 us -> 30 us (0.971)
  starting transfers between devices: 16.3 us -> 14.6 us
  waiting for transfers between devices: 8.19 us -> 8.94 us
    all_to_all x1, starting transfers between devices: 7.87 us -> 3.54 us  [gather_totals(): lax.all_to_all(total, ('gx', 'gy'), split_axis=0, concat_axis=0, tiled=True)]
    ppermute x6, starting transfers between devices: 8.41 us -> 11.1 us  [swap_near(): return lax.ppermute(rows, axis, pairs + [(j, i) for i, j in pairs])]
    ppermute x6, waiting for transfers between devices: 0.36 us -> 1.12 us  [swap_near(): return lax.ppermute(rows, axis, pairs + [(j, i) for i, j in pairs])]
  transfers between devices with their start and end apart: 7 -> 7, of which waited for: 2 -> 3; matrix products, arithmetic and copies ran while one was open for 0% -> 0% of each run, Pallas kernels for 4% -> 4%
where the time goes in v9:
time: 30 us; the launch traced here: 29.7 us
  starting transfers between devices  14.6 us (49%)
  waiting for transfers between devices  8.94 us (30%)
  Pallas kernels  5.35 us (18%)
  between operations  0.79 us (3%)
    ppermute x6, starting transfers between devices, swap_near(): return lax.ppermute(rows, axis, pairs + [(j, i) for i, j in pairs])  11.1 us
    all_to_all x1, waiting for transfers between devices, gather_totals(): lax.all_to_all(total, ('gx', 'gy'), split_axis=0, concat_axis=0, tiled=True)  7.83 us
    pallas_call x5, Pallas kernels, call(): pl.pallas_call(functools.partial(kernel, plan), out_shape=[jax.ShapeDtype...  5.35 us
    all_to_all x1, starting transfers between devices, gather_totals(): lax.all_to_all(total, ('gx', 'gy'), split_axis=0, concat_axis=0, tiled=True)  3.54 us
    ppermute x6, waiting for transfers between devices, swap_near(): return lax.ppermute(rows, axis, pairs + [(j, i) for i, j in pairs])  1.12 us
  transfers between devices with their start and end apart: 7, of which 3 were waited for; matrix products, arithmetic and copies ran while one was open for 0% of the time, Pallas kernels for 4%

profile of v9, /device:TPU:0, one launch (start us, length us, event | category | flops | bytes accessed | tf_op | source)
XLA Modules:
  0.0 29.7 jit_solution(12559699806343224651)
XLA Ops:
  0.6 0.0 copy-start.5
  0.6 0.0 copy-start.4
  0.7 0.0 copy-start.2
  0.7 0.0 copy-start.3
  0.7 1.3 %shard_map.95 = (f32[192,128]{1,0:T(8,128)S(1)}, f32[192,128]{1,0:T(8,128)S(1)}, f32[40,128]{1,0:T(8,128)S(1)}, f32[200,128]{1,0:T(8,128)S(1)}) custom-call(f32[4,64,128]{2,1,0:T(8,128)} %conc_ref.1, f32[4,64,128]{2,1,0:T(8,128)} %pot_ref.1, s32[4,64,128]{2,1,0:T(8,128)} %mask_ref, s32[4,64,128]{2,1,0:T(8,128)} %class_ref, f32[4,64,128]{2,1,0:T(8,128)} %mass_ref.3, ...), custom_call_target="tpu_custom_call" | custom-call | tf_op jit(solution)/shard_map/pallas_call | solution.py:546
  1.9 0.0 copy-start.6
  2.0 0.7 %collective-permute-start.2 = (f32[200,128]{1,0:T(8,128)S(1)}, f32[200,128]{1,0:T(8,128)S(1)}, u32[]{:S(2)}, u32[]{:S(2)}) collective-permute-start(f32[200,128]{1,0:T(8,128)S(1)} %get-tuple-element.25), channel_id=1, source_target_pairs={{1,2},{2,1},{5,6},{6,5},{9,10},{10,9},{13,14},{14,13},{17,18},{18,... | collective-permute-start | bytes 307208 | tf_op jit(solution)/shard_map/ppermute | solution.py:564
  2.6 0.7 %collective-permute-start = (f32[192,128]{1,0:T(8,128)S(1)}, f32[192,128]{1,0:T(8,128)S(1)}, u32[]{:S(2)}, u32[]{:S(2)}) collective-permute-start(f32[192,128]{1,0:T(8,128)S(1)} %get-tuple-element.23), channel_id=1, source_target_pairs={{4,8},{12,16},{20,24},{8,4},{16,12},{24,20},{5,9},{13,17},{21,25},... | collective-permute-start | bytes 294920 | tf_op jit(solution)/shard_map/ppermute | solution.py:564
  3.3 0.0 copy-start.7
  3.3 4.4 %collective-permute-start.1 = (f32[192,128]{1,0:T(8,128)S(1)}, f32[192,128]{1,0:T(8,128)S(1)}, u32[]{:S(2)}, u32[]{:S(2)}) collective-permute-start(f32[192,128]{1,0:T(8,128)S(1)} %get-tuple-element.24), channel_id=1, source_target_pairs={{0,4},{8,12},{16,20},{24,28},{4,0},{12,8},{20,16},{28,24},{1,5},{9... | collective-permute-start | bytes 294920 | tf_op jit(solution)/shard_map/ppermute | solution.py:564
  7.7 0.0 copy-start
  7.7 0.0 copy-start.1
  7.7 4.4 %collective-permute-start.3 = (f32[40,128]{1,0:T(8,128)S(1)}, f32[40,128]{1,0:T(8,128)S(1)}, u32[]{:S(2)}, u32[]{:S(2)}) collective-permute-start(f32[40,128]{1,0:T(8,128)S(1)} %get-tuple-element.27), channel_id=1, source_target_pairs={{0,1},{2,3},{1,0},{3,2},{4,5},{6,7},{5,4},{7,6},{8,9},{10,11},{9,8... | collective-permute-start | bytes 61448 | tf_op jit(solution)/shard_map/ppermute | solution.py:564
  12.1 0.0 collective-permute-done.2.y_far_ref.y_far_msg
  12.1 0.0 copy-done.5
  12.1 0.0 copy-done.4
  12.1 0.0 copy-done.6
  12.1 0.0 copy-done.7
  12.1 1.0 %shard_map.96 = (f32[4,64,128]{2,1,0:T(8,128)S(1)}, f32[8,256]{1,0:T(8,128)S(1)}, f32[256,24]{1,0:T(8,128)S(1)}, f32[8,128]{1,0:T(8,128)S(1)}) custom-call(s32[4,64,128]{2,1,0:T(8,128)S(1)} %copy-done.4, s32[4,64,128]{2,1,0:T(8,128)S(1)} %copy-done.5, f32[8]{0:T(128)S(1)} %copy-done.7, s32[8,64]{1,0:T(8,128)S(1)} %copy-done.6), custom_call_target="tpu_custom_call" | custom-call | tf_op jit(solution)/shard_map/pallas_call | solution.py:546
  13.1 0.8 %collective-permute-done.3.y_near_ref.y_near_msg = f32[40,128]{1,0:T(8,128)S(1)} collective-permute-done((f32[40,128]{1,0:T(8,128)S(1)}, f32[40,128]{1,0:T(8,128)S(1)}, u32[]{:S(2)}, u32[]{:S(2)}) %collective-permute-start.3) | collective-permute-done | bytes 20512 | tf_op jit(solution)/shard_map/ppermute | solution.py:564
  13.8 0.0 collective-permute-done.x_far_ref.x_far_msg
  13.8 0.0 collective-permute-done.1.x_near_ref.x_near_msg
  13.8 0.0 copy-done.2
  13.9 0.0 copy-done.3
  13.9 0.0 copy-done
  13.9 0.0 copy-done.1
  13.9 1.6 %shard_map.97 = (f32[4,64,128]{2,1,0:T(8,128)S(1)}, f32[4,64,128]{2,1,0:T(8,128)S(1)}, f32[32,3,4,128]{3,2,1,0:T(4,128)}, f32[16,128]{1,0:T(8,128)S(1)}, f32[136,128]{1,0:T(8,128)S(1)}, /*index=5*/f32[136,128]{1,0:T(8,128)S(1)}) custom-call(f32[192,128]{1,0:T(8,128)S(1)} %collective-permute-done.x_far_ref.x_far_msg, ...), custom_call_target="tpu_custom_call" | custom-call | tf_op jit(solution)/shard_map/pallas_call | solution.py:546
  15.5 3.5 %all-to-all-start = ((f32[32,3,4,128]{3,2,1,0:T(4,128)}), f32[32,3,4,128]{3,2,1,0:T(4,128)S(1)}, u32[]{:S(2)}, u32[]{:S(2)}) async-start(f32[32,3,4,128]{3,2,1,0:T(4,128)} %get-tuple-element.43), calls=%async_computation | async-start | bytes 393216 | tf_op jit(solution)/shard_map/all_to_all | solution.py:573
  19.0 0.3 %collective-permute-start.4 = (f32[136,128]{1,0:T(8,128)S(1)}, f32[136,128]{1,0:T(8,128)S(1)}, u32[]{:S(2)}, u32[]{:S(2)}) collective-permute-start(f32[136,128]{1,0:T(8,128)S(1)} %get-tuple-element.35), channel_id=1, source_target_pairs={{0,4},{8,12},{16,20},{24,28},{4,0},{12,8},{20,16},{28,24},{1,5},{9... | collective-permute-start | bytes 208904 | tf_op jit(solution)/shard_map/ppermute | solution.py:564
  19.4 0.7 %collective-permute-start.5 = (f32[136,128]{1,0:T(8,128)S(1)}, f32[136,128]{1,0:T(8,128)S(1)}, u32[]{:S(2)}, u32[]{:S(2)}) collective-permute-start(f32[136,128]{1,0:T(8,128)S(1)} %get-tuple-element.36), channel_id=1, source_target_pairs={{4,8},{12,16},{20,24},{8,4},{16,12},{24,20},{5,9},{13,17},{21,25},... | collective-permute-start | bytes 208904 | tf_op jit(solution)/shard_map/ppermute | solution.py:564
  20.0 0.3 %collective-permute-done.4.x_near_ref = f32[136,128]{1,0:T(8,128)S(1)} collective-permute-done((f32[136,128]{1,0:T(8,128)S(1)}, f32[136,128]{1,0:T(8,128)S(1)}, u32[]{:S(2)}, u32[]{:S(2)}) %collective-permute-start.4) | collective-permute-done | bytes 69664 | tf_op jit(solution)/shard_map/ppermute | solution.py:564
  20.4 0.0 collective-permute-done.5.x_far_ref
  20.4 0.2 shard_map.98
  20.5 7.8 %all-to-all-done.total_ref = f32[32,3,4,128]{3,2,1,0:T(4,128)S(1)} async-done(((f32[32,3,4,128]{3,2,1,0:T(4,128)}), f32[32,3,4,128]{3,2,1,0:T(4,128)S(1)}, u32[]{:S(2)}, u32[]{:S(2)}) %all-to-all-start) | async-done | bytes 196640 | tf_op jit(solution)/shard_map/all_to_all | solution.py:573
  28.4 1.4 %shard_map.99 = (f32[4,64,128]{2,1,0:T(8,128)}, f32[4,64,128]{2,1,0:T(8,128)}) custom-call(f32[4,64,128]{2,1,0:T(8,128)S(1)} %get-tuple-element.33.conc_ref, f32[4,64,128]{2,1,0:T(8,128)S(1)} %get-tuple-element.34.pot_ref, f32[4,64,128]{2,1,0:T(8,128)S(1)} %copy-done, f32[4,64,128]{2,1,0:T(8,128)S(1)} %copy-done.1, ...), custom_call_target="tpu_custom_call" | custom-call | tf_op jit(solution)/shard_map/pallas_call | solution.py:546
Async XLA Ops:
  0.6 11.5 %copy-start.5 = (s32[4,64,128]{2,1,0:T(8,128)S(1)}, s32[4,64,128]{2,1,0:T(8,128)}, u32[]{:S(2)}) copy-start(s32[4,64,128]{2,1,0:T(8,128)} %class_ref) | copy-start | bytes 393220
  0.6 11.4 %copy-start.4 = (s32[4,64,128]{2,1,0:T(8,128)S(1)}, s32[4,64,128]{2,1,0:T(8,128)}, u32[]{:S(2)}) copy-start(s32[4,64,128]{2,1,0:T(8,128)} %mask_ref) | copy-start | bytes 393220
  0.7 13.2 %copy-start.2 = (f32[4,64,128]{2,1,0:T(8,128)S(1)}, f32[4,64,128]{2,1,0:T(8,128)}, u32[]{:S(2)}) copy-start(f32[4,64,128]{2,1,0:T(8,128)} %conc_ref.1) | copy-start | bytes 393220
  0.7 13.2 %copy-start.3 = (f32[4,64,128]{2,1,0:T(8,128)S(1)}, f32[4,64,128]{2,1,0:T(8,128)}, u32[]{:S(2)}) copy-start(f32[4,64,128]{2,1,0:T(8,128)} %pot_ref.1) | copy-start | bytes 393220
  1.9 10.1 %copy-start.6 = (s32[8,64]{1,0:T(8,128)S(1)}, s32[8,64]{1,0:T(8,128)}, u32[]{:S(2)}) copy-start(s32[8,64]{1,0:T(8,128)} %owner_ref.3) | copy-start | bytes 6148
  2.0 10.1 %collective-permute-start.2 = (f32[200,128]{1,0:T(8,128)S(1)}, f32[200,128]{1,0:T(8,128)S(1)}, u32[]{:S(2)}, u32[]{:S(2)}) collective-permute-start(f32[200,128]{1,0:T(8,128)S(1)} %get-tuple-element.25), channel_id=1, source_target_pairs={{1,2},{2,1},{5,6},{6,5},{9,10},{10,9},{13,14},{14,13},{17,18},{18,... | collective-permute-start | bytes 307208 | tf_op jit(solution)/shard_map/ppermute | solution.py:564
  2.6 11.2 %collective-permute-start = (f32[192,128]{1,0:T(8,128)S(1)}, f32[192,128]{1,0:T(8,128)S(1)}, u32[]{:S(2)}, u32[]{:S(2)}) collective-permute-start(f32[192,128]{1,0:T(8,128)S(1)} %get-tuple-element.23), channel_id=1, source_target_pairs={{4,8},{12,16},{20,24},{8,4},{16,12},{24,20},{5,9},{13,17},{21,25},... | collective-permute-start | bytes 294920 | tf_op jit(solution)/shard_map/ppermute | solution.py:564
  3.3 8.8 %copy-start.7 = (f32[8]{0:T(128)S(1)}, f32[8]{0:T(128)}, u32[]{:S(2)}) copy-start(f32[8]{0:T(128)} %table_ref.1) | copy-start | bytes 100
  3.3 10.5 %collective-permute-start.1 = (f32[192,128]{1,0:T(8,128)S(1)}, f32[192,128]{1,0:T(8,128)S(1)}, u32[]{:S(2)}, u32[]{:S(2)}) collective-permute-start(f32[192,128]{1,0:T(8,128)S(1)} %get-tuple-element.24), channel_id=1, source_target_pairs={{0,4},{8,12},{16,20},{24,28},{4,0},{12,8},{20,16},{28,24},{1,5},{9... | collective-permute-start | bytes 294920 | tf_op jit(solution)/shard_map/ppermute | solution.py:564
  7.7 6.2 %copy-start = (f32[4,64,128]{2,1,0:T(8,128)S(1)}, f32[4,64,128]{2,1,0:T(8,128)}, u32[]{:S(2)}) copy-start(f32[4,64,128]{2,1,0:T(8,128)} %mass_ref.3) | copy-start | bytes 393220
  7.7 6.2 %copy-start.1 = (f32[4,64,128]{2,1,0:T(8,128)S(1)}, f32[4,64,128]{2,1,0:T(8,128)}, u32[]{:S(2)}) copy-start(f32[4,64,128]{2,1,0:T(8,128)} %pots_ref.3) | copy-start | bytes 393220
  7.7 6.2 %collective-permute-start.3 = (f32[40,128]{1,0:T(8,128)S(1)}, f32[40,128]{1,0:T(8,128)S(1)}, u32[]{:S(2)}, u32[]{:S(2)}) collective-permute-start(f32[40,128]{1,0:T(8,128)S(1)} %get-tuple-element.27), channel_id=1, source_target_pairs={{0,1},{2,3},{1,0},{3,2},{4,5},{6,7},{5,4},{7,6},{8,9},{10,11},{9,8... | collective-permute-start | bytes 61448 | tf_op jit(solution)/shard_map/ppermute | solution.py:564
  15.5 12.9 %all-to-all-start = ((f32[32,3,4,128]{3,2,1,0:T(4,128)}), f32[32,3,4,128]{3,2,1,0:T(4,128)S(1)}, u32[]{:S(2)}, u32[]{:S(2)}) async-start(f32[32,3,4,128]{3,2,1,0:T(4,128)} %get-tuple-element.43), calls=%async_computation | async-start | bytes 393216 | tf_op jit(solution)/shard_map/all_to_all | solution.py:573
  19.0 1.3 %collective-permute-start.4 = (f32[136,128]{1,0:T(8,128)S(1)}, f32[136,128]{1,0:T(8,128)S(1)}, u32[]{:S(2)}, u32[]{:S(2)}) collective-permute-start(f32[136,128]{1,0:T(8,128)S(1)} %get-tuple-element.35), channel_id=1, source_target_pairs={{0,4},{8,12},{16,20},{24,28},{4,0},{12,8},{20,16},{28,24},{1,5},{9... | collective-permute-start | bytes 208904 | tf_op jit(solution)/shard_map/ppermute | solution.py:564
  19.4 1.0 %collective-permute-start.5 = (f32[136,128]{1,0:T(8,128)S(1)}, f32[136,128]{1,0:T(8,128)S(1)}, u32[]{:S(2)}, u32[]{:S(2)}) collective-permute-start(f32[136,128]{1,0:T(8,128)S(1)} %get-tuple-element.36), channel_id=1, source_target_pairs={{4,8},{12,16},{20,24},{8,4},{16,12},{24,20},{5,9},{13,17},{21,25},... | collective-permute-start | bytes 208904 | tf_op jit(solution)/shard_map/ppermute | solution.py:564

commit v10 on v9

--- a/solution.py
+++ b/solution.py
@@ -235,66 +235,120 @@
         ref[pl.ds(plan.map_row, plan.owners), pl.ds(0, plan.columns)] = owner_ref[...].astype(F32)
 
 
+def inner_faces(mobility):
+    half = 0.5 * time_step
+    shape = mobility.shape
+    y, plane = iota(shape, 1), iota(shape, 2)
+    to_x = jnp.concatenate(
+        [half * (mobility[:-1] + mobility[1:]), jnp.zeros_like(mobility[:1])], axis=0
+    )
+    out = [to_x]
+    for dim, where, shift, edge in (
+        (1, y, 1, 0), (1, y, shape[1] - 1, shape[1] - 1),
+        (2, plane, 1, 0), (2, plane, shape[2] - 1, shape[2] - 1),
+    ):
+        face = half * (mobility + pltpu.roll(mobility, shift, dim))
+        out.append(jnp.where(where == edge, 0.0, face))
+    return out
+
+
+def inner_flux(faces, field):
+    to_x, y_low, y_high, plane_low, plane_high = faces
+    size_y, size_p = field.shape[1:]
+    from_x = to_x[:-1]
+    blank = jnp.zeros_like(field[:1])
+    flux = jnp.concatenate([from_x * field[1:], blank], axis=0)
+    flux = flux + jnp.concatenate([blank, from_x * field[:-1]], axis=0)
+    flux = flux + y_low * pltpu.roll(field, 1, 1) + y_high * pltpu.roll(field, size_y - 1, 1)
+    return flux + plane_low * pltpu.roll(field, 1, 2) + plane_high * pltpu.roll(field, size_p - 1, 2)
+
+
+def inner_excess(conc, pot, faces, diagonal, mass_source, pot_source):
+    excess_mass = (mass_source - conc) - diagonal * pot + inner_flux(faces, pot)
+    nothing = [jnp.zeros_like(conc[:1])] * 2 + [jnp.zeros_like(conc[:, :1])] * 2
+    beside = None
+    for other in neighbours(conc, nothing):
+        beside = other if beside is None else beside + other
+    excess_pot = (pot_source - pot) + (split_slope + 6.0 * interface) * conc - interface * beside
+    return excess_mass, excess_pot
+
+
+def add_edges(field, x_low, x_high, y_low, y_high):
+    field = jnp.concatenate(
+        [(field[0] + x_low)[None], field[1:-1], (field[-1] + x_high)[None]], axis=0
+    )
+    row = iota((field.shape[0], 8, field.shape[2]), 1)
+    size = field.shape[1]
+    low = field[:, :8] + jnp.where(row == 0, y_low, 0.0)
+    high = field[:, size - 8 :] + jnp.where(row == 7, y_high, 0.0)
+    return jnp.concatenate([low, field[:, 8 : size - 8], high], axis=1)
+
+
 def local_kernel(
-    plan, mask_ref, class_ref, table_ref, owner_ref, mob_ref, gather_ref, spread_ref, scale_ref
+    plan, conc_ref, pot_ref, mask_ref, class_ref, mass_ref, pots_ref, table_ref, owner_ref,
+    mob_ref, gather_ref, spread_ref, scale_ref, faces_ref, diagonal_ref, mass_out, pots_out,
 ):
     table = [table_ref[marker] for marker in range(table_ref.shape[0])]
-    mob_ref[...] = mobility_of(mask_ref[...], class_ref[...], table)
+    mobility = mobility_of(mask_ref[...], class_ref[...], table)
+    mob_ref[...] = mobility
     gather_ref[...], spread_ref[...] = membership(plan, owner_ref)
     scale_ref[...] = scale_of(plan, owner_ref[...])
+    faces = inner_faces(mobility)
+    diagonal = faces[0] + jnp.concatenate([jnp.zeros_like(mobility[:1]), faces[0][:-1]], axis=0)
+    for face in faces[1:]:
+        diagonal = diagonal + face
+    plane = iota(mobility.shape, 2)
+    ends = (plane == 0) | (plane == plan.p - 1)
+    diagonal = diagonal + jnp.where(ends, (0.5 * time_step) * mobility, 0.0)
+    for i, face in enumerate(faces):
+        faces_ref[i] = face
+    diagonal_ref[...] = diagonal
+    mass_out[...], pots_out[...] = inner_excess(
+        conc_ref[...], pot_ref[...], faces, diagonal, mass_ref[...], pots_ref[...]
+    )
 
 
 def first_kernel(
     plan, x_far_ref, x_near_ref, y_far_ref, y_near_ref,
     conc_ref, pot_ref, mob_ref, mass_ref, pots_ref, gather_ref, scale_ref, owner_ref,
+    faces_ref, diagonal_ref, mass_part_ref, pot_part_ref,
     conc_out, pot_out, total_hbm, raw_out, x_near_out, x_far_out, total_out, sems,
 ):
     sides = received("gx", x_near_ref, x_far_ref)
     ends = received("gy", y_near_ref, y_far_ref)
+    last_x, last_y = plan.x - 1, plan.y - 1
 
     def halo(which):
-        return tuple(side_rows(plan, rows, which) for rows in sides) + tuple(
+        return tuple(side_rows(plan, rows, which)[0] for rows in sides) + tuple(
             side_columns(plan, rows, which) for rows in ends
         )
 
-    mobility, mob_halo = mob_ref[...], halo(2)
-    faces, diagonal = faces_of(mobility, neighbours(mobility, mob_halo))
-    mass_source, pot_source = mass_ref[...], pots_ref[...]
-    conc, pot = conc_ref[...], pot_ref[...]
-    for at, field in enumerate((conc, pot)):
-        for x in range(plan.x):
-            raw_out[pl.ds(2 * at * plan.x + x, 1), :] = field[x, 0:1]
-            raw_out[pl.ds((2 * at + 1) * plan.x + x, 1), :] = field[x, plan.y - 1 : plan.y]
-    excess = excess_of(
-        conc, pot, neighbours(conc, halo(0)), neighbours(pot, halo(1)), faces, diagonal,
-        mass_source, pot_source,
-    )
-    conc, pot = relax_pair(conc, pot, *excess, diagonal, scale_from(diagonal))
-    conc_out[...] = conc
-    pot_out[...] = pot
-    put_x(plan, (conc[0], pot[0]), (conc[plan.x - 1], pot[plan.x - 1]), x_near_out, x_far_out)
-    up = even("gx")
-    base = 2 * plan.y
-    for which in range(3):
-        for end, rows in enumerate(ends):
-            low = rows[which * plan.x : which * plan.x + 1]
-            high = rows[(which + 1) * plan.x - 1 : (which + 1) * plan.x]
-            x_near_out[pl.ds(base + 2 * which + end, 1), :] = jnp.where(up, high, low)
-            x_far_out[pl.ds(base + 2 * which + end, 1), :] = jnp.where(up, low, high)
-    for ref in (x_near_out, x_far_out):
-        ref[pl.ds(base + 6, 2), :] = jnp.zeros((2, plan.p), F32)
-
-    nothing = tuple(jnp.zeros_like(part) for part in mob_halo)
-    own_mass, own_pot = excess_of(
-        conc, pot, neighbours(conc, nothing), neighbours(pot, nothing), faces, diagonal,
-        mass_source, pot_source,
+    def edges(field):
+        return field[0], field[last_x], field[:, :1], field[:, last_y:]
+
+    mobility = mob_ref[...]
+    raw_conc, raw_pot = conc_ref[...], pot_ref[...]
+    outer = [
+        (0.5 * time_step) * (own + other) for own, other in zip(edges(mobility), halo(2))
+    ]
+    diagonal = add_edges(diagonal_ref[...], *outer)
+    excess_mass = add_edges(
+        mass_part_ref[...],
+        *(f * (other - own) for f, own, other in zip(outer, edges(raw_pot), halo(1))),
+    )
+    excess_pot = add_edges(pot_part_ref[...], *(-interface * other for other in halo(0)))
+    conc, pot = relax_pair(
+        raw_conc, raw_pot, excess_mass, excess_pot, diagonal, scale_from(diagonal)
+    )
+
+    own_mass, own_pot = inner_excess(
+        conc, pot, [faces_ref[i] for i in range(5)], diagonal, mass_ref[...], pots_ref[...]
     )
     give_mass, give_pot = (
         [field[x] + field[x + 1] for x in range(0, plan.x, 2)] for field in (own_mass, own_pot)
     )
-    for x, side in ((0, 0), (plan.x - 1, 1)):
-        face = 0.5 * (mobility[x] + mob_halo[side][0])
-        give_mass.append(time_step * face * pot[x])
+    for x, side in ((0, 0), (last_x, 1)):
+        give_mass.append(outer[side] * pot[x])
         give_pot.append(-interface * conc[x])
 
     def packed(mass, other):
@@ -314,12 +368,11 @@
     sums = [None, split_dot(gather_ref[...].astype(BF16), give, ((1,), (0,))), None]
     sums[1] = sums[1] * scale_ref[...]
     for place, y, at, side in ((0, 0, plan.half_y - 1, 2), (2, plan.y - 1, 0, 3)):
-        edge_mob, edge_pot, edge_conc = (
+        edge_pot, edge_conc = (
             jnp.concatenate([field[x, y : y + 1] for x in range(plan.x)], axis=0)
-            for field in (mobility, pot, conc)
-        )
-        face = 0.5 * (edge_mob + mob_halo[side][:, 0])
-        both = packed(time_step * face * edge_pot, -interface * edge_conc)
+            for field in (pot, conc)
+        )
+        both = packed(outer[side][:, 0] * edge_pot, -interface * edge_conc)
         part = jnp.zeros((plan.owners, plan.p), F32)
         for i in range(plan.half_x):
             column = owner_column(plan, maps[place], i, at)
@@ -327,11 +380,31 @@
             pair = both[2 * i : 2 * i + 1] + both[2 * i + 1 : 2 * i + 2]
             part = part + jnp.where((owner.astype(F32) == ident) & inside[place], pair, 0.0)
         sums[place] = part * scale_of(plan, maps[place])
+    def store_fields():
+        conc_out[...] = conc
+        pot_out[...] = pot
+        for at, field in enumerate((raw_conc, raw_pot)):
+            for x in range(plan.x):
+                raw_out[pl.ds(2 * at * plan.x + x, 1), :] = field[x, 0:1]
+                raw_out[pl.ds((2 * at + 1) * plan.x + x, 1), :] = field[x, last_y : last_y + 1]
+        put_x(plan, (conc[0], pot[0]), (conc[last_x], pot[last_x]), x_near_out, x_far_out)
+        up = even("gx")
+        base = 2 * plan.y
+        for which in range(3):
+            for end, rows in enumerate(ends):
+                low = rows[which * plan.x : which * plan.x + 1]
+                high = rows[(which + 1) * plan.x - 1 : (which + 1) * plan.x]
+                x_near_out[pl.ds(base + 2 * which + end, 1), :] = jnp.where(up, high, low)
+                x_far_out[pl.ds(base + 2 * which + end, 1), :] = jnp.where(up, low, high)
+        for ref in (x_near_out, x_far_out):
+            ref[pl.ds(base + 6, 2), :] = jnp.zeros((2, plan.p), F32)
+
     if not plan.slots:
         total_out[...] = jnp.concatenate(sums, axis=0)
-        copy = pltpu.make_async_copy(total_out, total_hbm, sems.at[0])
-        copy.start()
-        copy.wait()
+        copies = [pltpu.make_async_copy(total_out, total_hbm, sems.at[0])]
+        copies[0].start()
+        store_fields()
+        copies[0].wait()
         return
 
     def picked(place, i, at):
@@ -375,6 +448,7 @@
                 pltpu.make_async_copy(total_out.at[some], total_hbm.at[some], sems.at[g // 2])
             )
             copies[-1].start()
+    store_fields()
     for copy in copies:
         copy.wait()
 
@@ -614,12 +688,15 @@
     x_near, x_far = swap_near("gx", messages[0]), swap_far("gx", messages[1])
     y_near, y_far = swap_near("gy", messages[2]), swap_far("gy", messages[3])
     y_far, mask, kind = lax.optimization_barrier((y_far, mask, kind))
-    mob, gather, spread, scale = call(
+    mob, gather, spread, scale, *parts = call(
         local_kernel,
         plan,
-        [block, (plan.owners, plan.rows), (plan.rows, 3 * plan.owners), (plan.owners, plan.p)],
-        [mask, kind, table, owner_map],
-        smem=(2,),
+        [
+            block, (plan.owners, plan.rows), (plan.rows, 3 * plan.owners), (plan.owners, plan.p),
+            (5, *block), block, block, block,
+        ],
+        [conc, pot, mask, kind, mass_source, pot_source, table, owner_map],
+        smem=(6,),
     )
     slots = (plan.slots, plan.slot_parts, 4, plan.p) if plan.slots else (3 * plan.owners, plan.p)
     conc, pot, total, raw, near, far = call(
@@ -634,7 +711,7 @@
         ],
         [
             x_far, x_near, y_far, y_near,
-            conc, pot, mob, mass_source, pot_source, gather, scale, owner_map,
+            conc, pot, mob, mass_source, pot_source, gather, scale, owner_map, *parts,
         ],
         out_far=(2,),
         scratch=(pltpu.VMEM(slots, F32), pltpu.SemaphoreType.DMA((plan.owners // 2,))),

time: 30 us -> 29.7 us (0.990)
  no operation moved by 1% of the time
where the time goes in v10:
time: 29.7 us; the launch traced here: 29.4 us
  starting transfers between devices  14.6 us (49%)
  waiting for transfers between devices  8.82 us (30%)
  Pallas kernels  5.16 us (17%)
  between operations  0.81 us (3%)
    ppermute x6, starting transfers between devices, swap_near(): return lax.ppermute(rows, axis, pairs + [(j, i) for i, j in pairs])  11.1 us
    all_to_all x1, waiting for transfers between devices, gather_totals(): lax.all_to_all(total, ('gx', 'gy'), split_axis=0, concat_axis=0, tiled=True)  7.83 us
    pallas_call x5, Pallas kernels, call(): pl.pallas_call(functools.partial(kernel, plan), out_shape=[jax.ShapeDtype...  5.16 us
    all_to_all x1, starting transfers between devices, gather_totals(): lax.all_to_all(total, ('gx', 'gy'), split_axis=0, concat_axis=0, tiled=True)  3.56 us
    ppermute x6, waiting for transfers between devices, swap_near(): return lax.ppermute(rows, axis, pairs + [(j, i) for i, j in pairs])  0.99 us
  transfers between devices with their start and end apart: 7, of which 3 were waited for; matrix products, arithmetic and copies ran while one was open for 0% of the time, Pallas kernels for 4%

profile of v10, /device:TPU:0, one launch (start us, length us, event | category | flops | bytes accessed | tf_op | source)
XLA Modules:
  0.0 29.4 jit_solution(8215002940486665868)
XLA Ops:
  0.6 0.0 copy-start.1
  0.6 0.0 copy-start
  0.7 0.0 copy-start.3
  0.7 0.0 copy-start.2
  0.7 0.0 copy-start.5
  0.7 0.0 copy-start.4
  0.7 1.3 %shard_map.95 = (f32[192,128]{1,0:T(8,128)S(1)}, f32[192,128]{1,0:T(8,128)S(1)}, f32[40,128]{1,0:T(8,128)S(1)}, f32[200,128]{1,0:T(8,128)S(1)}) custom-call(f32[4,64,128]{2,1,0:T(8,128)} %conc_ref.3, f32[4,64,128]{2,1,0:T(8,128)} %pot_ref.3, s32[4,64,128]{2,1,0:T(8,128)} %mask_ref, s32[4,64,128]{2,1,0:T(8,128)} %class_ref, f32[4,64,128]{2,1,0:T(8,128)} %mass_ref.5, ...), custom_call_target="tpu_custom_call" | custom-call | tf_op jit(solution)/shard_map/pallas_call | solution.py:620
  2.0 0.0 copy-start.6
  2.0 0.7 %collective-permute-start.2 = (f32[200,128]{1,0:T(8,128)S(1)}, f32[200,128]{1,0:T(8,128)S(1)}, u32[]{:S(2)}, u32[]{:S(2)}) collective-permute-start(f32[200,128]{1,0:T(8,128)S(1)} %get-tuple-element.29), channel_id=1, source_target_pairs={{1,2},{2,1},{5,6},{6,5},{9,10},{10,9},{13,14},{14,13},{17,18},{18,... | collective-permute-start | bytes 307208 | tf_op jit(solution)/shard_map/ppermute | solution.py:638
  2.7 0.7 %collective-permute-start = (f32[192,128]{1,0:T(8,128)S(1)}, f32[192,128]{1,0:T(8,128)S(1)}, u32[]{:S(2)}, u32[]{:S(2)}) collective-permute-start(f32[192,128]{1,0:T(8,128)S(1)} %get-tuple-element.27), channel_id=1, source_target_pairs={{4,8},{12,16},{20,24},{8,4},{16,12},{24,20},{5,9},{13,17},{21,25},... | collective-permute-start | bytes 294920 | tf_op jit(solution)/shard_map/ppermute | solution.py:638
  3.4 0.0 copy-start.7
  3.4 4.4 %collective-permute-start.1 = (f32[192,128]{1,0:T(8,128)S(1)}, f32[192,128]{1,0:T(8,128)S(1)}, u32[]{:S(2)}, u32[]{:S(2)}) collective-permute-start(f32[192,128]{1,0:T(8,128)S(1)} %get-tuple-element.28), channel_id=1, source_target_pairs={{0,4},{8,12},{16,20},{24,28},{4,0},{12,8},{20,16},{28,24},{1,5},{9... | collective-permute-start | bytes 294920 | tf_op jit(solution)/shard_map/ppermute | solution.py:638
  7.7 4.4 %collective-permute-start.3 = (f32[40,128]{1,0:T(8,128)S(1)}, f32[40,128]{1,0:T(8,128)S(1)}, u32[]{:S(2)}, u32[]{:S(2)}) collective-permute-start(f32[40,128]{1,0:T(8,128)S(1)} %get-tuple-element.31), channel_id=1, source_target_pairs={{0,1},{2,3},{1,0},{3,2},{4,5},{6,7},{5,4},{7,6},{8,9},{10,11},{9,8... | collective-permute-start | bytes 61448 | tf_op jit(solution)/shard_map/ppermute | solution.py:638
  12.1 0.0 collective-permute-done.2.y_far_ref.y_far_msg
  12.1 0.0 copy-done.1
  12.1 0.0 copy-done
  12.1 0.0 copy-done.3
  12.1 0.0 copy-done.2
  12.2 0.0 copy-done.5
  12.2 0.0 copy-done.4
  12.2 0.0 copy-done.6
  12.2 0.0 copy-done.7
  12.2 1.1 %shard_map.96 = (f32[4,64,128]{2,1,0:T(8,128)S(1)}, f32[8,256]{1,0:T(8,128)S(1)}, f32[256,24]{1,0:T(8,128)S(1)}, f32[8,128]{1,0:T(8,128)S(1)}, f32[5,4,64,128]{3...) custom-call(f32[4,64,128]{2,1,0:T(8,128)S(1)} %copy-done.2, ...), custom_call_target="tpu_custom_call" | custom-call | tf_op jit(solution)/shard_map/pallas_call | solution.py:620
  13.3 0.6 %collective-permute-done.3.y_near_ref.y_near_msg = f32[40,128]{1,0:T(8,128)S(1)} collective-permute-done((f32[40,128]{1,0:T(8,128)S(1)}, f32[40,128]{1,0:T(8,128)S(1)}, u32[]{:S(2)}, u32[]{:S(2)}) %collective-permute-start.3) | collective-permute-done | bytes 20512 | tf_op jit(solution)/shard_map/ppermute | solution.py:638
  13.9 0.0 collective-permute-done.x_far_ref.x_far_msg
  13.9 0.0 collective-permute-done.1.x_near_ref.x_near_msg
  13.9 1.3 %shard_map.97 = (f32[4,64,128]{2,1,0:T(8,128)S(1)}, f32[4,64,128]{2,1,0:T(8,128)S(1)}, f32[32,3,4,128]{3,2,1,0:T(4,128)}, f32[16,128]{1,0:T(8,128)S(1)}, f32[136,128]{1,0:T(8,128)S(1)}, /*index=5*/f32[136,128]{1,0:T(8,128)S(1)}) custom-call(f32[192,128]{1,0:T(8,128)S(1)} %collective-permute-done.x_far_ref.x_far_msg, ...), custom_call_target="tpu_custom_call" | custom-call | tf_op jit(solution)/shard_map/pallas_call | solution.py:620
  15.2 3.6 %all-to-all-start = ((f32[32,3,4,128]{3,2,1,0:T(4,128)}), f32[32,3,4,128]{3,2,1,0:T(4,128)S(1)}, u32[]{:S(2)}, u32[]{:S(2)}) async-start(f32[32,3,4,128]{3,2,1,0:T(4,128)} %get-tuple-element.51), calls=%async_computation | async-start | bytes 393216 | tf_op jit(solution)/shard_map/all_to_all | solution.py:647
  18.7 0.3 %collective-permute-start.4 = (f32[136,128]{1,0:T(8,128)S(1)}, f32[136,128]{1,0:T(8,128)S(1)}, u32[]{:S(2)}, u32[]{:S(2)}) collective-permute-start(f32[136,128]{1,0:T(8,128)S(1)} %get-tuple-element.43), channel_id=1, source_target_pairs={{0,4},{8,12},{16,20},{24,28},{4,0},{12,8},{20,16},{28,24},{1,5},{9... | collective-permute-start | bytes 208904 | tf_op jit(solution)/shard_map/ppermute | solution.py:638
  19.1 0.7 %collective-permute-start.5 = (f32[136,128]{1,0:T(8,128)S(1)}, f32[136,128]{1,0:T(8,128)S(1)}, u32[]{:S(2)}, u32[]{:S(2)}) collective-permute-start(f32[136,128]{1,0:T(8,128)S(1)} %get-tuple-element.44), channel_id=1, source_target_pairs={{4,8},{12,16},{20,24},{8,4},{16,12},{24,20},{5,9},{13,17},{21,25},... | collective-permute-start | bytes 208904 | tf_op jit(solution)/shard_map/ppermute | solution.py:638
  19.7 0.3 %collective-permute-done.4.x_near_ref = f32[136,128]{1,0:T(8,128)S(1)} collective-permute-done((f32[136,128]{1,0:T(8,128)S(1)}, f32[136,128]{1,0:T(8,128)S(1)}, u32[]{:S(2)}, u32[]{:S(2)}) %collective-permute-start.4) | collective-permute-done | bytes 69664 | tf_op jit(solution)/shard_map/ppermute | solution.py:638
  20.1 0.0 collective-permute-done.5.x_far_ref
  20.1 0.2 shard_map.98
  20.3 7.8 %all-to-all-done.total_ref = f32[32,3,4,128]{3,2,1,0:T(4,128)S(1)} async-done(((f32[32,3,4,128]{3,2,1,0:T(4,128)}), f32[32,3,4,128]{3,2,1,0:T(4,128)S(1)}, u32[]{:S(2)}, u32[]{:S(2)}) %all-to-all-start) | async-done | bytes 196640 | tf_op jit(solution)/shard_map/all_to_all | solution.py:647
  28.1 1.4 %shard_map.99 = (f32[4,64,128]{2,1,0:T(8,128)}, f32[4,64,128]{2,1,0:T(8,128)}) custom-call(f32[4,64,128]{2,1,0:T(8,128)S(1)} %get-tuple-element.41.conc_ref, f32[4,64,128]{2,1,0:T(8,128)S(1)} %get-tuple-element.42.pot_ref, f32[4,64,128]{2,1,0:T(8,128)S(1)} %copy-done, f32[4,64,128]{2,1,0:T(8,128)S(1)} %copy-done.1, ...), custom_call_target="tpu_custom_call" | custom-call | tf_op jit(solution)/shard_map/pallas_call | solution.py:620
Async XLA Ops:
  0.6 11.5 %copy-start.1 = (f32[4,64,128]{2,1,0:T(8,128)S(1)}, f32[4,64,128]{2,1,0:T(8,128)}, u32[]{:S(2)}) copy-start(f32[4,64,128]{2,1,0:T(8,128)} %pots_ref.5) | copy-start | bytes 393220
  0.6 11.5 %copy-start = (f32[4,64,128]{2,1,0:T(8,128)S(1)}, f32[4,64,128]{2,1,0:T(8,128)}, u32[]{:S(2)}) copy-start(f32[4,64,128]{2,1,0:T(8,128)} %mass_ref.5) | copy-start | bytes 393220
  0.7 11.5 %copy-start.3 = (f32[4,64,128]{2,1,0:T(8,128)S(1)}, f32[4,64,128]{2,1,0:T(8,128)}, u32[]{:S(2)}) copy-start(f32[4,64,128]{2,1,0:T(8,128)} %pot_ref.3) | copy-start | bytes 393220
  0.7 11.5 %copy-start.2 = (f32[4,64,128]{2,1,0:T(8,128)S(1)}, f32[4,64,128]{2,1,0:T(8,128)}, u32[]{:S(2)}) copy-start(f32[4,64,128]{2,1,0:T(8,128)} %conc_ref.3) | copy-start | bytes 393220
  0.7 11.5 %copy-start.5 = (s32[4,64,128]{2,1,0:T(8,128)S(1)}, s32[4,64,128]{2,1,0:T(8,128)}, u32[]{:S(2)}) copy-start(s32[4,64,128]{2,1,0:T(8,128)} %class_ref) | copy-start | bytes 393220
  0.7 11.5 %copy-start.4 = (s32[4,64,128]{2,1,0:T(8,128)S(1)}, s32[4,64,128]{2,1,0:T(8,128)}, u32[]{:S(2)}) copy-start(s32[4,64,128]{2,1,0:T(8,128)} %mask_ref) | copy-start | bytes 393220
  2.0 10.2 %copy-start.6 = (s32[8,64]{1,0:T(8,128)S(1)}, s32[8,64]{1,0:T(8,128)}, u32[]{:S(2)}) copy-start(s32[8,64]{1,0:T(8,128)} %owner_ref.3) | copy-start | bytes 6148
  2.0 10.1 %collective-permute-start.2 = (f32[200,128]{1,0:T(8,128)S(1)}, f32[200,128]{1,0:T(8,128)S(1)}, u32[]{:S(2)}, u32[]{:S(2)}) collective-permute-start(f32[200,128]{1,0:T(8,128)S(1)} %get-tuple-element.29), channel_id=1, source_target_pairs={{1,2},{2,1},{5,6},{6,5},{9,10},{10,9},{13,14},{14,13},{17,18},{18,... | collective-permute-start | bytes 307208 | tf_op jit(solution)/shard_map/ppermute | solution.py:638
  2.7 11.2 %collective-permute-start = (f32[192,128]{1,0:T(8,128)S(1)}, f32[192,128]{1,0:T(8,128)S(1)}, u32[]{:S(2)}, u32[]{:S(2)}) collective-permute-start(f32[192,128]{1,0:T(8,128)S(1)} %get-tuple-element.27), channel_id=1, source_target_pairs={{4,8},{12,16},{20,24},{8,4},{16,12},{24,20},{5,9},{13,17},{21,25},... | collective-permute-start | bytes 294920 | tf_op jit(solution)/shard_map/ppermute | solution.py:638
  3.4 8.8 %copy-start.7 = (f32[8]{0:T(128)S(1)}, f32[8]{0:T(128)}, u32[]{:S(2)}) copy-start(f32[8]{0:T(128)} %table_ref.1) | copy-start | bytes 100
  3.4 10.5 %collective-permute-start.1 = (f32[192,128]{1,0:T(8,128)S(1)}, f32[192,128]{1,0:T(8,128)S(1)}, u32[]{:S(2)}, u32[]{:S(2)}) collective-permute-start(f32[192,128]{1,0:T(8,128)S(1)} %get-tuple-element.28), channel_id=1, source_target_pairs={{0,4},{8,12},{16,20},{24,28},{4,0},{12,8},{20,16},{28,24},{1,5},{9... | collective-permute-start | bytes 294920 | tf_op jit(solution)/shard_map/ppermute | solution.py:638
  7.7 6.2 %collective-permute-start.3 = (f32[40,128]{1,0:T(8,128)S(1)}, f32[40,128]{1,0:T(8,128)S(1)}, u32[]{:S(2)}, u32[]{:S(2)}) collective-permute-start(f32[40,128]{1,0:T(8,128)S(1)} %get-tuple-element.31), channel_id=1, source_target_pairs={{0,1},{2,3},{1,0},{3,2},{4,5},{6,7},{5,4},{7,6},{8,9},{10,11},{9,8... | collective-permute-start | bytes 61448 | tf_op jit(solution)/shard_map/ppermute | solution.py:638
  15.2 12.9 %all-to-all-start = ((f32[32,3,4,128]{3,2,1,0:T(4,128)}), f32[32,3,4,128]{3,2,1,0:T(4,128)S(1)}, u32[]{:S(2)}, u32[]{:S(2)}) async-start(f32[32,3,4,128]{3,2,1,0:T(4,128)} %get-tuple-element.51), calls=%async_computation | async-start | bytes 393216 | tf_op jit(solution)/shard_map/all_to_all | solution.py:647
  18.7 1.3 %collective-permute-start.4 = (f32[136,128]{1,0:T(8,128)S(1)}, f32[136,128]{1,0:T(8,128)S(1)}, u32[]{:S(2)}, u32[]{:S(2)}) collective-permute-start(f32[136,128]{1,0:T(8,128)S(1)} %get-tuple-element.43), channel_id=1, source_target_pairs={{0,4},{8,12},{16,20},{24,28},{4,0},{12,8},{20,16},{28,24},{1,5},{9... | collective-permute-start | bytes 208904 | tf_op jit(solution)/shard_map/ppermute | solution.py:638
  19.1 1.0 %collective-permute-start.5 = (f32[136,128]{1,0:T(8,128)S(1)}, f32[136,128]{1,0:T(8,128)S(1)}, u32[]{:S(2)}, u32[]{:S(2)}) collective-permute-start(f32[136,128]{1,0:T(8,128)S(1)} %get-tuple-element.44), channel_id=1, source_target_pairs={{4,8},{12,16},{20,24},{8,4},{16,12},{24,20},{5,9},{13,17},{21,25},... | collective-permute-start | bytes 208904 | tf_op jit(solution)/shard_map/ppermute | solution.py:638

commit v11 on v10

--- a/solution.py
+++ b/solution.py
@@ -126,6 +126,9 @@
         self.slot_parts = -(-(owners + 2 * self.half_x) // 4)
         slots = owners * groups
         self.slots = slots if slots <= 64 else 0
+
+    def slot_of(self, g, h):
+        return (-h % self.groups) * self.owners + g
 
 
 def side_rows(plan, rows, which):
@@ -435,19 +438,18 @@
         beside += [(at, blank) for at in range(plan.high_row + plan.half_x, size)]
         rows.append((of_plane(plane, sums), beside))
     copies = []
-    for g in range(plan.owners):
-        for plane, (main, beside) in enumerate(rows):
-            slot = g * plan.groups + plane
+    for plane, (main, beside) in enumerate(rows):
+        for g in range(plan.owners):
+            slot = plan.slot_of(g, plane)
             for part in range(plan.owners // 4):
                 total_out[slot, part] = main[4 * part : 4 * part + 4]
             for row, values in beside:
                 total_out[slot, row // 4, pl.ds(row % 4, 1), :] = values[g : g + 1]
-        if g % 2:
-            some = pl.ds((g - 1) * plan.groups, 2 * plan.groups)
-            copies.append(
-                pltpu.make_async_copy(total_out.at[some], total_hbm.at[some], sems.at[g // 2])
-            )
-            copies[-1].start()
+        some = pl.ds(plan.slot_of(0, plane), plan.owners)
+        copies.append(
+            pltpu.make_async_copy(total_out.at[some], total_hbm.at[some], sems.at[plane])
+        )
+        copies[-1].start()
     store_fields()
     for copy in copies:
         copy.wait()
@@ -644,7 +646,13 @@
 
 def gather_totals(plan, total, y_near, y_far):
     if plan.slots:
-        return lax.all_to_all(total, ("gx", "gy"), split_axis=0, concat_axis=0, tiled=True)
+        order = [0] * plan.slots
+        for g in range(plan.owners):
+            for h in range(plan.groups):
+                order[plan.slot_of(g, h)] = g * plan.groups + h
+        return lax.all_to_all(
+            total, ("gx", "gy"), split_axis=0, concat_axis=0, axis_index_groups=[order], tiled=True
+        )
     shape = (plan.groups, 3, plan.owners, plan.p)
     parts = lax.all_gather(lax.psum(total, "gx"), "gy").reshape(shape)
     blank = jnp.zeros((1, plan.owners, plan.p), F32)
@@ -714,7 +722,7 @@
             conc, pot, mob, mass_source, pot_source, gather, scale, owner_map, *parts,
         ],
         out_far=(2,),
-        scratch=(pltpu.VMEM(slots, F32), pltpu.SemaphoreType.DMA((plan.owners // 2,))),
+        scratch=(pltpu.VMEM(slots, F32), pltpu.SemaphoreType.DMA((plan.groups,))),
     )
     total = gather_totals(plan, total, y_near, y_far)
     far = swap_far("gx", far)

time: 29.7 us -> 29.8 us (level)
  no operation moved by 1% of the time
where the time goes in v11:
time: 29.8 us; the launch traced here: 29.5 us
  starting transfers between devices  14.6 us (49%)
  waiting for transfers between devices  8.88 us (30%)
  Pallas kernels  5.15 us (17%)
  between operations  0.81 us (3%)
    ppermute x6, starting transfers between devices, swap_near(): return lax.ppermute(rows, axis, pairs + [(j, i) for i, j in pairs])  11.1 us
    all_to_all x1, waiting for transfers between devices, gather_totals(): lax.all_to_all(total, ('gx', 'gy'), split_axis=0, concat_axis=0, axis_ind...  7.89 us
    pallas_call x5, Pallas kernels, call(): pl.pallas_call(functools.partial(kernel, plan), out_shape=[jax.ShapeDtype...  5.15 us
    all_to_all x1, starting transfers between devices, gather_totals(): lax.all_to_all(total, ('gx', 'gy'), split_axis=0, concat_axis=0, axis_ind...  3.56 us
    ppermute x6, waiting for transfers between devices, swap_near(): return lax.ppermute(rows, axis, pairs + [(j, i) for i, j in pairs])  0.99 us
  transfers between devices with their start and end apart: 7, of which 3 were waited for; matrix products, arithmetic and copies ran while one was open for 0% of the time, Pallas kernels for 4%

profile of v11, /device:TPU:0, one launch (start us, length us, event | category | flops | bytes accessed | tf_op | source)
XLA Modules:
  0.0 29.5 jit_solution(3516458953901153875)
XLA Ops:
  0.6 0.0 copy-start.1
  0.6 0.0 copy-start
  0.7 0.0 copy-start.3
  0.7 0.0 copy-start.2
  0.7 0.0 copy-start.5
  0.7 0.0 copy-start.4
  0.7 1.3 %shard_map.95 = (f32[192,128]{1,0:T(8,128)S(1)}, f32[192,128]{1,0:T(8,128)S(1)}, f32[40,128]{1,0:T(8,128)S(1)}, f32[200,128]{1,0:T(8,128)S(1)}) custom-call(f32[4,64,128]{2,1,0:T(8,128)} %conc_ref.3, f32[4,64,128]{2,1,0:T(8,128)} %pot_ref.3, s32[4,64,128]{2,1,0:T(8,128)} %mask_ref, s32[4,64,128]{2,1,0:T(8,128)} %class_ref, f32[4,64,128]{2,1,0:T(8,128)} %mass_ref.5, ...), custom_call_target="tpu_custom_call" | custom-call | tf_op jit(solution)/shard_map/pallas_call | solution.py:622
  2.0 0.0 copy-start.6
  2.0 0.7 %collective-permute-start.2 = (f32[200,128]{1,0:T(8,128)S(1)}, f32[200,128]{1,0:T(8,128)S(1)}, u32[]{:S(2)}, u32[]{:S(2)}) collective-permute-start(f32[200,128]{1,0:T(8,128)S(1)} %get-tuple-element.29), channel_id=1, source_target_pairs={{1,2},{2,1},{5,6},{6,5},{9,10},{10,9},{13,14},{14,13},{17,18},{18,... | collective-permute-start | bytes 307208 | tf_op jit(solution)/shard_map/ppermute | solution.py:640
  2.7 0.7 %collective-permute-start = (f32[192,128]{1,0:T(8,128)S(1)}, f32[192,128]{1,0:T(8,128)S(1)}, u32[]{:S(2)}, u32[]{:S(2)}) collective-permute-start(f32[192,128]{1,0:T(8,128)S(1)} %get-tuple-element.27), channel_id=1, source_target_pairs={{4,8},{12,16},{20,24},{8,4},{16,12},{24,20},{5,9},{13,17},{21,25},... | collective-permute-start | bytes 294920 | tf_op jit(solution)/shard_map/ppermute | solution.py:640
  3.4 0.0 copy-start.7
  3.4 4.4 %collective-permute-start.1 = (f32[192,128]{1,0:T(8,128)S(1)}, f32[192,128]{1,0:T(8,128)S(1)}, u32[]{:S(2)}, u32[]{:S(2)}) collective-permute-start(f32[192,128]{1,0:T(8,128)S(1)} %get-tuple-element.28), channel_id=1, source_target_pairs={{0,4},{8,12},{16,20},{24,28},{4,0},{12,8},{20,16},{28,24},{1,5},{9... | collective-permute-start | bytes 294920 | tf_op jit(solution)/shard_map/ppermute | solution.py:640
  7.7 4.4 %collective-permute-start.3 = (f32[40,128]{1,0:T(8,128)S(1)}, f32[40,128]{1,0:T(8,128)S(1)}, u32[]{:S(2)}, u32[]{:S(2)}) collective-permute-start(f32[40,128]{1,0:T(8,128)S(1)} %get-tuple-element.31), channel_id=1, source_target_pairs={{0,1},{2,3},{1,0},{3,2},{4,5},{6,7},{5,4},{7,6},{8,9},{10,11},{9,8... | collective-permute-start | bytes 61448 | tf_op jit(solution)/shard_map/ppermute | solution.py:640
  12.1 0.0 collective-permute-done.2.y_far_ref.y_far_msg
  12.1 0.0 copy-done.1
  12.1 0.0 copy-done
  12.1 0.0 copy-done.3
  12.1 0.0 copy-done.2
  12.2 0.0 copy-done.5
  12.2 0.0 copy-done.4
  12.2 0.0 copy-done.6
  12.2 0.0 copy-done.7
  12.2 1.1 %shard_map.96 = (f32[4,64,128]{2,1,0:T(8,128)S(1)}, f32[8,256]{1,0:T(8,128)S(1)}, f32[256,24]{1,0:T(8,128)S(1)}, f32[8,128]{1,0:T(8,128)S(1)}, f32[5,4,64,128]{3...) custom-call(f32[4,64,128]{2,1,0:T(8,128)S(1)} %copy-done.2, ...), custom_call_target="tpu_custom_call" | custom-call | tf_op jit(solution)/shard_map/pallas_call | solution.py:622
  13.3 0.6 %collective-permute-done.3.y_near_ref.y_near_msg = f32[40,128]{1,0:T(8,128)S(1)} collective-permute-done((f32[40,128]{1,0:T(8,128)S(1)}, f32[40,128]{1,0:T(8,128)S(1)}, u32[]{:S(2)}, u32[]{:S(2)}) %collective-permute-start.3) | collective-permute-done | bytes 20512 | tf_op jit(solution)/shard_map/ppermute | solution.py:640
  13.9 0.0 collective-permute-done.x_far_ref.x_far_msg
  13.9 0.0 collective-permute-done.1.x_near_ref.x_near_msg
  13.9 1.3 %shard_map.97 = (f32[4,64,128]{2,1,0:T(8,128)S(1)}, f32[4,64,128]{2,1,0:T(8,128)S(1)}, f32[32,3,4,128]{3,2,1,0:T(4,128)}, f32[16,128]{1,0:T(8,128)S(1)}, f32[136,128]{1,0:T(8,128)S(1)}, /*index=5*/f32[136,128]{1,0:T(8,128)S(1)}) custom-call(f32[192,128]{1,0:T(8,128)S(1)} %collective-permute-done.x_far_ref.x_far_msg, ...), custom_call_target="tpu_custom_call" | custom-call | tf_op jit(solution)/shard_map/pallas_call | solution.py:622
  15.2 3.6 %all-to-all-start = ((f32[32,3,4,128]{3,2,1,0:T(4,128)}), f32[32,3,4,128]{3,2,1,0:T(4,128)S(1)}, u32[]{:S(2)}, u32[]{:S(2)}) async-start(f32[32,3,4,128]{3,2,1,0:T(4,128)} %get-tuple-element.51), calls=%async_computation | async-start | bytes 393216 | tf_op jit(solution)/shard_map/all_to_all | solution.py:653
  18.7 0.3 %collective-permute-start.4 = (f32[136,128]{1,0:T(8,128)S(1)}, f32[136,128]{1,0:T(8,128)S(1)}, u32[]{:S(2)}, u32[]{:S(2)}) collective-permute-start(f32[136,128]{1,0:T(8,128)S(1)} %get-tuple-element.43), channel_id=1, source_target_pairs={{0,4},{8,12},{16,20},{24,28},{4,0},{12,8},{20,16},{28,24},{1,5},{9... | collective-permute-start | bytes 208904 | tf_op jit(solution)/shard_map/ppermute | solution.py:640
  19.1 0.7 %collective-permute-start.5 = (f32[136,128]{1,0:T(8,128)S(1)}, f32[136,128]{1,0:T(8,128)S(1)}, u32[]{:S(2)}, u32[]{:S(2)}) collective-permute-start(f32[136,128]{1,0:T(8,128)S(1)} %get-tuple-element.44), channel_id=1, source_target_pairs={{4,8},{12,16},{20,24},{8,4},{16,12},{24,20},{5,9},{13,17},{21,25},... | collective-permute-start | bytes 208904 | tf_op jit(solution)/shard_map/ppermute | solution.py:640
  19.7 0.3 %collective-permute-done.4.x_near_ref = f32[136,128]{1,0:T(8,128)S(1)} collective-permute-done((f32[136,128]{1,0:T(8,128)S(1)}, f32[136,128]{1,0:T(8,128)S(1)}, u32[]{:S(2)}, u32[]{:S(2)}) %collective-permute-start.4) | collective-permute-done | bytes 69664 | tf_op jit(solution)/shard_map/ppermute | solution.py:640
  20.1 0.0 collective-permute-done.5.x_far_ref
  20.1 0.2 shard_map.98
  20.2 7.9 %all-to-all-done.total_ref = f32[32,3,4,128]{3,2,1,0:T(4,128)S(1)} async-done(((f32[32,3,4,128]{3,2,1,0:T(4,128)}), f32[32,3,4,128]{3,2,1,0:T(4,128)S(1)}, u32[]{:S(2)}, u32[]{:S(2)}) %all-to-all-start) | async-done | bytes 196640 | tf_op jit(solution)/shard_map/all_to_all | solution.py:653
  28.1 1.4 %shard_map.99 = (f32[4,64,128]{2,1,0:T(8,128)}, f32[4,64,128]{2,1,0:T(8,128)}) custom-call(f32[4,64,128]{2,1,0:T(8,128)S(1)} %get-tuple-element.41.conc_ref, f32[4,64,128]{2,1,0:T(8,128)S(1)} %get-tuple-element.42.pot_ref, f32[4,64,128]{2,1,0:T(8,128)S(1)} %copy-done, f32[4,64,128]{2,1,0:T(8,128)S(1)} %copy-done.1, ...), custom_call_target="tpu_custom_call" | custom-call | tf_op jit(solution)/shard_map/pallas_call | solution.py:622
Async XLA Ops:
  0.6 11.5 %copy-start.1 = (f32[4,64,128]{2,1,0:T(8,128)S(1)}, f32[4,64,128]{2,1,0:T(8,128)}, u32[]{:S(2)}) copy-start(f32[4,64,128]{2,1,0:T(8,128)} %pots_ref.5) | copy-start | bytes 393220
  0.6 11.5 %copy-start = (f32[4,64,128]{2,1,0:T(8,128)S(1)}, f32[4,64,128]{2,1,0:T(8,128)}, u32[]{:S(2)}) copy-start(f32[4,64,128]{2,1,0:T(8,128)} %mass_ref.5) | copy-start | bytes 393220
  0.7 11.5 %copy-start.3 = (f32[4,64,128]{2,1,0:T(8,128)S(1)}, f32[4,64,128]{2,1,0:T(8,128)}, u32[]{:S(2)}) copy-start(f32[4,64,128]{2,1,0:T(8,128)} %pot_ref.3) | copy-start | bytes 393220
  0.7 11.5 %copy-start.2 = (f32[4,64,128]{2,1,0:T(8,128)S(1)}, f32[4,64,128]{2,1,0:T(8,128)}, u32[]{:S(2)}) copy-start(f32[4,64,128]{2,1,0:T(8,128)} %conc_ref.3) | copy-start | bytes 393220
  0.7 11.5 %copy-start.5 = (s32[4,64,128]{2,1,0:T(8,128)S(1)}, s32[4,64,128]{2,1,0:T(8,128)}, u32[]{:S(2)}) copy-start(s32[4,64,128]{2,1,0:T(8,128)} %class_ref) | copy-start | bytes 393220
  0.7 11.5 %copy-start.4 = (s32[4,64,128]{2,1,0:T(8,128)S(1)}, s32[4,64,128]{2,1,0:T(8,128)}, u32[]{:S(2)}) copy-start(s32[4,64,128]{2,1,0:T(8,128)} %mask_ref) | copy-start | bytes 393220
  2.0 10.2 %copy-start.6 = (s32[8,64]{1,0:T(8,128)S(1)}, s32[8,64]{1,0:T(8,128)}, u32[]{:S(2)}) copy-start(s32[8,64]{1,0:T(8,128)} %owner_ref.3) | copy-start | bytes 6148
  2.0 10.1 %collective-permute-start.2 = (f32[200,128]{1,0:T(8,128)S(1)}, f32[200,128]{1,0:T(8,128)S(1)}, u32[]{:S(2)}, u32[]{:S(2)}) collective-permute-start(f32[200,128]{1,0:T(8,128)S(1)} %get-tuple-element.29), channel_id=1, source_target_pairs={{1,2},{2,1},{5,6},{6,5},{9,10},{10,9},{13,14},{14,13},{17,18},{18,... | collective-permute-start | bytes 307208 | tf_op jit(solution)/shard_map/ppermute | solution.py:640
  2.7 11.2 %collective-permute-start = (f32[192,128]{1,0:T(8,128)S(1)}, f32[192,128]{1,0:T(8,128)S(1)}, u32[]{:S(2)}, u32[]{:S(2)}) collective-permute-start(f32[192,128]{1,0:T(8,128)S(1)} %get-tuple-element.27), channel_id=1, source_target_pairs={{4,8},{12,16},{20,24},{8,4},{16,12},{24,20},{5,9},{13,17},{21,25},... | collective-permute-start | bytes 294920 | tf_op jit(solution)/shard_map/ppermute | solution.py:640
  3.4 8.8 %copy-start.7 = (f32[8]{0:T(128)S(1)}, f32[8]{0:T(128)}, u32[]{:S(2)}) copy-start(f32[8]{0:T(128)} %table_ref.1) | copy-start | bytes 100
  3.4 10.5 %collective-permute-start.1 = (f32[192,128]{1,0:T(8,128)S(1)}, f32[192,128]{1,0:T(8,128)S(1)}, u32[]{:S(2)}, u32[]{:S(2)}) collective-permute-start(f32[192,128]{1,0:T(8,128)S(1)} %get-tuple-element.28), channel_id=1, source_target_pairs={{0,4},{8,12},{16,20},{24,28},{4,0},{12,8},{20,16},{28,24},{1,5},{9... | collective-permute-start | bytes 294920 | tf_op jit(solution)/shard_map/ppermute | solution.py:640
  7.7 6.2 %collective-permute-start.3 = (f32[40,128]{1,0:T(8,128)S(1)}, f32[40,128]{1,0:T(8,128)S(1)}, u32[]{:S(2)}, u32[]{:S(2)}) collective-permute-start(f32[40,128]{1,0:T(8,128)S(1)} %get-tuple-element.31), channel_id=1, source_target_pairs={{0,1},{2,3},{1,0},{3,2},{4,5},{6,7},{5,4},{7,6},{8,9},{10,11},{9,8... | collective-permute-start | bytes 61448 | tf_op jit(solution)/shard_map/ppermute | solution.py:640
  15.2 13.0 %all-to-all-start = ((f32[32,3,4,128]{3,2,1,0:T(4,128)}), f32[32,3,4,128]{3,2,1,0:T(4,128)S(1)}, u32[]{:S(2)}, u32[]{:S(2)}) async-start(f32[32,3,4,128]{3,2,1,0:T(4,128)} %get-tuple-element.51), calls=%async_computation | async-start | bytes 393216 | tf_op jit(solution)/shard_map/all_to_all | solution.py:653
  18.7 1.3 %collective-permute-start.4 = (f32[136,128]{1,0:T(8,128)S(1)}, f32[136,128]{1,0:T(8,128)S(1)}, u32[]{:S(2)}, u32[]{:S(2)}) collective-permute-start(f32[136,128]{1,0:T(8,128)S(1)} %get-tuple-element.43), channel_id=1, source_target_pairs={{0,4},{8,12},{16,20},{24,28},{4,0},{12,8},{20,16},{28,24},{1,5},{9... | collective-permute-start | bytes 208904 | tf_op jit(solution)/shard_map/ppermute | solution.py:640
  19.1 1.0 %collective-permute-start.5 = (f32[136,128]{1,0:T(8,128)S(1)}, f32[136,128]{1,0:T(8,128)S(1)}, u32[]{:S(2)}, u32[]{:S(2)}) collective-permute-start(f32[136,128]{1,0:T(8,128)S(1)} %get-tuple-element.44), channel_id=1, source_target_pairs={{4,8},{12,16},{20,24},{8,4},{16,12},{24,20},{5,9},{13,17},{21,25},... | collective-permute-start | bytes 208904 | tf_op jit(solution)/shard_map/ppermute | solution.py:640

commit v12 on v11

--- a/solution.py
+++ b/solution.py
@@ -128,7 +128,7 @@
         self.slots = slots if slots <= 64 else 0
 
     def slot_of(self, g, h):
-        return (-h % self.groups) * self.owners + g
+        return (-h % self.groups) * self.owners + self.owners - 1 - g
 
 
 def side_rows(plan, rows, which):
@@ -445,7 +445,7 @@
                 total_out[slot, part] = main[4 * part : 4 * part + 4]
             for row, values in beside:
                 total_out[slot, row // 4, pl.ds(row % 4, 1), :] = values[g : g + 1]
-        some = pl.ds(plan.slot_of(0, plane), plan.owners)
+        some = pl.ds(plan.slot_of(plan.owners - 1, plane), plan.owners)
         copies.append(
             pltpu.make_async_copy(total_out.at[some], total_hbm.at[some], sems.at[plane])
         )
@@ -494,8 +494,9 @@
 
 
 def beside_kernel(
-    plan, x_near_ref, x_far_ref, mob_ref, raw_ref, x_near_msg, x_far_msg, y_near_msg, y_far_msg,
-    faces_out, diagonal_out, scale_out, ends_out,
+    plan, x_near_ref, x_far_ref, conc_ref, pot_ref, mass_ref, pots_ref, mob_ref, raw_ref,
+    x_near_msg, x_far_msg, y_near_msg, y_far_msg,
+    faces_out, diagonal_out, scale_out, mass_out, pots_out,
 ):
     mobility = mob_ref[...]
     sides = received("gx", x_near_msg, x_far_msg)
@@ -504,6 +505,7 @@
         side_columns(plan, rows, 2) for rows in ends
     )
     faces, diagonal = faces_of(mobility, neighbours(mobility, halo))
+    block_terms = faces, diagonal, mass_ref[...], pots_ref[...]
     for i, face in enumerate(faces):
         faces_out[i] = face
     diagonal_out[...] = diagonal
@@ -516,6 +518,7 @@
         jnp.concatenate([mobility[x, y : y + 1] for x in range(plan.x)], axis=0)
         for y in (0, plan.y - 1)
     ]
+    halos = [[side_rows(plan, rows, which) for rows in corners] for which in range(2)]
     for end, rows in enumerate(ends):
 
         def row(which):
@@ -539,14 +542,16 @@
         )
         new = relax_pair(row(0), row(1), *excess, diagonal, scale_from(diagonal))
         for which, values in enumerate(new):
-            ends_out[pl.ds((2 * which + end) * plan.x, plan.x), :] = jnp.where(
-                inside[end], values, 0.0
-            )
+            halos[which].append(jnp.where(inside[end], values, 0.0)[:, None])
+    conc, pot = conc_ref[...], pot_ref[...]
+    mass_out[...], pots_out[...] = excess_of(
+        conc, pot, neighbours(conc, halos[0]), neighbours(pot, halos[1]), *block_terms
+    )
 
 
 def last_kernel(
     plan, conc_ref, pot_ref, mass_ref, pots_ref, faces_ref, diagonal_ref, scale_ref,
-    x_near_ref, x_far_ref, ends_ref, spread_ref, total_ref,
+    spread_ref, total_ref,
     conc_hbm, pot_hbm, conc_out, pot_out, sems,
 ):
     parts = []
@@ -565,46 +570,37 @@
         (((1,), (0,)), ((), ())),
         preferred_element_type=F32,
     )
-    sides = received("gx", x_near_ref, x_far_ref)
-
-    def updated(which, ref):
+
+    def shifted(which):
         lanes = slice(which * plan.p, (which + 1) * plan.p)
-        corr = own[:, lanes]
-        slabs = [side_rows(plan, sides[0], which)]
-        slabs += [ref[pl.ds(x, 1)] for x in range(plan.x)]
-        slabs.append(side_rows(plan, sides[1], which))
-        order = [plan.half_x, *[x >> 1 for x in range(plan.x)], plan.half_x + 1]
-        slabs = [
-            slab + corr[x * plan.y : (x + 1) * plan.y][None] for slab, x in zip(slabs, order)
-        ]
-        ends = []
-        for end, begin in enumerate((plan.low_row, plan.high_row)):
-            rows = ends_ref[pl.ds((2 * which + end) * plan.x, plan.x), :]
-            ends.append([
-                (rows[x : x + 1] + solved[begin + (x >> 1) : begin + (x >> 1) + 1, lanes])[None]
-                for x in range(plan.x)
-            ])
-        return slabs, ends
-
-    conc, conc_ends = updated(0, conc_ref)
-    pot, pot_ends = updated(1, pot_ref)
-
-    def beside(slabs, ends, x):
-        here = slabs[x + 1]
-        return (
-            slabs[x], slabs[x + 2], *y_pair(here, ends[0][x], ends[1][x]), *plane_pair(here)
-        )
-
+        rows = [own[i * plan.y : (i + 1) * plan.y, lanes][None] for i in range(plan.half_x + 2)]
+        beside = []
+        for i in range(plan.half_x):
+            ends = [
+                solved[begin + i : begin + i + 1, lanes][None]
+                for begin in (plan.low_row, plan.high_row)
+            ]
+            beside.append((*y_pair(rows[i], *ends), *plane_pair(rows[i])))
+        return [rows[plan.half_x], *rows[: plan.half_x], rows[plan.half_x + 1]], beside
+
+    conc_rows, conc_beside = shifted(0)
+    pot_rows, pot_beside = shifted(1)
+    conc_sums = [a + b + c + d for a, b, c, d in conc_beside]
     copies = []
     for x in range(plan.x):
         one = pl.ds(x, 1)
+        i = x >> 1
+        low, high = (i, i + 1) if x % 2 == 0 else (i + 1, i + 2)
         diagonal = diagonal_ref[one]
-        excess = excess_of(
-            conc[x + 1], pot[x + 1], beside(conc, conc_ends, x), beside(pot, pot_ends, x),
-            [faces_ref[i, one] for i in range(6)], diagonal, mass_ref[one], pots_ref[one],
-        )
+        conc, pot = conc_rows[i + 1], pot_rows[i + 1]
+        excess_mass = mass_ref[one] - conc - diagonal * pot
+        beside = (pot_rows[low], pot_rows[high], *pot_beside[i])
+        for k, other in enumerate(beside):
+            excess_mass = excess_mass + faces_ref[k, one] * other
+        excess_pot = (pots_ref[one] - pot) + (split_slope + 6.0 * interface) * conc
+        excess_pot = excess_pot - interface * (conc_rows[low] + conc_rows[high] + conc_sums[i])
         conc_out[one], pot_out[one] = relax_pair(
-            conc[x + 1], pot[x + 1], *excess, diagonal, scale_ref[one]
+            conc_ref[one] + conc, pot_ref[one] + pot, excess_mass, excess_pot, diagonal, scale_ref[one]
         )
         for source, target in ((conc_out, conc_hbm), (pot_out, pot_hbm)):
             copies.append(
@@ -727,18 +723,21 @@
     total = gather_totals(plan, total, y_near, y_far)
     far = swap_far("gx", far)
     near = swap_near("gx", near)
-    faces, diagonal, scale, ends = call(
+    faces, diagonal, scale, mass_part, pot_part = call(
         beside_kernel,
         plan,
-        [(6, *block), block, block, (4 * plan.x, plan.p)],
-        [near, far, mob, raw, x_near, x_far, y_near, y_far],
+        [(6, *block), block, block, block, block],
+        [
+            near, far, conc, pot, mass_source, pot_source, mob, raw,
+            x_near, x_far, y_near, y_far,
+        ],
     )
     return tuple(
         call(
             last_kernel,
             plan,
             [block, block],
-            [conc, pot, mass_source, pot_source, faces, diagonal, scale, near, far, ends, spread, total],
+            [conc, pot, mass_part, pot_part, faces, diagonal, scale, spread, total],
             out_far=(0, 1),
             scratch=(
                 pltpu.VMEM(block, F32),

time: 29.8 us -> 29.4 us (0.987)
  the two profiles are of different devices: /device:TPU:0 before, /device:TPU:1 now
where the time goes in v12:
time: 29.4 us; the launch traced here: 29.1 us
  starting transfers between devices  17.8 us (61%)
  Pallas kernels  5.27 us (18%)
  waiting for transfers between devices  5.25 us (18%)
  between operations  0.82 us (3%)
    ppermute x6, starting transfers between devices, swap_near(): return lax.ppermute(rows, axis, pairs + [(j, i) for i, j in pairs])  13.2 us
    pallas_call x5, Pallas kernels, call(): pl.pallas_call(functools.partial(kernel, plan), out_shape=[jax.ShapeDtype...  5.27 us
    all_to_all x1, starting transfers between devices, gather_totals(): lax.all_to_all(total, ('gx', 'gy'), split_axis=0, concat_axis=0, axis_ind...  4.59 us
    ppermute x6, waiting for transfers between devices, swap_near(): return lax.ppermute(rows, axis, pairs + [(j, i) for i, j in pairs])  3.17 us
    all_to_all x1, waiting for transfers between devices, gather_totals(): lax.all_to_all(total, ('gx', 'gy'), split_axis=0, concat_axis=0, axis_ind...  2.08 us
  transfers between devices with their start and end apart: 7, of which 2 were waited for; matrix products, arithmetic and copies ran while one was open for 0% of the time, Pallas kernels for 5%

profile of v12, /device:TPU:1, one launch (start us, length us, event | category | flops | bytes accessed | tf_op | source)
XLA Modules:
  0.0 29.1 jit_solution(17635326802428710227)
XLA Ops:
  0.6 0.0 copy-start.1
  0.6 0.0 copy-start
  0.7 0.0 copy-start.3
  0.7 0.0 copy-start.2
  0.7 0.0 copy-start.5
  0.7 0.0 copy-start.4
  0.7 1.3 %shard_map.95 = (f32[192,128]{1,0:T(8,128)S(1)}, f32[192,128]{1,0:T(8,128)S(1)}, f32[40,128]{1,0:T(8,128)S(1)}, f32[200,128]{1,0:T(8,128)S(1)}) custom-call(f32[4,64,128]{2,1,0:T(8,128)} %conc_ref.3, f32[4,64,128]{2,1,0:T(8,128)} %pot_ref.3, s32[4,64,128]{2,1,0:T(8,128)} %mask_ref, s32[4,64,128]{2,1,0:T(8,128)} %class_ref, f32[4,64,128]{2,1,0:T(8,128)} %mass_ref.5, ...), custom_call_target="tpu_custom_call" | custom-call | tf_op jit(solution)/shard_map/pallas_call | solution.py:618
  2.0 0.0 copy-start.6
  2.0 0.7 %collective-permute-start.2 = (f32[200,128]{1,0:T(8,128)S(1)}, f32[200,128]{1,0:T(8,128)S(1)}, u32[]{:S(2)}, u32[]{:S(2)}) collective-permute-start(f32[200,128]{1,0:T(8,128)S(1)} %get-tuple-element.30), channel_id=1, source_target_pairs={{1,2},{2,1},{5,6},{6,5},{9,10},{10,9},{13,14},{14,13},{17,18},{18,... | collective-permute-start | bytes 307208 | tf_op jit(solution)/shard_map/ppermute | solution.py:636
  2.7 4.5 %collective-permute-start = (f32[192,128]{1,0:T(8,128)S(1)}, f32[192,128]{1,0:T(8,128)S(1)}, u32[]{:S(2)}, u32[]{:S(2)}) collective-permute-start(f32[192,128]{1,0:T(8,128)S(1)} %get-tuple-element.28), channel_id=1, source_target_pairs={{4,8},{12,16},{20,24},{8,4},{16,12},{24,20},{5,9},{13,17},{21,25},... | collective-permute-start | bytes 294920 | tf_op jit(solution)/shard_map/ppermute | solution.py:636
  7.2 0.0 copy-start.7
  7.2 0.1 collective-permute-start.1
  7.3 4.2 %collective-permute-start.3 = (f32[40,128]{1,0:T(8,128)S(1)}, f32[40,128]{1,0:T(8,128)S(1)}, u32[]{:S(2)}, u32[]{:S(2)}) collective-permute-start(f32[40,128]{1,0:T(8,128)S(1)} %get-tuple-element.32), channel_id=1, source_target_pairs={{0,1},{2,3},{1,0},{3,2},{4,5},{6,7},{5,4},{7,6},{8,9},{10,11},{9,8... | collective-permute-start | bytes 61448 | tf_op jit(solution)/shard_map/ppermute | solution.py:636
  11.5 0.0 collective-permute-done.2.y_far_ref.y_far_msg
  11.5 0.0 copy-done.1
  11.5 0.0 copy-done
  11.5 0.0 copy-done.3
  11.5 0.0 copy-done.2
  11.5 0.0 copy-done.5
  11.5 0.0 copy-done.4
  11.5 0.0 copy-done.6
  11.5 0.0 copy-done.7
  11.5 1.1 %shard_map.96 = (f32[4,64,128]{2,1,0:T(8,128)S(1)}, f32[8,256]{1,0:T(8,128)S(1)}, f32[256,24]{1,0:T(8,128)S(1)}, f32[8,128]{1,0:T(8,128)S(1)}, f32[5,4,64,128]{3...) custom-call(f32[4,64,128]{2,1,0:T(8,128)S(1)} %copy-done.2, ...), custom_call_target="tpu_custom_call" | custom-call | tf_op jit(solution)/shard_map/pallas_call | solution.py:618
  12.6 0.0 collective-permute-done.3.y_near_ref.y_near_msg
  12.6 0.0 collective-permute-done.x_far_ref.x_far_msg
  12.6 0.0 collective-permute-done.1.x_near_ref.x_near_msg
  12.6 1.3 %shard_map.97 = (f32[4,64,128]{2,1,0:T(8,128)S(1)}, f32[4,64,128]{2,1,0:T(8,128)S(1)}, f32[32,3,4,128]{3,2,1,0:T(4,128)}, f32[16,128]{1,0:T(8,128)S(1)}, f32[136,128]{1,0:T(8,128)S(1)}, /*index=5*/f32[136,128]{1,0:T(8,128)S(1)}) custom-call(f32[192,128]{1,0:T(8,128)S(1)} %collective-permute-done.x_far_ref.x_far_msg, ...), custom_call_target="tpu_custom_call" | custom-call | tf_op jit(solution)/shard_map/pallas_call | solution.py:618
  13.9 4.6 %all-to-all-start = ((f32[32,3,4,128]{3,2,1,0:T(4,128)}), f32[32,3,4,128]{3,2,1,0:T(4,128)S(1)}, u32[]{:S(2)}, u32[]{:S(2)}) async-start(f32[32,3,4,128]{3,2,1,0:T(4,128)} %get-tuple-element.53), calls=%async_computation | async-start | bytes 393216 | tf_op jit(solution)/shard_map/all_to_all | solution.py:649
  18.5 0.3 %collective-permute-start.4 = (f32[136,128]{1,0:T(8,128)S(1)}, f32[136,128]{1,0:T(8,128)S(1)}, u32[]{:S(2)}, u32[]{:S(2)}) collective-permute-start(f32[136,128]{1,0:T(8,128)S(1)} %get-tuple-element.44), channel_id=1, source_target_pairs={{0,4},{8,12},{16,20},{24,28},{4,0},{12,8},{20,16},{28,24},{1,5},{9... | collective-permute-start | bytes 208904 | tf_op jit(solution)/shard_map/ppermute | solution.py:636
  18.9 3.4 %collective-permute-start.5 = (f32[136,128]{1,0:T(8,128)S(1)}, f32[136,128]{1,0:T(8,128)S(1)}, u32[]{:S(2)}, u32[]{:S(2)}) collective-permute-start(f32[136,128]{1,0:T(8,128)S(1)} %get-tuple-element.45), channel_id=1, source_target_pairs={{4,8},{12,16},{20,24},{8,4},{16,12},{24,20},{5,9},{13,17},{21,25},... | collective-permute-start | bytes 208904 | tf_op jit(solution)/shard_map/ppermute | solution.py:636
  22.3 0.0 collective-permute-done.4.x_near_ref
  22.3 3.1 %collective-permute-done.5.x_far_ref = f32[136,128]{1,0:T(8,128)S(1)} collective-permute-done((f32[136,128]{1,0:T(8,128)S(1)}, f32[136,128]{1,0:T(8,128)S(1)}, u32[]{:S(2)}, u32[]{:S(2)}) %collective-permute-start.5) | collective-permute-done | bytes 69664 | tf_op jit(solution)/shard_map/ppermute | solution.py:636
  25.4 0.3 %shard_map.98 = (f32[6,4,64,128]{3,2,1,0:T(8,128)S(1)}, f32[4,64,128]{2,1,0:T(8,128)S(1)}, f32[4,64,128]{2,1,0:T(8,128)S(1)}, f32[4,64,128]{2,1,0:T(8,128)S(1)}, f32[4,64,128]{2,1,0:T(8,128)S(1)}) custom-call(f32[136,128]{1,0:T(8,128)S(1)} %collective-permute-done.4.x_near_ref, f32[136,128]{1,0:T(8,128)S(1)} %collective-permute-done.5.x_far_ref, ...), custom_call_target="tpu_custom_call" | custom-call | tf_op jit(solution)/shard_map/pallas_call | solution.py:618
  25.8 2.1 %all-to-all-done.total_ref = f32[32,3,4,128]{3,2,1,0:T(4,128)S(1)} async-done(((f32[32,3,4,128]{3,2,1,0:T(4,128)}), f32[32,3,4,128]{3,2,1,0:T(4,128)S(1)}, u32[]{:S(2)}, u32[]{:S(2)}) %all-to-all-start) | async-done | bytes 196640 | tf_op jit(solution)/shard_map/all_to_all | solution.py:649
  27.8 1.3 %shard_map.99 = (f32[4,64,128]{2,1,0:T(8,128)}, f32[4,64,128]{2,1,0:T(8,128)}) custom-call(f32[4,64,128]{2,1,0:T(8,128)S(1)} %get-tuple-element.42.conc_ref, f32[4,64,128]{2,1,0:T(8,128)S(1)} %get-tuple-element.43.pot_ref, f32[4,64,128]{2,1,0:T(8,128)S(1)} %get-tuple-element.47.mass_ref, f32[4,64,128]{2,1,0:T(8,128)S(1)} %get-tuple-element.48.pots_ref, ...), custom_call_target="tpu_custom_call" | custom-call | tf_op jit(solution)/shard_map/pallas_call | solution.py:618
Async XLA Ops:
  0.6 10.8 %copy-start.1 = (f32[4,64,128]{2,1,0:T(8,128)S(1)}, f32[4,64,128]{2,1,0:T(8,128)}, u32[]{:S(2)}) copy-start(f32[4,64,128]{2,1,0:T(8,128)} %pots_ref.5) | copy-start | bytes 393220
  0.6 10.8 %copy-start = (f32[4,64,128]{2,1,0:T(8,128)S(1)}, f32[4,64,128]{2,1,0:T(8,128)}, u32[]{:S(2)}) copy-start(f32[4,64,128]{2,1,0:T(8,128)} %mass_ref.5) | copy-start | bytes 393220
  0.7 10.8 %copy-start.3 = (f32[4,64,128]{2,1,0:T(8,128)S(1)}, f32[4,64,128]{2,1,0:T(8,128)}, u32[]{:S(2)}) copy-start(f32[4,64,128]{2,1,0:T(8,128)} %pot_ref.3) | copy-start | bytes 393220
  0.7 10.8 %copy-start.2 = (f32[4,64,128]{2,1,0:T(8,128)S(1)}, f32[4,64,128]{2,1,0:T(8,128)}, u32[]{:S(2)}) copy-start(f32[4,64,128]{2,1,0:T(8,128)} %conc_ref.3) | copy-start | bytes 393220
  0.7 10.8 %copy-start.5 = (s32[4,64,128]{2,1,0:T(8,128)S(1)}, s32[4,64,128]{2,1,0:T(8,128)}, u32[]{:S(2)}) copy-start(s32[4,64,128]{2,1,0:T(8,128)} %class_ref) | copy-start | bytes 393220
  0.7 10.8 %copy-start.4 = (s32[4,64,128]{2,1,0:T(8,128)S(1)}, s32[4,64,128]{2,1,0:T(8,128)}, u32[]{:S(2)}) copy-start(s32[4,64,128]{2,1,0:T(8,128)} %mask_ref) | copy-start | bytes 393220
  2.0 9.5 %copy-start.6 = (s32[8,64]{1,0:T(8,128)S(1)}, s32[8,64]{1,0:T(8,128)}, u32[]{:S(2)}) copy-start(s32[8,64]{1,0:T(8,128)} %owner_ref.3) | copy-start | bytes 6148
  2.0 9.5 %collective-permute-start.2 = (f32[200,128]{1,0:T(8,128)S(1)}, f32[200,128]{1,0:T(8,128)S(1)}, u32[]{:S(2)}, u32[]{:S(2)}) collective-permute-start(f32[200,128]{1,0:T(8,128)S(1)} %get-tuple-element.30), channel_id=1, source_target_pairs={{1,2},{2,1},{5,6},{6,5},{9,10},{10,9},{13,14},{14,13},{17,18},{18,... | collective-permute-start | bytes 307208 | tf_op jit(solution)/shard_map/ppermute | solution.py:636
  2.7 10.0 %collective-permute-start = (f32[192,128]{1,0:T(8,128)S(1)}, f32[192,128]{1,0:T(8,128)S(1)}, u32[]{:S(2)}, u32[]{:S(2)}) collective-permute-start(f32[192,128]{1,0:T(8,128)S(1)} %get-tuple-element.28), channel_id=1, source_target_pairs={{4,8},{12,16},{20,24},{8,4},{16,12},{24,20},{5,9},{13,17},{21,25},... | collective-permute-start | bytes 294920 | tf_op jit(solution)/shard_map/ppermute | solution.py:636
  7.2 4.3 %copy-start.7 = (f32[8]{0:T(128)S(1)}, f32[8]{0:T(128)}, u32[]{:S(2)}) copy-start(f32[8]{0:T(128)} %table_ref.1) | copy-start | bytes 100
  7.2 5.4 %collective-permute-start.1 = (f32[192,128]{1,0:T(8,128)S(1)}, f32[192,128]{1,0:T(8,128)S(1)}, u32[]{:S(2)}, u32[]{:S(2)}) collective-permute-start(f32[192,128]{1,0:T(8,128)S(1)} %get-tuple-element.29), channel_id=1, source_target_pairs={{0,4},{8,12},{16,20},{24,28},{4,0},{12,8},{20,16},{28,24},{1,5},{9... | collective-permute-start | bytes 294920 | tf_op jit(solution)/shard_map/ppermute | solution.py:636
  7.3 5.4 %collective-permute-start.3 = (f32[40,128]{1,0:T(8,128)S(1)}, f32[40,128]{1,0:T(8,128)S(1)}, u32[]{:S(2)}, u32[]{:S(2)}) collective-permute-start(f32[40,128]{1,0:T(8,128)S(1)} %get-tuple-element.32), channel_id=1, source_target_pairs={{0,1},{2,3},{1,0},{3,2},{4,5},{6,7},{5,4},{7,6},{8,9},{10,11},{9,8... | collective-permute-start | bytes 61448 | tf_op jit(solution)/shard_map/ppermute | solution.py:636
  13.9 13.9 %all-to-all-start = ((f32[32,3,4,128]{3,2,1,0:T(4,128)}), f32[32,3,4,128]{3,2,1,0:T(4,128)S(1)}, u32[]{:S(2)}, u32[]{:S(2)}) async-start(f32[32,3,4,128]{3,2,1,0:T(4,128)} %get-tuple-element.53), calls=%async_computation | async-start | bytes 393216 | tf_op jit(solution)/shard_map/all_to_all | solution.py:649
  18.5 3.8 %collective-permute-start.4 = (f32[136,128]{1,0:T(8,128)S(1)}, f32[136,128]{1,0:T(8,128)S(1)}, u32[]{:S(2)}, u32[]{:S(2)}) collective-permute-start(f32[136,128]{1,0:T(8,128)S(1)} %get-tuple-element.44), channel_id=1, source_target_pairs={{0,4},{8,12},{16,20},{24,28},{4,0},{12,8},{20,16},{28,24},{1,5},{9... | collective-permute-start | bytes 208904 | tf_op jit(solution)/shard_map/ppermute | solution.py:636
  18.9 6.6 %collective-permute-start.5 = (f32[136,128]{1,0:T(8,128)S(1)}, f32[136,128]{1,0:T(8,128)S(1)}, u32[]{:S(2)}, u32[]{:S(2)}) collective-permute-start(f32[136,128]{1,0:T(8,128)S(1)} %get-tuple-element.45), channel_id=1, source_target_pairs={{4,8},{12,16},{20,24},{8,4},{16,12},{24,20},{5,9},{13,17},{21,25},... | collective-permute-start | bytes 208904 | tf_op jit(solution)/shard_map/ppermute | solution.py:636

commit v13 on v12

--- a/solution.py
+++ b/solution.py
@@ -128,7 +128,9 @@
         self.slots = slots if slots <= 64 else 0
 
     def slot_of(self, g, h):
-        return (-h % self.groups) * self.owners + self.owners - 1 - g
+        last = self.groups - 1
+        place = 0 if h == 0 else 1 if h == last else h + 1
+        return place * self.owners + self.owners - 1 - g
 
 
 def side_rows(plan, rows, which):

time: 29.4 us -> 29.3 us (level)
  no operation moved by 1% of the time
where the time goes in v13:
time: 29.3 us; the launch traced here: 29.1 us
  starting transfers between devices  17.8 us (61%)
  Pallas kernels  5.26 us (18%)
  waiting for transfers between devices  5.18 us (18%)
  between operations  0.82 us (3%)
    ppermute x6, starting transfers between devices, swap_near(): return lax.ppermute(rows, axis, pairs + [(j, i) for i, j in pairs])  13.2 us
    pallas_call x5, Pallas kernels, call(): pl.pallas_call(functools.partial(kernel, plan), out_shape=[jax.ShapeDtype...  5.26 us
    all_to_all x1, starting transfers between devices, gather_totals(): lax.all_to_all(total, ('gx', 'gy'), split_axis=0, concat_axis=0, axis_ind...  4.59 us
    ppermute x6, waiting for transfers between devices, swap_near(): return lax.ppermute(rows, axis, pairs + [(j, i) for i, j in pairs])  2.98 us
    all_to_all x1, waiting for transfers between devices, gather_totals(): lax.all_to_all(total, ('gx', 'gy'), split_axis=0, concat_axis=0, axis_ind...  2.2 us
  transfers between devices with their start and end apart: 7, of which 2 were waited for; matrix products, arithmetic and copies ran while one was open for 0% of the time, Pallas kernels for 5%

profile of v13, /device:TPU:1, one launch (start us, length us, event | category | flops | bytes accessed | tf_op | source)
XLA Modules:
  0.0 29.1 jit_solution(16460333894256535451)
XLA Ops:
  0.6 0.0 copy-start.1
  0.6 0.0 copy-start
  0.7 0.0 copy-start.3
  0.7 0.0 copy-start.2
  0.7 0.0 copy-start.5
  0.7 0.0 copy-start.4
  0.7 1.3 %shard_map.95 = (f32[192,128]{1,0:T(8,128)S(1)}, f32[192,128]{1,0:T(8,128)S(1)}, f32[40,128]{1,0:T(8,128)S(1)}, f32[200,128]{1,0:T(8,128)S(1)}) custom-call(f32[4,64,128]{2,1,0:T(8,128)} %conc_ref.3, f32[4,64,128]{2,1,0:T(8,128)} %pot_ref.3, s32[4,64,128]{2,1,0:T(8,128)} %mask_ref, s32[4,64,128]{2,1,0:T(8,128)} %class_ref, f32[4,64,128]{2,1,0:T(8,128)} %mass_ref.5, ...), custom_call_target="tpu_custom_call" | custom-call | tf_op jit(solution)/shard_map/pallas_call | solution.py:620
  2.0 0.0 copy-start.6
  2.0 0.7 %collective-permute-start.2 = (f32[200,128]{1,0:T(8,128)S(1)}, f32[200,128]{1,0:T(8,128)S(1)}, u32[]{:S(2)}, u32[]{:S(2)}) collective-permute-start(f32[200,128]{1,0:T(8,128)S(1)} %get-tuple-element.30), channel_id=1, source_target_pairs={{1,2},{2,1},{5,6},{6,5},{9,10},{10,9},{13,14},{14,13},{17,18},{18,... | collective-permute-start | bytes 307208 | tf_op jit(solution)/shard_map/ppermute | solution.py:638
  2.7 4.5 %collective-permute-start = (f32[192,128]{1,0:T(8,128)S(1)}, f32[192,128]{1,0:T(8,128)S(1)}, u32[]{:S(2)}, u32[]{:S(2)}) collective-permute-start(f32[192,128]{1,0:T(8,128)S(1)} %get-tuple-element.28), channel_id=1, source_target_pairs={{4,8},{12,16},{20,24},{8,4},{16,12},{24,20},{5,9},{13,17},{21,25},... | collective-permute-start | bytes 294920 | tf_op jit(solution)/shard_map/ppermute | solution.py:638
  7.2 0.0 copy-start.7
  7.2 0.1 collective-permute-start.1
  7.3 4.2 %collective-permute-start.3 = (f32[40,128]{1,0:T(8,128)S(1)}, f32[40,128]{1,0:T(8,128)S(1)}, u32[]{:S(2)}, u32[]{:S(2)}) collective-permute-start(f32[40,128]{1,0:T(8,128)S(1)} %get-tuple-element.32), channel_id=1, source_target_pairs={{0,1},{2,3},{1,0},{3,2},{4,5},{6,7},{5,4},{7,6},{8,9},{10,11},{9,8... | collective-permute-start | bytes 61448 | tf_op jit(solution)/shard_map/ppermute | solution.py:638
  11.5 0.0 collective-permute-done.2.y_far_ref.y_far_msg
  11.5 0.0 copy-done.1
  11.5 0.0 copy-done
  11.5 0.0 copy-done.3
  11.5 0.0 copy-done.2
  11.5 0.0 copy-done.5
  11.5 0.0 copy-done.4
  11.5 0.0 copy-done.6
  11.5 0.0 copy-done.7
  11.5 1.1 %shard_map.96 = (f32[4,64,128]{2,1,0:T(8,128)S(1)}, f32[8,256]{1,0:T(8,128)S(1)}, f32[256,24]{1,0:T(8,128)S(1)}, f32[8,128]{1,0:T(8,128)S(1)}, f32[5,4,64,128]{3...) custom-call(f32[4,64,128]{2,1,0:T(8,128)S(1)} %copy-done.2, ...), custom_call_target="tpu_custom_call" | custom-call | tf_op jit(solution)/shard_map/pallas_call | solution.py:620
  12.6 0.0 collective-permute-done.3.y_near_ref.y_near_msg
  12.6 0.0 collective-permute-done.x_far_ref.x_far_msg
  12.6 0.0 collective-permute-done.1.x_near_ref.x_near_msg
  12.6 1.3 %shard_map.97 = (f32[4,64,128]{2,1,0:T(8,128)S(1)}, f32[4,64,128]{2,1,0:T(8,128)S(1)}, f32[32,3,4,128]{3,2,1,0:T(4,128)}, f32[16,128]{1,0:T(8,128)S(1)}, f32[136,128]{1,0:T(8,128)S(1)}, /*index=5*/f32[136,128]{1,0:T(8,128)S(1)}) custom-call(f32[192,128]{1,0:T(8,128)S(1)} %collective-permute-done.x_far_ref.x_far_msg, ...), custom_call_target="tpu_custom_call" | custom-call | tf_op jit(solution)/shard_map/pallas_call | solution.py:620
  13.9 4.6 %all-to-all-start = ((f32[32,3,4,128]{3,2,1,0:T(4,128)}), f32[32,3,4,128]{3,2,1,0:T(4,128)S(1)}, u32[]{:S(2)}, u32[]{:S(2)}) async-start(f32[32,3,4,128]{3,2,1,0:T(4,128)} %get-tuple-element.53), calls=%async_computation | async-start | bytes 393216 | tf_op jit(solution)/shard_map/all_to_all | solution.py:651
  18.5 0.3 %collective-permute-start.4 = (f32[136,128]{1,0:T(8,128)S(1)}, f32[136,128]{1,0:T(8,128)S(1)}, u32[]{:S(2)}, u32[]{:S(2)}) collective-permute-start(f32[136,128]{1,0:T(8,128)S(1)} %get-tuple-element.44), channel_id=1, source_target_pairs={{0,4},{8,12},{16,20},{24,28},{4,0},{12,8},{20,16},{28,24},{1,5},{9... | collective-permute-start | bytes 208904 | tf_op jit(solution)/shard_map/ppermute | solution.py:638
  18.9 3.4 %collective-permute-start.5 = (f32[136,128]{1,0:T(8,128)S(1)}, f32[136,128]{1,0:T(8,128)S(1)}, u32[]{:S(2)}, u32[]{:S(2)}) collective-permute-start(f32[136,128]{1,0:T(8,128)S(1)} %get-tuple-element.45), channel_id=1, source_target_pairs={{4,8},{12,16},{20,24},{8,4},{16,12},{24,20},{5,9},{13,17},{21,25},... | collective-permute-start | bytes 208904 | tf_op jit(solution)/shard_map/ppermute | solution.py:638
  22.3 0.0 collective-permute-done.4.x_near_ref
  22.3 2.9 %collective-permute-done.5.x_far_ref = f32[136,128]{1,0:T(8,128)S(1)} collective-permute-done((f32[136,128]{1,0:T(8,128)S(1)}, f32[136,128]{1,0:T(8,128)S(1)}, u32[]{:S(2)}, u32[]{:S(2)}) %collective-permute-start.5) | collective-permute-done | bytes 69664 | tf_op jit(solution)/shard_map/ppermute | solution.py:638
  25.2 0.3 %shard_map.98 = (f32[6,4,64,128]{3,2,1,0:T(8,128)S(1)}, f32[4,64,128]{2,1,0:T(8,128)S(1)}, f32[4,64,128]{2,1,0:T(8,128)S(1)}, f32[4,64,128]{2,1,0:T(8,128)S(1)}, f32[4,64,128]{2,1,0:T(8,128)S(1)}) custom-call(f32[136,128]{1,0:T(8,128)S(1)} %collective-permute-done.4.x_near_ref, f32[136,128]{1,0:T(8,128)S(1)} %collective-permute-done.5.x_far_ref, ...), custom_call_target="tpu_custom_call" | custom-call | tf_op jit(solution)/shard_map/pallas_call | solution.py:620
  25.6 2.2 %all-to-all-done.total_ref = f32[32,3,4,128]{3,2,1,0:T(4,128)S(1)} async-done(((f32[32,3,4,128]{3,2,1,0:T(4,128)}), f32[32,3,4,128]{3,2,1,0:T(4,128)S(1)}, u32[]{:S(2)}, u32[]{:S(2)}) %all-to-all-start) | async-done | bytes 196640 | tf_op jit(solution)/shard_map/all_to_all | solution.py:651
  27.8 1.3 %shard_map.99 = (f32[4,64,128]{2,1,0:T(8,128)}, f32[4,64,128]{2,1,0:T(8,128)}) custom-call(f32[4,64,128]{2,1,0:T(8,128)S(1)} %get-tuple-element.42.conc_ref, f32[4,64,128]{2,1,0:T(8,128)S(1)} %get-tuple-element.43.pot_ref, f32[4,64,128]{2,1,0:T(8,128)S(1)} %get-tuple-element.47.mass_ref, f32[4,64,128]{2,1,0:T(8,128)S(1)} %get-tuple-element.48.pots_ref, ...), custom_call_target="tpu_custom_call" | custom-call | tf_op jit(solution)/shard_map/pallas_call | solution.py:620
Async XLA Ops:
  0.6 10.8 %copy-start.1 = (f32[4,64,128]{2,1,0:T(8,128)S(1)}, f32[4,64,128]{2,1,0:T(8,128)}, u32[]{:S(2)}) copy-start(f32[4,64,128]{2,1,0:T(8,128)} %pots_ref.5) | copy-start | bytes 393220
  0.6 10.8 %copy-start = (f32[4,64,128]{2,1,0:T(8,128)S(1)}, f32[4,64,128]{2,1,0:T(8,128)}, u32[]{:S(2)}) copy-start(f32[4,64,128]{2,1,0:T(8,128)} %mass_ref.5) | copy-start | bytes 393220
  0.7 10.8 %copy-start.3 = (f32[4,64,128]{2,1,0:T(8,128)S(1)}, f32[4,64,128]{2,1,0:T(8,128)}, u32[]{:S(2)}) copy-start(f32[4,64,128]{2,1,0:T(8,128)} %pot_ref.3) | copy-start | bytes 393220
  0.7 10.8 %copy-start.2 = (f32[4,64,128]{2,1,0:T(8,128)S(1)}, f32[4,64,128]{2,1,0:T(8,128)}, u32[]{:S(2)}) copy-start(f32[4,64,128]{2,1,0:T(8,128)} %conc_ref.3) | copy-start | bytes 393220
  0.7 10.8 %copy-start.5 = (s32[4,64,128]{2,1,0:T(8,128)S(1)}, s32[4,64,128]{2,1,0:T(8,128)}, u32[]{:S(2)}) copy-start(s32[4,64,128]{2,1,0:T(8,128)} %class_ref) | copy-start | bytes 393220
  0.7 10.8 %copy-start.4 = (s32[4,64,128]{2,1,0:T(8,128)S(1)}, s32[4,64,128]{2,1,0:T(8,128)}, u32[]{:S(2)}) copy-start(s32[4,64,128]{2,1,0:T(8,128)} %mask_ref) | copy-start | bytes 393220
  2.0 9.5 %copy-start.6 = (s32[8,64]{1,0:T(8,128)S(1)}, s32[8,64]{1,0:T(8,128)}, u32[]{:S(2)}) copy-start(s32[8,64]{1,0:T(8,128)} %owner_ref.3) | copy-start | bytes 6148
  2.0 9.5 %collective-permute-start.2 = (f32[200,128]{1,0:T(8,128)S(1)}, f32[200,128]{1,0:T(8,128)S(1)}, u32[]{:S(2)}, u32[]{:S(2)}) collective-permute-start(f32[200,128]{1,0:T(8,128)S(1)} %get-tuple-element.30), channel_id=1, source_target_pairs={{1,2},{2,1},{5,6},{6,5},{9,10},{10,9},{13,14},{14,13},{17,18},{18,... | collective-permute-start | bytes 307208 | tf_op jit(solution)/shard_map/ppermute | solution.py:638
  2.7 10.0 %collective-permute-start = (f32[192,128]{1,0:T(8,128)S(1)}, f32[192,128]{1,0:T(8,128)S(1)}, u32[]{:S(2)}, u32[]{:S(2)}) collective-permute-start(f32[192,128]{1,0:T(8,128)S(1)} %get-tuple-element.28), channel_id=1, source_target_pairs={{4,8},{12,16},{20,24},{8,4},{16,12},{24,20},{5,9},{13,17},{21,25},... | collective-permute-start | bytes 294920 | tf_op jit(solution)/shard_map/ppermute | solution.py:638
  7.2 4.3 %copy-start.7 = (f32[8]{0:T(128)S(1)}, f32[8]{0:T(128)}, u32[]{:S(2)}) copy-start(f32[8]{0:T(128)} %table_ref.1) | copy-start | bytes 100
  7.2 5.4 %collective-permute-start.1 = (f32[192,128]{1,0:T(8,128)S(1)}, f32[192,128]{1,0:T(8,128)S(1)}, u32[]{:S(2)}, u32[]{:S(2)}) collective-permute-start(f32[192,128]{1,0:T(8,128)S(1)} %get-tuple-element.29), channel_id=1, source_target_pairs={{0,4},{8,12},{16,20},{24,28},{4,0},{12,8},{20,16},{28,24},{1,5},{9... | collective-permute-start | bytes 294920 | tf_op jit(solution)/shard_map/ppermute | solution.py:638
  7.3 5.4 %collective-permute-start.3 = (f32[40,128]{1,0:T(8,128)S(1)}, f32[40,128]{1,0:T(8,128)S(1)}, u32[]{:S(2)}, u32[]{:S(2)}) collective-permute-start(f32[40,128]{1,0:T(8,128)S(1)} %get-tuple-element.32), channel_id=1, source_target_pairs={{0,1},{2,3},{1,0},{3,2},{4,5},{6,7},{5,4},{7,6},{8,9},{10,11},{9,8... | collective-permute-start | bytes 61448 | tf_op jit(solution)/shard_map/ppermute | solution.py:638
  13.9 13.8 %all-to-all-start = ((f32[32,3,4,128]{3,2,1,0:T(4,128)}), f32[32,3,4,128]{3,2,1,0:T(4,128)S(1)}, u32[]{:S(2)}, u32[]{:S(2)}) async-start(f32[32,3,4,128]{3,2,1,0:T(4,128)} %get-tuple-element.53), calls=%async_computation | async-start | bytes 393216 | tf_op jit(solution)/shard_map/all_to_all | solution.py:651
  18.5 3.8 %collective-permute-start.4 = (f32[136,128]{1,0:T(8,128)S(1)}, f32[136,128]{1,0:T(8,128)S(1)}, u32[]{:S(2)}, u32[]{:S(2)}) collective-permute-start(f32[136,128]{1,0:T(8,128)S(1)} %get-tuple-element.44), channel_id=1, source_target_pairs={{0,4},{8,12},{16,20},{24,28},{4,0},{12,8},{20,16},{28,24},{1,5},{9... | collective-permute-start | bytes 208904 | tf_op jit(solution)/shard_map/ppermute | solution.py:638
  18.9 6.4 %collective-permute-start.5 = (f32[136,128]{1,0:T(8,128)S(1)}, f32[136,128]{1,0:T(8,128)S(1)}, u32[]{:S(2)}, u32[]{:S(2)}) collective-permute-start(f32[136,128]{1,0:T(8,128)S(1)} %get-tuple-element.45), channel_id=1, source_target_pairs={{4,8},{12,16},{20,24},{8,4},{16,12},{24,20},{5,9},{13,17},{21,25},... | collective-permute-start | bytes 208904 | tf_op jit(solution)/shard_map/ppermute | solution.py:638

commit v14 on v13

--- a/solution.py
+++ b/solution.py
@@ -86,24 +86,12 @@
     return faces, diagonal
 
 
-def split_dot(ones, values, contract):
-    dims = (contract, ((), ()))
-    total = None
-    rest = values
-    for _ in range(3):
-        term = rest.astype(BF16)
-        rest = rest - term.astype(F32)
-        part = lax.dot_general(ones, term, dims, preferred_element_type=F32)
-        total = part if total is None else total + part
-    return total
-
-
-def three_terms(values):
+def three_terms(values, dim=0):
     out = []
     for _ in range(3):
         out.append(values.astype(BF16).astype(F32))
         values = values - out[-1]
-    return jnp.concatenate(out, axis=0)
+    return jnp.concatenate(out, axis=dim)
 
 
 def round_up(value, unit):
@@ -130,7 +118,7 @@
     def slot_of(self, g, h):
         last = self.groups - 1
         place = 0 if h == 0 else 1 if h == last else h + 1
-        return place * self.owners + self.owners - 1 - g
+        return place * self.owners + self.owners - 1 - (g ^ 1)
 
 
 def side_rows(plan, rows, which):
@@ -370,8 +358,14 @@
     owner = iota((plan.owners, 1), 0)
     is_mine = owner == lax.axis_index("gx")
 
-    sums = [None, split_dot(gather_ref[...].astype(BF16), give, ((1,), (0,))), None]
-    sums[1] = sums[1] * scale_ref[...]
+    own = lax.dot_general(
+        gather_ref[...].astype(BF16),
+        three_terms(give, 1).astype(BF16),
+        (((1,), (0,)), ((), ())),
+        preferred_element_type=F32,
+    )
+    own = own[:, : plan.p] + own[:, plan.p : 2 * plan.p] + own[:, 2 * plan.p :]
+    sums = [None, own * scale_ref[...], None]
     for place, y, at, side in ((0, 0, plan.half_y - 1, 2), (2, plan.y - 1, 0, 3)):
         edge_pot, edge_conc = (
             jnp.concatenate([field[x, y : y + 1] for x in range(plan.x)], axis=0)
@@ -447,7 +441,7 @@
                 total_out[slot, part] = main[4 * part : 4 * part + 4]
             for row, values in beside:
                 total_out[slot, row // 4, pl.ds(row % 4, 1), :] = values[g : g + 1]
-        some = pl.ds(plan.slot_of(plan.owners - 1, plane), plan.owners)
+        some = pl.ds(plan.slot_of(plan.owners - 2, plane), plan.owners)
         copies.append(
             pltpu.make_async_copy(total_out.at[some], total_hbm.at[some], sems.at[plane])
         )

time: 29.3 us -> 29.1 us (level)
  the two profiles are of different devices: /device:TPU:1 before, /device:TPU:0 now
where the time goes in v14:
time: 29.1 us; the launch traced here: 28.6 us
  starting transfers between devices  14.6 us (50%)
  waiting for transfers between devices  7.9 us (27%)
  Pallas kernels  5.27 us (18%)
  between operations  0.81 us (3%)
    ppermute x6, starting transfers between devices, swap_near(): return lax.ppermute(rows, axis, pairs + [(j, i) for i, j in pairs])  11.1 us
    all_to_all x1, waiting for transfers between devices, gather_totals(): lax.all_to_all(total, ('gx', 'gy'), split_axis=0, concat_axis=0, axis_ind...  6.91 us
    pallas_call x5, Pallas kernels, call(): pl.pallas_call(functools.partial(kernel, plan), out_shape=[jax.ShapeDtype...  5.27 us
    all_to_all x1, starting transfers between devices, gather_totals(): lax.all_to_all(total, ('gx', 'gy'), split_axis=0, concat_axis=0, axis_ind...  3.56 us
    ppermute x6, waiting for transfers between devices, swap_near(): return lax.ppermute(rows, axis, pairs + [(j, i) for i, j in pairs])  0.99 us
  transfers between devices with their start and end apart: 7, of which 3 were waited for; matrix products, arithmetic and copies ran while one was open for 0% of the time, Pallas kernels for 5%

profile of v14, /device:TPU:0, one launch (start us, length us, event | category | flops | bytes accessed | tf_op | source)
XLA Modules:
  0.0 28.6 jit_solution(8333753458478184292)
XLA Ops:
  0.6 0.0 copy-start.1
  0.6 0.0 copy-start
  0.7 0.0 copy-start.3
  0.7 0.0 copy-start.2
  0.7 0.0 copy-start.5
  0.7 0.0 copy-start.4
  0.7 1.3 %shard_map.95 = (f32[192,128]{1,0:T(8,128)S(1)}, f32[192,128]{1,0:T(8,128)S(1)}, f32[40,128]{1,0:T(8,128)S(1)}, f32[200,128]{1,0:T(8,128)S(1)}) custom-call(f32[4,64,128]{2,1,0:T(8,128)} %conc_ref.3, f32[4,64,128]{2,1,0:T(8,128)} %pot_ref.3, s32[4,64,128]{2,1,0:T(8,128)} %mask_ref, s32[4,64,128]{2,1,0:T(8,128)} %class_ref, f32[4,64,128]{2,1,0:T(8,128)} %mass_ref.5, ...), custom_call_target="tpu_custom_call" | custom-call | tf_op jit(solution)/shard_map/pallas_call | solution.py:614
  2.0 0.0 copy-start.6
  2.0 0.7 %collective-permute-start.2 = (f32[200,128]{1,0:T(8,128)S(1)}, f32[200,128]{1,0:T(8,128)S(1)}, u32[]{:S(2)}, u32[]{:S(2)}) collective-permute-start(f32[200,128]{1,0:T(8,128)S(1)} %get-tuple-element.30), channel_id=1, source_target_pairs={{1,2},{2,1},{5,6},{6,5},{9,10},{10,9},{13,14},{14,13},{17,18},{18,... | collective-permute-start | bytes 307208 | tf_op jit(solution)/shard_map/ppermute | solution.py:632
  2.7 0.7 %collective-permute-start = (f32[192,128]{1,0:T(8,128)S(1)}, f32[192,128]{1,0:T(8,128)S(1)}, u32[]{:S(2)}, u32[]{:S(2)}) collective-permute-start(f32[192,128]{1,0:T(8,128)S(1)} %get-tuple-element.28), channel_id=1, source_target_pairs={{4,8},{12,16},{20,24},{8,4},{16,12},{24,20},{5,9},{13,17},{21,25},... | collective-permute-start | bytes 294920 | tf_op jit(solution)/shard_map/ppermute | solution.py:632
  3.4 0.0 copy-start.7
  3.4 4.4 %collective-permute-start.1 = (f32[192,128]{1,0:T(8,128)S(1)}, f32[192,128]{1,0:T(8,128)S(1)}, u32[]{:S(2)}, u32[]{:S(2)}) collective-permute-start(f32[192,128]{1,0:T(8,128)S(1)} %get-tuple-element.29), channel_id=1, source_target_pairs={{0,4},{8,12},{16,20},{24,28},{4,0},{12,8},{20,16},{28,24},{1,5},{9... | collective-permute-start | bytes 294920 | tf_op jit(solution)/shard_map/ppermute | solution.py:632
  7.7 4.4 %collective-permute-start.3 = (f32[40,128]{1,0:T(8,128)S(1)}, f32[40,128]{1,0:T(8,128)S(1)}, u32[]{:S(2)}, u32[]{:S(2)}) collective-permute-start(f32[40,128]{1,0:T(8,128)S(1)} %get-tuple-element.32), channel_id=1, source_target_pairs={{0,1},{2,3},{1,0},{3,2},{4,5},{6,7},{5,4},{7,6},{8,9},{10,11},{9,8... | collective-permute-start | bytes 61448 | tf_op jit(solution)/shard_map/ppermute | solution.py:632
  12.1 0.0 collective-permute-done.2.y_far_ref.y_far_msg
  12.1 0.0 copy-done.1
  12.1 0.0 copy-done
  12.1 0.0 copy-done.3
  12.1 0.0 copy-done.2
  12.2 0.0 copy-done.5
  12.2 0.0 copy-done.4
  12.2 0.0 copy-done.6
  12.2 0.0 copy-done.7
  12.2 1.1 %shard_map.96 = (f32[4,64,128]{2,1,0:T(8,128)S(1)}, f32[8,256]{1,0:T(8,128)S(1)}, f32[256,24]{1,0:T(8,128)S(1)}, f32[8,128]{1,0:T(8,128)S(1)}, f32[5,4,64,128]{3...) custom-call(f32[4,64,128]{2,1,0:T(8,128)S(1)} %copy-done.2, ...), custom_call_target="tpu_custom_call" | custom-call | tf_op jit(solution)/shard_map/pallas_call | solution.py:614
  13.3 0.6 %collective-permute-done.3.y_near_ref.y_near_msg = f32[40,128]{1,0:T(8,128)S(1)} collective-permute-done((f32[40,128]{1,0:T(8,128)S(1)}, f32[40,128]{1,0:T(8,128)S(1)}, u32[]{:S(2)}, u32[]{:S(2)}) %collective-permute-start.3) | collective-permute-done | bytes 20512 | tf_op jit(solution)/shard_map/ppermute | solution.py:632
  13.9 0.0 collective-permute-done.x_far_ref.x_far_msg
  13.9 0.0 collective-permute-done.1.x_near_ref.x_near_msg
  13.9 1.3 %shard_map.97 = (f32[4,64,128]{2,1,0:T(8,128)S(1)}, f32[4,64,128]{2,1,0:T(8,128)S(1)}, f32[32,3,4,128]{3,2,1,0:T(4,128)}, f32[16,128]{1,0:T(8,128)S(1)}, f32[136,128]{1,0:T(8,128)S(1)}, /*index=5*/f32[136,128]{1,0:T(8,128)S(1)}) custom-call(f32[192,128]{1,0:T(8,128)S(1)} %collective-permute-done.x_far_ref.x_far_msg, ...), custom_call_target="tpu_custom_call" | custom-call | tf_op jit(solution)/shard_map/pallas_call | solution.py:614
  15.2 3.6 %all-to-all-start = ((f32[32,3,4,128]{3,2,1,0:T(4,128)}), f32[32,3,4,128]{3,2,1,0:T(4,128)S(1)}, u32[]{:S(2)}, u32[]{:S(2)}) async-start(f32[32,3,4,128]{3,2,1,0:T(4,128)} %get-tuple-element.53), calls=%async_computation | async-start | bytes 393216 | tf_op jit(solution)/shard_map/all_to_all | solution.py:645
  18.7 0.3 %collective-permute-start.4 = (f32[136,128]{1,0:T(8,128)S(1)}, f32[136,128]{1,0:T(8,128)S(1)}, u32[]{:S(2)}, u32[]{:S(2)}) collective-permute-start(f32[136,128]{1,0:T(8,128)S(1)} %get-tuple-element.44), channel_id=1, source_target_pairs={{0,4},{8,12},{16,20},{24,28},{4,0},{12,8},{20,16},{28,24},{1,5},{9... | collective-permute-start | bytes 208904 | tf_op jit(solution)/shard_map/ppermute | solution.py:632
  19.1 0.7 %collective-permute-start.5 = (f32[136,128]{1,0:T(8,128)S(1)}, f32[136,128]{1,0:T(8,128)S(1)}, u32[]{:S(2)}, u32[]{:S(2)}) collective-permute-start(f32[136,128]{1,0:T(8,128)S(1)} %get-tuple-element.45), channel_id=1, source_target_pairs={{4,8},{12,16},{20,24},{8,4},{16,12},{24,20},{5,9},{13,17},{21,25},... | collective-permute-start | bytes 208904 | tf_op jit(solution)/shard_map/ppermute | solution.py:632
  19.7 0.3 %collective-permute-done.4.x_near_ref = f32[136,128]{1,0:T(8,128)S(1)} collective-permute-done((f32[136,128]{1,0:T(8,128)S(1)}, f32[136,128]{1,0:T(8,128)S(1)}, u32[]{:S(2)}, u32[]{:S(2)}) %collective-permute-start.4) | collective-permute-done | bytes 69664 | tf_op jit(solution)/shard_map/ppermute | solution.py:632
  20.1 0.0 collective-permute-done.5.x_far_ref
  20.1 0.3 %shard_map.98 = (f32[6,4,64,128]{3,2,1,0:T(8,128)S(1)}, f32[4,64,128]{2,1,0:T(8,128)S(1)}, f32[4,64,128]{2,1,0:T(8,128)S(1)}, f32[4,64,128]{2,1,0:T(8,128)S(1)}, f32[4,64,128]{2,1,0:T(8,128)S(1)}) custom-call(f32[136,128]{1,0:T(8,128)S(1)} %collective-permute-done.4.x_near_ref, f32[136,128]{1,0:T(8,128)S(1)} %collective-permute-done.5.x_far_ref, ...), custom_call_target="tpu_custom_call" | custom-call | tf_op jit(solution)/shard_map/pallas_call | solution.py:614
  20.4 6.9 %all-to-all-done.total_ref = f32[32,3,4,128]{3,2,1,0:T(4,128)S(1)} async-done(((f32[32,3,4,128]{3,2,1,0:T(4,128)}), f32[32,3,4,128]{3,2,1,0:T(4,128)S(1)}, u32[]{:S(2)}, u32[]{:S(2)}) %all-to-all-start) | async-done | bytes 196640 | tf_op jit(solution)/shard_map/all_to_all | solution.py:645
  27.3 1.3 %shard_map.99 = (f32[4,64,128]{2,1,0:T(8,128)}, f32[4,64,128]{2,1,0:T(8,128)}) custom-call(f32[4,64,128]{2,1,0:T(8,128)S(1)} %get-tuple-element.42.conc_ref, f32[4,64,128]{2,1,0:T(8,128)S(1)} %get-tuple-element.43.pot_ref, f32[4,64,128]{2,1,0:T(8,128)S(1)} %get-tuple-element.47.mass_ref, f32[4,64,128]{2,1,0:T(8,128)S(1)} %get-tuple-element.48.pots_ref, ...), custom_call_target="tpu_custom_call" | custom-call | tf_op jit(solution)/shard_map/pallas_call | solution.py:614
Async XLA Ops:
  0.6 11.5 %copy-start.1 = (f32[4,64,128]{2,1,0:T(8,128)S(1)}, f32[4,64,128]{2,1,0:T(8,128)}, u32[]{:S(2)}) copy-start(f32[4,64,128]{2,1,0:T(8,128)} %pots_ref.5) | copy-start | bytes 393220
  0.6 11.5 %copy-start = (f32[4,64,128]{2,1,0:T(8,128)S(1)}, f32[4,64,128]{2,1,0:T(8,128)}, u32[]{:S(2)}) copy-start(f32[4,64,128]{2,1,0:T(8,128)} %mass_ref.5) | copy-start | bytes 393220
  0.7 11.5 %copy-start.3 = (f32[4,64,128]{2,1,0:T(8,128)S(1)}, f32[4,64,128]{2,1,0:T(8,128)}, u32[]{:S(2)}) copy-start(f32[4,64,128]{2,1,0:T(8,128)} %pot_ref.3) | copy-start | bytes 393220
  0.7 11.5 %copy-start.2 = (f32[4,64,128]{2,1,0:T(8,128)S(1)}, f32[4,64,128]{2,1,0:T(8,128)}, u32[]{:S(2)}) copy-start(f32[4,64,128]{2,1,0:T(8,128)} %conc_ref.3) | copy-start | bytes 393220
  0.7 11.5 %copy-start.5 = (s32[4,64,128]{2,1,0:T(8,128)S(1)}, s32[4,64,128]{2,1,0:T(8,128)}, u32[]{:S(2)}) copy-start(s32[4,64,128]{2,1,0:T(8,128)} %class_ref) | copy-start | bytes 393220
  0.7 11.5 %copy-start.4 = (s32[4,64,128]{2,1,0:T(8,128)S(1)}, s32[4,64,128]{2,1,0:T(8,128)}, u32[]{:S(2)}) copy-start(s32[4,64,128]{2,1,0:T(8,128)} %mask_ref) | copy-start | bytes 393220
  2.0 10.2 %copy-start.6 = (s32[8,64]{1,0:T(8,128)S(1)}, s32[8,64]{1,0:T(8,128)}, u32[]{:S(2)}) copy-start(s32[8,64]{1,0:T(8,128)} %owner_ref.3) | copy-start | bytes 6148
  2.0 10.1 %collective-permute-start.2 = (f32[200,128]{1,0:T(8,128)S(1)}, f32[200,128]{1,0:T(8,128)S(1)}, u32[]{:S(2)}, u32[]{:S(2)}) collective-permute-start(f32[200,128]{1,0:T(8,128)S(1)} %get-tuple-element.30), channel_id=1, source_target_pairs={{1,2},{2,1},{5,6},{6,5},{9,10},{10,9},{13,14},{14,13},{17,18},{18,... | collective-permute-start | bytes 307208 | tf_op jit(solution)/shard_map/ppermute | solution.py:632
  2.7 11.2 %collective-permute-start = (f32[192,128]{1,0:T(8,128)S(1)}, f32[192,128]{1,0:T(8,128)S(1)}, u32[]{:S(2)}, u32[]{:S(2)}) collective-permute-start(f32[192,128]{1,0:T(8,128)S(1)} %get-tuple-element.28), channel_id=1, source_target_pairs={{4,8},{12,16},{20,24},{8,4},{16,12},{24,20},{5,9},{13,17},{21,25},... | collective-permute-start | bytes 294920 | tf_op jit(solution)/shard_map/ppermute | solution.py:632
  3.4 8.8 %copy-start.7 = (f32[8]{0:T(128)S(1)}, f32[8]{0:T(128)}, u32[]{:S(2)}) copy-start(f32[8]{0:T(128)} %table_ref.1) | copy-start | bytes 100
  3.4 10.5 %collective-permute-start.1 = (f32[192,128]{1,0:T(8,128)S(1)}, f32[192,128]{1,0:T(8,128)S(1)}, u32[]{:S(2)}, u32[]{:S(2)}) collective-permute-start(f32[192,128]{1,0:T(8,128)S(1)} %get-tuple-element.29), channel_id=1, source_target_pairs={{0,4},{8,12},{16,20},{24,28},{4,0},{12,8},{20,16},{28,24},{1,5},{9... | collective-permute-start | bytes 294920 | tf_op jit(solution)/shard_map/ppermute | solution.py:632
  7.7 6.2 %collective-permute-start.3 = (f32[40,128]{1,0:T(8,128)S(1)}, f32[40,128]{1,0:T(8,128)S(1)}, u32[]{:S(2)}, u32[]{:S(2)}) collective-permute-start(f32[40,128]{1,0:T(8,128)S(1)} %get-tuple-element.32), channel_id=1, source_target_pairs={{0,1},{2,3},{1,0},{3,2},{4,5},{6,7},{5,4},{7,6},{8,9},{10,11},{9,8... | collective-permute-start | bytes 61448 | tf_op jit(solution)/shard_map/ppermute | solution.py:632
  15.2 12.2 %all-to-all-start = ((f32[32,3,4,128]{3,2,1,0:T(4,128)}), f32[32,3,4,128]{3,2,1,0:T(4,128)S(1)}, u32[]{:S(2)}, u32[]{:S(2)}) async-start(f32[32,3,4,128]{3,2,1,0:T(4,128)} %get-tuple-element.53), calls=%async_computation | async-start | bytes 393216 | tf_op jit(solution)/shard_map/all_to_all | solution.py:645
  18.7 1.3 %collective-permute-start.4 = (f32[136,128]{1,0:T(8,128)S(1)}, f32[136,128]{1,0:T(8,128)S(1)}, u32[]{:S(2)}, u32[]{:S(2)}) collective-permute-start(f32[136,128]{1,0:T(8,128)S(1)} %get-tuple-element.44), channel_id=1, source_target_pairs={{0,4},{8,12},{16,20},{24,28},{4,0},{12,8},{20,16},{28,24},{1,5},{9... | collective-permute-start | bytes 208904 | tf_op jit(solution)/shard_map/ppermute | solution.py:632
  19.1 1.0 %collective-permute-start.5 = (f32[136,128]{1,0:T(8,128)S(1)}, f32[136,128]{1,0:T(8,128)S(1)}, u32[]{:S(2)}, u32[]{:S(2)}) collective-permute-start(f32[136,128]{1,0:T(8,128)S(1)} %get-tuple-element.45), channel_id=1, source_target_pairs={{4,8},{12,16},{20,24},{8,4},{16,12},{24,20},{5,9},{13,17},{21,25},... | collective-permute-start | bytes 208904 | tf_op jit(solution)/shard_map/ppermute | solution.py:632

commit v15 on v14

--- a/solution.py
+++ b/solution.py
@@ -192,7 +192,7 @@
 def prepare_kernel(plan, *refs):
     hbm, refs = refs[:8], refs[8:]
     x_near_ref, x_far_ref, y_near_ref, y_far_ref = refs[:4]
-    x_refs, y_refs, (owner_ref, table_ref, sems) = refs[4:8], refs[8:14], refs[14:]
+    whole_refs, y_refs, (owner_ref, table_ref, sems) = refs[4:8], refs[8:10], refs[10:]
     copies = []
 
     def start(source, target):
@@ -201,25 +201,31 @@
 
     start(hbm[7], table_ref)
     start(hbm[6], owner_ref)
-    for source, target in zip(hbm[:4], x_refs):
-        start(source.at[0], target.at[0])
-        start(source.at[plan.x - 1], target.at[1])
-    for source, target in zip(hbm[:6], y_refs):
+    for source, target in zip(hbm[:4], whole_refs):
+        start(source, target)
+    for source, target in zip(hbm[4:6], y_refs):
         start(source.at[:, pl.ds(0, 8)], target.at[0])
         start(source.at[:, pl.ds(plan.y - 8, 8)], target.at[1])
     for copy in copies:
         copy.wait()
     table = [table_ref[marker] for marker in range(table_ref.shape[0])]
-    conc, pot, mask, kind = (ref[...] for ref in x_refs)
-    fields = (conc, pot, mobility_of(mask, kind, table))
-    put_x(plan, [f[0] for f in fields], [f[1] for f in fields], x_near_ref, x_far_ref)
-    conc, pot, mask, kind, mass, pots = (ref[...] for ref in y_refs)
-    fields = (conc, pot, mobility_of(mask, kind, table))
+    last = plan.x - 1
+
+    def part(pick):
+        conc, pot, mask, kind = (pick(ref) for ref in whole_refs)
+        return conc, pot, mobility_of(mask, kind, table)
+
+    lows, highs = part(lambda ref: ref[0]), part(lambda ref: ref[last])
+    put_x(plan, lows, highs, x_near_ref, x_far_ref)
+    lows = part(lambda ref: ref[:, pl.ds(0, 8), :])
+    highs = part(lambda ref: ref[:, pl.ds(plan.y - 8, 8), :])
+    fields = [*zip(lows, highs)]
+    mass, pots = (ref[...] for ref in y_refs)
     up = even("gy")
     rows = [(field, at) for at in range(2) for field in fields] + [(mass, 0), (pots, 0)]
     for which, (field, at) in enumerate(rows):
         for x in range(plan.x):
-            low, high = field[0, x, at : at + 1], field[1, x, 7 - at : 8 - at]
+            low, high = field[0][x, at : at + 1], field[1][x, 7 - at : 8 - at]
             y_near_ref[pl.ds(which * plan.x + x, 1), :] = jnp.where(up, high, low)
             y_far_ref[pl.ds(which * plan.x + x, 1), :] = jnp.where(up, low, high)
     used = 8 * plan.x
@@ -678,11 +684,11 @@
         [*fields, owner_map, table],
         far=range(8),
         scratch=(
-            *[pltpu.VMEM((2, plan.y, plan.p), field.dtype) for field in fields[:4]],
-            *[pltpu.VMEM((2, plan.x, 8, plan.p), field.dtype) for field in fields],
+            *[pltpu.VMEM(block, field.dtype) for field in fields[:4]],
+            *[pltpu.VMEM((2, plan.x, 8, plan.p), field.dtype) for field in fields[4:]],
             pltpu.VMEM(owner_map.shape, owner_map.dtype),
             pltpu.SMEM(table.shape, table.dtype),
-            pltpu.SemaphoreType.DMA((22,)),
+            pltpu.SemaphoreType.DMA((10,)),
         ),
     )
     x_near, x_far = swap_near("gx", messages[0]), swap_far("gx", messages[1])

time: 29.1 us -> 29.1 us (level)
  no operation moved by 1% of the time
where the time goes in v15:
time: 29.1 us; the launch traced here: 28.7 us
  starting transfers between devices  14.6 us (50%)
  waiting for transfers between devices  7.9 us (27%)
  Pallas kernels  5.36 us (18%)
  between operations  0.81 us (3%)
    ppermute x6, starting transfers between devices, swap_near(): return lax.ppermute(rows, axis, pairs + [(j, i) for i, j in pairs])  11.1 us
    all_to_all x1, waiting for transfers between devices, gather_totals(): lax.all_to_all(total, ('gx', 'gy'), split_axis=0, concat_axis=0, axis_ind...  6.91 us
    pallas_call x5, Pallas kernels, call(): pl.pallas_call(functools.partial(kernel, plan), out_shape=[jax.ShapeDtype...  5.36 us
    all_to_all x1, starting transfers between devices, gather_totals(): lax.all_to_all(total, ('gx', 'gy'), split_axis=0, concat_axis=0, axis_ind...  3.56 us
    ppermute x6, waiting for transfers between devices, swap_near(): return lax.ppermute(rows, axis, pairs + [(j, i) for i, j in pairs])  0.99 us
  transfers between devices with their start and end apart: 7, of which 3 were waited for; matrix products, arithmetic and copies ran while one was open for 0% of the time, Pallas kernels for 5%

profile of v15, /device:TPU:0, one launch (start us, length us, event | category | flops | bytes accessed | tf_op | source)
XLA Modules:
  0.0 28.7 jit_solution(10231514135986727955)
XLA Ops:
  0.6 0.0 copy-start.1
  0.6 0.0 copy-start
  0.7 0.0 copy-start.3
  0.7 0.0 copy-start.2
  0.7 0.0 copy-start.5
  0.7 0.0 copy-start.4
  0.7 1.4 %shard_map.95 = (f32[192,128]{1,0:T(8,128)S(1)}, f32[192,128]{1,0:T(8,128)S(1)}, f32[40,128]{1,0:T(8,128)S(1)}, f32[200,128]{1,0:T(8,128)S(1)}) custom-call(f32[4,64,128]{2,1,0:T(8,128)} %conc_ref.3, f32[4,64,128]{2,1,0:T(8,128)} %pot_ref.3, s32[4,64,128]{2,1,0:T(8,128)} %mask_ref, s32[4,64,128]{2,1,0:T(8,128)} %class_ref, f32[4,64,128]{2,1,0:T(8,128)} %mass_ref.5, ...), custom_call_target="tpu_custom_call" | custom-call | tf_op jit(solution)/shard_map/pallas_call | solution.py:620
  2.1 0.0 copy-start.6
  2.1 0.7 %collective-permute-start.2 = (f32[200,128]{1,0:T(8,128)S(1)}, f32[200,128]{1,0:T(8,128)S(1)}, u32[]{:S(2)}, u32[]{:S(2)}) collective-permute-start(f32[200,128]{1,0:T(8,128)S(1)} %get-tuple-element.30), channel_id=1, source_target_pairs={{1,2},{2,1},{5,6},{6,5},{9,10},{10,9},{13,14},{14,13},{17,18},{18,... | collective-permute-start | bytes 307208 | tf_op jit(solution)/shard_map/ppermute | solution.py:638
  2.8 0.7 %collective-permute-start = (f32[192,128]{1,0:T(8,128)S(1)}, f32[192,128]{1,0:T(8,128)S(1)}, u32[]{:S(2)}, u32[]{:S(2)}) collective-permute-start(f32[192,128]{1,0:T(8,128)S(1)} %get-tuple-element.28), channel_id=1, source_target_pairs={{4,8},{12,16},{20,24},{8,4},{16,12},{24,20},{5,9},{13,17},{21,25},... | collective-permute-start | bytes 294920 | tf_op jit(solution)/shard_map/ppermute | solution.py:638
  3.4 0.0 copy-start.7
  3.5 4.4 %collective-permute-start.1 = (f32[192,128]{1,0:T(8,128)S(1)}, f32[192,128]{1,0:T(8,128)S(1)}, u32[]{:S(2)}, u32[]{:S(2)}) collective-permute-start(f32[192,128]{1,0:T(8,128)S(1)} %get-tuple-element.29), channel_id=1, source_target_pairs={{0,4},{8,12},{16,20},{24,28},{4,0},{12,8},{20,16},{28,24},{1,5},{9... | collective-permute-start | bytes 294920 | tf_op jit(solution)/shard_map/ppermute | solution.py:638
  7.8 4.4 %collective-permute-start.3 = (f32[40,128]{1,0:T(8,128)S(1)}, f32[40,128]{1,0:T(8,128)S(1)}, u32[]{:S(2)}, u32[]{:S(2)}) collective-permute-start(f32[40,128]{1,0:T(8,128)S(1)} %get-tuple-element.32), channel_id=1, source_target_pairs={{0,1},{2,3},{1,0},{3,2},{4,5},{6,7},{5,4},{7,6},{8,9},{10,11},{9,8... | collective-permute-start | bytes 61448 | tf_op jit(solution)/shard_map/ppermute | solution.py:638
  12.2 0.0 collective-permute-done.2.y_far_ref.y_far_msg
  12.2 0.0 copy-done.1
  12.2 0.0 copy-done
  12.2 0.0 copy-done.3
  12.2 0.0 copy-done.2
  12.2 0.0 copy-done.5
  12.2 0.0 copy-done.4
  12.3 0.0 copy-done.6
  12.3 0.0 copy-done.7
  12.3 1.1 %shard_map.96 = (f32[4,64,128]{2,1,0:T(8,128)S(1)}, f32[8,256]{1,0:T(8,128)S(1)}, f32[256,24]{1,0:T(8,128)S(1)}, f32[8,128]{1,0:T(8,128)S(1)}, f32[5,4,64,128]{3...) custom-call(f32[4,64,128]{2,1,0:T(8,128)S(1)} %copy-done.2, ...), custom_call_target="tpu_custom_call" | custom-call | tf_op jit(solution)/shard_map/pallas_call | solution.py:620
  13.3 0.6 %collective-permute-done.3.y_near_ref.y_near_msg = f32[40,128]{1,0:T(8,128)S(1)} collective-permute-done((f32[40,128]{1,0:T(8,128)S(1)}, f32[40,128]{1,0:T(8,128)S(1)}, u32[]{:S(2)}, u32[]{:S(2)}) %collective-permute-start.3) | collective-permute-done | bytes 20512 | tf_op jit(solution)/shard_map/ppermute | solution.py:638
  14.0 0.0 collective-permute-done.x_far_ref.x_far_msg
  14.0 0.0 collective-permute-done.1.x_near_ref.x_near_msg
  14.0 1.3 %shard_map.97 = (f32[4,64,128]{2,1,0:T(8,128)S(1)}, f32[4,64,128]{2,1,0:T(8,128)S(1)}, f32[32,3,4,128]{3,2,1,0:T(4,128)}, f32[16,128]{1,0:T(8,128)S(1)}, f32[136,128]{1,0:T(8,128)S(1)}, /*index=5*/f32[136,128]{1,0:T(8,128)S(1)}) custom-call(f32[192,128]{1,0:T(8,128)S(1)} %collective-permute-done.x_far_ref.x_far_msg, ...), custom_call_target="tpu_custom_call" | custom-call | tf_op jit(solution)/shard_map/pallas_call | solution.py:620
  15.3 3.6 %all-to-all-start = ((f32[32,3,4,128]{3,2,1,0:T(4,128)}), f32[32,3,4,128]{3,2,1,0:T(4,128)S(1)}, u32[]{:S(2)}, u32[]{:S(2)}) async-start(f32[32,3,4,128]{3,2,1,0:T(4,128)} %get-tuple-element.53), calls=%async_computation | async-start | bytes 393216 | tf_op jit(solution)/shard_map/all_to_all | solution.py:651
  18.8 0.3 %collective-permute-start.4 = (f32[136,128]{1,0:T(8,128)S(1)}, f32[136,128]{1,0:T(8,128)S(1)}, u32[]{:S(2)}, u32[]{:S(2)}) collective-permute-start(f32[136,128]{1,0:T(8,128)S(1)} %get-tuple-element.44), channel_id=1, source_target_pairs={{0,4},{8,12},{16,20},{24,28},{4,0},{12,8},{20,16},{28,24},{1,5},{9... | collective-permute-start | bytes 208904 | tf_op jit(solution)/shard_map/ppermute | solution.py:638
  19.1 0.7 %collective-permute-start.5 = (f32[136,128]{1,0:T(8,128)S(1)}, f32[136,128]{1,0:T(8,128)S(1)}, u32[]{:S(2)}, u32[]{:S(2)}) collective-permute-start(f32[136,128]{1,0:T(8,128)S(1)} %get-tuple-element.45), channel_id=1, source_target_pairs={{4,8},{12,16},{20,24},{8,4},{16,12},{24,20},{5,9},{13,17},{21,25},... | collective-permute-start | bytes 208904 | tf_op jit(solution)/shard_map/ppermute | solution.py:638
  19.8 0.3 %collective-permute-done.4.x_near_ref = f32[136,128]{1,0:T(8,128)S(1)} collective-permute-done((f32[136,128]{1,0:T(8,128)S(1)}, f32[136,128]{1,0:T(8,128)S(1)}, u32[]{:S(2)}, u32[]{:S(2)}) %collective-permute-start.4) | collective-permute-done | bytes 69664 | tf_op jit(solution)/shard_map/ppermute | solution.py:638
  20.2 0.0 collective-permute-done.5.x_far_ref
  20.2 0.3 %shard_map.98 = (f32[6,4,64,128]{3,2,1,0:T(8,128)S(1)}, f32[4,64,128]{2,1,0:T(8,128)S(1)}, f32[4,64,128]{2,1,0:T(8,128)S(1)}, f32[4,64,128]{2,1,0:T(8,128)S(1)}, f32[4,64,128]{2,1,0:T(8,128)S(1)}) custom-call(f32[136,128]{1,0:T(8,128)S(1)} %collective-permute-done.4.x_near_ref, f32[136,128]{1,0:T(8,128)S(1)} %collective-permute-done.5.x_far_ref, ...), custom_call_target="tpu_custom_call" | custom-call | tf_op jit(solution)/shard_map/pallas_call | solution.py:620
  20.5 6.9 %all-to-all-done.total_ref = f32[32,3,4,128]{3,2,1,0:T(4,128)S(1)} async-done(((f32[32,3,4,128]{3,2,1,0:T(4,128)}), f32[32,3,4,128]{3,2,1,0:T(4,128)S(1)}, u32[]{:S(2)}, u32[]{:S(2)}) %all-to-all-start) | async-done | bytes 196640 | tf_op jit(solution)/shard_map/all_to_all | solution.py:651
  27.4 1.3 %shard_map.99 = (f32[4,64,128]{2,1,0:T(8,128)}, f32[4,64,128]{2,1,0:T(8,128)}) custom-call(f32[4,64,128]{2,1,0:T(8,128)S(1)} %get-tuple-element.42.conc_ref, f32[4,64,128]{2,1,0:T(8,128)S(1)} %get-tuple-element.43.pot_ref, f32[4,64,128]{2,1,0:T(8,128)S(1)} %get-tuple-element.47.mass_ref, f32[4,64,128]{2,1,0:T(8,128)S(1)} %get-tuple-element.48.pots_ref, ...), custom_call_target="tpu_custom_call" | custom-call | tf_op jit(solution)/shard_map/pallas_call | solution.py:620
Async XLA Ops:
  0.6 11.6 %copy-start.1 = (f32[4,64,128]{2,1,0:T(8,128)S(1)}, f32[4,64,128]{2,1,0:T(8,128)}, u32[]{:S(2)}) copy-start(f32[4,64,128]{2,1,0:T(8,128)} %pots_ref.5) | copy-start | bytes 393220
  0.6 11.6 %copy-start = (f32[4,64,128]{2,1,0:T(8,128)S(1)}, f32[4,64,128]{2,1,0:T(8,128)}, u32[]{:S(2)}) copy-start(f32[4,64,128]{2,1,0:T(8,128)} %mass_ref.5) | copy-start | bytes 393220
  0.7 11.6 %copy-start.3 = (f32[4,64,128]{2,1,0:T(8,128)S(1)}, f32[4,64,128]{2,1,0:T(8,128)}, u32[]{:S(2)}) copy-start(f32[4,64,128]{2,1,0:T(8,128)} %pot_ref.3) | copy-start | bytes 393220
  0.7 11.6 %copy-start.2 = (f32[4,64,128]{2,1,0:T(8,128)S(1)}, f32[4,64,128]{2,1,0:T(8,128)}, u32[]{:S(2)}) copy-start(f32[4,64,128]{2,1,0:T(8,128)} %conc_ref.3) | copy-start | bytes 393220
  0.7 11.6 %copy-start.5 = (s32[4,64,128]{2,1,0:T(8,128)S(1)}, s32[4,64,128]{2,1,0:T(8,128)}, u32[]{:S(2)}) copy-start(s32[4,64,128]{2,1,0:T(8,128)} %class_ref) | copy-start | bytes 393220
  0.7 11.6 %copy-start.4 = (s32[4,64,128]{2,1,0:T(8,128)S(1)}, s32[4,64,128]{2,1,0:T(8,128)}, u32[]{:S(2)}) copy-start(s32[4,64,128]{2,1,0:T(8,128)} %mask_ref) | copy-start | bytes 393220
  2.1 10.2 %copy-start.6 = (s32[8,64]{1,0:T(8,128)S(1)}, s32[8,64]{1,0:T(8,128)}, u32[]{:S(2)}) copy-start(s32[8,64]{1,0:T(8,128)} %owner_ref.3) | copy-start | bytes 6148
  2.1 10.1 %collective-permute-start.2 = (f32[200,128]{1,0:T(8,128)S(1)}, f32[200,128]{1,0:T(8,128)S(1)}, u32[]{:S(2)}, u32[]{:S(2)}) collective-permute-start(f32[200,128]{1,0:T(8,128)S(1)} %get-tuple-element.30), channel_id=1, source_target_pairs={{1,2},{2,1},{5,6},{6,5},{9,10},{10,9},{13,14},{14,13},{17,18},{18,... | collective-permute-start | bytes 307208 | tf_op jit(solution)/shard_map/ppermute | solution.py:638
  2.8 11.2 %collective-permute-start = (f32[192,128]{1,0:T(8,128)S(1)}, f32[192,128]{1,0:T(8,128)S(1)}, u32[]{:S(2)}, u32[]{:S(2)}) collective-permute-start(f32[192,128]{1,0:T(8,128)S(1)} %get-tuple-element.28), channel_id=1, source_target_pairs={{4,8},{12,16},{20,24},{8,4},{16,12},{24,20},{5,9},{13,17},{21,25},... | collective-permute-start | bytes 294920 | tf_op jit(solution)/shard_map/ppermute | solution.py:638
  3.4 8.8 %copy-start.7 = (f32[8]{0:T(128)S(1)}, f32[8]{0:T(128)}, u32[]{:S(2)}) copy-start(f32[8]{0:T(128)} %table_ref.1) | copy-start | bytes 100
  3.5 10.5 %collective-permute-start.1 = (f32[192,128]{1,0:T(8,128)S(1)}, f32[192,128]{1,0:T(8,128)S(1)}, u32[]{:S(2)}, u32[]{:S(2)}) collective-permute-start(f32[192,128]{1,0:T(8,128)S(1)} %get-tuple-element.29), channel_id=1, source_target_pairs={{0,4},{8,12},{16,20},{24,28},{4,0},{12,8},{20,16},{28,24},{1,5},{9... | collective-permute-start | bytes 294920 | tf_op jit(solution)/shard_map/ppermute | solution.py:638
  7.8 6.2 %collective-permute-start.3 = (f32[40,128]{1,0:T(8,128)S(1)}, f32[40,128]{1,0:T(8,128)S(1)}, u32[]{:S(2)}, u32[]{:S(2)}) collective-permute-start(f32[40,128]{1,0:T(8,128)S(1)} %get-tuple-element.32), channel_id=1, source_target_pairs={{0,1},{2,3},{1,0},{3,2},{4,5},{6,7},{5,4},{7,6},{8,9},{10,11},{9,8... | collective-permute-start | bytes 61448 | tf_op jit(solution)/shard_map/ppermute | solution.py:638
  15.3 12.2 %all-to-all-start = ((f32[32,3,4,128]{3,2,1,0:T(4,128)}), f32[32,3,4,128]{3,2,1,0:T(4,128)S(1)}, u32[]{:S(2)}, u32[]{:S(2)}) async-start(f32[32,3,4,128]{3,2,1,0:T(4,128)} %get-tuple-element.53), calls=%async_computation | async-start | bytes 393216 | tf_op jit(solution)/shard_map/all_to_all | solution.py:651
  18.8 1.3 %collective-permute-start.4 = (f32[136,128]{1,0:T(8,128)S(1)}, f32[136,128]{1,0:T(8,128)S(1)}, u32[]{:S(2)}, u32[]{:S(2)}) collective-permute-start(f32[136,128]{1,0:T(8,128)S(1)} %get-tuple-element.44), channel_id=1, source_target_pairs={{0,4},{8,12},{16,20},{24,28},{4,0},{12,8},{20,16},{28,24},{1,5},{9... | collective-permute-start | bytes 208904 | tf_op jit(solution)/shard_map/ppermute | solution.py:638
  19.1 1.0 %collective-permute-start.5 = (f32[136,128]{1,0:T(8,128)S(1)}, f32[136,128]{1,0:T(8,128)S(1)}, u32[]{:S(2)}, u32[]{:S(2)}) collective-permute-start(f32[136,128]{1,0:T(8,128)S(1)} %get-tuple-element.45), channel_id=1, source_target_pairs={{4,8},{12,16},{20,24},{8,4},{16,12},{24,20},{5,9},{13,17},{21,25},... | collective-permute-start | bytes 208904 | tf_op jit(solution)/shard_map/ppermute | solution.py:638

commit v16 on v14

--- a/solution.py
+++ b/solution.py
@@ -279,13 +279,12 @@
 
 def local_kernel(
     plan, conc_ref, pot_ref, mask_ref, class_ref, mass_ref, pots_ref, table_ref, owner_ref,
-    mob_ref, gather_ref, spread_ref, scale_ref, faces_ref, diagonal_ref, mass_out, pots_out,
+    mob_ref, gather_ref, spread_ref, faces_ref, diagonal_ref, mass_out, pots_out,
 ):
     table = [table_ref[marker] for marker in range(table_ref.shape[0])]
     mobility = mobility_of(mask_ref[...], class_ref[...], table)
     mob_ref[...] = mobility
     gather_ref[...], spread_ref[...] = membership(plan, owner_ref)
-    scale_ref[...] = scale_of(plan, owner_ref[...])
     faces = inner_faces(mobility)
     diagonal = faces[0] + jnp.concatenate([jnp.zeros_like(mobility[:1]), faces[0][:-1]], axis=0)
     for face in faces[1:]:
@@ -303,7 +302,7 @@
 
 def first_kernel(
     plan, x_far_ref, x_near_ref, y_far_ref, y_near_ref,
-    conc_ref, pot_ref, mob_ref, mass_ref, pots_ref, gather_ref, scale_ref, owner_ref,
+    conc_ref, pot_ref, mob_ref, mass_ref, pots_ref, gather_ref, owner_ref,
     faces_ref, diagonal_ref, mass_part_ref, pot_part_ref,
     conc_out, pot_out, total_hbm, raw_out, x_near_out, x_far_out, total_out, sems,
 ):
@@ -365,7 +364,7 @@
         preferred_element_type=F32,
     )
     own = own[:, : plan.p] + own[:, plan.p : 2 * plan.p] + own[:, 2 * plan.p :]
-    sums = [None, own * scale_ref[...], None]
+    sums = [None, own, None]
     for place, y, at, side in ((0, 0, plan.half_y - 1, 2), (2, plan.y - 1, 0, 3)):
         edge_pot, edge_conc = (
             jnp.concatenate([field[x, y : y + 1] for x in range(plan.x)], axis=0)
@@ -378,7 +377,7 @@
             ident = jnp.sum(jnp.where(is_mine, column, 0.0), axis=0, keepdims=True)
             pair = both[2 * i : 2 * i + 1] + both[2 * i + 1 : 2 * i + 2]
             part = part + jnp.where((owner.astype(F32) == ident) & inside[place], pair, 0.0)
-        sums[place] = part * scale_of(plan, maps[place])
+        sums[place] = part
     def store_fields():
         conc_out[...] = conc
         pot_out[...] = pot
@@ -489,10 +488,28 @@
     return coarse_conc, coarse_pot
 
 
+def weights(plan, own_map, ends):
+    owner = iota((plan.owners, 1), 0)
+    is_mine = owner == lax.axis_index("gx")
+    rows = [scale_of(plan, own_map)]
+    for end, at in zip(ends, (plan.half_y - 1, 0)):
+        owners = end[plan.map_row : plan.map_row + plan.owners, : plan.columns]
+        scale = scale_of(plan, owners)
+        for i in range(plan.half_x):
+            column = owner_column(plan, owners, i, at)
+            ident = jnp.sum(jnp.where(is_mine, column, 0.0), axis=0, keepdims=True)
+            mine = jnp.where(owner.astype(F32) == ident, scale, 0.0)
+            rows.append(jnp.sum(mine, axis=0, keepdims=True))
+    blank = 4 * plan.slot_parts - plan.high_row - plan.half_x
+    if blank:
+        rows.append(jnp.zeros((blank, plan.p), F32))
+    return jnp.concatenate(rows, axis=0)
+
+
 def beside_kernel(
     plan, x_near_ref, x_far_ref, conc_ref, pot_ref, mass_ref, pots_ref, mob_ref, raw_ref,
-    x_near_msg, x_far_msg, y_near_msg, y_far_msg,
-    faces_out, diagonal_out, scale_out, mass_out, pots_out,
+    x_near_msg, x_far_msg, y_near_msg, y_far_msg, owner_ref,
+    faces_out, diagonal_out, scale_out, mass_out, pots_out, weight_out,
 ):
     mobility = mob_ref[...]
     sides = received("gx", x_near_msg, x_far_msg)
@@ -501,6 +518,7 @@
         side_columns(plan, rows, 2) for rows in ends
     )
     faces, diagonal = faces_of(mobility, neighbours(mobility, halo))
+    weight_out[...] = weights(plan, owner_ref[...].astype(F32), ends)
     block_terms = faces, diagonal, mass_ref[...], pots_ref[...]
     for i, face in enumerate(faces):
         faces_out[i] = face
@@ -547,7 +565,7 @@
 
 def last_kernel(
     plan, conc_ref, pot_ref, mass_ref, pots_ref, faces_ref, diagonal_ref, scale_ref,
-    spread_ref, total_ref,
+    spread_ref, weight_ref, total_ref,
     conc_hbm, pot_hbm, conc_out, pot_out, sems,
 ):
     parts = []
@@ -557,9 +575,8 @@
             pairs = [a + b for a, b in zip(terms[::2], terms[1::2])]
             terms = pairs + terms[len(pairs) * 2 :]
         parts.append(terms[0])
-    solved = jnp.concatenate(
-        coarse_solve(jnp.concatenate(parts, axis=0), plan.p), axis=1
-    )
+    means = jnp.concatenate(parts, axis=0) * weight_ref[...]
+    solved = jnp.concatenate(coarse_solve(means, plan.p), axis=1)
     own = lax.dot_general(
         spread_ref[...].astype(BF16),
         three_terms(solved[: plan.owners]).astype(BF16),
@@ -688,11 +705,11 @@
     x_near, x_far = swap_near("gx", messages[0]), swap_far("gx", messages[1])
     y_near, y_far = swap_near("gy", messages[2]), swap_far("gy", messages[3])
     y_far, mask, kind = lax.optimization_barrier((y_far, mask, kind))
-    mob, gather, spread, scale, *parts = call(
+    mob, gather, spread, *parts = call(
         local_kernel,
         plan,
         [
-            block, (plan.owners, plan.rows), (plan.rows, 3 * plan.owners), (plan.owners, plan.p),
+            block, (plan.owners, plan.rows), (plan.rows, 3 * plan.owners),
             (5, *block), block, block, block,
         ],
         [conc, pot, mask, kind, mass_source, pot_source, table, owner_map],
@@ -711,7 +728,7 @@
         ],
         [
             x_far, x_near, y_far, y_near,
-            conc, pot, mob, mass_source, pot_source, gather, scale, owner_map, *parts,
+            conc, pot, mob, mass_source, pot_source, gather, owner_map, *parts,
         ],
         out_far=(2,),
         scratch=(pltpu.VMEM(slots, F32), pltpu.SemaphoreType.DMA((plan.groups,))),
@@ -719,13 +736,13 @@
     total = gather_totals(plan, total, y_near, y_far)
     far = swap_far("gx", far)
     near = swap_near("gx", near)
-    faces, diagonal, scale, mass_part, pot_part = call(
+    faces, diagonal, scale, mass_part, pot_part, weight = call(
         beside_kernel,
         plan,
-        [(6, *block), block, block, block, block],
+        [(6, *block), block, block, block, block, (4 * plan.slot_parts, plan.p)],
         [
             near, far, conc, pot, mass_source, pot_source, mob, raw,
-            x_near, x_far, y_near, y_far,
+            x_near, x_far, y_near, y_far, owner_map,
         ],
     )
     return tuple(
@@ -733,7 +750,7 @@
             last_kernel,
             plan,
             [block, block],
-            [conc, pot, mass_part, pot_part, faces, diagonal, scale, spread, total],
+            [conc, pot, mass_part, pot_part, faces, diagonal, scale, spread, weight, total],
             out_far=(0, 1),
             scratch=(
                 pltpu.VMEM(block, F32),

time: 29.1 us -> 29.1 us (level)
  no operation moved by 1% of the time
where the time goes in v16:
time: 29.1 us; the launch traced here: 28.6 us
  starting transfers between devices  14.6 us (50%)
  waiting for transfers between devices  7.86 us (27%)
  Pallas kernels  5.31 us (18%)
  between operations  0.81 us (3%)
    ppermute x6, starting transfers between devices, swap_near(): return lax.ppermute(rows, axis, pairs + [(j, i) for i, j in pairs])  11.1 us
    all_to_all x1, waiting for transfers between devices, gather_totals(): lax.all_to_all(total, ('gx', 'gy'), split_axis=0, concat_axis=0, axis_ind...  6.86 us
    pallas_call x5, Pallas kernels, call(): pl.pallas_call(functools.partial(kernel, plan), out_shape=[jax.ShapeDtype...  5.31 us
    all_to_all x1, starting transfers between devices, gather_totals(): lax.all_to_all(total, ('gx', 'gy'), split_axis=0, concat_axis=0, axis_ind...  3.56 us
    ppermute x6, waiting for transfers between devices, swap_near(): return lax.ppermute(rows, axis, pairs + [(j, i) for i, j in pairs])  1 us
  transfers between devices with their start and end apart: 7, of which 3 were waited for; matrix products, arithmetic and copies ran while one was open for 0% of the time, Pallas kernels for 5%

profile of v16, /device:TPU:0, one launch (start us, length us, event | category | flops | bytes accessed | tf_op | source)
XLA Modules:
  0.0 28.6 jit_solution(14776712873357883781)
XLA Ops:
  0.6 0.0 copy-start.1
  0.6 0.0 copy-start
  0.7 0.0 copy-start.3
  0.7 0.0 copy-start.2
  0.7 0.0 copy-start.5
  0.7 0.0 copy-start.4
  0.7 1.3 %shard_map.95 = (f32[192,128]{1,0:T(8,128)S(1)}, f32[192,128]{1,0:T(8,128)S(1)}, f32[40,128]{1,0:T(8,128)S(1)}, f32[200,128]{1,0:T(8,128)S(1)}) custom-call(f32[4,64,128]{2,1,0:T(8,128)} %conc_ref.3, f32[4,64,128]{2,1,0:T(8,128)} %pot_ref.3, s32[4,64,128]{2,1,0:T(8,128)} %mask_ref, s32[4,64,128]{2,1,0:T(8,128)} %class_ref, f32[4,64,128]{2,1,0:T(8,128)} %mass_ref.5, ...), custom_call_target="tpu_custom_call" | custom-call | tf_op jit(solution)/shard_map/pallas_call | solution.py:631
  2.0 0.0 copy-start.6
  2.0 0.7 %collective-permute-start.2 = (f32[200,128]{1,0:T(8,128)S(1)}, f32[200,128]{1,0:T(8,128)S(1)}, u32[]{:S(2)}, u32[]{:S(2)}) collective-permute-start(f32[200,128]{1,0:T(8,128)S(1)} %get-tuple-element.30), channel_id=1, source_target_pairs={{1,2},{2,1},{5,6},{6,5},{9,10},{10,9},{13,14},{14,13},{17,18},{18,... | collective-permute-start | bytes 307208 | tf_op jit(solution)/shard_map/ppermute | solution.py:649
  2.7 0.7 %collective-permute-start = (f32[192,128]{1,0:T(8,128)S(1)}, f32[192,128]{1,0:T(8,128)S(1)}, u32[]{:S(2)}, u32[]{:S(2)}) collective-permute-start(f32[192,128]{1,0:T(8,128)S(1)} %get-tuple-element.28), channel_id=1, source_target_pairs={{4,8},{12,16},{20,24},{8,4},{16,12},{24,20},{5,9},{13,17},{21,25},... | collective-permute-start | bytes 294920 | tf_op jit(solution)/shard_map/ppermute | solution.py:649
  3.4 0.0 copy-start.7
  3.4 4.4 %collective-permute-start.1 = (f32[192,128]{1,0:T(8,128)S(1)}, f32[192,128]{1,0:T(8,128)S(1)}, u32[]{:S(2)}, u32[]{:S(2)}) collective-permute-start(f32[192,128]{1,0:T(8,128)S(1)} %get-tuple-element.29), channel_id=1, source_target_pairs={{0,4},{8,12},{16,20},{24,28},{4,0},{12,8},{20,16},{28,24},{1,5},{9... | collective-permute-start | bytes 294920 | tf_op jit(solution)/shard_map/ppermute | solution.py:649
  7.7 4.4 %collective-permute-start.3 = (f32[40,128]{1,0:T(8,128)S(1)}, f32[40,128]{1,0:T(8,128)S(1)}, u32[]{:S(2)}, u32[]{:S(2)}) collective-permute-start(f32[40,128]{1,0:T(8,128)S(1)} %get-tuple-element.32), channel_id=1, source_target_pairs={{0,1},{2,3},{1,0},{3,2},{4,5},{6,7},{5,4},{7,6},{8,9},{10,11},{9,8... | collective-permute-start | bytes 61448 | tf_op jit(solution)/shard_map/ppermute | solution.py:649
  12.1 0.0 collective-permute-done.2.y_far_ref.y_far_msg
  12.1 0.0 copy-done.1
  12.1 0.0 copy-done
  12.1 0.0 copy-done.3
  12.1 0.0 copy-done.2
  12.2 0.0 copy-done.5
  12.2 0.0 copy-done.4
  12.2 0.0 copy-done.6
  12.2 0.0 copy-done.7
  12.2 1.0 %shard_map.96 = (f32[4,64,128]{2,1,0:T(8,128)S(1)}, f32[8,256]{1,0:T(8,128)S(1)}, f32[256,24]{1,0:T(8,128)S(1)}, f32[5,4,64,128]{3,2,1,0:T(8,128)S(1)}, f32[4,64...) custom-call(f32[4,64,128]{2,1,0:T(8,128)S(1)} %copy-done.2, f32[4,64,128]{2,1,0:T(8,128)S(1)} %copy-done.3, ...), custom_call_target="tpu_custom_call" | custom-call | tf_op jit(solution)/shard_map/pallas_call | solution.py:631
  13.2 0.6 %collective-permute-done.3.y_near_ref.y_near_msg = f32[40,128]{1,0:T(8,128)S(1)} collective-permute-done((f32[40,128]{1,0:T(8,128)S(1)}, f32[40,128]{1,0:T(8,128)S(1)}, u32[]{:S(2)}, u32[]{:S(2)}) %collective-permute-start.3) | collective-permute-done | bytes 20512 | tf_op jit(solution)/shard_map/ppermute | solution.py:649
  13.9 0.0 collective-permute-done.x_far_ref.x_far_msg
  13.9 0.0 collective-permute-done.1.x_near_ref.x_near_msg
  13.9 1.3 %shard_map.97 = (f32[4,64,128]{2,1,0:T(8,128)S(1)}, f32[4,64,128]{2,1,0:T(8,128)S(1)}, f32[32,3,4,128]{3,2,1,0:T(4,128)}, f32[16,128]{1,0:T(8,128)S(1)}, f32[136,128]{1,0:T(8,128)S(1)}, /*index=5*/f32[136,128]{1,0:T(8,128)S(1)}) custom-call(f32[192,128]{1,0:T(8,128)S(1)} %collective-permute-done.x_far_ref.x_far_msg, ...), custom_call_target="tpu_custom_call" | custom-call | tf_op jit(solution)/shard_map/pallas_call | solution.py:631
  15.2 3.6 %all-to-all-start = ((f32[32,3,4,128]{3,2,1,0:T(4,128)}), f32[32,3,4,128]{3,2,1,0:T(4,128)S(1)}, u32[]{:S(2)}, u32[]{:S(2)}) async-start(f32[32,3,4,128]{3,2,1,0:T(4,128)} %get-tuple-element.53), calls=%async_computation | async-start | bytes 393216 | tf_op jit(solution)/shard_map/all_to_all | solution.py:662
  18.7 0.3 %collective-permute-start.4 = (f32[136,128]{1,0:T(8,128)S(1)}, f32[136,128]{1,0:T(8,128)S(1)}, u32[]{:S(2)}, u32[]{:S(2)}) collective-permute-start(f32[136,128]{1,0:T(8,128)S(1)} %get-tuple-element.43), channel_id=1, source_target_pairs={{0,4},{8,12},{16,20},{24,28},{4,0},{12,8},{20,16},{28,24},{1,5},{9... | collective-permute-start | bytes 208904 | tf_op jit(solution)/shard_map/ppermute | solution.py:649
  19.1 0.7 %collective-permute-start.5 = (f32[136,128]{1,0:T(8,128)S(1)}, f32[136,128]{1,0:T(8,128)S(1)}, u32[]{:S(2)}, u32[]{:S(2)}) collective-permute-start(f32[136,128]{1,0:T(8,128)S(1)} %get-tuple-element.44), channel_id=1, source_target_pairs={{4,8},{12,16},{20,24},{8,4},{16,12},{24,20},{5,9},{13,17},{21,25},... | collective-permute-start | bytes 208904 | tf_op jit(solution)/shard_map/ppermute | solution.py:649
  19.7 0.3 %collective-permute-done.4.x_near_ref = f32[136,128]{1,0:T(8,128)S(1)} collective-permute-done((f32[136,128]{1,0:T(8,128)S(1)}, f32[136,128]{1,0:T(8,128)S(1)}, u32[]{:S(2)}, u32[]{:S(2)}) %collective-permute-start.4) | collective-permute-done | bytes 69664 | tf_op jit(solution)/shard_map/ppermute | solution.py:649
  20.1 0.0 collective-permute-done.5.x_far_ref
  20.1 0.4 %shard_map.98 = (f32[6,4,64,128]{3,2,1,0:T(8,128)S(1)}, f32[4,64,128]{2,1,0:T(8,128)S(1)}, f32[4,64,128]{2,1,0:T(8,128)S(1)}, f32[4,64,128]{2,1,0:T(8,128)S(1)},...) custom-call(f32[136,128]{1,0:T(8,128)S(1)} %collective-permute-done.4.x_near_ref, ...), custom_call_target="tpu_custom_call" | custom-call | tf_op jit(solution)/shard_map/pallas_call | solution.py:631
  20.5 6.9 %all-to-all-done.total_ref = f32[32,3,4,128]{3,2,1,0:T(4,128)S(1)} async-done(((f32[32,3,4,128]{3,2,1,0:T(4,128)}), f32[32,3,4,128]{3,2,1,0:T(4,128)S(1)}, u32[]{:S(2)}, u32[]{:S(2)}) %all-to-all-start) | async-done | bytes 196640 | tf_op jit(solution)/shard_map/all_to_all | solution.py:662
  27.3 1.3 %shard_map.99 = (f32[4,64,128]{2,1,0:T(8,128)}, f32[4,64,128]{2,1,0:T(8,128)}) custom-call(f32[4,64,128]{2,1,0:T(8,128)S(1)} %get-tuple-element.41.conc_ref, f32[4,64,128]{2,1,0:T(8,128)S(1)} %get-tuple-element.42.pot_ref, f32[4,64,128]{2,1,0:T(8,128)S(1)} %get-tuple-element.46.mass_ref, f32[4,64,128]{2,1,0:T(8,128)S(1)} %get-tuple-element.47.pots_ref, ...), custom_call_target="tpu_custom_call" | custom-call | tf_op jit(solution)/shard_map/pallas_call | solution.py:631
Async XLA Ops:
  0.6 11.5 %copy-start.1 = (f32[4,64,128]{2,1,0:T(8,128)S(1)}, f32[4,64,128]{2,1,0:T(8,128)}, u32[]{:S(2)}) copy-start(f32[4,64,128]{2,1,0:T(8,128)} %pots_ref.5) | copy-start | bytes 393220
  0.6 11.5 %copy-start = (f32[4,64,128]{2,1,0:T(8,128)S(1)}, f32[4,64,128]{2,1,0:T(8,128)}, u32[]{:S(2)}) copy-start(f32[4,64,128]{2,1,0:T(8,128)} %mass_ref.5) | copy-start | bytes 393220
  0.7 11.5 %copy-start.3 = (f32[4,64,128]{2,1,0:T(8,128)S(1)}, f32[4,64,128]{2,1,0:T(8,128)}, u32[]{:S(2)}) copy-start(f32[4,64,128]{2,1,0:T(8,128)} %pot_ref.3) | copy-start | bytes 393220
  0.7 11.5 %copy-start.2 = (f32[4,64,128]{2,1,0:T(8,128)S(1)}, f32[4,64,128]{2,1,0:T(8,128)}, u32[]{:S(2)}) copy-start(f32[4,64,128]{2,1,0:T(8,128)} %conc_ref.3) | copy-start | bytes 393220
  0.7 11.5 %copy-start.5 = (s32[4,64,128]{2,1,0:T(8,128)S(1)}, s32[4,64,128]{2,1,0:T(8,128)}, u32[]{:S(2)}) copy-start(s32[4,64,128]{2,1,0:T(8,128)} %class_ref) | copy-start | bytes 393220
  0.7 11.5 %copy-start.4 = (s32[4,64,128]{2,1,0:T(8,128)S(1)}, s32[4,64,128]{2,1,0:T(8,128)}, u32[]{:S(2)}) copy-start(s32[4,64,128]{2,1,0:T(8,128)} %mask_ref) | copy-start | bytes 393220
  2.0 10.2 %copy-start.6 = (s32[8,64]{1,0:T(8,128)S(1)}, s32[8,64]{1,0:T(8,128)}, u32[]{:S(2)}) copy-start(s32[8,64]{1,0:T(8,128)} %owner_ref.5) | copy-start | bytes 6148
  2.0 10.1 %collective-permute-start.2 = (f32[200,128]{1,0:T(8,128)S(1)}, f32[200,128]{1,0:T(8,128)S(1)}, u32[]{:S(2)}, u32[]{:S(2)}) collective-permute-start(f32[200,128]{1,0:T(8,128)S(1)} %get-tuple-element.30), channel_id=1, source_target_pairs={{1,2},{2,1},{5,6},{6,5},{9,10},{10,9},{13,14},{14,13},{17,18},{18,... | collective-permute-start | bytes 307208 | tf_op jit(solution)/shard_map/ppermute | solution.py:649
  2.7 11.2 %collective-permute-start = (f32[192,128]{1,0:T(8,128)S(1)}, f32[192,128]{1,0:T(8,128)S(1)}, u32[]{:S(2)}, u32[]{:S(2)}) collective-permute-start(f32[192,128]{1,0:T(8,128)S(1)} %get-tuple-element.28), channel_id=1, source_target_pairs={{4,8},{12,16},{20,24},{8,4},{16,12},{24,20},{5,9},{13,17},{21,25},... | collective-permute-start | bytes 294920 | tf_op jit(solution)/shard_map/ppermute | solution.py:649
  3.4 8.8 %copy-start.7 = (f32[8]{0:T(128)S(1)}, f32[8]{0:T(128)}, u32[]{:S(2)}) copy-start(f32[8]{0:T(128)} %table_ref.1) | copy-start | bytes 100
  3.4 10.5 %collective-permute-start.1 = (f32[192,128]{1,0:T(8,128)S(1)}, f32[192,128]{1,0:T(8,128)S(1)}, u32[]{:S(2)}, u32[]{:S(2)}) collective-permute-start(f32[192,128]{1,0:T(8,128)S(1)} %get-tuple-element.29), channel_id=1, source_target_pairs={{0,4},{8,12},{16,20},{24,28},{4,0},{12,8},{20,16},{28,24},{1,5},{9... | collective-permute-start | bytes 294920 | tf_op jit(solution)/shard_map/ppermute | solution.py:649
  7.7 6.2 %collective-permute-start.3 = (f32[40,128]{1,0:T(8,128)S(1)}, f32[40,128]{1,0:T(8,128)S(1)}, u32[]{:S(2)}, u32[]{:S(2)}) collective-permute-start(f32[40,128]{1,0:T(8,128)S(1)} %get-tuple-element.32), channel_id=1, source_target_pairs={{0,1},{2,3},{1,0},{3,2},{4,5},{6,7},{5,4},{7,6},{8,9},{10,11},{9,8... | collective-permute-start | bytes 61448 | tf_op jit(solution)/shard_map/ppermute | solution.py:649
  15.2 12.2 %all-to-all-start = ((f32[32,3,4,128]{3,2,1,0:T(4,128)}), f32[32,3,4,128]{3,2,1,0:T(4,128)S(1)}, u32[]{:S(2)}, u32[]{:S(2)}) async-start(f32[32,3,4,128]{3,2,1,0:T(4,128)} %get-tuple-element.53), calls=%async_computation | async-start | bytes 393216 | tf_op jit(solution)/shard_map/all_to_all | solution.py:662
  18.7 1.3 %collective-permute-start.4 = (f32[136,128]{1,0:T(8,128)S(1)}, f32[136,128]{1,0:T(8,128)S(1)}, u32[]{:S(2)}, u32[]{:S(2)}) collective-permute-start(f32[136,128]{1,0:T(8,128)S(1)} %get-tuple-element.43), channel_id=1, source_target_pairs={{0,4},{8,12},{16,20},{24,28},{4,0},{12,8},{20,16},{28,24},{1,5},{9... | collective-permute-start | bytes 208904 | tf_op jit(solution)/shard_map/ppermute | solution.py:649
  19.1 1.0 %collective-permute-start.5 = (f32[136,128]{1,0:T(8,128)S(1)}, f32[136,128]{1,0:T(8,128)S(1)}, u32[]{:S(2)}, u32[]{:S(2)}) collective-permute-start(f32[136,128]{1,0:T(8,128)S(1)} %get-tuple-element.44), channel_id=1, source_target_pairs={{4,8},{12,16},{20,24},{8,4},{16,12},{24,20},{5,9},{13,17},{21,25},... | collective-permute-start | bytes 208904 | tf_op jit(solution)/shard_map/ppermute | solution.py:649

commit v17 on v14

--- a/solution.py
+++ b/solution.py
@@ -118,7 +118,8 @@
     def slot_of(self, g, h):
         last = self.groups - 1
         place = 0 if h == 0 else 1 if h == last else h + 1
-        return place * self.owners + self.owners - 1 - (g ^ 1)
+        low = self.owners - 1 if g == 0 else 0 if g == 1 else self.owners - g
+        return place * self.owners + low
 
 
 def side_rows(plan, rows, which):
@@ -441,7 +442,7 @@
                 total_out[slot, part] = main[4 * part : 4 * part + 4]
             for row, values in beside:
                 total_out[slot, row // 4, pl.ds(row % 4, 1), :] = values[g : g + 1]
-        some = pl.ds(plan.slot_of(plan.owners - 2, plane), plan.owners)
+        some = pl.ds(plan.slot_of(1, plane), plan.owners)
         copies.append(
             pltpu.make_async_copy(total_out.at[some], total_hbm.at[some], sems.at[plane])
         )

time: 29.1 us -> 30 us (1.031)
  waiting for transfers between devices: 7.9 us -> 8.98 us
    all_to_all x1, waiting for transfers between devices: 6.91 us -> 7.99 us  [gather_totals(): lax.all_to_all(total, ('gx', 'gy'), split_axis=0, concat_axis=0, axis_ind...]
where the time goes in v17:
time: 30 us; the launch traced here: 29.7 us
  starting transfers between devices  14.6 us (49%)
  waiting for transfers between devices  8.98 us (30%)
  Pallas kernels  5.27 us (18%)
  between operations  0.81 us (3%)
    ppermute x6, starting transfers between devices, swap_near(): return lax.ppermute(rows, axis, pairs + [(j, i) for i, j in pairs])  11.1 us
    all_to_all x1, waiting for transfers between devices, gather_totals(): lax.all_to_all(total, ('gx', 'gy'), split_axis=0, concat_axis=0, axis_ind...  7.99 us
    pallas_call x5, Pallas kernels, call(): pl.pallas_call(functools.partial(kernel, plan), out_shape=[jax.ShapeDtype...  5.27 us
    all_to_all x1, starting transfers between devices, gather_totals(): lax.all_to_all(total, ('gx', 'gy'), split_axis=0, concat_axis=0, axis_ind...  3.56 us
    ppermute x6, waiting for transfers between devices, swap_near(): return lax.ppermute(rows, axis, pairs + [(j, i) for i, j in pairs])  0.99 us
  transfers between devices with their start and end apart: 7, of which 3 were waited for; matrix products, arithmetic and copies ran while one was open for 0% of the time, Pallas kernels for 5%

profile of v17, /device:TPU:0, one launch (start us, length us, event | category | flops | bytes accessed | tf_op | source)
XLA Modules:
  0.0 29.7 jit_solution(6743205909792510297)
XLA Ops:
  0.6 0.0 copy-start.1
  0.6 0.0 copy-start
  0.7 0.0 copy-start.3
  0.7 0.0 copy-start.2
  0.7 0.0 copy-start.5
  0.7 0.0 copy-start.4
  0.7 1.3 %shard_map.95 = (f32[192,128]{1,0:T(8,128)S(1)}, f32[192,128]{1,0:T(8,128)S(1)}, f32[40,128]{1,0:T(8,128)S(1)}, f32[200,128]{1,0:T(8,128)S(1)}) custom-call(f32[4,64,128]{2,1,0:T(8,128)} %conc_ref.3, f32[4,64,128]{2,1,0:T(8,128)} %pot_ref.3, s32[4,64,128]{2,1,0:T(8,128)} %mask_ref, s32[4,64,128]{2,1,0:T(8,128)} %class_ref, f32[4,64,128]{2,1,0:T(8,128)} %mass_ref.5, ...), custom_call_target="tpu_custom_call" | custom-call | tf_op jit(solution)/shard_map/pallas_call | solution.py:615
  2.0 0.0 copy-start.6
  2.0 0.7 %collective-permute-start.2 = (f32[200,128]{1,0:T(8,128)S(1)}, f32[200,128]{1,0:T(8,128)S(1)}, u32[]{:S(2)}, u32[]{:S(2)}) collective-permute-start(f32[200,128]{1,0:T(8,128)S(1)} %get-tuple-element.30), channel_id=1, source_target_pairs={{1,2},{2,1},{5,6},{6,5},{9,10},{10,9},{13,14},{14,13},{17,18},{18,... | collective-permute-start | bytes 307208 | tf_op jit(solution)/shard_map/ppermute | solution.py:633
  2.7 0.7 %collective-permute-start = (f32[192,128]{1,0:T(8,128)S(1)}, f32[192,128]{1,0:T(8,128)S(1)}, u32[]{:S(2)}, u32[]{:S(2)}) collective-permute-start(f32[192,128]{1,0:T(8,128)S(1)} %get-tuple-element.28), channel_id=1, source_target_pairs={{4,8},{12,16},{20,24},{8,4},{16,12},{24,20},{5,9},{13,17},{21,25},... | collective-permute-start | bytes 294920 | tf_op jit(solution)/shard_map/ppermute | solution.py:633
  3.4 0.0 copy-start.7
  3.4 4.4 %collective-permute-start.1 = (f32[192,128]{1,0:T(8,128)S(1)}, f32[192,128]{1,0:T(8,128)S(1)}, u32[]{:S(2)}, u32[]{:S(2)}) collective-permute-start(f32[192,128]{1,0:T(8,128)S(1)} %get-tuple-element.29), channel_id=1, source_target_pairs={{0,4},{8,12},{16,20},{24,28},{4,0},{12,8},{20,16},{28,24},{1,5},{9... | collective-permute-start | bytes 294920 | tf_op jit(solution)/shard_map/ppermute | solution.py:633
  7.7 4.4 %collective-permute-start.3 = (f32[40,128]{1,0:T(8,128)S(1)}, f32[40,128]{1,0:T(8,128)S(1)}, u32[]{:S(2)}, u32[]{:S(2)}) collective-permute-start(f32[40,128]{1,0:T(8,128)S(1)} %get-tuple-element.32), channel_id=1, source_target_pairs={{0,1},{2,3},{1,0},{3,2},{4,5},{6,7},{5,4},{7,6},{8,9},{10,11},{9,8... | collective-permute-start | bytes 61448 | tf_op jit(solution)/shard_map/ppermute | solution.py:633
  12.1 0.0 collective-permute-done.2.y_far_ref.y_far_msg
  12.1 0.0 copy-done.1
  12.1 0.0 copy-done
  12.1 0.0 copy-done.3
  12.1 0.0 copy-done.2
  12.2 0.0 copy-done.5
  12.2 0.0 copy-done.4
  12.2 0.0 copy-done.6
  12.2 0.0 copy-done.7
  12.2 1.1 %shard_map.96 = (f32[4,64,128]{2,1,0:T(8,128)S(1)}, f32[8,256]{1,0:T(8,128)S(1)}, f32[256,24]{1,0:T(8,128)S(1)}, f32[8,128]{1,0:T(8,128)S(1)}, f32[5,4,64,128]{3...) custom-call(f32[4,64,128]{2,1,0:T(8,128)S(1)} %copy-done.2, ...), custom_call_target="tpu_custom_call" | custom-call | tf_op jit(solution)/shard_map/pallas_call | solution.py:615
  13.3 0.6 %collective-permute-done.3.y_near_ref.y_near_msg = f32[40,128]{1,0:T(8,128)S(1)} collective-permute-done((f32[40,128]{1,0:T(8,128)S(1)}, f32[40,128]{1,0:T(8,128)S(1)}, u32[]{:S(2)}, u32[]{:S(2)}) %collective-permute-start.3) | collective-permute-done | bytes 20512 | tf_op jit(solution)/shard_map/ppermute | solution.py:633
  13.9 0.0 collective-permute-done.x_far_ref.x_far_msg
  13.9 0.0 collective-permute-done.1.x_near_ref.x_near_msg
  13.9 1.3 %shard_map.97 = (f32[4,64,128]{2,1,0:T(8,128)S(1)}, f32[4,64,128]{2,1,0:T(8,128)S(1)}, f32[32,3,4,128]{3,2,1,0:T(4,128)}, f32[16,128]{1,0:T(8,128)S(1)}, f32[136,128]{1,0:T(8,128)S(1)}, /*index=5*/f32[136,128]{1,0:T(8,128)S(1)}) custom-call(f32[192,128]{1,0:T(8,128)S(1)} %collective-permute-done.x_far_ref.x_far_msg, ...), custom_call_target="tpu_custom_call" | custom-call | tf_op jit(solution)/shard_map/pallas_call | solution.py:615
  15.2 3.6 %all-to-all-start = ((f32[32,3,4,128]{3,2,1,0:T(4,128)}), f32[32,3,4,128]{3,2,1,0:T(4,128)S(1)}, u32[]{:S(2)}, u32[]{:S(2)}) async-start(f32[32,3,4,128]{3,2,1,0:T(4,128)} %get-tuple-element.53), calls=%async_computation | async-start | bytes 393216 | tf_op jit(solution)/shard_map/all_to_all | solution.py:646
  18.7 0.3 %collective-permute-start.4 = (f32[136,128]{1,0:T(8,128)S(1)}, f32[136,128]{1,0:T(8,128)S(1)}, u32[]{:S(2)}, u32[]{:S(2)}) collective-permute-start(f32[136,128]{1,0:T(8,128)S(1)} %get-tuple-element.44), channel_id=1, source_target_pairs={{0,4},{8,12},{16,20},{24,28},{4,0},{12,8},{20,16},{28,24},{1,5},{9... | collective-permute-start | bytes 208904 | tf_op jit(solution)/shard_map/ppermute | solution.py:633
  19.1 0.7 %collective-permute-start.5 = (f32[136,128]{1,0:T(8,128)S(1)}, f32[136,128]{1,0:T(8,128)S(1)}, u32[]{:S(2)}, u32[]{:S(2)}) collective-permute-start(f32[136,128]{1,0:T(8,128)S(1)} %get-tuple-element.45), channel_id=1, source_target_pairs={{4,8},{12,16},{20,24},{8,4},{16,12},{24,20},{5,9},{13,17},{21,25},... | collective-permute-start | bytes 208904 | tf_op jit(solution)/shard_map/ppermute | solution.py:633
  19.7 0.3 %collective-permute-done.4.x_near_ref = f32[136,128]{1,0:T(8,128)S(1)} collective-permute-done((f32[136,128]{1,0:T(8,128)S(1)}, f32[136,128]{1,0:T(8,128)S(1)}, u32[]{:S(2)}, u32[]{:S(2)}) %collective-permute-start.4) | collective-permute-done | bytes 69664 | tf_op jit(solution)/shard_map/ppermute | solution.py:633
  20.1 0.0 collective-permute-done.5.x_far_ref
  20.1 0.3 %shard_map.98 = (f32[6,4,64,128]{3,2,1,0:T(8,128)S(1)}, f32[4,64,128]{2,1,0:T(8,128)S(1)}, f32[4,64,128]{2,1,0:T(8,128)S(1)}, f32[4,64,128]{2,1,0:T(8,128)S(1)}, f32[4,64,128]{2,1,0:T(8,128)S(1)}) custom-call(f32[136,128]{1,0:T(8,128)S(1)} %collective-permute-done.4.x_near_ref, f32[136,128]{1,0:T(8,128)S(1)} %collective-permute-done.5.x_far_ref, ...), custom_call_target="tpu_custom_call" | custom-call | tf_op jit(solution)/shard_map/pallas_call | solution.py:615
  20.4 8.0 %all-to-all-done.total_ref = f32[32,3,4,128]{3,2,1,0:T(4,128)S(1)} async-done(((f32[32,3,4,128]{3,2,1,0:T(4,128)}), f32[32,3,4,128]{3,2,1,0:T(4,128)S(1)}, u32[]{:S(2)}, u32[]{:S(2)}) %all-to-all-start) | async-done | bytes 196640 | tf_op jit(solution)/shard_map/all_to_all | solution.py:646
  28.4 1.3 %shard_map.99 = (f32[4,64,128]{2,1,0:T(8,128)}, f32[4,64,128]{2,1,0:T(8,128)}) custom-call(f32[4,64,128]{2,1,0:T(8,128)S(1)} %get-tuple-element.42.conc_ref, f32[4,64,128]{2,1,0:T(8,128)S(1)} %get-tuple-element.43.pot_ref, f32[4,64,128]{2,1,0:T(8,128)S(1)} %get-tuple-element.47.mass_ref, f32[4,64,128]{2,1,0:T(8,128)S(1)} %get-tuple-element.48.pots_ref, ...), custom_call_target="tpu_custom_call" | custom-call | tf_op jit(solution)/shard_map/pallas_call | solution.py:615
Async XLA Ops:
  0.6 11.5 %copy-start.1 = (f32[4,64,128]{2,1,0:T(8,128)S(1)}, f32[4,64,128]{2,1,0:T(8,128)}, u32[]{:S(2)}) copy-start(f32[4,64,128]{2,1,0:T(8,128)} %pots_ref.5) | copy-start | bytes 393220
  0.6 11.5 %copy-start = (f32[4,64,128]{2,1,0:T(8,128)S(1)}, f32[4,64,128]{2,1,0:T(8,128)}, u32[]{:S(2)}) copy-start(f32[4,64,128]{2,1,0:T(8,128)} %mass_ref.5) | copy-start | bytes 393220
  0.7 11.5 %copy-start.3 = (f32[4,64,128]{2,1,0:T(8,128)S(1)}, f32[4,64,128]{2,1,0:T(8,128)}, u32[]{:S(2)}) copy-start(f32[4,64,128]{2,1,0:T(8,128)} %pot_ref.3) | copy-start | bytes 393220
  0.7 11.5 %copy-start.2 = (f32[4,64,128]{2,1,0:T(8,128)S(1)}, f32[4,64,128]{2,1,0:T(8,128)}, u32[]{:S(2)}) copy-start(f32[4,64,128]{2,1,0:T(8,128)} %conc_ref.3) | copy-start | bytes 393220
  0.7 11.5 %copy-start.5 = (s32[4,64,128]{2,1,0:T(8,128)S(1)}, s32[4,64,128]{2,1,0:T(8,128)}, u32[]{:S(2)}) copy-start(s32[4,64,128]{2,1,0:T(8,128)} %class_ref) | copy-start | bytes 393220
  0.7 11.5 %copy-start.4 = (s32[4,64,128]{2,1,0:T(8,128)S(1)}, s32[4,64,128]{2,1,0:T(8,128)}, u32[]{:S(2)}) copy-start(s32[4,64,128]{2,1,0:T(8,128)} %mask_ref) | copy-start | bytes 393220
  2.0 10.2 %copy-start.6 = (s32[8,64]{1,0:T(8,128)S(1)}, s32[8,64]{1,0:T(8,128)}, u32[]{:S(2)}) copy-start(s32[8,64]{1,0:T(8,128)} %owner_ref.3) | copy-start | bytes 6148
  2.0 10.1 %collective-permute-start.2 = (f32[200,128]{1,0:T(8,128)S(1)}, f32[200,128]{1,0:T(8,128)S(1)}, u32[]{:S(2)}, u32[]{:S(2)}) collective-permute-start(f32[200,128]{1,0:T(8,128)S(1)} %get-tuple-element.30), channel_id=1, source_target_pairs={{1,2},{2,1},{5,6},{6,5},{9,10},{10,9},{13,14},{14,13},{17,18},{18,... | collective-permute-start | bytes 307208 | tf_op jit(solution)/shard_map/ppermute | solution.py:633
  2.7 11.2 %collective-permute-start = (f32[192,128]{1,0:T(8,128)S(1)}, f32[192,128]{1,0:T(8,128)S(1)}, u32[]{:S(2)}, u32[]{:S(2)}) collective-permute-start(f32[192,128]{1,0:T(8,128)S(1)} %get-tuple-element.28), channel_id=1, source_target_pairs={{4,8},{12,16},{20,24},{8,4},{16,12},{24,20},{5,9},{13,17},{21,25},... | collective-permute-start | bytes 294920 | tf_op jit(solution)/shard_map/ppermute | solution.py:633
  3.4 8.8 %copy-start.7 = (f32[8]{0:T(128)S(1)}, f32[8]{0:T(128)}, u32[]{:S(2)}) copy-start(f32[8]{0:T(128)} %table_ref.1) | copy-start | bytes 100
  3.4 10.5 %collective-permute-start.1 = (f32[192,128]{1,0:T(8,128)S(1)}, f32[192,128]{1,0:T(8,128)S(1)}, u32[]{:S(2)}, u32[]{:S(2)}) collective-permute-start(f32[192,128]{1,0:T(8,128)S(1)} %get-tuple-element.29), channel_id=1, source_target_pairs={{0,4},{8,12},{16,20},{24,28},{4,0},{12,8},{20,16},{28,24},{1,5},{9... | collective-permute-start | bytes 294920 | tf_op jit(solution)/shard_map/ppermute | solution.py:633
  7.7 6.2 %collective-permute-start.3 = (f32[40,128]{1,0:T(8,128)S(1)}, f32[40,128]{1,0:T(8,128)S(1)}, u32[]{:S(2)}, u32[]{:S(2)}) collective-permute-start(f32[40,128]{1,0:T(8,128)S(1)} %get-tuple-element.32), channel_id=1, source_target_pairs={{0,1},{2,3},{1,0},{3,2},{4,5},{6,7},{5,4},{7,6},{8,9},{10,11},{9,8... | collective-permute-start | bytes 61448 | tf_op jit(solution)/shard_map/ppermute | solution.py:633
  15.2 13.2 %all-to-all-start = ((f32[32,3,4,128]{3,2,1,0:T(4,128)}), f32[32,3,4,128]{3,2,1,0:T(4,128)S(1)}, u32[]{:S(2)}, u32[]{:S(2)}) async-start(f32[32,3,4,128]{3,2,1,0:T(4,128)} %get-tuple-element.53), calls=%async_computation | async-start | bytes 393216 | tf_op jit(solution)/shard_map/all_to_all | solution.py:646
  18.7 1.3 %collective-permute-start.4 = (f32[136,128]{1,0:T(8,128)S(1)}, f32[136,128]{1,0:T(8,128)S(1)}, u32[]{:S(2)}, u32[]{:S(2)}) collective-permute-start(f32[136,128]{1,0:T(8,128)S(1)} %get-tuple-element.44), channel_id=1, source_target_pairs={{0,4},{8,12},{16,20},{24,28},{4,0},{12,8},{20,16},{28,24},{1,5},{9... | collective-permute-start | bytes 208904 | tf_op jit(solution)/shard_map/ppermute | solution.py:633
  19.1 1.0 %collective-permute-start.5 = (f32[136,128]{1,0:T(8,128)S(1)}, f32[136,128]{1,0:T(8,128)S(1)}, u32[]{:S(2)}, u32[]{:S(2)}) collective-permute-start(f32[136,128]{1,0:T(8,128)S(1)} %get-tuple-element.45), channel_id=1, source_target_pairs={{4,8},{12,16},{20,24},{8,4},{16,12},{24,20},{5,9},{13,17},{21,25},... | collective-permute-start | bytes 208904 | tf_op jit(solution)/shard_map/ppermute | solution.py:633

commit v18 on v14

--- a/solution.py
+++ b/solution.py
@@ -490,7 +490,7 @@
 
 
 def beside_kernel(
-    plan, x_near_ref, x_far_ref, conc_ref, pot_ref, mass_ref, pots_ref, mob_ref, raw_ref,
+    plan, x_far_ref, x_near_ref, conc_ref, pot_ref, mass_ref, pots_ref, mob_ref, raw_ref,
     x_near_msg, x_far_msg, y_near_msg, y_far_msg,
     faces_out, diagonal_out, scale_out, mass_out, pots_out,
 ):
@@ -724,7 +724,7 @@
         plan,
         [(6, *block), block, block, block, block],
         [
-            near, far, conc, pot, mass_source, pot_source, mob, raw,
+            far, near, conc, pot, mass_source, pot_source, mob, raw,
             x_near, x_far, y_near, y_far,
         ],
     )

time: 29.1 us -> 29.1 us (level)
  starting transfers between devices: 14.6 us -> 17.5 us
  waiting for transfers between devices: 7.9 us -> 5.01 us
    all_to_all x1, waiting for transfers between devices: 6.91 us -> 3.47 us  [gather_totals(): lax.all_to_all(total, ('gx', 'gy'), split_axis=0, concat_axis=0, axis_ind...]
    ppermute x6, starting transfers between devices: 11.1 us -> 13.9 us  [swap_near(): return lax.ppermute(rows, axis, pairs + [(j, i) for i, j in pairs])]
    ppermute x6, waiting for transfers between devices: 0.99 us -> 1.54 us  [swap_near(): return lax.ppermute(rows, axis, pairs + [(j, i) for i, j in pairs])]
where the time goes in v18:
time: 29.1 us; the launch traced here: 28.6 us
  starting transfers between devices  17.5 us (60%)
  Pallas kernels  5.27 us (18%)
  waiting for transfers between devices  5.01 us (17%)
  between operations  0.81 us (3%)
    ppermute x6, starting transfers between devices, swap_near(): return lax.ppermute(rows, axis, pairs + [(j, i) for i, j in pairs])  13.9 us
    pallas_call x5, Pallas kernels, call(): pl.pallas_call(functools.partial(kernel, plan), out_shape=[jax.ShapeDtype...  5.27 us
    all_to_all x1, starting transfers between devices, gather_totals(): lax.all_to_all(total, ('gx', 'gy'), split_axis=0, concat_axis=0, axis_ind...  3.56 us
    all_to_all x1, waiting for transfers between devices, gather_totals(): lax.all_to_all(total, ('gx', 'gy'), split_axis=0, concat_axis=0, axis_ind...  3.47 us
    ppermute x6, waiting for transfers between devices, swap_near(): return lax.ppermute(rows, axis, pairs + [(j, i) for i, j in pairs])  1.54 us
  transfers between devices with their start and end apart: 7, of which 3 were waited for; matrix products, arithmetic and copies ran while one was open for 0% of the time, Pallas kernels for 5%

profile of v18, /device:TPU:0, one launch (start us, length us, event | category | flops | bytes accessed | tf_op | source)
XLA Modules:
  0.0 28.6 jit_solution(6615600088300454867)
XLA Ops:
  0.6 0.0 copy-start.1
  0.6 0.0 copy-start
  0.7 0.0 copy-start.3
  0.7 0.0 copy-start.2
  0.7 0.0 copy-start.5
  0.7 0.0 copy-start.4
  0.7 1.3 %shard_map.95 = (f32[192,128]{1,0:T(8,128)S(1)}, f32[192,128]{1,0:T(8,128)S(1)}, f32[40,128]{1,0:T(8,128)S(1)}, f32[200,128]{1,0:T(8,128)S(1)}) custom-call(f32[4,64,128]{2,1,0:T(8,128)} %conc_ref.3, f32[4,64,128]{2,1,0:T(8,128)} %pot_ref.3, s32[4,64,128]{2,1,0:T(8,128)} %mask_ref, s32[4,64,128]{2,1,0:T(8,128)} %class_ref, f32[4,64,128]{2,1,0:T(8,128)} %mass_ref.5, ...), custom_call_target="tpu_custom_call" | custom-call | tf_op jit(solution)/shard_map/pallas_call | solution.py:614
  2.0 0.0 copy-start.6
  2.0 0.7 %collective-permute-start.2 = (f32[200,128]{1,0:T(8,128)S(1)}, f32[200,128]{1,0:T(8,128)S(1)}, u32[]{:S(2)}, u32[]{:S(2)}) collective-permute-start(f32[200,128]{1,0:T(8,128)S(1)} %get-tuple-element.30), channel_id=1, source_target_pairs={{1,2},{2,1},{5,6},{6,5},{9,10},{10,9},{13,14},{14,13},{17,18},{18,... | collective-permute-start | bytes 307208 | tf_op jit(solution)/shard_map/ppermute | solution.py:632
  2.7 0.7 %collective-permute-start = (f32[192,128]{1,0:T(8,128)S(1)}, f32[192,128]{1,0:T(8,128)S(1)}, u32[]{:S(2)}, u32[]{:S(2)}) collective-permute-start(f32[192,128]{1,0:T(8,128)S(1)} %get-tuple-element.28), channel_id=1, source_target_pairs={{4,8},{12,16},{20,24},{8,4},{16,12},{24,20},{5,9},{13,17},{21,25},... | collective-permute-start | bytes 294920 | tf_op jit(solution)/shard_map/ppermute | solution.py:632
  3.4 0.0 copy-start.7
  3.4 4.4 %collective-permute-start.1 = (f32[192,128]{1,0:T(8,128)S(1)}, f32[192,128]{1,0:T(8,128)S(1)}, u32[]{:S(2)}, u32[]{:S(2)}) collective-permute-start(f32[192,128]{1,0:T(8,128)S(1)} %get-tuple-element.29), channel_id=1, source_target_pairs={{0,4},{8,12},{16,20},{24,28},{4,0},{12,8},{20,16},{28,24},{1,5},{9... | collective-permute-start | bytes 294920 | tf_op jit(solution)/shard_map/ppermute | solution.py:632
  7.7 4.4 %collective-permute-start.3 = (f32[40,128]{1,0:T(8,128)S(1)}, f32[40,128]{1,0:T(8,128)S(1)}, u32[]{:S(2)}, u32[]{:S(2)}) collective-permute-start(f32[40,128]{1,0:T(8,128)S(1)} %get-tuple-element.32), channel_id=1, source_target_pairs={{0,1},{2,3},{1,0},{3,2},{4,5},{6,7},{5,4},{7,6},{8,9},{10,11},{9,8... | collective-permute-start | bytes 61448 | tf_op jit(solution)/shard_map/ppermute | solution.py:632
  12.1 0.0 collective-permute-done.2.y_far_ref.y_far_msg
  12.1 0.0 copy-done.1
  12.1 0.0 copy-done
  12.1 0.0 copy-done.3
  12.1 0.0 copy-done.2
  12.2 0.0 copy-done.5
  12.2 0.0 copy-done.4
  12.2 0.0 copy-done.6
  12.2 0.0 copy-done.7
  12.2 1.1 %shard_map.96 = (f32[4,64,128]{2,1,0:T(8,128)S(1)}, f32[8,256]{1,0:T(8,128)S(1)}, f32[256,24]{1,0:T(8,128)S(1)}, f32[8,128]{1,0:T(8,128)S(1)}, f32[5,4,64,128]{3...) custom-call(f32[4,64,128]{2,1,0:T(8,128)S(1)} %copy-done.2, ...), custom_call_target="tpu_custom_call" | custom-call | tf_op jit(solution)/shard_map/pallas_call | solution.py:614
  13.3 0.6 %collective-permute-done.3.y_near_ref.y_near_msg = f32[40,128]{1,0:T(8,128)S(1)} collective-permute-done((f32[40,128]{1,0:T(8,128)S(1)}, f32[40,128]{1,0:T(8,128)S(1)}, u32[]{:S(2)}, u32[]{:S(2)}) %collective-permute-start.3) | collective-permute-done | bytes 20512 | tf_op jit(solution)/shard_map/ppermute | solution.py:632
  13.9 0.0 collective-permute-done.x_far_ref.x_far_msg
  13.9 0.0 collective-permute-done.1.x_near_ref.x_near_msg
  13.9 1.3 %shard_map.97 = (f32[4,64,128]{2,1,0:T(8,128)S(1)}, f32[4,64,128]{2,1,0:T(8,128)S(1)}, f32[32,3,4,128]{3,2,1,0:T(4,128)}, f32[16,128]{1,0:T(8,128)S(1)}, f32[136,128]{1,0:T(8,128)S(1)}, /*index=5*/f32[136,128]{1,0:T(8,128)S(1)}) custom-call(f32[192,128]{1,0:T(8,128)S(1)} %collective-permute-done.x_far_ref.x_far_msg, ...), custom_call_target="tpu_custom_call" | custom-call | tf_op jit(solution)/shard_map/pallas_call | solution.py:614
  15.2 3.6 %all-to-all-start = ((f32[32,3,4,128]{3,2,1,0:T(4,128)}), f32[32,3,4,128]{3,2,1,0:T(4,128)S(1)}, u32[]{:S(2)}, u32[]{:S(2)}) async-start(f32[32,3,4,128]{3,2,1,0:T(4,128)} %get-tuple-element.53), calls=%async_computation | async-start | bytes 393216 | tf_op jit(solution)/shard_map/all_to_all | solution.py:645
  18.7 0.7 %collective-permute-start.4 = (f32[136,128]{1,0:T(8,128)S(1)}, f32[136,128]{1,0:T(8,128)S(1)}, u32[]{:S(2)}, u32[]{:S(2)}) collective-permute-start(f32[136,128]{1,0:T(8,128)S(1)} %get-tuple-element.44), channel_id=1, source_target_pairs={{4,8},{12,16},{20,24},{8,4},{16,12},{24,20},{5,9},{13,17},{21,25},... | collective-permute-start | bytes 208904 | tf_op jit(solution)/shard_map/ppermute | solution.py:632
  19.4 3.2 %collective-permute-start.5 = (f32[136,128]{1,0:T(8,128)S(1)}, f32[136,128]{1,0:T(8,128)S(1)}, u32[]{:S(2)}, u32[]{:S(2)}) collective-permute-start(f32[136,128]{1,0:T(8,128)S(1)} %get-tuple-element.45), channel_id=1, source_target_pairs={{0,4},{8,12},{16,20},{24,28},{4,0},{12,8},{20,16},{28,24},{1,5},{9... | collective-permute-start | bytes 208904 | tf_op jit(solution)/shard_map/ppermute | solution.py:632
  22.6 0.0 collective-permute-done.4.x_far_ref
  22.6 0.9 %collective-permute-done.5.x_near_ref = f32[136,128]{1,0:T(8,128)S(1)} collective-permute-done((f32[136,128]{1,0:T(8,128)S(1)}, f32[136,128]{1,0:T(8,128)S(1)}, u32[]{:S(2)}, u32[]{:S(2)}) %collective-permute-start.5) | collective-permute-done | bytes 69664 | tf_op jit(solution)/shard_map/ppermute | solution.py:632
  23.5 0.3 %shard_map.98 = (f32[6,4,64,128]{3,2,1,0:T(8,128)S(1)}, f32[4,64,128]{2,1,0:T(8,128)S(1)}, f32[4,64,128]{2,1,0:T(8,128)S(1)}, f32[4,64,128]{2,1,0:T(8,128)S(1)}, f32[4,64,128]{2,1,0:T(8,128)S(1)}) custom-call(f32[136,128]{1,0:T(8,128)S(1)} %collective-permute-done.4.x_far_ref, f32[136,128]{1,0:T(8,128)S(1)} %collective-permute-done.5.x_near_ref, ...), custom_call_target="tpu_custom_call" | custom-call | tf_op jit(solution)/shard_map/pallas_call | solution.py:614
  23.9 3.5 %all-to-all-done.total_ref = f32[32,3,4,128]{3,2,1,0:T(4,128)S(1)} async-done(((f32[32,3,4,128]{3,2,1,0:T(4,128)}), f32[32,3,4,128]{3,2,1,0:T(4,128)S(1)}, u32[]{:S(2)}, u32[]{:S(2)}) %all-to-all-start) | async-done | bytes 196640 | tf_op jit(solution)/shard_map/all_to_all | solution.py:645
  27.3 1.3 %shard_map.99 = (f32[4,64,128]{2,1,0:T(8,128)}, f32[4,64,128]{2,1,0:T(8,128)}) custom-call(f32[4,64,128]{2,1,0:T(8,128)S(1)} %get-tuple-element.42.conc_ref, f32[4,64,128]{2,1,0:T(8,128)S(1)} %get-tuple-element.43.pot_ref, f32[4,64,128]{2,1,0:T(8,128)S(1)} %get-tuple-element.47.mass_ref, f32[4,64,128]{2,1,0:T(8,128)S(1)} %get-tuple-element.48.pots_ref, ...), custom_call_target="tpu_custom_call" | custom-call | tf_op jit(solution)/shard_map/pallas_call | solution.py:614
Async XLA Ops:
  0.6 11.5 %copy-start.1 = (f32[4,64,128]{2,1,0:T(8,128)S(1)}, f32[4,64,128]{2,1,0:T(8,128)}, u32[]{:S(2)}) copy-start(f32[4,64,128]{2,1,0:T(8,128)} %pots_ref.5) | copy-start | bytes 393220
  0.6 11.5 %copy-start = (f32[4,64,128]{2,1,0:T(8,128)S(1)}, f32[4,64,128]{2,1,0:T(8,128)}, u32[]{:S(2)}) copy-start(f32[4,64,128]{2,1,0:T(8,128)} %mass_ref.5) | copy-start | bytes 393220
  0.7 11.5 %copy-start.3 = (f32[4,64,128]{2,1,0:T(8,128)S(1)}, f32[4,64,128]{2,1,0:T(8,128)}, u32[]{:S(2)}) copy-start(f32[4,64,128]{2,1,0:T(8,128)} %pot_ref.3) | copy-start | bytes 393220
  0.7 11.5 %copy-start.2 = (f32[4,64,128]{2,1,0:T(8,128)S(1)}, f32[4,64,128]{2,1,0:T(8,128)}, u32[]{:S(2)}) copy-start(f32[4,64,128]{2,1,0:T(8,128)} %conc_ref.3) | copy-start | bytes 393220
  0.7 11.5 %copy-start.5 = (s32[4,64,128]{2,1,0:T(8,128)S(1)}, s32[4,64,128]{2,1,0:T(8,128)}, u32[]{:S(2)}) copy-start(s32[4,64,128]{2,1,0:T(8,128)} %class_ref) | copy-start | bytes 393220
  0.7 11.5 %copy-start.4 = (s32[4,64,128]{2,1,0:T(8,128)S(1)}, s32[4,64,128]{2,1,0:T(8,128)}, u32[]{:S(2)}) copy-start(s32[4,64,128]{2,1,0:T(8,128)} %mask_ref) | copy-start | bytes 393220
  2.0 10.2 %copy-start.6 = (s32[8,64]{1,0:T(8,128)S(1)}, s32[8,64]{1,0:T(8,128)}, u32[]{:S(2)}) copy-start(s32[8,64]{1,0:T(8,128)} %owner_ref.3) | copy-start | bytes 6148
  2.0 10.1 %collective-permute-start.2 = (f32[200,128]{1,0:T(8,128)S(1)}, f32[200,128]{1,0:T(8,128)S(1)}, u32[]{:S(2)}, u32[]{:S(2)}) collective-permute-start(f32[200,128]{1,0:T(8,128)S(1)} %get-tuple-element.30), channel_id=1, source_target_pairs={{1,2},{2,1},{5,6},{6,5},{9,10},{10,9},{13,14},{14,13},{17,18},{18,... | collective-permute-start | bytes 307208 | tf_op jit(solution)/shard_map/ppermute | solution.py:632
  2.7 11.2 %collective-permute-start = (f32[192,128]{1,0:T(8,128)S(1)}, f32[192,128]{1,0:T(8,128)S(1)}, u32[]{:S(2)}, u32[]{:S(2)}) collective-permute-start(f32[192,128]{1,0:T(8,128)S(1)} %get-tuple-element.28), channel_id=1, source_target_pairs={{4,8},{12,16},{20,24},{8,4},{16,12},{24,20},{5,9},{13,17},{21,25},... | collective-permute-start | bytes 294920 | tf_op jit(solution)/shard_map/ppermute | solution.py:632
  3.4 8.8 %copy-start.7 = (f32[8]{0:T(128)S(1)}, f32[8]{0:T(128)}, u32[]{:S(2)}) copy-start(f32[8]{0:T(128)} %table_ref.1) | copy-start | bytes 100
  3.4 10.5 %collective-permute-start.1 = (f32[192,128]{1,0:T(8,128)S(1)}, f32[192,128]{1,0:T(8,128)S(1)}, u32[]{:S(2)}, u32[]{:S(2)}) collective-permute-start(f32[192,128]{1,0:T(8,128)S(1)} %get-tuple-element.29), channel_id=1, source_target_pairs={{0,4},{8,12},{16,20},{24,28},{4,0},{12,8},{20,16},{28,24},{1,5},{9... | collective-permute-start | bytes 294920 | tf_op jit(solution)/shard_map/ppermute | solution.py:632
  7.7 6.2 %collective-permute-start.3 = (f32[40,128]{1,0:T(8,128)S(1)}, f32[40,128]{1,0:T(8,128)S(1)}, u32[]{:S(2)}, u32[]{:S(2)}) collective-permute-start(f32[40,128]{1,0:T(8,128)S(1)} %get-tuple-element.32), channel_id=1, source_target_pairs={{0,1},{2,3},{1,0},{3,2},{4,5},{6,7},{5,4},{7,6},{8,9},{10,11},{9,8... | collective-permute-start | bytes 61448 | tf_op jit(solution)/shard_map/ppermute | solution.py:632
  15.2 12.2 %all-to-all-start = ((f32[32,3,4,128]{3,2,1,0:T(4,128)}), f32[32,3,4,128]{3,2,1,0:T(4,128)S(1)}, u32[]{:S(2)}, u32[]{:S(2)}) async-start(f32[32,3,4,128]{3,2,1,0:T(4,128)} %get-tuple-element.53), calls=%async_computation | async-start | bytes 393216 | tf_op jit(solution)/shard_map/all_to_all | solution.py:645
  18.7 3.9 %collective-permute-start.4 = (f32[136,128]{1,0:T(8,128)S(1)}, f32[136,128]{1,0:T(8,128)S(1)}, u32[]{:S(2)}, u32[]{:S(2)}) collective-permute-start(f32[136,128]{1,0:T(8,128)S(1)} %get-tuple-element.44), channel_id=1, source_target_pairs={{4,8},{12,16},{20,24},{8,4},{16,12},{24,20},{5,9},{13,17},{21,25},... | collective-permute-start | bytes 208904 | tf_op jit(solution)/shard_map/ppermute | solution.py:632
  19.4 4.1 %collective-permute-start.5 = (f32[136,128]{1,0:T(8,128)S(1)}, f32[136,128]{1,0:T(8,128)S(1)}, u32[]{:S(2)}, u32[]{:S(2)}) collective-permute-start(f32[136,128]{1,0:T(8,128)S(1)} %get-tuple-element.45), channel_id=1, source_target_pairs={{0,4},{8,12},{16,20},{24,28},{4,0},{12,8},{20,16},{28,24},{1,5},{9... | collective-permute-start | bytes 208904 | tf_op jit(solution)/shard_map/ppermute | solution.py:632
